TPU v7x, 32 devices: a whole 2x2x4 slice. The times are simulated.
32 devices in a mesh: dp: 16 (over z, y, core), ctx: 2 (over x).
Axes of the slice: x: 2, y: 2, z: 4, core: 2. Of those that a mesh axis runs over, the one named last changes fastest.
Arguments:
- patch_in: bfloat16 [32, 1024, 1024], P('dp', 'ctx'), may hold values from -6 to 6
- cls_in: bfloat16 [32, 1024], P('dp'), may hold values from -6 to 6
- d_patch: bfloat16 [32, 1024, 1024], P('dp', 'ctx'), may hold values from -6 to 6
- d_cls: bfloat16 [32, 1024], P('dp'), may hold values from -6 to 6
- image_valid: int32 [32], P('dp'), may hold values 0 or 1
- patch_coords: int32 [1024, 2], P('ctx'), may hold values from 0 to 31
- w_query: bfloat16 [1024, 1024], P(('dp', 'ctx')), may hold values from -0.1875 to 0.1875
- w_key: bfloat16 [1024, 1024], P(('dp', 'ctx')), may hold values from -0.1875 to 0.1875
- w_value: bfloat16 [1024, 1024], P(('dp', 'ctx')), may hold values from -0.1875 to 0.1875
- w_gate: bfloat16 [1024, 2730], P(('dp', 'ctx')), may hold values from -0.1875 to 0.1875
- w_up: bfloat16 [1024, 2730], P(('dp', 'ctx')), may hold values from -0.1875 to 0.1875
- w_out: bfloat16 [1024, 1024], P(None, ('dp', 'ctx')), may hold values from -1 to 1
- w_down: bfloat16 [2730, 1024], P(None, ('dp', 'ctx')), may hold values from -0.109375 to 0.109375
- layer_vectors: bfloat16 [8, 1024], P(None, ('dp', 'ctx')), may hold values from -1.25 to 1.25
- ffn_vectors: bfloat16 [4, 2730], replicated, may hold values from -2 to 2
Outputs:
- patch_out: bfloat16 [32, 1024, 1024], P('dp', 'ctx')
- cls_out: bfloat16 [32, 1024], P('dp')
- patch_grad: bfloat16 [32, 1024, 1024], P('dp', 'ctx')
- cls_grad: bfloat16 [32, 1024], P('dp')
- grad_w_query: float32 [1024, 1024], P(('dp', 'ctx'))
- grad_w_key: float32 [1024, 1024], P(('dp', 'ctx'))
- grad_w_value: float32 [1024, 1024], P(('dp', 'ctx'))
- grad_w_gate: float32 [1024, 2730], P(('dp', 'ctx'))
- grad_w_up: float32 [1024, 2730], P(('dp', 'ctx'))
- grad_w_out: float32 [1024, 1024], P(None, ('dp', 'ctx'))
- grad_w_down: float32 [2730, 1024], P(None, ('dp', 'ctx'))
- grad_layer_vectors: float32 [8, 1024], P(None, ('dp', 'ctx'))
- grad_ffn_vectors: float32 [4, 2730], replicated
All inputs are finite; a program needn't handle non-finite values. No bound on the sum of `image_valid` on one device may be relied on, other than what follows from the above.
Results may differ from a plain program's by a relative error of at most 0.015.
Values may be sent and summed in bfloat16 or wider, within the bound.
No kernel may reach another device: no remote copies, remote signals or barrier semaphores. Data moves between devices by JAX's collectives and lax.ppermute only.
A program may use at most 256 MiB of HBM per device.

v0:
```python
import jax
import jax.numpy as jnp
from jax import lax
from jax.sharding import PartitionSpec as P

HD = 64
MICRO = 2


epsilon = 1e-06


def layer_norm(values, gain, shift):
    centred = values - jnp.mean(values, axis=-1, keepdims=True)
    inv_std = lax.rsqrt(jnp.mean(centred * centred, axis=-1, keepdims=True) + epsilon)
    unit_rows = centred * inv_std
    return (unit_rows * gain + shift, unit_rows, inv_std)


def norm_back(grad_out, gain, unit_rows, inv_std, row_mask):
    scaled = grad_out * gain
    grad_in = inv_std * (
        scaled
        - jnp.mean(scaled, axis=-1, keepdims=True)
        - unit_rows * jnp.mean(scaled * unit_rows, axis=-1, keepdims=True)
    )
    weighted = grad_out * row_mask
    return (grad_in, jnp.sum(weighted * unit_rows, axis=(0, 1)), jnp.sum(weighted, axis=(0, 1)))


def rotary_tables(coords):
    freqs = 10000.0 ** (-jnp.arange(16).astype(jnp.float32) / 16.0)
    along_rows = coords[:, 0:1].astype(jnp.float32) * freqs[None, :]
    along_cols = coords[:, 1:2].astype(jnp.float32) * freqs[None, :]
    angles = jnp.concatenate([along_rows, along_rows, along_cols, along_cols], axis=1)
    cosines = jnp.concatenate([jnp.ones((1, 64), jnp.float32), jnp.cos(angles)], axis=0)
    sines = jnp.concatenate([jnp.zeros((1, 64), jnp.float32), jnp.sin(angles)], axis=0)
    return (cosines, sines)


def rotate(values, cosines, sines):
    swapped = jnp.concatenate(
        [-values[..., 16:32], values[..., 0:16], -values[..., 48:64], values[..., 32:48]], axis=-1
    )
    return values * cosines[:, None, :] + swapped * sines[:, None, :]


def unrotate(grads, cosines, sines):
    with_sin = grads * sines[:, None, :]
    moved = jnp.concatenate(
        [with_sin[..., 16:32], -with_sin[..., 0:16], with_sin[..., 48:64], -with_sin[..., 32:48]],
        axis=-1,
    )
    return grads * cosines[:, None, :] + moved


def project(rows_in, weight):
    return jnp.einsum("brd,de->bre", rows_in, weight, preferred_element_type=jnp.float32)


def project_back(grads, weight):
    return jnp.einsum("bre,de->brd", grads, weight, preferred_element_type=jnp.float32)


def weight_grad(rows_in, grads):
    return jnp.einsum("brd,bre->de", rows_in, grads, preferred_element_type=jnp.float32)


def fetch_forward(w_query, w_key, w_value, w_gate, w_up, w_out, w_down, layer_vectors):
    first_group = (
        lax.all_gather(w_query, ("dp", "ctx"), axis=0, tiled=True),
        lax.all_gather(w_key, ("dp", "ctx"), axis=0, tiled=True),
        lax.all_gather(w_value, ("dp", "ctx"), axis=0, tiled=True),
        lax.all_gather(w_gate, ("dp", "ctx"), axis=0, tiled=True),
        lax.all_gather(w_up, ("dp", "ctx"), axis=0, tiled=True),
    )
    second_group = (
        lax.all_gather(w_out, ("dp", "ctx"), axis=1, tiled=True),
        lax.all_gather(w_down, ("dp", "ctx"), axis=1, tiled=True),
        lax.all_gather(layer_vectors, ("dp", "ctx"), axis=1, tiled=True),
    )
    return tuple(first_group) + tuple(second_group)


def fetch_backward(w_query, w_key, w_value, w_gate, w_up, w_out, w_down, layer_vectors):
    first_group = (
        lax.all_gather(w_query, ("dp", "ctx"), axis=0, tiled=True),
        lax.all_gather(w_key, ("dp", "ctx"), axis=0, tiled=True),
        lax.all_gather(w_value, ("dp", "ctx"), axis=0, tiled=True),
        lax.all_gather(w_gate, ("dp", "ctx"), axis=0, tiled=True),
        lax.all_gather(w_up, ("dp", "ctx"), axis=0, tiled=True),
    )
    second_group = (
        lax.all_gather(w_out, ("dp", "ctx"), axis=1, tiled=True),
        lax.all_gather(w_down, ("dp", "ctx"), axis=1, tiled=True),
        lax.all_gather(layer_vectors, ("dp", "ctx"), axis=1, tiled=True),
    )
    return tuple(first_group) + tuple(second_group)


def head_forward(item):
    block_of_queries, block_of_keys, block_of_values = item
    logit_scores = jnp.einsum(
        "wey,wmy->wem", block_of_queries, block_of_keys, preferred_element_type=jnp.float32
    )
    row_peak = jnp.max(logit_scores, axis=-1, keepdims=True)
    shifted = jnp.exp(logit_scores - row_peak)
    denominator = jnp.sum(shifted, axis=-1, keepdims=True)
    reduced_probabilities = (shifted / denominator).astype(jnp.bfloat16)
    blended_values = jnp.einsum(
        "sce,sem->scm", reduced_probabilities, block_of_values, preferred_element_type=jnp.float32
    )
    return (blended_values, (row_peak + jnp.log(denominator))[..., 0])


def forward_pass(tokens, weights, ffn_vec, cosines, sines):
    w_query, w_key, w_value, w_gate, w_up, w_out, w_down, vectors_low = weights
    vectors = vectors_low.astype(jnp.float32)
    batch, row_count, model_width = tokens.shape
    heads = model_width // HD
    normed, unit_one, std_one = layer_norm(tokens, vectors[0], vectors[1])
    normed_low = normed.astype(jnp.bfloat16)
    queries = project(normed_low, w_query) + vectors[2]
    keys_raw = project(normed_low, w_key)
    values_low = (project(normed_low, w_value) + vectors[3]).astype(jnp.bfloat16)
    q_rot = (
        rotate(queries.reshape(batch, row_count, heads, HD), cosines, sines) * HD ** (-0.5)
    ).astype(jnp.bfloat16)
    k_flat = (
        rotate(keys_raw.reshape(batch, row_count, heads, HD), cosines, sines)
        .astype(jnp.bfloat16)
        .reshape(batch, row_count, model_width)
    )
    far_keys, far_values = (
        lax.all_gather(k_flat[:, 1:], "ctx", axis=1, tiled=True),
        lax.all_gather(values_low[:, 1:], "ctx", axis=1, tiled=True),
    )
    all_keys = jnp.concatenate([k_flat[:, :1], far_keys], axis=1)
    all_values = jnp.concatenate([values_low[:, :1], far_values], axis=1)
    length = all_keys.shape[1]
    head_queries = q_rot.transpose(2, 0, 1, 3)
    head_keys = all_keys.reshape(batch, length, heads, HD).transpose(2, 0, 1, 3)
    head_values = all_values.reshape(batch, length, heads, HD).transpose(2, 0, 1, 3)
    head_out, log_sums = lax.map(head_forward, (head_queries, head_keys, head_values))
    attended = (
        head_out.transpose(1, 2, 0, 3).reshape(batch, row_count, model_width).astype(jnp.bfloat16)
    )
    middle = tokens + (project(attended, w_out) + vectors[4])
    normed_two, unit_two, std_two = layer_norm(middle, vectors[5], vectors[6])
    normed_two_low = normed_two.astype(jnp.bfloat16)
    gate_proj = project(normed_two_low, w_gate) + ffn_vec[0]
    up_proj = project(normed_two_low, w_up) + ffn_vec[1]
    activated = jax.nn.silu(gate_proj)
    inner_act, unit_three, std_three = layer_norm(activated * up_proj, ffn_vec[2], ffn_vec[3])
    inner_low = inner_act.astype(jnp.bfloat16)
    result = middle + (project(inner_low, w_down) + vectors[7])
    saved = (
        normed_low,
        unit_one,
        std_one,
        head_queries,
        head_keys,
        head_values,
        log_sums,
        attended,
        unit_two,
        std_two,
        normed_two_low,
        gate_proj,
        up_proj,
        activated,
        unit_three,
        std_three,
        inner_low,
    )
    return (result, saved)


def backward_pass(grad_rows, weights, ffn_vec, cosines, sines, saved, row_mask):
    w_query, w_key, w_value, w_gate, w_up, w_out, w_down, vectors_low = weights
    vectors = vectors_low.astype(jnp.float32)
    (
        normed_low,
        unit_one,
        std_one,
        head_queries,
        head_keys,
        head_values,
        log_sums,
        attended,
        unit_two,
        std_two,
        normed_two_low,
        gate_proj,
        up_proj,
        activated,
        unit_three,
        std_three,
        inner_low,
    ) = saved
    batch, row_count, model_width = grad_rows.shape
    heads = model_width // HD
    reduced_mask = row_mask.astype(jnp.bfloat16)
    branch_low = grad_rows.astype(jnp.bfloat16)
    grad_down = weight_grad(inner_low, branch_low * reduced_mask)
    grad_inner = project_back(branch_low, w_down)
    grad_mix, gain_three, shift_three = norm_back(
        grad_inner, ffn_vec[2], unit_three, std_three, row_mask
    )
    sigmoid_gate = jax.nn.sigmoid(gate_proj)
    gate_low = (
        grad_mix * up_proj * sigmoid_gate * (1.0 + gate_proj * (1.0 - sigmoid_gate))
    ).astype(jnp.bfloat16)
    up_low = (grad_mix * activated).astype(jnp.bfloat16)
    grad_gate_w = weight_grad(normed_two_low * reduced_mask, gate_low)
    grad_up_w = weight_grad(normed_two_low * reduced_mask, up_low)
    grad_normed_two = project_back(gate_low, w_gate) + project_back(up_low, w_up)
    grad_mid_norm, gain_two, shift_two = norm_back(
        grad_normed_two, vectors[5], unit_two, std_two, row_mask
    )
    grad_middle = grad_rows + grad_mid_norm
    out_low = grad_middle.astype(jnp.bfloat16)
    grad_out_w = weight_grad(attended * reduced_mask, out_low)
    attended_grad = project_back(out_low, w_out).astype(jnp.bfloat16)
    head_grads = attended_grad.reshape(batch, row_count, heads, HD).transpose(2, 0, 1, 3)

    def head_backward(item):
        block_of_queries, block_of_keys, block_of_values, block_gradient, log_block = item
        logit_scores = jnp.einsum(
            "wey,wmy->wem", block_of_queries, block_of_keys, preferred_element_type=jnp.float32
        )
        attn_probs = jnp.exp(logit_scores - log_block[..., None])
        grad_probs = jnp.einsum(
            "wey,wmy->wem", block_gradient, block_of_values, preferred_element_type=jnp.float32
        )
        inner_sum = jnp.sum(attn_probs * grad_probs, axis=-1, keepdims=True)
        score_gradients = (attn_probs * (grad_probs - inner_sum)).astype(jnp.bfloat16)
        grad_query = jnp.einsum(
            "sce,sem->scm", score_gradients, block_of_keys, preferred_element_type=jnp.float32
        )
        grad_key = jnp.einsum(
            "ipz,iph->izh",
            score_gradients * reduced_mask,
            block_of_queries,
            preferred_element_type=jnp.float32,
        )
        grad_value = jnp.einsum(
            "ipz,iph->izh",
            attn_probs.astype(jnp.bfloat16) * reduced_mask,
            block_gradient,
            preferred_element_type=jnp.float32,
        )
        return (grad_query, grad_key, grad_value)

    grad_q_heads, grad_k_heads, grad_v_heads = lax.map(
        head_backward, (head_queries, head_keys, head_values, head_grads, log_sums)
    )
    length = head_keys.shape[2]
    grad_keys = grad_k_heads.transpose(1, 2, 0, 3).reshape(batch, length, model_width)
    grad_values = grad_v_heads.transpose(1, 2, 0, 3).reshape(batch, length, model_width)
    own_keys, own_values = (
        lax.psum_scatter(
            grad_keys[:, 1:].astype(jnp.bfloat16), "ctx", scatter_dimension=1, tiled=True
        ).astype(jnp.float32),
        lax.psum_scatter(
            grad_values[:, 1:].astype(jnp.bfloat16), "ctx", scatter_dimension=1, tiled=True
        ).astype(jnp.float32),
    )
    class_keys, class_values = lax.psum((grad_keys[:, :1], grad_values[:, :1]), "ctx")
    key_rows = jnp.concatenate([class_keys, own_keys], axis=1).reshape(batch, row_count, heads, HD)
    value_rows = jnp.concatenate([class_values, own_values], axis=1)
    key_low = (
        unrotate(key_rows, cosines, sines)
        .reshape(batch, row_count, model_width)
        .astype(jnp.bfloat16)
    )
    value_low = value_rows.astype(jnp.bfloat16)
    query_rows = grad_q_heads.transpose(1, 2, 0, 3)
    query_low = (
        (unrotate(query_rows, cosines, sines) * HD ** (-0.5))
        .reshape(batch, row_count, model_width)
        .astype(jnp.bfloat16)
    )
    grad_query_w = weight_grad(normed_low * reduced_mask, query_low)
    grad_key_w = weight_grad(normed_low * reduced_mask, key_low)
    grad_value_w = weight_grad(normed_low * reduced_mask, value_low)
    grad_normed = (
        project_back(query_low, w_query)
        + project_back(key_low, w_key)
        + project_back(value_low, w_value)
    )
    grad_in_norm, gain_one, shift_one = norm_back(
        grad_normed, vectors[0], unit_one, std_one, row_mask
    )
    grad_tokens = grad_middle + grad_in_norm

    def column_sum(rounded):
        return jnp.sum(rounded.astype(jnp.float32) * row_mask, axis=(0, 1))

    vector_grads = jnp.stack(
        [
            gain_one,
            shift_one,
            column_sum(query_low),
            column_sum(value_low),
            column_sum(out_low),
            gain_two,
            shift_two,
            column_sum(branch_low),
        ]
    )
    ffn_grads = jnp.stack([column_sum(gate_low), column_sum(up_low), gain_three, shift_three])
    return (
        grad_tokens,
        (
            (grad_query_w, grad_key_w, grad_value_w, grad_gate_w, grad_up_w),
            (grad_out_w, grad_down, vector_grads),
            ffn_grads,
        ),
    )


def on_device(
    patch_in,
    cls_in,
    d_patch,
    d_cls,
    image_valid,
    patch_coords,
    w_query,
    w_key,
    w_value,
    w_gate,
    w_up,
    w_out,
    w_down,
    layer_vectors,
    ffn_vectors,
):
    images, patch_rows, model_width = patch_in.shape
    group_size = images // MICRO
    cosines, sines = rotary_tables(patch_coords)
    first_flag = (lax.axis_index("ctx") == 0).astype(jnp.float32)
    row_weight = jnp.concatenate([first_flag[None], jnp.ones((patch_rows,), jnp.float32)])
    row_mask = row_weight[None, :, None]
    ffn_vec = ffn_vectors.astype(jnp.float32)
    keep_mask = image_valid.astype(jnp.float32)
    results = []
    totals = None
    for micro_step in range(MICRO):
        first_image = micro_step * group_size
        last_image = first_image + group_size
        tokens = jnp.concatenate(
            [cls_in[first_image:last_image, None, :], patch_in[first_image:last_image]], axis=1
        ).astype(jnp.float32)
        weights = fetch_forward(w_query, w_key, w_value, w_gate, w_up, w_out, w_down, layer_vectors)
        result, saved = forward_pass(tokens, weights, ffn_vec, cosines, sines)
        keep_rows = keep_mask[first_image:last_image][:, None, None]
        grad_rows = (
            jnp.concatenate(
                [d_cls[first_image:last_image, None, :], d_patch[first_image:last_image]], axis=1
            ).astype(jnp.float32)
            * keep_rows
        )
        back_weights = fetch_backward(
            w_query, w_key, w_value, w_gate, w_up, w_out, w_down, layer_vectors
        )
        grad_tokens, weight_grads = backward_pass(
            grad_rows, back_weights, ffn_vec, cosines, sines, saved, row_mask
        )
        if totals is None:
            totals = weight_grads
        else:
            totals = jax.tree.map(lambda first, second: first + second, totals, weight_grads)
        results.append(
            ((result * keep_rows).astype(jnp.bfloat16), grad_tokens.astype(jnp.bfloat16))
        )
    out_rows = jnp.concatenate([entry[0] for entry in results], axis=0)
    grad_out_rows = jnp.concatenate([entry[1] for entry in results], axis=0)
    in_grads, out_grads, ffn_total = totals
    owned_in = (
        lax.psum_scatter(in_grads[0], ("dp", "ctx"), scatter_dimension=0, tiled=True),
        lax.psum_scatter(in_grads[1], ("dp", "ctx"), scatter_dimension=0, tiled=True),
        lax.psum_scatter(in_grads[2], ("dp", "ctx"), scatter_dimension=0, tiled=True),
        lax.psum_scatter(in_grads[3], ("dp", "ctx"), scatter_dimension=0, tiled=True),
        lax.psum_scatter(in_grads[4], ("dp", "ctx"), scatter_dimension=0, tiled=True),
    )
    owned_out = (
        lax.psum_scatter(out_grads[0], ("dp", "ctx"), scatter_dimension=1, tiled=True),
        lax.psum_scatter(out_grads[1], ("dp", "ctx"), scatter_dimension=1, tiled=True),
        lax.psum_scatter(out_grads[2], ("dp", "ctx"), scatter_dimension=1, tiled=True),
    )
    ffn_summed = lax.psum(ffn_total, ("dp", "ctx"))
    return (
        out_rows[:, 1:],
        out_rows[:, 0],
        grad_out_rows[:, 1:],
        grad_out_rows[:, 0],
        owned_in[0],
        owned_in[1],
        owned_in[2],
        owned_in[3],
        owned_in[4],
        owned_out[0],
        owned_out[1],
        owned_out[2],
        ffn_summed,
    )


def solution(mesh):
    in_specs = (
        P("dp", "ctx", None),
        P("dp", None),
        P("dp", "ctx", None),
        P("dp", None),
        P("dp"),
        P("ctx", None),
        P(("dp", "ctx"), None),
        P(("dp", "ctx"), None),
        P(("dp", "ctx"), None),
        P(("dp", "ctx"), None),
        P(("dp", "ctx"), None),
        P(None, ("dp", "ctx")),
        P(None, ("dp", "ctx")),
        P(None, ("dp", "ctx")),
        P(),
    )
    out_specs = (
        P("dp", "ctx", None),
        P("dp", None),
        P("dp", "ctx", None),
        P("dp", None),
        P(("dp", "ctx"), None),
        P(("dp", "ctx"), None),
        P(("dp", "ctx"), None),
        P(("dp", "ctx"), None),
        P(("dp", "ctx"), None),
        P(None, ("dp", "ctx")),
        P(None, ("dp", "ctx")),
        P(None, ("dp", "ctx")),
        P(),
    )
    return jax.shard_map(
        on_device, mesh=mesh, in_specs=in_specs, out_specs=out_specs, check_vma=False
    )
```

profile of v0, /device:TPU:0, one launch (start us, length us, event | category | flops | bytes accessed | tf_op | source)
XLA Modules:
  0.0 2692.3 jit_solution(989970054586246763)
XLA Ops:
  9.5 70.5 %all-gather = bf16[32,32,8]{1,2,0:T(8,128)(2,1)S(1)} all-gather(bf16[1,32,8]{1,2,0:T(8,128)(2,1)} %bitcast.532), channel_id=1, replica_groups=mesh['dp'=16,'ctx'=2] {'dp','ctx'}, dimensions={0}, use_global_device_ids=true | all-gather | bytes 16896 | tf_op jit(solution)/shard_map/all_gather | solution.py:80
  80.8 4.7 slice_bitcast_fusion.8
  96.4 4.7 fusion.210
  105.7 4.9 fusion.215
  115.2 6.4 fusion.147
  123.8 12.4 all-gather.21.cloned.1.call-start
  162.1 24.9 all-gather.13.cloned.1.call-done
  187.0 5.0 convolution_add_fusion.9
  194.2 5.2 convolution_add_fusion.10
  213.4 7.0 all-gather.17.cloned.1.call-done
  226.9 3.8 copy.118
  230.7 24.2 all-gather.21.cloned.1.call-done
  259.7 5.5 copy.119
  265.3 62.3 %while.52 = (s32[]{:T(128)}, bf16[16,1,513,64]{2,3,1,0:T(8,128)(2,1)S(1)}, f32[16,1,513]{2,1,0:T(1,128)S(1)}, bf16[16,1,513,64]{3,2,1,0:T(8,128)(2,1)}, bf16[16,...) while((s32[]{:T(128)}, bf16[16,1,513,64]{2,3,1,0:T(8,128)(2,1)S(1)}, ...), condition=%wide.region_5.6_spmd, body=%wide.region_2.5_spmd.sunk | while | flops 137765632 | bytes 7457401 | solution.py:144
  333.4 5.4 copy.128
  343.5 5.5 copy.129
  349.0 62.6 %while.53 = (s32[]{:T(128)}, bf16[16,1,513,64]{2,3,1,0:T(8,128)(2,1)S(1)}, f32[16,1,513]{2,1,0:T(1,128)S(1)}, bf16[16,1,513,64]{3,2,1,0:T(8,128)(2,1)}, bf16[16,...) while((s32[]{:T(128)}, bf16[16,1,513,64]{2,3,1,0:T(8,128)(2,1)S(1)}, ...), condition=%wide.region_15.16_spmd, body=%wide.region_12.15_spmd.sunk | while | flops 137765632 | bytes 7457401 | solution.py:144
  411.7 4.1 fusion.232
  421.7 31.2 %all-gather.25.cloned.1.call-done = bf16[1024,2730]{1,0:T(8,128)(2,1)} async-done(((bf16[32,2730]{1,0:T(8,128)(2,1)}), bf16[1024,2730]{1,0:T(8,128)(2,1)}) %all-gather.25.cloned.1.call-update) | async-done | bytes 5591056 | tf_op jit(solution)/shard_map/all_gather | solution.py:74
  452.9 7.8 fusion.236
  460.8 5.0 fusion.234
  465.8 56.1 %all-gather.27.cloned.1.call-done = bf16[1024,2730]{1,0:T(8,128)(2,1)} async-done(((bf16[32,2730]{1,0:T(8,128)(2,1)}), bf16[1024,2730]{1,0:T(8,128)(2,1)}) %all-gather.27.cloned.1.call-update) | async-done | bytes 5591056 | tf_op jit(solution)/shard_map/all_gather | solution.py:75
  521.9 7.7 fusion.235
  529.6 12.7 fusion.218
  546.5 44.5 %all-gather.29.cloned.1.call-done = bf16[2730,1024]{0,1:T(8,128)(2,1)} async-done(((bf16[2730,32]{0,1:T(8,128)(2,1)}), bf16[2730,1024]{0,1:T(8,128)(2,1)}) %all-gather.29.cloned.1.call-update) | async-done | bytes 5591056 | tf_op jit(solution)/shard_map/all_gather | solution.py:79
  591.1 9.0 fusion.173
  600.2 12.8 multiply_reduce_fusion.5
  613.0 17.6 multiply_reduce_fusion.4
  630.6 7.5 fusion.239
  638.2 5.3 fusion.237
  643.5 5.9 convolution_add_fusion.7
  649.4 7.6 multiply_reduce_fusion.22
  657.1 4.7 multiply_add_fusion
  672.9 191.5 %while.55 = (s32[]{:T(128)}, f32[16,1,513,64]{2,3,1,0:T(8,128)}, f32[16,1,1025,64]{2,3,1,0:T(8,128)}, f32[16,1,1025,64]{2,3,1,0:T(8,128)}, bf16[16,1,513,64]{3,2...) while((s32[]{:T(128)}, f32[16,1,513,64]{2,3,1,0:T(8,128)}, ...), condition=%wide.region_39.40_spmd, body=%wide.region_37.39_spmd.sunk | while | flops 341259904 | bytes 22123744 | solution.py:255
  869.6 4.4 slice.444
  881.2 191.7 %while.54 = (s32[]{:T(128)}, f32[16,1,513,64]{2,3,1,0:T(8,128)}, f32[16,1,1025,64]{2,3,1,0:T(8,128)}, f32[16,1,1025,64]{2,3,1,0:T(8,128)}, bf16[16,1,513,64]{3,2...) while((s32[]{:T(128)}, f32[16,1,513,64]{2,3,1,0:T(8,128)}, ...), condition=%wide.region_26.27_spmd, body=%wide.region_24.26_spmd.sunk | while | flops 341259904 | bytes 22123744 | solution.py:255
  1072.9 4.4 slice.445
  1091.8 4.3 slice.381
  1096.5 4.1 copy.159
  1111.1 52.6 %all-reduce.3 = (bf16[1,1,1024]{2,1,0:T(2,128)(2,1)S(1)}, f32[1,1,1024]{1,2,0:T(8,128)S(1)}, bf16[1,1,1024]{2,1,0:T(2,128)(2,1)S(1)}, f32[1,1,1024]{1,2,0:T(8,128)}) all-reduce(f32[1,1,1024]{2,1,0:T(1,128)S(1)} %copy.158, f32[1,1,1024]{1,2,0:T(8,128)} %slice.374, ...), channel_id=1, replica_groups=mesh['dp'=16,'ctx'=2] {'ctx'}, use_global_device_ids=true, to_apply=%region_29.30 | all-reduce | flops 4096 | bytes 28672 | tf_op jit(solution)/shard_map/psum | solution.py:269
  1194.7 7.1 fusion.99
  1201.8 4.0 fusion.175
  1220.1 5.6 fusion.118
  1230.8 6.0 convolution_add_fusion.3
  1241.0 4.4 convolution_add_fusion.6
  1249.1 4.4 convolution_add_fusion.5
  1258.4 4.5 convolution_add_fusion.4
  1262.9 7.1 fusion.167
  1270.1 7.6 convolution_add_fusion.2
  1278.1 7.2 fusion.165
  1285.4 7.6 convolution_add_fusion.1
  1294.3 9.2 fusion.155
  1303.6 9.0 convolution_add_fusion
  1313.3 9.4 fusion.141
  1322.7 6.6 fusion.143
  1331.3 41.3 %psum.39 = f32[4,2730]{1,0:T(4,128)} all-reduce(f32[4,2730]{1,0:T(4,128)S(1)} %maximum_add_fusion.2), channel_id=1, replica_groups=mesh['dp'=16,'ctx'=2] {'dp','ctx'}, use_global_device_ids=true, to_apply=%region_78.79 | all-reduce | flops 10920 | bytes 87360 | tf_op jit(solution)/shard_map/psum | solution.py:393
  1376.2 3.9 fusion.152
  1384.2 121.2 %reduce-scatter.33.cloned.1.call-done = f32[1024,32]{0,1:T(8,128)} async-done(((f32[1024,1024]{0,1:T(8,128)}), f32[1024,32]{0,1:T(8,128)}) %reduce-scatter.33.cloned.1.call-update) | async-done | bytes 131088 | tf_op jit(solution)/shard_map/reduce_scatter | solution.py:389
  1505.4 141.5 %reduce-scatter.23.cloned.1.call-done = f32[32,1024]{1,0:T(8,128)} async-done(((f32[1024,1024]{1,0:T(8,128)}), f32[32,1024]{1,0:T(8,128)}) %reduce-scatter.23.cloned.1.call-update) | async-done | bytes 131088 | tf_op jit(solution)/shard_map/reduce_scatter | solution.py:382
  1646.9 141.5 %reduce-scatter.25.cloned.1.call-done = f32[32,1024]{1,0:T(8,128)} async-done(((f32[1024,1024]{1,0:T(8,128)}), f32[32,1024]{1,0:T(8,128)}) %reduce-scatter.25.cloned.1.call-update) | async-done | bytes 131088 | tf_op jit(solution)/shard_map/reduce_scatter | solution.py:383
  1788.4 142.0 %reduce-scatter.27.cloned.1.call-done = f32[32,1024]{1,0:T(8,128)} async-done(((f32[1024,1024]{1,0:T(8,128)}), f32[32,1024]{1,0:T(8,128)}) %reduce-scatter.27.cloned.1.call-update) | async-done | bytes 131088 | tf_op jit(solution)/shard_map/reduce_scatter | solution.py:384
  1930.5 248.9 %reduce-scatter.29.cloned.1.call-done = f32[32,2730]{1,0:T(8,128)} async-done(((f32[1024,2730]{1,0:T(8,128)}), f32[32,2730]{1,0:T(8,128)}) %reduce-scatter.29.cloned.1.call-update) | async-done | bytes 349456 | tf_op jit(solution)/shard_map/reduce_scatter | solution.py:385
  2179.4 253.1 %reduce-scatter.31.cloned.1.call-done = f32[32,2730]{1,0:T(8,128)} async-done(((f32[1024,2730]{1,0:T(8,128)}), f32[32,2730]{1,0:T(8,128)}) %reduce-scatter.31.cloned.1.call-update) | async-done | bytes 349456 | tf_op jit(solution)/shard_map/reduce_scatter | solution.py:386
  2432.4 253.1 %reduce-scatter.35.cloned.1.call-done = f32[2730,32]{0,1:T(8,128)} async-done(((f32[2730,1024]{0,1:T(8,128)}), f32[2730,32]{0,1:T(8,128)}) %reduce-scatter.35.cloned.1.call-update) | async-done | bytes 349456 | tf_op jit(solution)/shard_map/reduce_scatter | solution.py:390
  (1028 shorter events, 728.1 us)
Async XLA Ops:
  7.2 89.2 %all-gather.15.cloned.1.call-start = ((), (), s32[]{:S(2)}) async-start(), calls=%async_computation.13 | async-start | bytes 2162688 | tf_op jit(solution)/shard_map/all_gather | solution.py:72
  7.9 128.3 %all-gather.19.cloned.1.call-start = ((), (), s32[]{:S(2)}) async-start(), calls=%async_computation.15 | async-start | bytes 2162688 | tf_op jit(solution)/shard_map/all_gather | solution.py:73
  8.7 178.4 %all-gather.13.cloned.1.call-start = ((), (), s32[]{:S(2)}) async-start(), calls=%async_computation.12 | async-start | bytes 2162688 | tf_op jit(solution)/shard_map/all_gather | solution.py:71
  9.4 211.0 %all-gather.17.cloned.1.call-start = ((), (), s32[]{:S(2)}) async-start(), calls=%async_computation.14 | async-start | bytes 3145728 | tf_op jit(solution)/shard_map/all_gather | solution.py:135
  86.1 325.6 %copy-start.122 = (bf16[1,1024]{1,0:T(2,128)(2,1)}, bf16[1,1024]{1,0:T(2,128)(2,1)S(1)}, u32[]{:S(2)}) copy-start(bf16[1,1024]{1,0:T(2,128)(2,1)S(1)} %get-tuple-element.515) | copy-start | bytes 6148
  86.1 330.1 %copy-start.124 = (bf16[1,1024]{1,0:T(2,128)(2,1)}, bf16[1,1024]{1,0:T(2,128)(2,1)S(1)}, u32[]{:S(2)}) copy-start(bf16[1,1024]{1,0:T(2,128)(2,1)S(1)} %get-tuple-element.516) | copy-start | bytes 6148
  86.5 118.3 %copy-start.62 = (f32[513,64]{0,1:T(8,128)}, f32[513,64]{0,1:T(8,128)S(1)}, u32[]{:S(2)}) copy-start(f32[513,64]{0,1:T(8,128)S(1)} %concatenate.365) | copy-start | bytes 393988
  88.9 116.0 %copy-start.24 = (f32[513,64]{0,1:T(8,128)}, f32[513,64]{0,1:T(8,128)S(1)}, u32[]{:S(2)}) copy-start(f32[513,64]{0,1:T(8,128)S(1)} %concatenate.363) | copy-start | bytes 393988
  94.5 92.6 %copy-start.104 = (f32[513]{0:T(1024)}, f32[513]{0:T(1024)S(1)}, u32[]{:S(2)}) copy-start(f32[513]{0:T(1024)S(1)} %broadcast_multiply_fusion.19) | copy-start | bytes 6160
  95.1 99.0 %copy-start.106 = (f32[513]{0:T(1024)}, f32[513]{0:T(1024)S(1)}, u32[]{:S(2)}) copy-start(f32[513]{0:T(1024)S(1)} %broadcast_multiply_fusion.21) | copy-start | bytes 6160
  95.8 91.3 %copy-start.118 = (f32[513]{0:T(1024)}, f32[513]{0:T(1024)S(1)}, u32[]{:S(2)}) copy-start(f32[513]{0:T(1024)S(1)} %add_rsqrt_fusion.2) | copy-start | bytes 6160
  95.8 98.4 %copy-start.120 = (f32[513]{0:T(1024)}, f32[513]{0:T(1024)S(1)}, u32[]{:S(2)}) copy-start(f32[513]{0:T(1024)S(1)} %add_rsqrt_fusion.5) | copy-start | bytes 6160
  96.4 97.7 %copy-start.116 = (f32[1,1024]{1,0:T(1,128)}, f32[1,1024]{1,0:T(1,128)S(1)}, u32[]{:S(2)}) copy-start(f32[1,1024]{1,0:T(1,128)S(1)} %get-tuple-element.502) | copy-start | bytes 12292
  96.4 97.7 %copy-start.144 = (f32[1,1024]{1,0:T(1,128)}, f32[1,1024]{1,0:T(1,128)S(1)}, u32[]{:S(2)}) copy-start(f32[1,1024]{1,0:T(1,128)S(1)} %get-tuple-element.501) | copy-start | bytes 12292
  121.6 14.7 copy-start.53
  123.8 131.1 %all-gather.21.cloned.1.call-start = ((), (), s32[]{:S(2)}) async-start(), calls=%async_computation.16 | async-start | bytes 3145728 | tf_op jit(solution)/shard_map/all_gather | solution.py:136
  141.8 186.4 %all-gather.31.cloned.1.call-start = ((), (), s32[]{:S(2)}) async-start(), calls=%async_computation.21 | async-start | bytes 3145728 | tf_op jit(solution)/shard_map/all_gather | solution.py:135
  143.2 195.7 %all-gather.33.cloned.1.call-start = ((), (), s32[]{:S(2)}) async-start(), calls=%async_computation.22 | async-start | bytes 3145728 | tf_op jit(solution)/shard_map/all_gather | solution.py:136
  148.8 262.9 %all-gather.23.cloned.1.call-start = ((), (), s32[]{:S(2)}) async-start(), calls=%async_computation.17 | async-start | bytes 2162688 | tf_op jit(solution)/shard_map/all_gather | solution.py:78
  149.5 303.4 %all-gather.25.cloned.1.call-start = ((), (), s32[]{:S(2)}) async-start(), calls=%async_computation.18 | async-start | bytes 5947392 | tf_op jit(solution)/shard_map/all_gather | solution.py:74
  150.3 371.6 %all-gather.27.cloned.1.call-start = ((), (), s32[]{:S(2)}) async-start(), calls=%async_computation.19 | async-start | bytes 5947392 | tf_op jit(solution)/shard_map/all_gather | solution.py:75
  150.9 440.2 %all-gather.29.cloned.1.call-start = ((), (), s32[]{:S(2)}) async-start(), calls=%async_computation.20 | async-start | bytes 5947392 | tf_op jit(solution)/shard_map/all_gather | solution.py:79
  151.6 1012.1 %reduce-scatter.19.cloned.1.call-start = ((), (), s32[]{:S(2)}) async-start(), calls=%async_computation.25 | async-start | bytes 3145728 | tf_op jit(solution)/shard_map/reduce_scatter | solution.py:262
  159.4 497.7 %copy-start.134 = (bf16[1,1024]{1,0:T(2,128)(2,1)}, bf16[1,1024]{1,0:T(2,128)(2,1)S(1)}, u32[]{:S(2)}) copy-start(bf16[1,1024]{1,0:T(2,128)(2,1)S(1)} %get-tuple-element.509) | copy-start | bytes 6148
  328.2 88.0 %copy-start.22 = (bf16[16,1,513,64]{2,3,1,0:T(8,128)(2,1)}, bf16[16,1,513,64]{2,3,1,0:T(8,128)(2,1)S(1)}, u32[]{:S(2)}) copy-start(bf16[16,1,513,64]{2,3,1,0:T(8,128)(2,1)S(1)} %get-tuple-element.187) | copy-start | bytes 3151876
  421.7 100.2 %copy-start.86 = (bf16[513,1024]{1,0:T(8,128)(2,1)}, bf16[513,1024]{1,0:T(8,128)(2,1)S(1)}, u32[]{:S(2)}) copy-start(bf16[513,1024]{1,0:T(8,128)(2,1)S(1)} %get-tuple-element.506) | copy-start | bytes 3151876
  421.7 107.9 %copy-start.83 = (bf16[513,1024]{1,0:T(8,128)(2,1)}, bf16[513,1024]{1,0:T(8,128)(2,1)S(1)}, u32[]{:S(2)}) copy-start(bf16[513,1024]{1,0:T(8,128)(2,1)S(1)} %get-tuple-element.505) | copy-start | bytes 3151876
  452.9 7.8 copy-start.152
  542.3 70.7 %copy-start.111 = (f32[513]{0:T(1024)}, f32[513]{0:T(1024)S(1)}, u32[]{:S(2)}) copy-start(f32[513]{0:T(1024)S(1)} %broadcast_multiply_fusion.9) | copy-start | bytes 6160
  543.1 69.9 %copy-start.128 = (f32[513]{0:T(1024)}, f32[513]{0:T(1024)S(1)}, u32[]{:S(2)}) copy-start(f32[513]{0:T(1024)S(1)} %add_rsqrt_fusion.3) | copy-start | bytes 6160
  543.1 69.9 %copy-start.109 = (f32[513]{0:T(1024)}, f32[513]{0:T(1024)S(1)}, u32[]{:S(2)}) copy-start(f32[513]{0:T(1024)S(1)} %broadcast_multiply_fusion.8) | copy-start | bytes 6160
  544.7 46.3 %copy-start.47 = (bf16[512,1024]{1,0:T(8,128)(2,1)S(1)}, bf16[512,1024]{1,0:T(8,128)(2,1)}, u32[]{:S(2)}) copy-start(bf16[512,1024]{1,0:T(8,128)(2,1)} %get-tuple-element.471) | copy-start | bytes 3145732
  546.5 66.5 %copy-start.126 = (f32[513]{0:T(1024)}, f32[513]{0:T(1024)S(1)}, u32[]{:S(2)}) copy-start(f32[513]{0:T(1024)S(1)} %add_rsqrt_fusion) | copy-start | bytes 6160
  591.0 9.1 copy-start.6
  591.0 9.1 copy-start.8
  591.0 9.1 copy-start.49
  591.0 9.1 copy-start.102
  591.1 9.1 copy-start.108
  591.1 9.1 copy-start.136
  600.1 12.9 slice-start.4
  600.2 12.8 slice-start.5
  630.6 12.8 copy-start.64
  874.0 293.5 %reduce-scatter.15.cloned.1.call-start = ((), (), s32[]{:S(2)}) async-start(), calls=%async_computation.23 | async-start | bytes 3145728 | tf_op jit(solution)/shard_map/reduce_scatter | solution.py:262
  1077.3 124.5 %reduce-scatter.21.cloned.1.call-start = ((), (), s32[]{:S(2)}) async-start(), calls=%async_computation.26 | async-start | bytes 3145728 | tf_op jit(solution)/shard_map/reduce_scatter | solution.py:265
  1082.9 128.9 %reduce-scatter.17.cloned.1.call-start = ((), (), s32[]{:S(2)}) async-start(), calls=%async_computation.24 | async-start | bytes 3145728 | tf_op jit(solution)/shard_map/reduce_scatter | solution.py:265
  1111.0 271.9 %reduce-scatter.37.cloned.1.call-start = ((), (), s32[]{:S(2)}) async-start(), calls=%async_computation.34 | async-start | bytes 540672
  1217.1 8.6 copy-start.78
  1230.8 274.6 %reduce-scatter.33.cloned.1.call-start = ((), (), s32[]{:S(2)}) async-start(), calls=%async_computation.32 | async-start | bytes 4325376 | tf_op jit(solution)/shard_map/reduce_scatter | solution.py:389
  1236.9 410.0 %reduce-scatter.23.cloned.1.call-start = ((), (), s32[]{:S(2)}) async-start(), calls=%async_computation.27 | async-start | bytes 4325376 | tf_op jit(solution)/shard_map/reduce_scatter | solution.py:382
  1245.4 543.0 %reduce-scatter.25.cloned.1.call-start = ((), (), s32[]{:S(2)}) async-start(), calls=%async_computation.28 | async-start | bytes 4325376 | tf_op jit(solution)/shard_map/reduce_scatter | solution.py:383
  1253.6 676.9 %reduce-scatter.27.cloned.1.call-start = ((), (), s32[]{:S(2)}) async-start(), calls=%async_computation.29 | async-start | bytes 4325376 | tf_op jit(solution)/shard_map/reduce_scatter | solution.py:384
  1262.9 916.5 %reduce-scatter.29.cloned.1.call-start = ((), (), s32[]{:S(2)}) async-start(), calls=%async_computation.30 | async-start | bytes 11894784 | tf_op jit(solution)/shard_map/reduce_scatter | solution.py:385
  1277.7 1154.7 %reduce-scatter.31.cloned.1.call-start = ((), (), s32[]{:S(2)}) async-start(), calls=%async_computation.31 | async-start | bytes 11894784 | tf_op jit(solution)/shard_map/reduce_scatter | solution.py:386
  1293.0 10.5 slice-start
  1293.1 1392.5 %reduce-scatter.35.cloned.1.call-start = ((), (), s32[]{:S(2)}) async-start(), calls=%async_computation.33 | async-start | bytes 11894784 | tf_op jit(solution)/shard_map/reduce_scatter | solution.py:390
  1294.2 9.3 slice-start.1
  1294.3 9.3 copy-start.48
  1294.3 9.3 copy-start.110
  1294.3 9.3 copy-start.127
  1294.3 9.3 copy-start.135
  1312.6 10.1 slice-start.2
  1313.3 9.4 slice-start.3
  1313.3 9.4 copy-start.14
  1330.4 45.8 %copy-start.57 = (bf16[512,1024]{1,0:T(8,128)(2,1)S(1)}, bf16[512,1024]{1,0:T(8,128)(2,1)}, u32[]{:S(2)}) copy-start(bf16[512,1024]{1,0:T(8,128)(2,1)} %get-tuple-element.474) | copy-start | bytes 3145732
  (157 other events, 439.9 us)
Sparse Core Ops, SparseCore 0:
  11.0 59.2 all-gather.14
  73.3 55.3 all-gather.18
  131.6 55.3 all-gather.12
  188.4 31.9 all-gather.16
  221.8 33.1 all-gather.20
  256.4 33.1 all-gather.30
  291.1 33.1 all-gather.32
  327.2 56.5 all-gather.22
  386.7 66.1 all-gather.24
  455.7 66.1 all-gather.26
  524.8 66.1 all-gather.28
  874.1 30.7 reduce-scatter.18
  1077.4 30.8 reduce-scatter.14
  1110.9 50.6 reduce-scatter.20
  1163.8 33.7 reduce-scatter.16
  1230.9 133.4 reduce-scatter.36
  1367.2 138.1 reduce-scatter.32
  1508.2 138.6 reduce-scatter.22
  1649.9 138.5 reduce-scatter.24
  1791.2 139.1 reduce-scatter.26
  1933.5 245.8 reduce-scatter.28
  2182.4 250.0 reduce-scatter.30
  2435.4 250.0 reduce-scatter.34
where the time goes:
time: 2710 us; the launch traced here: 2690 us
  waiting for transfers between devices  1490 us (55%)
  matrix products  657 us (24%)
  local copies, waits for them, and re-layouts  218 us (8%)
  blocking collectives  164 us (6%)
  other arithmetic  126 us (5%)
    reduce_scatter x1, waiting for transfers between devices, on_device(): lax.psum_scatter(out_grads[1], ('dp', 'ctx'), scatter_dimension=1, tiled=...  253 us
    reduce_scatter x1, waiting for transfers between devices, on_device(): lax.psum_scatter(in_grads[4], ('dp', 'ctx'), scatter_dimension=0, tiled=T...  253 us
    reduce_scatter x1, waiting for transfers between devices, on_device(): lax.psum_scatter(in_grads[3], ('dp', 'ctx'), scatter_dimension=0, tiled=T...  249 us
    reduce_scatter x1, waiting for transfers between devices, on_device(): lax.psum_scatter(in_grads[2], ('dp', 'ctx'), scatter_dimension=0, tiled=T...  142 us
    reduce_scatter x1, waiting for transfers between devices, on_device(): lax.psum_scatter(in_grads[1], ('dp', 'ctx'), scatter_dimension=0, tiled=T...  142 us
    reduce_scatter x1, waiting for transfers between devices, on_device(): lax.psum_scatter(in_grads[0], ('dp', 'ctx'), scatter_dimension=0, tiled=T...  142 us
    reduce_scatter x1, waiting for transfers between devices, on_device(): lax.psum_scatter(out_grads[0], ('dp', 'ctx'), scatter_dimension=1, tiled=...  121 us
    dot_general x14, matrix products, project(): jnp.einsum('brd,de->bre', rows_in, weight, preferred_element_type=jnp.flo...  81.4 us
  transfers between devices with their start and end apart: 23, of which 13 were waited for; matrix products, arithmetic and copies ran while one was open for 25% of the time, Pallas kernels for 0%

commit v1 on v0

--- a/solution.py
+++ b/solution.py
@@ -1,6 +1,11 @@
+import functools
+import math
+
 import jax
 import jax.numpy as jnp
 from jax import lax
+from jax.experimental import pallas as pl
+from jax.experimental.pallas import tpu as pltpu
 from jax.sharding import PartitionSpec as P
 
 HD = 64
@@ -408,6 +413,424 @@
     )
 
 
+BOTH = ("dp", "ctx")
+BIT_X, BIT_CORE, BIT_Y, BIT_Z0, BIT_Z1 = 1, 2, 4, 8, 16
+ROWS = 1040
+KEYS = 1024
+HEAD_COLS = 256
+LOG2E = math.log2(math.e)
+F32 = jnp.float32
+BF16 = jnp.bfloat16
+
+
+def swap_over(value, bit):
+    count = lax.axis_size(BOTH)
+    return lax.ppermute(value, BOTH, [(i, i ^ bit) for i in range(count)])
+
+
+def joined(*parts, axis=0):
+    return jnp.concatenate(parts, axis=axis)
+
+
+def after(value, *deps):
+    return lax.optimization_barrier((value,) + deps)[0]
+
+
+def dot_nn(a, b):
+    return lax.dot_general(a, b, (((1,), (0,)), ((), ())), preferred_element_type=F32)
+
+
+def dot_nt(a, b):
+    return lax.dot_general(a, b, (((1,), (1,)), ((), ())), preferred_element_type=F32)
+
+
+def dot_tn(a, b):
+    return lax.dot_general(a, b, (((0,), (0,)), ((), ())), preferred_element_type=F32)
+
+
+def gather_columns(local, split, deps):
+    z_dep, xy_dep = deps
+    part = after(local, *z_dep)
+    part = joined(part, swap_over(part, BIT_Z0))
+    part = joined(part, swap_over(part, BIT_Z1))
+    left, right = after(part[:, :split], *xy_dep), after(part[:, split:], *xy_dep)
+    left = joined(left, swap_over(left, BIT_Y))
+    right = joined(right, swap_over(right, BIT_X))
+    left_far, right_far = swap_over(left, BIT_X), swap_over(right, BIT_Y)
+    left = joined(left, left_far)
+    right = joined(right[:128], right_far[:128], right[128:], right_far[128:])
+    near = joined(left, right, axis=1)
+    far = swap_over(near, BIT_CORE)
+    return joined(near, far), ((part,), (left_far, right_far))
+
+
+def add_rounded(a, b):
+    return (a.astype(F32) + b.astype(F32)).astype(BF16)
+
+
+def scatter_columns(keep, send, split):
+    total = add_rounded(keep, swap_over(send, BIT_CORE))
+    left, right = total[:, :split], total[:, split:].reshape(2, 2, 128, -1)
+    left = add_rounded(left[:256], swap_over(left[256:], BIT_X))
+    right = add_rounded(right[:, 0], swap_over(right[:, 1], BIT_Y))
+    left = add_rounded(left[:128], swap_over(left[128:], BIT_Y))
+    right = add_rounded(right[0], swap_over(right[1], BIT_X))
+    total = joined(left, right, axis=1)
+    total = add_rounded(total[:64], swap_over(total[64:], BIT_Z1))
+    return total[:32].astype(F32) + swap_over(total[32:], BIT_Z0).astype(F32)
+
+
+def sum_small(value):
+    for bit in (BIT_CORE, BIT_X, BIT_Y, BIT_Z0, BIT_Z1):
+        value = value + swap_over(value, bit)
+    return value
+
+
+def scatter_small(value):
+    for rows, bit in ((512, BIT_CORE), (256, BIT_X), (128, BIT_Y), (64, BIT_Z1), (32, BIT_Z0)):
+        value = value[:rows] + swap_over(value[rows:], bit)
+    return value
+
+
+def rotate_lanes(x, cosines, sines_up, sines_down):
+    width = x.shape[1]
+    return x * cosines + pltpu.roll(x, width - 16, 1) * sines_up + pltpu.roll(x, 16, 1) * sines_down
+
+
+def twice(table):
+    return jnp.concatenate([table, table], axis=1)
+
+
+def attention_kernel(
+    x_ref, wq_ref, wk_ref, wv_ref, b_ref, c_ref, s1_ref, s2_ref, q_ref, k_ref, v_ref, o_ref, l_ref, stat_ref, *, step
+):
+    x = x_ref[...]
+    c, s1, s2 = twice(c_ref[...]), twice(s1_ref[...]), twice(s2_ref[...])
+    q = dot_nn(x, wq_ref[...]) + b_ref[2:3, :]
+    q_ref[...] = (rotate_lanes(q, c, s1, s2) * (LOG2E / 8)).astype(BF16)
+    k = dot_nn(x, wk_ref[...])
+    k_ref[...] = rotate_lanes(k, c, s1, s2).astype(BF16)
+    v_ref[...] = (dot_nn(x, wv_ref[...]) + b_ref[3:4, :]).astype(BF16)
+    lane = lax.broadcasted_iota(jnp.int32, (1, 128), 1)
+    low_half = lane < 64
+
+    def tile(i, carry):
+        rows = pl.ds(pl.multiple_of(i * step, 16), step)
+        stats = jnp.zeros((step, 128), F32)
+        for pair in range(2):
+            cols = slice(pair * 128, pair * 128 + 128)
+            q_pair = q_ref[rows, cols]
+            k_pair, v_pair = k_ref[0:KEYS, cols], v_ref[0:KEYS, cols]
+            k_class = k_ref[KEYS : KEYS + 16, cols].astype(F32)[0:1]
+            v_class = v_ref[KEYS : KEYS + 16, cols].astype(F32)[0:1]
+            product = q_pair.astype(F32) * k_class
+            outs = []
+            for h in range(2):
+                own = low_half if h == 0 else ~low_half
+                scores = dot_nt(jnp.where(own, q_pair, jnp.zeros_like(q_pair)), k_pair)
+                class_score = jnp.sum(jnp.where(own, product, 0.0), axis=1, keepdims=True)
+                peak = jnp.maximum(jnp.max(scores, axis=1, keepdims=True), class_score)
+                p = jnp.exp2(scores - peak)
+                class_p = jnp.exp2(class_score - peak)
+                total = jnp.sum(p, axis=1, keepdims=True) + class_p
+                out = dot_nn(p.astype(BF16), v_pair) + class_p * v_class
+                outs.append(out * (1.0 / total))
+                stats = jnp.where(lane == pair * 2 + h, peak + jnp.log2(total), stats)
+            o_ref[rows, cols] = jnp.where(low_half, outs[0], outs[1]).astype(BF16)
+        stat_ref[rows, :] = stats
+        return carry
+
+    lax.fori_loop(0, ROWS // step, tile, 0)
+    l_ref[...] = stat_ref[...].T[0:8, :]
+
+
+def attention_forward(x, w, vectors, tables, step=208):
+    def block(first):
+        return pl.BlockSpec((1024, HEAD_COLS), lambda j: (0, first + j))
+
+    def whole(a):
+        return pl.BlockSpec(a.shape, lambda j: (0, 0))
+
+    out = pl.BlockSpec((ROWS, HEAD_COLS), lambda j: (0, j))
+    return pl.pallas_call(
+        functools.partial(attention_kernel, step=step),
+        grid=(4,),
+        in_specs=[whole(x), block(0), block(4), block(8), pl.BlockSpec((8, HEAD_COLS), lambda j: (0, j))]
+        + [whole(t) for t in tables],
+        out_specs=[out] * 4 + [pl.BlockSpec((8, ROWS), lambda j: (j, 0))],
+        out_shape=[jax.ShapeDtypeStruct((ROWS, 1024), BF16)] * 4 + [jax.ShapeDtypeStruct((32, ROWS), F32)],
+        scratch_shapes=[pltpu.VMEM((ROWS, 128), F32)],
+        compiler_params=pltpu.CompilerParams(vmem_limit_bytes=48 << 20),
+        cost_estimate=pl.CostEstimate(flops=30_000_000_000, bytes_accessed=20_000_000, transcendentals=17_000_000),
+        name="attention_forward",
+    )(x, w, w, w, vectors, *tables)
+
+
+def attention_back_kernel(
+    q_ref, k_ref, v_ref, g_ref, o_ref, l_ref, c_ref, s1_ref, s2_ref,
+    dq_ref, dk_ref, dv_ref, dq_sum, dk_sum, dv_sum, delta_ref, *, step
+):
+    lane = lax.broadcasted_iota(jnp.int32, (1, 128), 1)
+    low_half = lane < 64
+    deltas = jnp.zeros((ROWS, 128), F32)
+    for pair in range(2):
+        cols = slice(pair * 128, pair * 128 + 128)
+        product = g_ref[:, cols].astype(F32) * o_ref[:, cols].astype(F32)
+        for h in range(2):
+            own = low_half if h == 0 else ~low_half
+            delta = jnp.sum(jnp.where(own, product, 0.0), axis=1, keepdims=True)
+            deltas = jnp.where(lane == pair * 2 + h, delta, deltas)
+    delta_ref[...] = deltas.T[0:8, :]
+    real_key = lax.broadcasted_iota(jnp.int32, (ROWS, 1), 0) <= KEYS
+    dk_sum[...] = jnp.zeros_like(dk_sum)
+    dv_sum[...] = jnp.zeros_like(dv_sum)
+    for t in range(KEYS // step):
+        rows = pl.ds(t * step, step)
+        for pair in range(2):
+            cols = slice(pair * 128, pair * 128 + 128)
+            q_pair, g_pair = q_ref[rows, cols], g_ref[rows, cols]
+            k_pair, v_pair = k_ref[:, cols], v_ref[:, cols]
+            dqs, dk, dv = [], None, None
+            for h in range(2):
+                own = low_half if h == 0 else ~low_half
+                head = pair * 2 + h
+                q_head = jnp.where(own, q_pair, jnp.zeros_like(q_pair))
+                g_head = jnp.where(own, g_pair, jnp.zeros_like(g_pair))
+                scores = dot_nt(k_pair, q_head)
+                p = jnp.where(real_key, jnp.exp2(scores - l_ref[head : head + 1, rows]), 0.0)
+                gp = dot_nt(v_pair, g_head)
+                ds = (p * (gp - delta_ref[head : head + 1, rows])).astype(BF16)
+                dv_part, dk_part = dot_nn(p.astype(BF16), g_head), dot_nn(ds, q_head)
+                dv = dv_part if dv is None else dv + dv_part
+                dk = dk_part if dk is None else dk + dk_part
+                dqs.append(dot_tn(ds, k_pair))
+            dq_sum[rows, cols] = jnp.where(low_half, dqs[0], dqs[1])
+            dk_sum[:, cols] += dk
+            dv_sum[:, cols] += dv
+    q_class = q_ref[KEYS : KEYS + 16, :][0:1].astype(F32)
+    g_class = g_ref[KEYS : KEYS + 16, :][0:1].astype(F32)
+    shape = (128, HEAD_COLS)
+    own = lax.broadcasted_iota(jnp.int32, shape, 0) == lax.broadcasted_iota(jnp.int32, shape, 1) // 64
+    q_diag = jnp.where(own, q_class, 0.0).astype(BF16)
+    g_diag = jnp.where(own, g_class, 0.0).astype(BF16)
+    scores, gp = dot_nt(k_ref[...], q_diag), dot_nt(v_ref[...], g_diag)
+    log_class, delta_class = jnp.zeros((1, 128), F32), jnp.zeros((1, 128), F32)
+    for head in range(4):
+        log_class = jnp.where(lane == head, l_ref[head : head + 1, KEYS : KEYS + 1], log_class)
+        delta_class = jnp.where(lane == head, delta_ref[head : head + 1, KEYS : KEYS + 1], delta_class)
+    p = jnp.where(real_key & (lane < 4), jnp.exp2(scores - log_class), 0.0)
+    ds = (p * (gp - delta_class)).astype(BF16)
+    dv_sum[...] += dot_nn(p.astype(BF16), g_diag)
+    dk_sum[...] += dot_nn(ds, q_diag)
+    dq_class = jnp.sum(jnp.where(own, dot_tn(ds, k_ref[...]), 0.0), axis=0, keepdims=True)
+    first = lax.broadcasted_iota(jnp.int32, (16, 1), 0) == 0
+    dq_sum[KEYS : KEYS + 16, :] = jnp.where(first, dq_class, 0.0)
+    c, s1, s2 = twice(c_ref[...]), twice(s1_ref[...]), twice(s2_ref[...])
+    dq_ref[...] = (rotate_lanes(dq_sum[...], c, -s1, -s2) * 0.125).astype(BF16)
+    dk_ref[...] = (rotate_lanes(dk_sum[...], c, -s1, -s2) * (1.0 / LOG2E)).astype(BF16)
+    dv_ref[...] = dv_sum[...].astype(BF16)
+
+
+def attention_backward(q, k, v, g, o, log_sums, tables, step=256):
+    def whole(a):
+        return pl.BlockSpec(a.shape, lambda j: (0, 0))
+
+    block = pl.BlockSpec((ROWS, HEAD_COLS), lambda j: (0, j))
+    return pl.pallas_call(
+        functools.partial(attention_back_kernel, step=step),
+        grid=(4,),
+        in_specs=[block] * 5 + [pl.BlockSpec((8, ROWS), lambda j: (j, 0))] + [whole(t) for t in tables],
+        out_specs=[block] * 3,
+        out_shape=[jax.ShapeDtypeStruct((ROWS, 1024), BF16)] * 3,
+        scratch_shapes=[pltpu.VMEM((ROWS, HEAD_COLS), F32)] * 3 + [pltpu.VMEM((8, ROWS), F32)],
+        compiler_params=pltpu.CompilerParams(vmem_limit_bytes=48 << 20),
+        cost_estimate=pl.CostEstimate(flops=50_000_000_000, bytes_accessed=20_000_000, transcendentals=17_000_000),
+        name="attention_backward",
+    )(q, k, v, g, o, log_sums, *tables)
+
+
+def unit_norm(values):
+    centred = values - jnp.mean(values, axis=-1, keepdims=True)
+    inv_std = lax.rsqrt(jnp.mean(centred * centred, axis=-1, keepdims=True) + epsilon)
+    return centred * inv_std, inv_std
+
+
+def unit_norm_back(scaled, unit, inv_std):
+    return inv_std * (
+        scaled
+        - jnp.mean(scaled, axis=-1, keepdims=True)
+        - unit * jnp.mean(scaled * unit, axis=-1, keepdims=True)
+    )
+
+
+def pair_tables(coords):
+    cosines, sines = rotary_tables(coords)
+    pad = ((0, ROWS - KEYS - 1), (0, 0))
+    cosines = jnp.pad(joined(cosines[1:], cosines[:1]), pad)
+    sines = jnp.pad(joined(sines[1:], sines[:1]), pad)
+    even = (jnp.arange(64) % 32 < 16)[None, :]
+    up, down = jnp.where(even, -sines, 0.0), jnp.where(even, 0.0, sines)
+    return tuple(jnp.tile(t, (1, 2)) for t in (cosines, up, down))
+
+
+def paired_device(
+    patch_in, cls_in, d_patch, d_cls, image_valid, patch_coords,
+    w_query, w_key, w_value, w_gate, w_up, w_out, w_down, layer_vectors, ffn_vectors,
+):
+    me, pos = lax.axis_index(BOTH), lax.axis_index("ctx")
+    hidden = w_gate.shape[1]
+
+    vectors_local = jnp.pad(layer_vectors.T, ((0, 0), (0, 120)))
+    first_local = joined(w_query, w_key, w_value, vectors_local, axis=1)
+    out_local, down_local = w_out.T, w_down.T
+    wide = (hidden + 127) // 128 * 128
+    extra = ((0, 0), (0, wide - hidden))
+    second_local = joined(
+        jnp.pad(w_gate, extra), out_local[:, :512], jnp.pad(w_up, extra), out_local[:, 512:], axis=1
+    )
+    half_two = wide + 512
+    third_split = (hidden // 2 + 127) // 128 * 128
+    first, deps = gather_columns(first_local, 1664, ((), ()))
+    second, deps = gather_columns(second_local, half_two, deps)
+    third, deps = gather_columns(down_local, third_split, deps)
+    vectors = first[:, 3072:3080].T.astype(F32)
+    gate_w, up_w = second[:, :hidden], second[:, half_two : half_two + hidden]
+    out_w = joined(second[:, wide:half_two], second[:, half_two + wide :], axis=1)
+    down_w = third
+    ffn = ffn_vectors.astype(F32)
+
+    natural = lax.broadcasted_iota(jnp.int32, (1024, 1024), 0)
+    place = lax.broadcasted_iota(jnp.int32, (1024, 1024), 1)
+    block = place // 32
+    owner = (
+        (block // 16) * BIT_CORE
+        + (block // 8 % 2) * BIT_X
+        + (block // 4 % 2) * BIT_Y
+        + (block // 2 % 2) * BIT_Z1
+        + (block % 2) * BIT_Z0
+    ) ^ me
+    order = (natural == owner * 32 + place % 32).astype(BF16)
+
+    def own_image(patches, classes):
+        near = lax.dynamic_index_in_dim(patches, pos, 0, keepdims=False)
+        far = swap_over(lax.dynamic_index_in_dim(patches, 1 - pos, 0, keepdims=False), BIT_X)
+        class_row = lax.dynamic_index_in_dim(classes, pos, 0)
+        rows = joined(near, far, jnp.pad(class_row, ((0, ROWS - KEYS - 1), (0, 0))))
+        return dot_nn(rows, order)
+
+    def to_pair(rows):
+        rows = dot_nt(rows, order).astype(BF16)
+        near, far = rows[:512], swap_over(rows[512:], BIT_X)
+        is_first = pos == 0
+        near_class, far_class = rows[KEYS], far[512]
+        patches = jnp.where(is_first, jnp.stack([near, far[:512]]), jnp.stack([far[:512], near]))
+        classes = jnp.where(is_first, jnp.stack([near_class, far_class]), jnp.stack([far_class, near_class]))
+        return patches, classes
+
+    coords = joined(patch_coords, swap_over(patch_coords, BIT_X))
+    tables = pair_tables(coords)
+    keep = lax.dynamic_index_in_dim(image_valid, pos, 0, keepdims=False).astype(F32)
+    tokens = own_image(patch_in, cls_in)
+    grad_rows = own_image(d_patch, d_cls) * keep
+
+    unit_one, std_one = unit_norm(tokens)
+    normed = (unit_one * vectors[0] + vectors[1]).astype(BF16)
+    head_biases = dot_nt(first[:, 3072:3080].T, order)
+    q_rot, k_rot, values, attended, log_sums = attention_forward(normed, first, head_biases, tables)
+    middle = tokens + (dot_nt(attended, out_w) + vectors[4])
+    unit_two, std_two = unit_norm(middle)
+    normed_two = (unit_two * vectors[5] + vectors[6]).astype(BF16)
+    gate = dot_nn(normed_two, gate_w) + ffn[0]
+    up = dot_nn(normed_two, up_w) + ffn[1]
+    silu = jax.nn.silu(gate)
+    unit_three, std_three = unit_norm(silu * up)
+    inner = (unit_three * ffn[2] + ffn[3]).astype(BF16)
+    result = middle + (dot_nt(inner, down_w) + vectors[7])
+    patch_out, cls_out = to_pair((result * keep).astype(BF16))
+
+    def weight_grad_halves(rows_in, grads):
+        near = dot_tn(rows_in[:, :512], grads).astype(BF16)
+        far = dot_tn(rows_in[:, 512:], grads).astype(BF16)
+        return near, far
+
+    def column_sum(rounded):
+        return jnp.sum(rounded.astype(F32), axis=0)
+
+    branch = grad_rows.astype(BF16)
+    down_grad = scatter_columns(*weight_grad_halves(branch, inner), third_split)
+    grad_inner = dot_nn(branch, down_w)
+    grad_mix = unit_norm_back(grad_inner * ffn[2], unit_three, std_three)
+    sigmoid = jax.nn.sigmoid(gate)
+    gate_low = (grad_mix * up * sigmoid * (1.0 + gate * (1.0 - sigmoid))).astype(BF16)
+    up_low = (grad_mix * silu).astype(BF16)
+    ffn_grads = sum_small(
+        jnp.stack(
+            [column_sum(gate_low), column_sum(up_low), jnp.sum(grad_inner * unit_three, axis=0), jnp.sum(grad_inner, axis=0)]
+        )
+    )
+    gate_near, gate_far = weight_grad_halves(normed_two, gate_low)
+    up_near, up_far = weight_grad_halves(normed_two, up_low)
+    grad_two = dot_nt(gate_low, gate_w) + dot_nt(up_low, up_w)
+    grad_middle = grad_rows + unit_norm_back(grad_two * vectors[5], unit_two, std_two)
+    att_low = grad_middle.astype(BF16)
+    out_near, out_far = weight_grad_halves(att_low, attended)
+    pads = ((0, 0), (0, wide - hidden))
+    second_grad = scatter_columns(
+        joined(jnp.pad(gate_near, pads), out_near[:, :512], jnp.pad(up_near, pads), out_near[:, 512:], axis=1),
+        joined(jnp.pad(gate_far, pads), out_far[:, :512], jnp.pad(up_far, pads), out_far[:, 512:], axis=1),
+        half_two,
+    )
+    grad_attended = dot_nn(att_low, out_w).astype(BF16)
+    query_low, key_low, value_low = attention_backward(
+        q_rot, k_rot, values, grad_attended, attended, log_sums, tables
+    )
+    halves = [weight_grad_halves(normed, low) for low in (query_low, key_low, value_low)]
+    first_grad = scatter_columns(
+        joined(*[h[0] for h in halves], axis=1), joined(*[h[1] for h in halves], axis=1), 1536
+    )
+    grad_one = (
+        dot_nt(query_low, first[:, :1024])
+        + dot_nt(key_low, first[:, 1024:2048])
+        + dot_nt(value_low, first[:, 2048:3072])
+    )
+    grad_tokens = grad_middle + unit_norm_back(grad_one * vectors[0], unit_one, std_one)
+    head_sums = jnp.dot(
+        jnp.stack([column_sum(query_low), column_sum(value_low)]),
+        order.astype(F32),
+        precision=lax.Precision.HIGHEST,
+    )
+    vector_grads = scatter_small(
+        jnp.stack(
+            [
+                jnp.sum(grad_one * unit_one, axis=0),
+                jnp.sum(grad_one, axis=0),
+                head_sums[0],
+                head_sums[1],
+                column_sum(att_low),
+                jnp.sum(grad_two * unit_two, axis=0),
+                jnp.sum(grad_two, axis=0),
+                column_sum(branch),
+            ]
+        ).T
+    )
+    patch_grad, cls_grad = to_pair(grad_tokens.astype(BF16))
+    return (
+        patch_out,
+        cls_out,
+        patch_grad,
+        cls_grad,
+        first_grad[:, :1024],
+        first_grad[:, 1024:2048],
+        first_grad[:, 2048:],
+        second_grad[:, :hidden],
+        second_grad[:, half_two : half_two + hidden],
+        joined(second_grad[:, wide:half_two], second_grad[:, half_two + wide :], axis=1).T,
+        down_grad.T,
+        vector_grads.T,
+        ffn_grads,
+    )
+
+
 def solution(mesh):
     in_specs = (
         P("dp", "ctx", None),
@@ -441,6 +864,9 @@
         P(None, ("dp", "ctx")),
         P(),
     )
+    sizes = dict(mesh.shape)
+    pairs = sizes["dp"] == 16 and sizes["ctx"] == 2
+    body = paired_device if pairs else on_device
     return jax.shard_map(
-        on_device, mesh=mesh, in_specs=in_specs, out_specs=out_specs, check_vma=False
-    )
+        body, mesh=mesh, in_specs=in_specs, out_specs=out_specs, check_vma=False
+    )

time: 2710 us -> 922 us (0.34)
  waiting for transfers between devices: 1490 us -> 254 us
  matrix products: 657 us -> 196 us
  blocking collectives: 164 us -> 0 us
  local copies, waits for them, and re-layouts: 218 us -> 87.6 us
  Pallas kernels: 0 us -> 109 us
  other arithmetic: 126 us -> 207 us
  starting transfers between devices: 13.9 us -> 55.6 us
    reduce_scatter x11 -> x0, waiting for transfers between devices: 1300 us -> none  [the longest x1 253 us: on_device(): lax.psum_scatter(out_grads[1], ('dp', 'ctx'), scatter_dimension=1, tiled=...]
    dot_general x266 -> x30, matrix products: 657 us -> 196 us  [the longest x9 71.9 us: dot_nt(): lax.dot_general(a, b, (((1,), (1,)), ((), ())), preferred_element_type=F32)]
    ppermute x0 -> x57, waiting for transfers between devices: none -> 254 us  [swap_over(): return lax.ppermute(value, BOTH, [(i, i ^ bit) for i in range(count)])]
    all_gather x11 -> x0, waiting for transfers between devices: 188 us -> none  [the longest x1 56.1 us: fetch_forward(): lax.all_gather(w_up, ('dp', 'ctx'), axis=0, tiled=True)]
    concatenate x13 -> x23, other arithmetic: 18.8 us -> 130 us  [joined(): return jnp.concatenate(parts, axis=axis)]
    pallas_call x0 -> x2, Pallas kernels: none -> 109 us  [the longest x1 58.7 us: attention_backward(): pl.pallas_call(functools.partial(attention_back_kernel, step=step), grid=...]
    psum x2 -> x0, blocking collectives: 93.9 us -> none  [the longest x1 52.6 us: backward_pass(): lax.psum((grad_keys[:, :1], grad_values[:, :1]), 'ctx')]
    all_gather x1 -> x0, blocking collectives: 70.5 us -> none  [fetch_forward(): lax.all_gather(layer_vectors, ('dp', 'ctx'), axis=1, tiled=True)]
  transfers between devices with their start and end apart: 23 -> 57, of which waited for: 13 -> 24; matrix products, arithmetic and copies ran while one was open for 25% -> 23% of each run, Pallas kernels for 0% -> 5%
where the time goes in v1:
time: 922 us; the launch traced here: 913 us
  waiting for transfers between devices  254 us (28%)
  other arithmetic  207 us (22%)
  matrix products  196 us (21%)
  Pallas kernels  109 us (12%)
  local copies, waits for them, and re-layouts  87.6 us (10%)
  starting transfers between devices  55.6 us (6%)
    ppermute x57, waiting for transfers between devices, swap_over(): return lax.ppermute(value, BOTH, [(i, i ^ bit) for i in range(count)])  254 us
    concatenate x23, other arithmetic, joined(): return jnp.concatenate(parts, axis=axis)  130 us
    dot_general x9, matrix products, dot_nt(): lax.dot_general(a, b, (((1,), (1,)), ((), ())), preferred_element_type=F32)  71.9 us
    dot_general x6, matrix products, dot_nn(): lax.dot_general(a, b, (((1,), (0,)), ((), ())), preferred_element_type=F32)  62.1 us
    dot_general x14, matrix products, dot_tn(): lax.dot_general(a, b, (((0,), (0,)), ((), ())), preferred_element_type=F32)  60.2 us
    pallas_call x1, Pallas kernels, attention_backward(): pl.pallas_call(functools.partial(attention_back_kernel, step=step), grid=...  58.7 us
    ppermute x57, starting transfers between devices, swap_over(): return lax.ppermute(value, BOTH, [(i, i ^ bit) for i in range(count)])  55.6 us
    pallas_call x1, Pallas kernels, attention_forward(): pl.pallas_call(functools.partial(attention_kernel, step=step), grid=(4,),...  50.1 us
  transfers between devices with their start and end apart: 57, of which 24 were waited for; matrix products, arithmetic and copies ran while one was open for 23% of the time, Pallas kernels for 5%

profile of v1, /device:TPU:0, one launch (start us, length us, event | category | flops | bytes accessed | tf_op | source)
XLA Modules:
  0.0 913.1 jit_solution(5154852023427496170)
XLA Ops:
  0.7 3.0 collective-permute-start.8
  7.0 3.2 dynamic-slice_bitcast_fusion.3
  17.9 2.6 collective-permute-start.2
  21.3 16.5 %collective-permute-done.2 = bf16[64,3200]{1,0:T(8,128)(2,1)} collective-permute-done((bf16[64,3200]{1,0:T(8,128)(2,1)}, bf16[64,3200]{1,0:T(8,128)(2,1)}, u32[]{:S(2)}, u32[]{:S(2)}) %collective-permute-start.2) | collective-permute-done | bytes 409632 | tf_op jit(solution)/shard_map/ppermute | solution.py:428
  41.3 24.3 %collective-permute-done.5 = bf16[128,1536]{1,0:T(8,128)(2,1)S(1)} collective-permute-done((bf16[128,1536]{1,0:T(8,128)(2,1)S(1)}, bf16[128,1536]{1,0:T(8,128)(2,1)S(1)}, u32[]{:S(2)}, u32[]{:S(2)}) %collective-permute-start.5) | collective-permute-done | bytes 393248 | tf_op jit(solution)/shard_map/ppermute | solution.py:428
  68.2 2.7 collective-permute-start.10
  70.9 7.2 convert_reduce_fusion.2
  78.1 3.8 fusion.177
  82.0 24.1 %collective-permute-done.10 = bf16[64,6656]{1,0:T(8,128)(2,1)S(1)} collective-permute-done((bf16[64,6656]{1,0:T(8,128)(2,1)S(1)}, bf16[64,6656]{1,0:T(8,128)(2,1)S(1)}, u32[]{:S(2)}, u32[]{:S(2)}) %collective-permute-start.10) | collective-permute-done | bytes 852000 | tf_op jit(solution)/shard_map/ppermute | solution.py:428
  108.9 18.3 %collective-permute-done.13 = bf16[128,3328]{1,0:T(8,128)(2,1)S(1)} collective-permute-done((bf16[128,3328]{1,0:T(8,128)(2,1)S(1)}, bf16[128,3328]{1,0:T(8,128)(2,1)S(1)}, u32[]{:S(2)}, u32[]{:S(2)}) %collective-permute-start.13) | collective-permute-done | bytes 852000 | tf_op jit(solution)/shard_map/ppermute | solution.py:428
  129.9 20.8 %maximum_maximum_fusion.1 = bf16[512,3200]{1,0:T(8,128)(2,1)} fusion(bf16[128,1536]{1,0:T(8,128)(2,1)S(1)} %get-tuple-element.200, bf16[128,1536]{1,0:T(8,128)(2,1)S(1)} %collective-permute-done.5, bf16[128,1536]{1,0:T(8,128)(2,1)S(1)} %get-tuple-element.199, bf16[128,1536]{1,0:T(8,128)(2,1)S(1)} %slice.473, ...), kind=kLoop, calls=%fused_computation.159 | loop fusion | flops 22937600 | bytes 6553600 | tf_op jit(solution)/shard_map/concatenate | solution.py:432
  151.0 15.1 %collective-permute-done.17 = bf16[64,2730]{1,0:T(8,128)(2,1)S(1)} collective-permute-done((bf16[64,2730]{1,0:T(8,128)(2,1)S(1)}, bf16[64,2730]{1,0:T(8,128)(2,1)S(1)}, u32[]{:S(2)}, u32[]{:S(2)}) %collective-permute-start.17) | collective-permute-done | bytes 349472 | tf_op jit(solution)/shard_map/ppermute | solution.py:428
  169.1 23.9 %maximum_maximum_fusion = bf16[512,6656]{1,0:T(8,128)(2,1)} fusion(bf16[128,3328]{1,0:T(8,128)(2,1)S(1)} %get-tuple-element.194, bf16[128,3328]{1,0:T(8,128)(2,1)S(1)} %collective-permute-done.13, bf16[128,3328]{1,0:T(8,128)(2,1)S(1)} %get-tuple-element.193, bf16[128,3328]{1,0:T(8,128)(2,1)S(1)} %get-tuple-element.30, ...), kind=kLoop, calls=%fused_computation.34 | loop fusion | flops 47710208 | bytes 13631488 | tf_op jit(solution)/shard_map/concatenate | solution.py:432
  201.2 5.0 pad_maximum_fusion.wq_ref.wk_ref.wv_ref
  219.5 6.9 maximum_maximum_fusion.2
  226.3 4.7 copy.225
  231.0 50.1 %attention_forward.1 = (bf16[1040,1024]{1,0:T(8,128)(2,1)S(1)}, bf16[1040,1024]{1,0:T(8,128)(2,1)S(1)}, bf16[1040,1024]{1,0:T(8,128)(2,1)}, bf16[1040,1024]{1,0:T(8,128)(2,1)}, f32[32,1040]{1,0:T(8,128)S(1)}) custom-call(bf16[1040,1024]{1,0:T(8,128)(2,1)} %add_convert_fusion.6.x_ref, bf16[1024,3200]{1,0:T(8,128)(2,1)} %copy-done.20, ...), custom_call_target="tpu_custom_call" | custom-call | flops 30000001024 | bytes 20000000 | tf_op jit(solution)/shard_map/attention_forward/pallas_call | solution.py:555
  283.8 4.6 copy.226
  288.4 4.5 fusion.89
  292.9 5.5 fusion.178
  302.4 55.8 %pad_maximum_fusion.1 = bf16[1024,2730]{1,0:T(8,128)(2,1)S(1)} fusion(bf16[512,6656]{1,0:T(8,128)(2,1)} %collective-permute-done.15, bf16[128,3328]{1,0:T(8,128)(2,1)S(1)} %copy-done.18, bf16[256,3328]{1,0:T(8,128)(2,1)S(1)} %copy-done.10, bf16[128,3328]{1,0:T(8,128)(2,1)S(1)} %copy-done.12, bf16[128,3328]{1,0:T(8,128)(2,1)S(1)} %copy-done.14, ...), kind=kLoop, calls=%fused_computation.59 | loop fusion | flops 44728320 | bytes 19222528 | tf_op jit(solution)/shard_map/concatenate | solution.py:432
  358.2 14.8 %convolution_add_fusion.1 = f32[1040,2730]{1,0:T(8,128)} fusion(bf16[1040,1024]{1,0:T(8,128)(2,1)S(1)} %add_convert_fusion.5, f32[2730]{0:T(1024)S(1)} %copy-done.92, bf16[512,6656]{1,0:T(8,128)(2,1)} %collective-permute-done.15, bf16[128,3328]{1,0:T(8,128)(2,1)S(1)} %copy-done.18, bf16[256,3328]{1,0:T(8,128)(2,1)S(1)} %copy-done.10, ...), kind=kOutput, calls=%fused_computation.3 | convolution fusion | flops 5862248960 | bytes 27129128 | tf_op jit(solution)/shard_map/dot_general | solution.py:440
  373.0 15.1 %fusion.164 = (f32[1040]{0:T(1024)S(1)}, f32[1040,2730]{1,0:T(8,128)}, f32[1040,2730]{1,0:T(8,128)}) fusion(f32[1040,2730]{1,0:T(8,128)} %convolution_add_fusion.1, f32[2730]{0:T(1024)S(1)} %copy-done.91, bf16[1040,1024]{1,0:T(8,128)(2,1)S(1)} %add_convert_fusion.5, bf16[1024,2730]{1,0:T(8,128)(2,1)S(1)} %pad_maximum_fusion.1), kind=kOutput, calls=%fused_computation.378 | convolution fusion | flops 5834554368 | bytes 41806440 | tf_op jit(solution)/shard_map/dot_general | solution.py:440
  388.1 5.8 multiply_reduce_fusion.2
  393.9 17.5 %multiply_reduce_fusion = (f32[2730]{0:T(1024)}, f32[1040]{0:T(1024)S(1)}, f32[1040]{0:T(1024)S(1)}, f32[2730]{0:T(1024)}, f32[1040,2730]{1,0:T(8,128)}) fusion(f32[1040,2730]{1,0:T(8,128)} %get-tuple-element.177, f32[1040]{0:T(1024)S(1)} %add_rsqrt_fusion, f32[1040]{0:T(1024)S(1)} %broadcast_multiply_fusion.4, f32[2730]{0:T(1024)S(1)} %copy-done.81, ...), kind=kOutput, calls=%fused_computation.9 | convolution fusion | flops 5884954112 | bytes 30483960 | tf_op jit(solution)/shard_map/dot_general | solution.py:440
  411.5 22.2 %convert_reduce_fusion.1 = (f32[2730]{0:T(1024)}, bf16[1040,2730]{1,0:T(8,128)(2,1)}, f32[2730]{0:T(1024)}, bf16[1040,2730]{1,0:T(8,128)(2,1)S(1)}, bf16[1040,2730]{1,0:T(8,128)(2,1)}) fusion(f32[1040,2730]{1,0:T(8,128)} %convolution_add_fusion.1, f32[1040,2730]{1,0:T(8,128)} %get-tuple-element.221, f32[1040]{0:T(1024)S(1)} %broadcast_multiply_fusion.2, ...), kind=kLoop, calls=%fused_computation.11 | loop fusion | flops 76652944 | bytes 62522720 | tf_op jit(solution)/shard_map/reduce_sum | solution.py:757
  433.7 8.1 fusion.179
  441.7 16.3 %multiply_reduce_fusion.4 = (f32[1024]{0:T(1024)}, f32[1040]{0:T(1024)S(1)}, f32[1040]{0:T(1024)S(1)}, f32[1024]{0:T(1024)}, f32[1040,1024]{1,0:T(8,128)}) fusion(f32[1040,1024]{1,0:T(8,128)} %copy-done.6, f32[1040]{0:T(1024)S(1)} %add_rsqrt_fusion.1, f32[1040]{0:T(1024)S(1)} %broadcast_multiply_fusion.9, f32[1024]{0:T(1024)S(1)} %get-tuple-element.159, ...), kind=kOutput, calls=%fused_computation.88 | convolution fusion | flops 5870055424 | bytes 32118336 | tf_op jit(solution)/shard_map/dot_general | solution.py:444
  458.1 7.6 convert_reduce_fusion.3
  465.7 3.7 convolution_convert_fusion.8.g_ref
  469.4 58.7 %attention_backward.1 = (bf16[1040,1024]{1,0:T(8,128)(2,1)S(1)}, bf16[1040,1024]{1,0:T(8,128)(2,1)S(1)}, bf16[1040,1024]{1,0:T(8,128)(2,1)}) custom-call(bf16[1040,1024]{1,0:T(8,128)(2,1)} %copy-done.4, bf16[1040,1024]{1,0:T(8,128)(2,1)} %copy-done.5, bf16[1040,1024]{1,0:T(8,128)(2,1)} %get-tuple-element.36.v_ref, ...), custom_call_target="tpu_custom_call" | custom-call | flops 49999998976 | bytes 20000000 | tf_op jit(solution)/shard_map/attention_backward/pallas_call | solution.py:639
  545.4 14.8 %convolution_convert_fusion.7 = bf16[1040,1024]{1,0:T(8,128)(2,1)} fusion(f32[1040,1024]{1,0:T(8,128)} %copy-done.6, bf16[1040,2730]{1,0:T(8,128)(2,1)} %get-tuple-element.180, f32[]{:T(128)} %bitcast.11, f32[1024]{0:T(1024)S(1)} %copy-done.93, bf16[512,2730]{1,0:T(8,128)(2,1)S(1)} %copy-done.41, bf16[128,1322]{1,0:T(8,128)(2,1)} %copy.257, ...), kind=kOutput, calls=%fused_computation.149 | convolution fusion | flops 8146436096 | bytes 17681736 | tf_op jit(solution)/shard_map/dot_general | solution.py:444
  564.1 6.2 fusion.97
  570.3 4.4 fusion.99
  574.8 6.8 convolution_convert_fusion.3
  581.6 7.2 convolution_convert_fusion.5
  588.8 6.8 convolution_convert_fusion.4
  595.6 6.8 convolution_convert_fusion.2
  602.4 6.8 convolution_convert_fusion
  609.3 5.5 convolution_convert_fusion.1
  617.8 7.3 multiply_reduce_fusion.5
  627.3 8.4 convolution_convert_fusion.6
  639.7 3.7 fusion.9
  646.4 2.6 convolution_convert_fusion.14
  649.0 17.0 %collective-permute-done.48 = f32[256,8]{0,1:T(8,128)S(1)} collective-permute-done((f32[256,8]{0,1:T(8,128)S(1)}, f32[256,8]{0,1:T(8,128)S(1)}, u32[]{:S(2)}, u32[]{:S(2)}) %collective-permute-start.48) | collective-permute-done | bytes 8224 | tf_op jit(solution)/shard_map/ppermute | solution.py:428
  672.3 3.4 collective-permute-done.54
  677.2 2.7 collective-permute-done.55
  685.5 2.9 collective-permute-done.56
  695.7 3.1 copy.243
  707.3 3.4 add_convert_fusion.2
  714.8 9.8 %collective-permute-done.43 = bf16[2,128,1322]{1,0,2:T(2,128)(2,1)} collective-permute-done((bf16[2,128,1322]{1,0,2:T(2,128)(2,1)}, bf16[2,128,1322]{1,0,2:T(2,128)(2,1)}, u32[]{:S(2)}, u32[]{:S(2)}) %collective-permute-start.43) | collective-permute-done | bytes 676896 | tf_op jit(solution)/shard_map/ppermute | solution.py:428
  724.6 3.0 copy.248
  732.7 13.9 %collective-permute-done.44 = bf16[128,1322]{1,0:T(8,128)(2,1)S(1)} collective-permute-done((bf16[128,1322]{1,0:T(8,128)(2,1)S(1)}, bf16[128,1322]{1,0:T(8,128)(2,1)S(1)}, u32[]{:S(2)}, u32[]{:S(2)}) %collective-permute-start.44) | collective-permute-done | bytes 338464 | tf_op jit(solution)/shard_map/ppermute | solution.py:428
  756.3 11.3 %collective-permute-done.45 = bf16[64,2730]{1,0:T(8,128)(2,1)S(1)} collective-permute-done((bf16[64,2730]{1,0:T(8,128)(2,1)S(1)}, bf16[64,2730]{1,0:T(8,128)(2,1)S(1)}, u32[]{:S(2)}, u32[]{:S(2)}) %collective-permute-start.45) | collective-permute-done | bytes 349472 | tf_op jit(solution)/shard_map/ppermute | solution.py:428
  769.3 4.5 add_convert_fusion
  778.9 6.8 reshape.138
  785.7 5.1 fusion.168
  794.2 2.8 collective-permute-start.31
  797.1 19.9 %collective-permute-done.34 = bf16[256,3328]{0,1:T(8,128)(2,1)} collective-permute-done((bf16[256,3328]{0,1:T(8,128)(2,1)}, bf16[256,3328]{0,1:T(8,128)(2,1)}, u32[]{:S(2)}, u32[]{:S(2)}) %collective-permute-start.34) | collective-permute-done | bytes 1703968 | tf_op jit(solution)/shard_map/ppermute | solution.py:428
  820.5 10.9 %collective-permute-done.36 = bf16[2,128,3328]{1,2,0:T(8,128)(2,1)S(1)} collective-permute-done((bf16[2,128,3328]{1,2,0:T(8,128)(2,1)S(1)}, bf16[2,128,3328]{1,2,0:T(8,128)(2,1)S(1)}, u32[]{:S(2)}, u32[]{:S(2)}) %collective-permute-start.36) | collective-permute-done | bytes 1703968 | tf_op jit(solution)/shard_map/ppermute | solution.py:428
  833.1 14.5 %collective-permute-done.35 = bf16[128,3328]{0,1:T(8,128)(2,1)S(1)} collective-permute-done((bf16[128,3328]{0,1:T(8,128)(2,1)S(1)}, bf16[128,3328]{0,1:T(8,128)(2,1)S(1)}, u32[]{:S(2)}, u32[]{:S(2)}) %collective-permute-start.35) | collective-permute-done | bytes 852000 | tf_op jit(solution)/shard_map/ppermute | solution.py:428
  851.1 3.8 collective-permute-start.38
  860.0 29.7 %collective-permute-done.38 = bf16[64,6656]{1,0:T(8,128)(2,1)S(1)} collective-permute-done((bf16[64,6656]{1,0:T(8,128)(2,1)}, bf16[64,6656]{1,0:T(8,128)(2,1)S(1)}, u32[]{:S(2)}, u32[]{:S(2)}) %collective-permute-start.38) | collective-permute-done | bytes 852000 | tf_op jit(solution)/shard_map/ppermute | solution.py:428
  896.9 10.2 %collective-permute-done.39 = bf16[32,6656]{1,0:T(8,128)(2,1)} collective-permute-done((bf16[32,6656]{1,0:T(8,128)(2,1)}, bf16[32,6656]{1,0:T(8,128)(2,1)}, u32[]{:S(2)}, u32[]{:S(2)}) %collective-permute-start.39) | collective-permute-done | bytes 426016 | tf_op jit(solution)/shard_map/ppermute | solution.py:428
  (540 shorter events, 171.3 us)
Async XLA Ops:
  0.7 15.3 %collective-permute-start.8 = (s32[512,2]{0,1:T(2,128)}, s32[512,2]{0,1:T(2,128)S(1)}, u32[]{:S(2)}, u32[]{:S(2)}) collective-permute-start(s32[512,2]{0,1:T(2,128)} %param.20), channel_id=1, source_target_pairs={{0,1},{1,0},{2,3},{3,2},{4,5},{5,4},{6,7},{7,6},{8,9},{9,8},{10,11... | collective-permute-start | bytes 12296 | tf_op jit(solution)/shard_map/ppermute | solution.py:428
  5.3 11.7 %collective-permute-start.1 = (bf16[32,3200]{1,0:T(8,128)(2,1)S(1)}, bf16[32,3200]{1,0:T(8,128)(2,1)S(1)}, u32[]{:S(2)}, u32[]{:S(2)}) collective-permute-start(bf16[32,3200]{1,0:T(8,128)(2,1)S(1)} %fusion.137), channel_id=1, source_target_pairs={{0,8},{1,9},{2,10},{3,11},{4,12},{5,13},{6,14},{7,15},{8,0},{9,1},... | collective-permute-start | bytes 614408 | tf_op jit(solution)/shard_map/ppermute | solution.py:428
  10.2 67.9 %collective-permute-start = (bf16[512,1024]{1,0:T(8,128)(2,1)}, bf16[512,1024]{1,0:T(8,128)(2,1)}, u32[]{:S(2)}, u32[]{:S(2)}) collective-permute-start(bf16[512,1024]{1,0:T(8,128)(2,1)} %get-tuple-element.190), channel_id=1, source_target_pairs={{0,1},{1,0},{2,3},{3,2},{4,5},{5,4},{6,7},{7,6},{8,9},{9,8},{10,11... | collective-permute-start | bytes 3145736 | tf_op jit(solution)/shard_map/ppermute | solution.py:428
  12.3 58.6 %collective-permute-start.24 = (bf16[512,1024]{1,0:T(8,128)(2,1)}, bf16[512,1024]{1,0:T(8,128)(2,1)}, u32[]{:S(2)}, u32[]{:S(2)}) collective-permute-start(bf16[512,1024]{1,0:T(8,128)(2,1)} %get-tuple-element.188), channel_id=1, source_target_pairs={{0,1},{1,0},{2,3},{3,2},{4,5},{5,4},{6,7},{7,6},{8,9},{9,8},{10,11... | collective-permute-start | bytes 3145736 | tf_op jit(solution)/shard_map/ppermute | solution.py:428
  13.8 194.4 %copy-start.110 = (pred[1024]{0:T(1024)(128)(4,1)}, pred[1024]{0:T(1024)(128)(4,1)S(1)}, u32[]{:S(2)}) copy-start(pred[1024]{0:T(1024)(128)(4,1)S(1)} %get-tuple-element.231) | copy-start | bytes 3076
  13.8 194.4 %copy-start.112 = (pred[1024]{0:T(1024)(128)(4,1)}, pred[1024]{0:T(1024)(128)(4,1)S(1)}, u32[]{:S(2)}) copy-start(pred[1024]{0:T(1024)(128)(4,1)S(1)} %get-tuple-element.232) | copy-start | bytes 3076
  13.8 194.4 %copy-start.100 = (s32[1024]{0:T(1024)}, s32[1024]{0:T(1024)S(1)}, u32[]{:S(2)}) copy-start(s32[1024]{0:T(1024)S(1)} %get-tuple-element.229) | copy-start | bytes 12292
  13.8 194.4 %copy-start.102 = (s32[1024]{0:T(1024)}, s32[1024]{0:T(1024)S(1)}, u32[]{:S(2)}) copy-start(s32[1024]{0:T(1024)S(1)} %get-tuple-element.230) | copy-start | bytes 12292
  13.8 194.4 %copy-start.104 = (s32[1024]{0:T(1024)}, s32[1024]{0:T(1024)S(1)}, u32[]{:S(2)}) copy-start(s32[1024]{0:T(1024)S(1)} %get-tuple-element.227) | copy-start | bytes 12292
  13.8 194.4 %copy-start.106 = (s32[1024]{0:T(1024)}, s32[1024]{0:T(1024)S(1)}, u32[]{:S(2)}) copy-start(s32[1024]{0:T(1024)S(1)} %get-tuple-element.228) | copy-start | bytes 12292
  17.9 20.0 %collective-permute-start.2 = (bf16[64,3200]{1,0:T(8,128)(2,1)}, bf16[64,3200]{1,0:T(8,128)(2,1)}, u32[]{:S(2)}, u32[]{:S(2)}) collective-permute-start(bf16[64,3200]{1,0:T(8,128)(2,1)} %pad_maximum_fusion.21), channel_id=1, source_target_pairs={{0,16},{1,17},{2,18},{3,19},{4,20},{5,21},{6,22},{7,23},{8,24},{9,... | collective-permute-start | bytes 1228808 | tf_op jit(solution)/shard_map/ppermute | solution.py:428
  39.0 26.7 %collective-permute-start.5 = (bf16[128,1536]{1,0:T(8,128)(2,1)S(1)}, bf16[128,1536]{1,0:T(8,128)(2,1)S(1)}, u32[]{:S(2)}, u32[]{:S(2)}) collective-permute-start(bf16[128,1536]{1,0:T(8,128)(2,1)S(1)} %slice.473), channel_id=1, source_target_pairs={{0,1},{1,0},{2,3},{3,2},{4,5},{5,4},{6,7},{7,6},{8,9},{9,8},{10,11... | collective-permute-start | bytes 1179656 | tf_op jit(solution)/shard_map/ppermute | solution.py:428
  39.7 27.6 %collective-permute-start.3 = (bf16[128,1664]{1,0:T(8,128)(2,1)S(1)}, bf16[128,1664]{1,0:T(8,128)(2,1)S(1)}, u32[]{:S(2)}, u32[]{:S(2)}) collective-permute-start(bf16[128,1664]{1,0:T(8,128)(2,1)S(1)} %slice.472), channel_id=1, source_target_pairs={{0,4},{1,5},{2,6},{3,7},{4,0},{5,1},{6,2},{7,3},{8,12},{9,13},{10,... | collective-permute-start | bytes 1277960 | tf_op jit(solution)/shard_map/ppermute | solution.py:428
  41.3 26.9 %collective-permute-start.9 = (bf16[32,6656]{1,0:T(8,128)(2,1)S(1)}, bf16[32,6656]{1,0:T(8,128)(2,1)S(1)}, u32[]{:S(2)}, u32[]{:S(2)}) collective-permute-start(bf16[32,6656]{1,0:T(8,128)(2,1)S(1)} %fusion.128), channel_id=1, source_target_pairs={{0,8},{1,9},{2,10},{3,11},{4,12},{5,13},{6,14},{7,15},{8,0},{9,1},... | collective-permute-start | bytes 1277960 | tf_op jit(solution)/shard_map/ppermute | solution.py:428
  65.7 40.6 %collective-permute-start.6 = (bf16[256,1536]{1,0:T(8,128)(2,1)S(1)}, bf16[256,1536]{1,0:T(8,128)(2,1)S(1)}, u32[]{:S(2)}, u32[]{:S(2)}) collective-permute-start(bf16[256,1536]{1,0:T(8,128)(2,1)S(1)} %pad_maximum_fusion.18), channel_id=1, source_target_pairs={{0,4},{1,5},{2,6},{3,7},{4,0},{5,1},{6,2},{7,3},{8,12},{9,13},{10,... | collective-permute-start | bytes 2359304 | tf_op jit(solution)/shard_map/ppermute | solution.py:428
  67.4 38.9 %collective-permute-start.4 = (bf16[256,1664]{1,0:T(8,128)(2,1)S(1)}, bf16[256,1664]{1,0:T(8,128)(2,1)S(1)}, u32[]{:S(2)}, u32[]{:S(2)}) collective-permute-start(bf16[256,1664]{1,0:T(8,128)(2,1)S(1)} %pad_maximum_fusion.15), channel_id=1, source_target_pairs={{0,1},{1,0},{2,3},{3,2},{4,5},{5,4},{6,7},{7,6},{8,9},{9,8},{10,11... | collective-permute-start | bytes 2555912 | tf_op jit(solution)/shard_map/ppermute | solution.py:428
  68.2 37.9 %collective-permute-start.10 = (bf16[64,6656]{1,0:T(8,128)(2,1)S(1)}, bf16[64,6656]{1,0:T(8,128)(2,1)S(1)}, u32[]{:S(2)}, u32[]{:S(2)}) collective-permute-start(bf16[64,6656]{1,0:T(8,128)(2,1)S(1)} %pad_maximum_fusion.16), channel_id=1, source_target_pairs={{0,16},{1,17},{2,18},{3,19},{4,20},{5,21},{6,22},{7,23},{8,24},{9,... | collective-permute-start | bytes 2555912 | tf_op jit(solution)/shard_map/ppermute | solution.py:428
  82.0 127.5 %copy-start.76 = (f32[1040]{0:T(1024)}, f32[1040]{0:T(1024)S(1)}, u32[]{:S(2)}) copy-start(f32[1040]{0:T(1024)S(1)} %broadcast_multiply_fusion.10) | copy-start | bytes 12484
  106.3 20.9 %collective-permute-start.13 = (bf16[128,3328]{1,0:T(8,128)(2,1)S(1)}, bf16[128,3328]{1,0:T(8,128)(2,1)S(1)}, u32[]{:S(2)}, u32[]{:S(2)}) collective-permute-start(bf16[128,3328]{1,0:T(8,128)(2,1)S(1)} %get-tuple-element.30), channel_id=1, source_target_pairs={{0,1},{1,0},{2,3},{3,2},{4,5},{5,4},{6,7},{7,6},{8,9},{9,8},{10,11... | collective-permute-start | bytes 2555912 | tf_op jit(solution)/shard_map/ppermute | solution.py:428
  108.2 20.7 %collective-permute-start.11 = (bf16[128,3328]{1,0:T(8,128)(2,1)S(1)}, bf16[128,3328]{1,0:T(8,128)(2,1)S(1)}, u32[]{:S(2)}, u32[]{:S(2)}) collective-permute-start(bf16[128,3328]{1,0:T(8,128)(2,1)S(1)} %get-tuple-element.29), channel_id=1, source_target_pairs={{0,4},{1,5},{2,6},{3,7},{4,0},{5,1},{6,2},{7,3},{8,12},{9,13},{10,... | collective-permute-start | bytes 2555912 | tf_op jit(solution)/shard_map/ppermute | solution.py:428
  108.8 41.9 %collective-permute-start.16 = (bf16[32,2730]{1,0:T(8,128)(2,1)S(1)}, bf16[32,2730]{1,0:T(8,128)(2,1)S(1)}, u32[]{:S(2)}, u32[]{:S(2)}) collective-permute-start(bf16[32,2730]{1,0:T(8,128)(2,1)S(1)} %bitcast.145), channel_id=1, source_target_pairs={{0,8},{1,9},{2,10},{3,11},{4,12},{5,13},{6,14},{7,15},{8,0},{9,1},... | collective-permute-start | bytes 524168 | tf_op jit(solution)/shard_map/ppermute | solution.py:428
  127.4 39.7 %collective-permute-start.14 = (bf16[256,3328]{1,0:T(8,128)(2,1)S(1)}, bf16[256,3328]{1,0:T(8,128)(2,1)S(1)}, u32[]{:S(2)}, u32[]{:S(2)}) collective-permute-start(bf16[256,3328]{1,0:T(8,128)(2,1)S(1)} %pad_maximum_fusion.14), channel_id=1, source_target_pairs={{0,4},{1,5},{2,6},{3,7},{4,0},{5,1},{6,2},{7,3},{8,12},{9,13},{10,... | collective-permute-start | bytes 5111816 | tf_op jit(solution)/shard_map/ppermute | solution.py:428
  129.0 38.1 %collective-permute-start.12 = (bf16[256,3328]{1,0:T(8,128)(2,1)S(1)}, bf16[256,3328]{1,0:T(8,128)(2,1)S(1)}, u32[]{:S(2)}, u32[]{:S(2)}) collective-permute-start(bf16[256,3328]{1,0:T(8,128)(2,1)S(1)} %pad_maximum_fusion.13), channel_id=1, source_target_pairs={{0,1},{1,0},{2,3},{3,2},{4,5},{5,4},{6,7},{7,6},{8,9},{9,8},{10,11... | collective-permute-start | bytes 5111816 | tf_op jit(solution)/shard_map/ppermute | solution.py:428
  150.8 15.3 %collective-permute-start.17 = (bf16[64,2730]{1,0:T(8,128)(2,1)S(1)}, bf16[64,2730]{1,0:T(8,128)(2,1)S(1)}, u32[]{:S(2)}, u32[]{:S(2)}) collective-permute-start(bf16[64,2730]{1,0:T(8,128)(2,1)S(1)} %pad_maximum_fusion.24), channel_id=1, source_target_pairs={{0,16},{1,17},{2,18},{3,19},{4,20},{5,21},{6,22},{7,23},{8,24},{9,... | collective-permute-start | bytes 1048328 | tf_op jit(solution)/shard_map/ppermute | solution.py:428
  150.9 50.3 %collective-permute-start.7 = (bf16[512,3200]{1,0:T(8,128)(2,1)}, bf16[512,3200]{1,0:T(8,128)(2,1)}, u32[]{:S(2)}, u32[]{:S(2)}) collective-permute-start(bf16[512,3200]{1,0:T(8,128)(2,1)} %maximum_maximum_fusion.1), channel_id=1, source_target_pairs={{0,2},{1,3},{2,0},{3,1},{4,6},{5,7},{6,4},{7,5},{8,10},{9,11},{10,... | collective-permute-start | bytes 9830408 | tf_op jit(solution)/shard_map/ppermute | solution.py:428
  167.0 31.3 %collective-permute-start.18 = (bf16[128,1408]{1,0:T(8,128)(2,1)}, bf16[128,1408]{1,0:T(8,128)(2,1)}, u32[]{:S(2)}, u32[]{:S(2)}) collective-permute-start(bf16[128,1408]{1,0:T(8,128)(2,1)} %slice.494), channel_id=1, source_target_pairs={{0,4},{1,5},{2,6},{3,7},{4,0},{5,1},{6,2},{7,3},{8,12},{9,13},{10,... | collective-permute-start | bytes 1081352 | tf_op jit(solution)/shard_map/ppermute | solution.py:428
  168.1 24.9 %collective-permute-start.20 = (bf16[128,1322]{1,0:T(8,128)(2,1)S(1)}, bf16[128,1322]{1,0:T(8,128)(2,1)S(1)}, u32[]{:S(2)}, u32[]{:S(2)}) collective-permute-start(bf16[128,1322]{1,0:T(8,128)(2,1)S(1)} %slice.495), channel_id=1, source_target_pairs={{0,1},{1,0},{2,3},{3,2},{4,5},{5,4},{6,7},{7,6},{8,9},{9,8},{10,11... | collective-permute-start | bytes 1015304 | tf_op jit(solution)/shard_map/ppermute | solution.py:428
  192.9 95.4 %collective-permute-start.15 = (bf16[512,6656]{1,0:T(8,128)(2,1)}, bf16[512,6656]{1,0:T(8,128)(2,1)}, u32[]{:S(2)}, u32[]{:S(2)}) collective-permute-start(bf16[512,6656]{1,0:T(8,128)(2,1)} %maximum_maximum_fusion), channel_id=1, source_target_pairs={{0,2},{1,3},{2,0},{3,1},{4,6},{5,7},{6,4},{7,5},{8,10},{9,11},{10,... | collective-permute-start | bytes 20447240 | tf_op jit(solution)/shard_map/ppermute | solution.py:428
  196.9 17.9 %collective-permute-start.21 = (bf16[256,1322]{0,1:T(8,128)(2,1)}, bf16[256,1322]{0,1:T(8,128)(2,1)S(1)}, u32[]{:S(2)}, u32[]{:S(2)}) collective-permute-start(bf16[256,1322]{0,1:T(8,128)(2,1)} %copy.222), channel_id=1, source_target_pairs={{0,4},{1,5},{2,6},{3,7},{4,0},{5,1},{6,2},{7,3},{8,12},{9,13},{10,... | collective-permute-start | bytes 2030600 | tf_op jit(solution)/shard_map/ppermute | solution.py:428
  200.4 19.1 %collective-permute-start.19 = (bf16[256,1408]{1,0:T(8,128)(2,1)}, bf16[256,1408]{1,0:T(8,128)(2,1)}, u32[]{:S(2)}, u32[]{:S(2)}) collective-permute-start(bf16[256,1408]{1,0:T(8,128)(2,1)} %pad_maximum_fusion.19), channel_id=1, source_target_pairs={{0,1},{1,0},{2,3},{3,2},{4,5},{5,4},{6,7},{7,6},{8,9},{9,8},{10,11... | collective-permute-start | bytes 2162696 | tf_op jit(solution)/shard_map/ppermute | solution.py:428
  231.0 52.7 %collective-permute-start.22 = (bf16[512,2730]{0,1:T(8,128)(2,1)}, bf16[512,2730]{0,1:T(8,128)(2,1)}, u32[]{:S(2)}, u32[]{:S(2)}) collective-permute-start(bf16[512,2730]{0,1:T(8,128)(2,1)} %copy.225), channel_id=1, source_target_pairs={{0,2},{1,3},{2,0},{3,1},{4,6},{5,7},{6,4},{7,5},{8,10},{9,11},{10,... | collective-permute-start | bytes 8386568 | tf_op jit(solution)/shard_map/ppermute | solution.py:428
  614.9 52.4 %collective-permute-start.52 = (f32[4,2730]{1,0:T(4,128)S(1)}, f32[4,2730]{1,0:T(4,128)S(1)}, u32[]{:S(2)}, u32[]{:S(2)}) collective-permute-start(f32[4,2730]{1,0:T(4,128)S(1)} %pad_maximum_fusion.26), channel_id=1, source_target_pairs={{0,2},{1,3},{2,0},{3,1},{4,6},{5,7},{6,4},{7,5},{8,10},{9,11},{10,... | collective-permute-start | bytes 131048 | tf_op jit(solution)/shard_map/ppermute | solution.py:428
  616.6 72.5 %collective-permute-start.23 = (bf16[528,1024]{1,0:T(8,128)(2,1)}, bf16[528,1024]{1,0:T(8,128)(2,1)}, u32[]{:S(2)}, u32[]{:S(2)}) collective-permute-start(bf16[528,1024]{1,0:T(8,128)(2,1)} %slice.500), channel_id=1, source_target_pairs={{0,1},{1,0},{2,3},{3,2},{4,5},{5,4},{6,7},{7,6},{8,9},{9,8},{10,11... | collective-permute-start | bytes 3244040 | tf_op jit(solution)/shard_map/ppermute | solution.py:428
  627.2 18.8 %collective-permute-start.47 = (f32[512,8]{0,1:T(8,128)S(1)}, f32[512,8]{0,1:T(8,128)S(1)}, u32[]{:S(2)}, u32[]{:S(2)}) collective-permute-start(f32[512,8]{0,1:T(8,128)S(1)} %slice.571), channel_id=1, source_target_pairs={{0,2},{1,3},{2,0},{3,1},{4,6},{5,7},{6,4},{7,5},{8,10},{9,11},{10,... | collective-permute-start | bytes 49160 | tf_op jit(solution)/shard_map/ppermute | solution.py:428
  635.8 54.0 %collective-permute-start.25 = (bf16[528,1024]{1,0:T(8,128)(2,1)S(1)}, bf16[528,1024]{1,0:T(8,128)(2,1)S(1)}, u32[]{:S(2)}, u32[]{:S(2)}) collective-permute-start(bf16[528,1024]{1,0:T(8,128)(2,1)S(1)} %slice.508), channel_id=1, source_target_pairs={{0,1},{1,0},{2,3},{3,2},{4,5},{5,4},{6,7},{7,6},{8,9},{9,8},{10,11... | collective-permute-start | bytes 3244040 | tf_op jit(solution)/shard_map/ppermute | solution.py:428
  636.7 59.0 %collective-permute-start.40 = (bf16[512,2730]{0,1:T(8,128)(2,1)S(1)}, bf16[512,2730]{0,1:T(8,128)(2,1)}, u32[]{:S(2)}, u32[]{:S(2)}) collective-permute-start(bf16[512,2730]{0,1:T(8,128)(2,1)S(1)} %copy-done.114), channel_id=1, source_target_pairs={{0,2},{1,3},{2,0},{3,1},{4,6},{5,7},{6,4},{7,5},{8,10},{9,11},{10,... | collective-permute-start | bytes 8386568 | tf_op jit(solution)/shard_map/ppermute | solution.py:428
  646.0 19.9 %collective-permute-start.48 = (f32[256,8]{0,1:T(8,128)S(1)}, f32[256,8]{0,1:T(8,128)S(1)}, u32[]{:S(2)}, u32[]{:S(2)}) collective-permute-start(f32[256,8]{0,1:T(8,128)S(1)} %slice.573), channel_id=1, source_target_pairs={{0,1},{1,0},{2,3},{3,2},{4,5},{5,4},{6,7},{7,6},{8,9},{9,8},{10,11... | collective-permute-start | bytes 24584 | tf_op jit(solution)/shard_map/ppermute | solution.py:428
  665.9 3.6 collective-permute-start.49
  667.4 4.1 collective-permute-start.53
  669.6 6.1 collective-permute-start.50
  671.6 4.1 collective-permute-start.54
  675.7 31.6 %collective-permute-start.26 = (bf16[512,3072]{1,0:T(8,128)(2,1)}, bf16[512,3072]{1,0:T(8,128)(2,1)}, u32[]{:S(2)}, u32[]{:S(2)}) collective-permute-start(bf16[512,3072]{1,0:T(8,128)(2,1)} %pad_maximum_fusion.9), channel_id=1, source_target_pairs={{0,2},{1,3},{2,0},{3,1},{4,6},{5,7},{6,4},{7,5},{8,10},{9,11},{10,... | collective-permute-start | bytes 9437192 | tf_op jit(solution)/shard_map/ppermute | solution.py:428
  675.7 4.1 collective-permute-start.55
  679.9 3.6 collective-permute-start.51
  683.5 4.9 collective-permute-start.56
  688.4 80.8 %collective-permute-start.33 = (bf16[512,6656]{0,1:T(8,128)(2,1)}, bf16[512,6656]{0,1:T(8,128)(2,1)}, u32[]{:S(2)}, u32[]{:S(2)}) collective-permute-start(bf16[512,6656]{0,1:T(8,128)(2,1)} %fusion.9), channel_id=1, source_target_pairs={{0,2},{1,3},{2,0},{3,1},{4,6},{5,7},{6,4},{7,5},{8,10},{9,11},{10,... | collective-permute-start | bytes 20447240 | tf_op jit(solution)/shard_map/ppermute | solution.py:428
  703.2 26.9 %collective-permute-start.41 = (bf16[256,1408]{1,0:T(8,128)(2,1)}, bf16[256,1408]{1,0:T(8,128)(2,1)}, u32[]{:S(2)}, u32[]{:S(2)}) collective-permute-start(bf16[256,1408]{1,0:T(8,128)(2,1)} %slice.558), channel_id=1, source_target_pairs={{0,1},{1,0},{2,3},{3,2},{4,5},{5,4},{6,7},{7,6},{8,9},{9,8},{10,11... | collective-permute-start | bytes 2162696 | tf_op jit(solution)/shard_map/ppermute | solution.py:428
  706.3 18.3 %collective-permute-start.43 = (bf16[2,128,1322]{1,0,2:T(2,128)(2,1)}, bf16[2,128,1322]{1,0,2:T(2,128)(2,1)}, u32[]{:S(2)}, u32[]{:S(2)}) collective-permute-start(bf16[2,128,1322]{1,0,2:T(2,128)(2,1)} %copy.247), channel_id=1, source_target_pairs={{0,4},{1,5},{2,6},{3,7},{4,0},{5,1},{6,2},{7,3},{8,12},{9,13},{10,... | collective-permute-start | bytes 2030600 | tf_op jit(solution)/shard_map/ppermute | solution.py:428
  711.7 38.7 %collective-permute-start.27 = (bf16[256,1536]{1,0:T(8,128)(2,1)}, bf16[256,1536]{1,0:T(8,128)(2,1)}, u32[]{:S(2)}, u32[]{:S(2)}) collective-permute-start(bf16[256,1536]{1,0:T(8,128)(2,1)} %slice.515), channel_id=1, source_target_pairs={{0,1},{1,0},{2,3},{3,2},{4,5},{5,4},{6,7},{7,6},{8,9},{9,8},{10,11... | collective-permute-start | bytes 2359304 | tf_op jit(solution)/shard_map/ppermute | solution.py:428
  713.8 39.5 %collective-permute-start.29 = (bf16[2,128,1536]{2,1,0:T(8,128)(2,1)}, bf16[2,128,1536]{2,1,0:T(8,128)(2,1)}, u32[]{:S(2)}, u32[]{:S(2)}) collective-permute-start(bf16[2,128,1536]{2,1,0:T(8,128)(2,1)} %slice_bitcast_fusion.6), channel_id=1, source_target_pairs={{0,4},{1,5},{2,6},{3,7},{4,0},{5,1},{6,2},{7,3},{8,12},{9,13},{10,... | collective-permute-start | bytes 2359304 | tf_op jit(solution)/shard_map/ppermute | solution.py:428
  729.1 17.5 %collective-permute-start.44 = (bf16[128,1322]{1,0:T(8,128)(2,1)S(1)}, bf16[128,1322]{1,0:T(8,128)(2,1)S(1)}, u32[]{:S(2)}, u32[]{:S(2)}) collective-permute-start(bf16[128,1322]{1,0:T(8,128)(2,1)S(1)} %slice_bitcast_fusion.12), channel_id=1, source_target_pairs={{0,1},{1,0},{2,3},{3,2},{4,5},{5,4},{6,7},{7,6},{8,9},{9,8},{10,11... | collective-permute-start | bytes 1015304 | tf_op jit(solution)/shard_map/ppermute | solution.py:428
  731.6 17.0 %collective-permute-start.42 = (bf16[128,1408]{1,0:T(8,128)(2,1)S(1)}, bf16[128,1408]{1,0:T(8,128)(2,1)S(1)}, u32[]{:S(2)}, u32[]{:S(2)}) collective-permute-start(bf16[128,1408]{1,0:T(8,128)(2,1)S(1)} %slice.560), channel_id=1, source_target_pairs={{0,4},{1,5},{2,6},{3,7},{4,0},{5,1},{6,2},{7,3},{8,12},{9,13},{10,... | collective-permute-start | bytes 1081352 | tf_op jit(solution)/shard_map/ppermute | solution.py:428
  748.8 18.7 %collective-permute-start.45 = (bf16[64,2730]{1,0:T(8,128)(2,1)S(1)}, bf16[64,2730]{1,0:T(8,128)(2,1)S(1)}, u32[]{:S(2)}, u32[]{:S(2)}) collective-permute-start(bf16[64,2730]{1,0:T(8,128)(2,1)S(1)} %pad_maximum_fusion.23), channel_id=1, source_target_pairs={{0,16},{1,17},{2,18},{3,19},{4,20},{5,21},{6,22},{7,23},{8,24},{9,... | collective-permute-start | bytes 1048328 | tf_op jit(solution)/shard_map/ppermute | solution.py:428
  752.2 16.2 %collective-permute-start.28 = (bf16[128,1536]{1,0:T(8,128)(2,1)S(1)}, bf16[128,1536]{1,0:T(8,128)(2,1)S(1)}, u32[]{:S(2)}, u32[]{:S(2)}) collective-permute-start(bf16[128,1536]{1,0:T(8,128)(2,1)S(1)} %slice.517), channel_id=1, source_target_pairs={{0,4},{1,5},{2,6},{3,7},{4,0},{5,1},{6,2},{7,3},{8,12},{9,13},{10,... | collective-permute-start | bytes 1179656 | tf_op jit(solution)/shard_map/ppermute | solution.py:428
  755.4 36.9 %collective-permute-start.30 = (bf16[128,1536]{1,0:T(8,128)(2,1)}, bf16[128,1536]{1,0:T(8,128)(2,1)}, u32[]{:S(2)}, u32[]{:S(2)}) collective-permute-start(bf16[128,1536]{1,0:T(8,128)(2,1)} %slice_bitcast_fusion.10), channel_id=1, source_target_pairs={{0,1},{1,0},{2,3},{3,2},{4,5},{5,4},{6,7},{7,6},{8,9},{9,8},{10,11... | collective-permute-start | bytes 1179656 | tf_op jit(solution)/shard_map/ppermute | solution.py:428
  768.4 86.5 %collective-permute-start.46 = (bf16[32,2730]{1,0:T(8,128)(2,1)}, bf16[32,2730]{1,0:T(8,128)(2,1)}, u32[]{:S(2)}, u32[]{:S(2)}) collective-permute-start(bf16[32,2730]{1,0:T(8,128)(2,1)} %slice.569), channel_id=1, source_target_pairs={{0,8},{1,9},{2,10},{3,11},{4,12},{5,13},{6,14},{7,15},{8,0},{9,1},... | collective-permute-start | bytes 524168 | tf_op jit(solution)/shard_map/ppermute | solution.py:428
  778.2 38.7 %collective-permute-start.34 = (bf16[256,3328]{0,1:T(8,128)(2,1)}, bf16[256,3328]{0,1:T(8,128)(2,1)}, u32[]{:S(2)}, u32[]{:S(2)}) collective-permute-start(bf16[256,3328]{0,1:T(8,128)(2,1)} %slice.539), channel_id=1, source_target_pairs={{0,1},{1,0},{2,3},{3,2},{4,5},{5,4},{6,7},{7,6},{8,9},{9,8},{10,11... | collective-permute-start | bytes 5111816 | tf_op jit(solution)/shard_map/ppermute | solution.py:428
  791.2 40.2 %collective-permute-start.36 = (bf16[2,128,3328]{1,2,0:T(8,128)(2,1)S(1)}, bf16[2,128,3328]{1,2,0:T(8,128)(2,1)S(1)}, u32[]{:S(2)}, u32[]{:S(2)}) collective-permute-start(bf16[2,128,3328]{1,2,0:T(8,128)(2,1)S(1)} %bitcast.144), channel_id=1, source_target_pairs={{0,4},{1,5},{2,6},{3,7},{4,0},{5,1},{6,2},{7,3},{8,12},{9,13},{10,... | collective-permute-start | bytes 5111816 | tf_op jit(solution)/shard_map/ppermute | solution.py:428
  794.2 62.5 %collective-permute-start.31 = (bf16[64,3072]{1,0:T(8,128)(2,1)}, bf16[64,3072]{1,0:T(8,128)(2,1)}, u32[]{:S(2)}, u32[]{:S(2)}) collective-permute-start(bf16[64,3072]{1,0:T(8,128)(2,1)} %pad_maximum_fusion.22), channel_id=1, source_target_pairs={{0,16},{1,17},{2,18},{3,19},{4,20},{5,21},{6,22},{7,23},{8,24},{9,... | collective-permute-start | bytes 1179656 | tf_op jit(solution)/shard_map/ppermute | solution.py:428
  819.4 28.3 %collective-permute-start.35 = (bf16[128,3328]{0,1:T(8,128)(2,1)S(1)}, bf16[128,3328]{0,1:T(8,128)(2,1)S(1)}, u32[]{:S(2)}, u32[]{:S(2)}) collective-permute-start(bf16[128,3328]{0,1:T(8,128)(2,1)S(1)} %slice.541), channel_id=1, source_target_pairs={{0,4},{1,5},{2,6},{3,7},{4,0},{5,1},{6,2},{7,3},{8,12},{9,13},{10,... | collective-permute-start | bytes 2555912 | tf_op jit(solution)/shard_map/ppermute | solution.py:428
  831.8 17.1 %collective-permute-start.37 = (bf16[128,3328]{0,1:T(8,128)(2,1)S(1)}, bf16[128,3328]{0,1:T(8,128)(2,1)S(1)}, u32[]{:S(2)}, u32[]{:S(2)}) collective-permute-start(bf16[128,3328]{0,1:T(8,128)(2,1)S(1)} %slice_bitcast_fusion.4), channel_id=1, source_target_pairs={{0,1},{1,0},{2,3},{3,2},{4,5},{5,4},{6,7},{7,6},{8,9},{9,8},{10,11... | collective-permute-start | bytes 2555912 | tf_op jit(solution)/shard_map/ppermute | solution.py:428
  851.1 38.5 %collective-permute-start.38 = (bf16[64,6656]{1,0:T(8,128)(2,1)}, bf16[64,6656]{1,0:T(8,128)(2,1)S(1)}, u32[]{:S(2)}, u32[]{:S(2)}) collective-permute-start(bf16[64,6656]{1,0:T(8,128)(2,1)} %copy.236), channel_id=1, source_target_pairs={{0,16},{1,17},{2,18},{3,19},{4,20},{5,21},{6,22},{7,23},{8,24},{9,... | collective-permute-start | bytes 2555912 | tf_op jit(solution)/shard_map/ppermute | solution.py:428
  859.4 35.7 %collective-permute-start.32 = (bf16[32,3072]{1,0:T(8,128)(2,1)}, bf16[32,3072]{1,0:T(8,128)(2,1)}, u32[]{:S(2)}, u32[]{:S(2)}) collective-permute-start(bf16[32,3072]{1,0:T(8,128)(2,1)} %slice.526), channel_id=1, source_target_pairs={{0,8},{1,9},{2,10},{3,11},{4,12},{5,13},{6,14},{7,15},{8,0},{9,1},... | collective-permute-start | bytes 589832 | tf_op jit(solution)/shard_map/ppermute | solution.py:428
  895.1 12.0 %collective-permute-start.39 = (bf16[32,6656]{1,0:T(8,128)(2,1)}, bf16[32,6656]{1,0:T(8,128)(2,1)}, u32[]{:S(2)}, u32[]{:S(2)}) collective-permute-start(bf16[32,6656]{1,0:T(8,128)(2,1)} %copy.238), channel_id=1, source_target_pairs={{0,8},{1,9},{2,10},{3,11},{4,12},{5,13},{6,14},{7,15},{8,0},{9,1},... | collective-permute-start | bytes 1277960 | tf_op jit(solution)/shard_map/ppermute | solution.py:428
  (127 other events, 1714.1 us)

commit v2 on v1

--- a/solution.py
+++ b/solution.py
@@ -417,8 +417,12 @@
 BIT_X, BIT_CORE, BIT_Y, BIT_Z0, BIT_Z1 = 1, 2, 4, 8, 16
 ROWS = 1040
 KEYS = 1024
+WIDTH = 1024
+HALF = 512
 HEAD_COLS = 256
+STEP = 208
 LOG2E = math.log2(math.e)
+COST = 4
 F32 = jnp.float32
 BF16 = jnp.bfloat16
 
@@ -448,42 +452,110 @@
     return lax.dot_general(a, b, (((0,), (0,)), ((), ())), preferred_element_type=F32)
 
 
-def gather_columns(local, split, deps):
-    z_dep, xy_dep = deps
-    part = after(local, *z_dep)
-    part = joined(part, swap_over(part, BIT_Z0))
-    part = joined(part, swap_over(part, BIT_Z1))
-    left, right = after(part[:, :split], *xy_dep), after(part[:, split:], *xy_dep)
-    left = joined(left, swap_over(left, BIT_Y))
-    right = joined(right, swap_over(right, BIT_X))
-    left_far, right_far = swap_over(left, BIT_X), swap_over(right, BIT_Y)
-    left = joined(left, left_far)
-    right = joined(right[:128], right_far[:128], right[128:], right_far[128:])
-    near = joined(left, right, axis=1)
-    far = swap_over(near, BIT_CORE)
-    return joined(near, far), ((part,), (left_far, right_far))
-
-
-def add_rounded(a, b):
-    return (a.astype(F32) + b.astype(F32)).astype(BF16)
-
-
-def scatter_columns(keep, send, split):
-    total = add_rounded(keep, swap_over(send, BIT_CORE))
-    left, right = total[:, :split], total[:, split:].reshape(2, 2, 128, -1)
-    left = add_rounded(left[:256], swap_over(left[256:], BIT_X))
-    right = add_rounded(right[:, 0], swap_over(right[:, 1], BIT_Y))
-    left = add_rounded(left[:128], swap_over(left[128:], BIT_Y))
-    right = add_rounded(right[0], swap_over(right[1], BIT_X))
-    total = joined(left, right, axis=1)
-    total = add_rounded(total[:64], swap_over(total[64:], BIT_Z1))
-    return total[:32].astype(F32) + swap_over(total[32:], BIT_Z0).astype(F32)
-
-
-def sum_small(value):
-    for bit in (BIT_CORE, BIT_X, BIT_Y, BIT_Z0, BIT_Z1):
-        value = value + swap_over(value, bit)
-    return value
+def cost_of(flops, bytes_accessed, transcendentals):
+    return pl.CostEstimate(
+        flops=int(COST * flops), bytes_accessed=int(COST * bytes_accessed), transcendentals=int(COST * transcendentals)
+    )
+
+
+def pack_rows(*parts):
+    total, columns = sum(p.shape[0] for p in parts), parts[0].shape[1]
+    blocks = columns // 128
+    steps = next(n for n in (4, 5, 3, 2, 1) if blocks % n == 0)
+    tile = columns // steps
+
+    def kernel(*refs):
+        out, start = refs[len(parts)], 0
+        for ref in refs[: len(parts)]:
+            out[start : start + ref.shape[0], :] = ref[...]
+            start += ref.shape[0]
+
+    return pl.pallas_call(
+        kernel,
+        grid=(steps,),
+        in_specs=[pl.BlockSpec((p.shape[0], tile), lambda j: (0, j)) for p in parts],
+        out_specs=pl.BlockSpec((total, tile), lambda j: (0, j)),
+        out_shape=jax.ShapeDtypeStruct((total, columns), parts[0].dtype),
+        compiler_params=pltpu.CompilerParams(vmem_limit_bytes=32 << 20),
+        cost_estimate=cost_of(flops=0, bytes_accessed=4 * total * columns, transcendentals=0),
+        name="pack_rows",
+    )(*parts)
+
+
+class Gather:
+    def __init__(self, local):
+        self.part = local
+
+    def along_z0(self, *deps):
+        part = after(self.part, *deps)
+        far = swap_over(part, BIT_Z0)
+        self.part = joined(part, far)
+        return far
+
+    def along_z1(self, *deps):
+        part = after(self.part, *deps)
+        far = swap_over(part, BIT_Z1)
+        self.part = joined(part, far)
+        return far
+
+    def along_xy(self, *deps):
+        part = after(self.part, *deps)
+        self.over = swap_over(part, BIT_X), swap_over(part, BIT_Y)
+        return self.over
+
+    def corners(self, *deps):
+        over_x, over_y = after(self.over, *deps)
+        self.corner = swap_over(over_y[:64], BIT_X), swap_over(over_x[64:], BIT_Y)
+        return self.corner
+
+    def whole(self, *deps):
+        parts = after((self.part, self.over, self.corner), *deps)
+        self.near = pack_rows(parts[0], parts[1][1], parts[1][0], *parts[2])
+        self.far = swap_over(self.near, BIT_CORE)
+        return self.near
+
+
+def rounded_sum(*terms):
+    total = terms[0].astype(F32)
+    for term in terms[1:]:
+        total = total + term.astype(F32)
+    return total.astype(BF16)
+
+
+class Scatter:
+    def __init__(self, near, far):
+        self.near, self.far = near, far
+
+    def over_core(self, *deps):
+        self.total = rounded_sum(self.near, swap_over(after(self.far, *deps), BIT_CORE))
+        return self.total
+
+    def corners(self, *deps):
+        total = after(self.total, *deps)
+        from_x, from_y = swap_over(total[384:448], BIT_X), swap_over(total[448:512], BIT_Y)
+        to_y = joined(rounded_sum(total[128:192], from_x), total[192:256])
+        to_x = joined(total[256:320], rounded_sum(total[320:384], from_y))
+        self.sides = to_x, to_y
+        return self.sides
+
+    def over_xy(self, *deps):
+        to_x, to_y = after(self.sides, *deps)
+        self.total = rounded_sum(self.total[:128], swap_over(to_y, BIT_Y), swap_over(to_x, BIT_X))
+        return self.total
+
+    def along_z1(self, *deps):
+        total = after(self.total, *deps)
+        self.total = rounded_sum(total[:64], swap_over(total[64:], BIT_Z1))
+        return self.total
+
+    def along_z0(self, *deps):
+        total = after(self.total, *deps)
+        return total[:32].astype(F32) + swap_over(total[32:], BIT_Z0).astype(F32)
+
+
+def sum_over(value, bit, *deps):
+    value = after(value, *deps)
+    return value + swap_over(value, bit)
 
 
 def scatter_small(value):
@@ -502,15 +574,17 @@
 
 
 def attention_kernel(
-    x_ref, wq_ref, wk_ref, wv_ref, b_ref, c_ref, s1_ref, s2_ref, q_ref, k_ref, v_ref, o_ref, l_ref, stat_ref, *, step
+    x_ref, qn_ref, qf_ref, kn_ref, kf_ref, vn_ref, vf_ref, b_ref, c_ref, s1_ref, s2_ref,
+    q_ref, k_ref, v_ref, o_ref, l_ref, stat_ref, *, step
 ):
-    x = x_ref[...]
+    def project(near_ref, far_ref):
+        return dot_nn(x_ref[:, :HALF], near_ref[...]) + dot_nn(x_ref[:, HALF:], far_ref[...])
+
     c, s1, s2 = twice(c_ref[...]), twice(s1_ref[...]), twice(s2_ref[...])
-    q = dot_nn(x, wq_ref[...]) + b_ref[2:3, :]
+    q = project(qn_ref, qf_ref) + b_ref[2:3, :]
     q_ref[...] = (rotate_lanes(q, c, s1, s2) * (LOG2E / 8)).astype(BF16)
-    k = dot_nn(x, wk_ref[...])
-    k_ref[...] = rotate_lanes(k, c, s1, s2).astype(BF16)
-    v_ref[...] = (dot_nn(x, wv_ref[...]) + b_ref[3:4, :]).astype(BF16)
+    k_ref[...] = rotate_lanes(project(kn_ref, kf_ref), c, s1, s2).astype(BF16)
+    v_ref[...] = (project(vn_ref, vf_ref) + b_ref[3:4, :]).astype(BF16)
     lane = lax.broadcasted_iota(jnp.int32, (1, 128), 1)
     low_half = lane < 64
 
@@ -544,31 +618,33 @@
     l_ref[...] = stat_ref[...].T[0:8, :]
 
 
-def attention_forward(x, w, vectors, tables, step=208):
-    def block(first):
-        return pl.BlockSpec((1024, HEAD_COLS), lambda j: (0, first + j))
+def attention_forward(x, near, far, biases, head_block, at, tables, step=STEP):
+    def block(index):
+        return pl.BlockSpec((HALF, HEAD_COLS), lambda j: (0, index))
 
     def whole(a):
         return pl.BlockSpec(a.shape, lambda j: (0, 0))
 
-    out = pl.BlockSpec((ROWS, HEAD_COLS), lambda j: (0, j))
+    out = pl.BlockSpec((ROWS, HEAD_COLS), lambda j: (0, 0))
     return pl.pallas_call(
         functools.partial(attention_kernel, step=step),
-        grid=(4,),
-        in_specs=[whole(x), block(0), block(4), block(8), pl.BlockSpec((8, HEAD_COLS), lambda j: (0, j))]
+        grid=(1,),
+        in_specs=[whole(x)]
+        + [block(at + first) for first in (0, 0, 2, 2, 4, 4)]
+        + [pl.BlockSpec((8, HEAD_COLS), lambda j: (0, head_block))]
         + [whole(t) for t in tables],
-        out_specs=[out] * 4 + [pl.BlockSpec((8, ROWS), lambda j: (j, 0))],
-        out_shape=[jax.ShapeDtypeStruct((ROWS, 1024), BF16)] * 4 + [jax.ShapeDtypeStruct((32, ROWS), F32)],
+        out_specs=[out] * 4 + [pl.BlockSpec((8, ROWS), lambda j: (0, 0))],
+        out_shape=[jax.ShapeDtypeStruct((ROWS, HEAD_COLS), BF16)] * 4 + [jax.ShapeDtypeStruct((8, ROWS), F32)],
         scratch_shapes=[pltpu.VMEM((ROWS, 128), F32)],
         compiler_params=pltpu.CompilerParams(vmem_limit_bytes=48 << 20),
-        cost_estimate=pl.CostEstimate(flops=30_000_000_000, bytes_accessed=20_000_000, transcendentals=17_000_000),
+        cost_estimate=cost_of(flops=7_500_000_000, bytes_accessed=7_000_000, transcendentals=4_300_000),
         name="attention_forward",
-    )(x, w, w, w, vectors, *tables)
+    )(x, near, far, near, far, near, far, biases, *tables)
 
 
 def attention_back_kernel(
     q_ref, k_ref, v_ref, g_ref, o_ref, l_ref, c_ref, s1_ref, s2_ref,
-    dq_ref, dk_ref, dv_ref, dq_sum, dk_sum, dv_sum, delta_ref, *, step
+    dq_ref, dk_ref, dv_ref, sum_ref, dq_sum, dk_sum, dv_sum, delta_ref, *, step
 ):
     lane = lax.broadcasted_iota(jnp.int32, (1, 128), 1)
     low_half = lane < 64
@@ -626,27 +702,70 @@
     first = lax.broadcasted_iota(jnp.int32, (16, 1), 0) == 0
     dq_sum[KEYS : KEYS + 16, :] = jnp.where(first, dq_class, 0.0)
     c, s1, s2 = twice(c_ref[...]), twice(s1_ref[...]), twice(s2_ref[...])
-    dq_ref[...] = (rotate_lanes(dq_sum[...], c, -s1, -s2) * 0.125).astype(BF16)
+    dq = (rotate_lanes(dq_sum[...], c, -s1, -s2) * 0.125).astype(BF16)
+    dv = dv_sum[...].astype(BF16)
+    dq_ref[...] = dq
     dk_ref[...] = (rotate_lanes(dk_sum[...], c, -s1, -s2) * (1.0 / LOG2E)).astype(BF16)
-    dv_ref[...] = dv_sum[...].astype(BF16)
-
-
-def attention_backward(q, k, v, g, o, log_sums, tables, step=256):
+    dv_ref[...] = dv
+    sum_ref[0:1, :] = jnp.sum(dq.astype(F32), axis=0, keepdims=True)
+    sum_ref[1:2, :] = jnp.sum(dv.astype(F32), axis=0, keepdims=True)
+    sum_ref[2:8, :] = jnp.zeros((6, HEAD_COLS), F32)
+
+
+def attention_backward(q, k, v, o, log_sums, g, tables, step=256):
     def whole(a):
         return pl.BlockSpec(a.shape, lambda j: (0, 0))
 
-    block = pl.BlockSpec((ROWS, HEAD_COLS), lambda j: (0, j))
+    block = pl.BlockSpec((ROWS, HEAD_COLS), lambda j: (0, 0))
     return pl.pallas_call(
         functools.partial(attention_back_kernel, step=step),
-        grid=(4,),
-        in_specs=[block] * 5 + [pl.BlockSpec((8, ROWS), lambda j: (j, 0))] + [whole(t) for t in tables],
-        out_specs=[block] * 3,
-        out_shape=[jax.ShapeDtypeStruct((ROWS, 1024), BF16)] * 3,
+        grid=(1,),
+        in_specs=[block] * 5 + [pl.BlockSpec((8, ROWS), lambda j: (0, 0))] + [whole(t) for t in tables],
+        out_specs=[block] * 3 + [pl.BlockSpec((8, HEAD_COLS), lambda j: (0, 0))],
+        out_shape=[jax.ShapeDtypeStruct((ROWS, HEAD_COLS), BF16)] * 3
+        + [jax.ShapeDtypeStruct((8, HEAD_COLS), F32)],
         scratch_shapes=[pltpu.VMEM((ROWS, HEAD_COLS), F32)] * 3 + [pltpu.VMEM((8, ROWS), F32)],
         compiler_params=pltpu.CompilerParams(vmem_limit_bytes=48 << 20),
-        cost_estimate=pl.CostEstimate(flops=50_000_000_000, bytes_accessed=20_000_000, transcendentals=17_000_000),
+        cost_estimate=cost_of(
+            flops=13_000_000_000, bytes_accessed=5_000_000, transcendentals=4_300_000
+        ),
         name="attention_backward",
     )(q, k, v, g, o, log_sums, *tables)
+
+
+def over_rows(kernel, name, tiled, held, outs, sums=(), flops=0, step=STEP):
+    in_specs = [pl.BlockSpec((step, a.shape[1]), lambda i: (i, 0)) for a in tiled]
+    held = [h if isinstance(h, tuple) else (h, h.shape, 0) for h in held]
+    in_specs += [
+        pl.BlockSpec(shape, lambda i, column=column: (0, column), pipeline_mode=pl.Buffered(1))
+        for _, shape, column in held
+    ]
+    held = [h[0] for h in held]
+    out_specs = [pl.BlockSpec((step, n), lambda i: (i, 0)) for n, _ in outs]
+    out_specs += [pl.BlockSpec((8, n), lambda i: (0, 0)) for n in sums]
+    out_shape = [jax.ShapeDtypeStruct((ROWS, n), t) for n, t in outs]
+    out_shape += [jax.ShapeDtypeStruct((8, n), F32) for n in sums]
+    moved = sum(a.size * a.dtype.itemsize for a in list(tiled) + list(held))
+    moved += sum(s.size * s.dtype.itemsize for s in out_shape)
+    return pl.pallas_call(
+        kernel,
+        grid=(ROWS // step,),
+        in_specs=in_specs,
+        out_specs=out_specs,
+        out_shape=out_shape,
+        compiler_params=pltpu.CompilerParams(vmem_limit_bytes=56 << 20),
+        cost_estimate=cost_of(flops=flops, bytes_accessed=moved, transcendentals=0),
+        name=name,
+    )(*tiled, *held)
+
+
+def add_sums(ref, *rows):
+    @pl.when(pl.program_id(0) == 0)
+    def _():
+        ref[...] = jnp.zeros_like(ref)
+
+    for i, value in enumerate(rows):
+        ref[i : i + 1, :] += jnp.sum(value, axis=0, keepdims=True)
 
 
 def unit_norm(values):
@@ -663,44 +782,216 @@
     )
 
 
+def vectors_kernel(near_ref, far_ref, order_ref, vec_ref, head_ref):
+    rows = jnp.concatenate([near_ref[...].astype(F32).T, far_ref[...].astype(F32).T], axis=1)[0:8]
+    vec_ref[...] = rows
+    head_ref[...] = dot_nt(rows.astype(BF16), order_ref[...])
+
+
+def gathered_vectors(near, far, order):
+    block = pl.BlockSpec((HALF, 128), lambda j: (0, 3 * HALF // 128))
+    out = pl.BlockSpec((8, WIDTH), lambda j: (0, 0))
+    return pl.pallas_call(
+        vectors_kernel,
+        grid=(1,),
+        in_specs=[block, block, pl.BlockSpec(order.shape, lambda j: (0, 0))],
+        out_specs=[out, out],
+        out_shape=[jax.ShapeDtypeStruct((8, WIDTH), F32)] * 2,
+        cost_estimate=cost_of(flops=40_000_000, bytes_accessed=2_400_000, transcendentals=0),
+        name="vectors",
+    )(near, far, order)
+
+
+def sigmoid_of(x):
+    return 0.5 * jnp.tanh(0.5 * x) + 0.5
+
+
+def start_kernel(rows_ref, order_ref, vec_ref, tokens_ref, normed_ref):
+    tokens = dot_nn(rows_ref[...], order_ref[...])
+    tokens_ref[...] = tokens.astype(BF16)
+    unit, _ = unit_norm(tokens)
+    normed_ref[...] = (unit * vec_ref[0:1, :] + vec_ref[1:2, :]).astype(BF16)
+
+
+def middle_kernel(a0_ref, a1_ref, a2_ref, a3_ref, tokens_ref, na_ref, nb_ref, fa_ref, fb_ref, vec_ref, middle_ref, normed_ref):
+    low = jnp.concatenate([a0_ref[...], a1_ref[...]], axis=1)
+    high = jnp.concatenate([a2_ref[...], a3_ref[...]], axis=1)
+    branch = jnp.concatenate(
+        [
+            dot_nt(low, na_ref[...]) + dot_nt(high, nb_ref[...]),
+            dot_nt(low, fa_ref[...]) + dot_nt(high, fb_ref[...]),
+        ],
+        axis=1,
+    )
+    middle = tokens_ref[...].astype(F32) + (branch + vec_ref[4:5, :])
+    middle_ref[...] = middle.astype(BF16)
+    unit, _ = unit_norm(middle)
+    normed_ref[...] = (unit * vec_ref[5:6, :] + vec_ref[6:7, :]).astype(BF16)
+
+
+def hidden_kernel(x_ref, gn_ref, gf_ref, un_ref, uf_ref, ffn_ref, gate_ref, up_ref, inner_ref, stat_ref, *, hidden):
+    near, far = x_ref[:, :HALF], x_ref[:, HALF:]
+    gate = dot_nn(near, gn_ref[...]) + dot_nn(far, gf_ref[...]) + ffn_ref[0:1, :]
+    up = dot_nn(near, un_ref[...]) + dot_nn(far, uf_ref[...]) + ffn_ref[1:2, :]
+    gate_ref[...] = gate.astype(gate_ref.dtype)
+    up_ref[...] = up.astype(up_ref.dtype)
+    mix = gate * sigmoid_of(gate) * up
+    mean = jnp.sum(mix, axis=1, keepdims=True) * (1.0 / hidden)
+    real = lax.broadcasted_iota(jnp.int32, (1, mix.shape[1]), 1) < hidden
+    centred = jnp.where(real, mix - mean, 0.0)
+    inv_std = lax.rsqrt(jnp.sum(centred * centred, axis=1, keepdims=True) * (1.0 / hidden) + epsilon)
+    inner_ref[...] = (centred * inv_std * ffn_ref[2:3, :] + ffn_ref[3:4, :]).astype(BF16)
+    lane = lax.broadcasted_iota(jnp.int32, (1, 128), 1)
+    stat_ref[...] = jnp.where(lane == 0, mean, inv_std)
+
+
+def result_kernel(inner_ref, middle_ref, near_ref, far_ref, vec_ref, order_ref, keep_ref, out_ref):
+    inner = inner_ref[...]
+    branch = jnp.concatenate([dot_nt(inner, near_ref[...]), dot_nt(inner, far_ref[...])], axis=1)
+    result = middle_ref[...].astype(F32) + (branch + vec_ref[7:8, :])
+    rounded = (result * keep_ref[0:1, 0:1]).astype(BF16)
+    out_ref[...] = dot_nt(rounded, order_ref[...]).astype(BF16)
+
+
+def hidden_back_kernel(
+    d_ref, gate_ref, up_ref, stat_ref, order_ref, keep_ref, near_ref, far_ref, ffn_ref,
+    branch_ref, dgate_ref, dup_ref, wide_ref, sum_ref, *, hidden
+):
+    branch = (dot_nn(d_ref[...], order_ref[...]) * keep_ref[0:1, 0:1]).astype(BF16)
+    branch_ref[...] = branch
+    g_inner = dot_nn(branch[:, :HALF], near_ref[...]) + dot_nn(branch[:, HALF:], far_ref[...])
+    gate, up = gate_ref[...].astype(F32), up_ref[...].astype(F32)
+    sigmoid = sigmoid_of(gate)
+    silu = gate * sigmoid
+    mean, inv_std = stat_ref[:, 0:1], stat_ref[:, 1:2]
+    unit = (silu * up - mean) * inv_std
+    g_unit = g_inner * ffn_ref[2:3, :]
+    share = 1.0 / hidden
+    g_mix = inv_std * (
+        g_unit
+        - jnp.sum(g_unit, axis=1, keepdims=True) * share
+        - unit * (jnp.sum(g_unit * unit, axis=1, keepdims=True) * share)
+    )
+    d_gate = (g_mix * up * (sigmoid * (1.0 + gate * (1.0 - sigmoid)))).astype(BF16)
+    d_up = (g_mix * silu).astype(BF16)
+    dgate_ref[...] = d_gate
+    dup_ref[...] = d_up
+    add_sums(wide_ref, d_gate.astype(F32), d_up.astype(F32), g_inner * unit, g_inner)
+    add_sums(sum_ref, branch.astype(F32))
+
+
+def middle_back_kernel(
+    dgate_ref, dup_ref, branch_ref, middle_ref, gn_ref, gf_ref, un_ref, uf_ref, na_ref, nb_ref, fa_ref, fb_ref, vec_ref,
+    low_ref, d0_ref, d1_ref, d2_ref, d3_ref, sum_ref
+):
+    d_gate, d_up = dgate_ref[...], dup_ref[...]
+    g_two = jnp.concatenate(
+        [
+            dot_nt(d_gate, gn_ref[...]) + dot_nt(d_up, un_ref[...]),
+            dot_nt(d_gate, gf_ref[...]) + dot_nt(d_up, uf_ref[...]),
+        ],
+        axis=1,
+    )
+    unit, inv_std = unit_norm(middle_ref[...].astype(F32))
+    g_middle = branch_ref[...].astype(F32) + unit_norm_back(g_two * vec_ref[5:6, :], unit, inv_std)
+    low = g_middle.astype(BF16)
+    low_ref[...] = low
+    near, far = low[:, :HALF], low[:, HALF:]
+    d_low = (dot_nn(near, na_ref[...]) + dot_nn(far, fa_ref[...])).astype(BF16)
+    d_high = (dot_nn(near, nb_ref[...]) + dot_nn(far, fb_ref[...])).astype(BF16)
+    d0_ref[...], d1_ref[...] = d_low[:, :HEAD_COLS], d_low[:, HEAD_COLS:]
+    d2_ref[...], d3_ref[...] = d_high[:, :HEAD_COLS], d_high[:, HEAD_COLS:]
+    add_sums(sum_ref, low.astype(F32), g_two * unit, g_two)
+
+
+def last_kernel(*refs):
+    grads = refs[:12]
+    gmid_ref, tokens_ref, an_ref, af_ref, bn_ref, bf_ref, vec_ref, order_ref, grad_ref, sum_ref = refs[12:]
+
+    def back(low_w, high_w):
+        total = 0.0
+        for first, w_ref in ((0, low_w), (6, high_w)):
+            for i in range(3):
+                g = jnp.concatenate([grads[first + i][...], grads[first + 3 + i][...]], axis=1)
+                total = total + dot_nt(g, w_ref[:, i * HALF : i * HALF + HALF])
+        return total
+
+    g_one = jnp.concatenate([back(an_ref, bn_ref), back(af_ref, bf_ref)], axis=1)
+    unit, inv_std = unit_norm(tokens_ref[...].astype(F32))
+    grad = gmid_ref[...].astype(F32) + unit_norm_back(g_one * vec_ref[0:1, :], unit, inv_std)
+    grad_ref[...] = dot_nt(grad.astype(BF16), order_ref[...]).astype(BF16)
+    add_sums(sum_ref, g_one * unit, g_one)
+
+
+def weight_grads(pairs, tile=HEAD_COLS):
+    sources = []
+    for x, _ in pairs:
+        if not any(x is s for s in sources):
+            sources.append(x)
+    starts, count = [], 0
+    for x, g in pairs:
+        starts.append(count)
+        count += g.shape[1] // tile
+    ends = starts[1:] + [count]
+
+    def kernel(*refs):
+        xs, gs = refs[: len(sources)], refs[len(sources) : len(sources) + len(pairs)]
+        near_ref, far_ref, turned, last = refs[len(sources) + len(pairs) :]
+        j = pl.program_id(0)
+        for s, x in enumerate(sources):
+            begin = min(a for a, (px, _) in zip(starts, pairs) if px is x)
+
+            @pl.when(j == begin)
+            def _(s=s):
+                turned[...] = xs[s][0:KEYS, :].T
+                last[...] = xs[s][KEYS : KEYS + 16, :].astype(F32).T
+
+        for i in range(len(pairs)):
+
+            @pl.when((j >= starts[i]) & (j < ends[i]))
+            def _(i=i):
+                main = dot_nn(turned[...], gs[i][0:KEYS, :])
+                row = gs[i][KEYS : KEYS + 16, :].astype(F32)[0:1]
+                out = (main + last[:, 0:1] * row).astype(BF16)
+                near_ref[...] = out[:HALF]
+                far_ref[...] = out[HALF:]
+
+    def g_spec(i):
+        blocks = ends[i] - starts[i]
+        return pl.BlockSpec((ROWS, tile), lambda j: (0, jnp.clip(j - starts[i], 0, blocks - 1)))
+
+    out = pl.BlockSpec((HALF, tile), lambda j: (0, j))
+    columns = count * tile
+    return pl.pallas_call(
+        kernel,
+        grid=(count,),
+        in_specs=[pl.BlockSpec((ROWS, WIDTH), lambda j: (0, 0), pipeline_mode=pl.Buffered(1)) for _ in sources]
+        + [g_spec(i) for i in range(len(pairs))],
+        out_specs=[out, out],
+        out_shape=[jax.ShapeDtypeStruct((HALF, columns), BF16)] * 2,
+        scratch_shapes=[pltpu.VMEM((WIDTH, KEYS), BF16), pltpu.VMEM((WIDTH, 16), F32)],
+        compiler_params=pltpu.CompilerParams(vmem_limit_bytes=48 << 20),
+        cost_estimate=cost_of(
+            flops=2 * ROWS * WIDTH * columns, bytes_accessed=4 * ROWS * columns, transcendentals=0
+        ),
+        name="weight_grads",
+    )(*sources, *[g for _, g in pairs])
+
+
 def pair_tables(coords):
-    cosines, sines = rotary_tables(coords)
-    pad = ((0, ROWS - KEYS - 1), (0, 0))
-    cosines = jnp.pad(joined(cosines[1:], cosines[:1]), pad)
-    sines = jnp.pad(joined(sines[1:], sines[:1]), pad)
-    even = (jnp.arange(64) % 32 < 16)[None, :]
-    up, down = jnp.where(even, -sines, 0.0), jnp.where(even, 0.0, sines)
-    return tuple(jnp.tile(t, (1, 2)) for t in (cosines, up, down))
-
-
-def paired_device(
-    patch_in, cls_in, d_patch, d_cls, image_valid, patch_coords,
-    w_query, w_key, w_value, w_gate, w_up, w_out, w_down, layer_vectors, ffn_vectors,
-):
-    me, pos = lax.axis_index(BOTH), lax.axis_index("ctx")
-    hidden = w_gate.shape[1]
-
-    vectors_local = jnp.pad(layer_vectors.T, ((0, 0), (0, 120)))
-    first_local = joined(w_query, w_key, w_value, vectors_local, axis=1)
-    out_local, down_local = w_out.T, w_down.T
-    wide = (hidden + 127) // 128 * 128
-    extra = ((0, 0), (0, wide - hidden))
-    second_local = joined(
-        jnp.pad(w_gate, extra), out_local[:, :512], jnp.pad(w_up, extra), out_local[:, 512:], axis=1
-    )
-    half_two = wide + 512
-    third_split = (hidden // 2 + 127) // 128 * 128
-    first, deps = gather_columns(first_local, 1664, ((), ()))
-    second, deps = gather_columns(second_local, half_two, deps)
-    third, deps = gather_columns(down_local, third_split, deps)
-    vectors = first[:, 3072:3080].T.astype(F32)
-    gate_w, up_w = second[:, :hidden], second[:, half_two : half_two + hidden]
-    out_w = joined(second[:, wide:half_two], second[:, half_two + wide :], axis=1)
-    down_w = third
-    ffn = ffn_vectors.astype(F32)
-
-    natural = lax.broadcasted_iota(jnp.int32, (1024, 1024), 0)
-    place = lax.broadcasted_iota(jnp.int32, (1024, 1024), 1)
+    lane = jnp.arange(128)
+    freqs = 10000.0 ** (-(lane % 16).astype(F32) / 16.0)
+    along_rows = (lane % 64 < 32)[None, :]
+    places = jnp.where(along_rows, coords[:, 0:1], coords[:, 1:2]).astype(F32)
+    angles = jnp.pad(places * freqs[None, :], ((0, ROWS - KEYS), (0, 0)))
+    cosines, sines = jnp.cos(angles), jnp.sin(angles)
+    even = (lane % 32 < 16)[None, :]
+    return cosines, jnp.where(even, -sines, 0.0), jnp.where(even, 0.0, sines)
+
+
+def feature_order(me):
+    natural = lax.broadcasted_iota(jnp.int32, (WIDTH, WIDTH), 0)
+    place = lax.broadcasted_iota(jnp.int32, (WIDTH, WIDTH), 1)
     block = place // 32
     owner = (
         (block // 16) * BIT_CORE
@@ -709,17 +1000,26 @@
         + (block // 2 % 2) * BIT_Z1
         + (block % 2) * BIT_Z0
     ) ^ me
-    order = (natural == owner * 32 + place % 32).astype(BF16)
-
-    def own_image(patches, classes):
+    return (natural == owner * 32 + place % 32).astype(BF16)
+
+
+def paired_device(
+    patch_in, cls_in, d_patch, d_cls, image_valid, patch_coords,
+    w_query, w_key, w_value, w_gate, w_up, w_out, w_down, layer_vectors, ffn_vectors,
+):
+    me, pos = lax.axis_index(BOTH), lax.axis_index("ctx")
+    hidden = w_gate.shape[1]
+    wide = (hidden + 255) // 256 * 256
+    extra = ((0, 0), (0, wide - hidden))
+
+    def own_image(patches, classes, *deps):
         near = lax.dynamic_index_in_dim(patches, pos, 0, keepdims=False)
-        far = swap_over(lax.dynamic_index_in_dim(patches, 1 - pos, 0, keepdims=False), BIT_X)
+        sent = after(lax.dynamic_index_in_dim(patches, 1 - pos, 0, keepdims=False), *deps)
+        far = swap_over(sent, BIT_X)
         class_row = lax.dynamic_index_in_dim(classes, pos, 0)
-        rows = joined(near, far, jnp.pad(class_row, ((0, ROWS - KEYS - 1), (0, 0))))
-        return dot_nn(rows, order)
+        return joined(near, far, jnp.pad(class_row, ((0, ROWS - KEYS - 1), (0, 0)))), far
 
     def to_pair(rows):
-        rows = dot_nt(rows, order).astype(BF16)
         near, far = rows[:512], swap_over(rows[512:], BIT_X)
         is_first = pos == 0
         near_class, far_class = rows[KEYS], far[512]
@@ -727,105 +1027,199 @@
         classes = jnp.where(is_first, jnp.stack([near_class, far_class]), jnp.stack([far_class, near_class]))
         return patches, classes
 
+    vectors_local = jnp.pad(layer_vectors.T, ((0, 0), (0, 120)))
+    low_heads = [w[:, :HALF] for w in (w_query, w_key, w_value)]
+    high_heads = [w[:, HALF:] for w in (w_query, w_key, w_value)]
+    g_low = Gather(joined(*low_heads, vectors_local, axis=1))
+    g_high = Gather(joined(*high_heads, w_out.T, axis=1))
+    g_gate = Gather(jnp.pad(w_gate, extra))
+    g_up = Gather(jnp.pad(w_up, extra))
+    g_down = Gather(jnp.pad(w_down.T, extra))
+
+    image_rows, image_far = own_image(patch_in, cls_in)
     coords = joined(patch_coords, swap_over(patch_coords, BIT_X))
+    order = feature_order(me)
     tables = pair_tables(coords)
     keep = lax.dynamic_index_in_dim(image_valid, pos, 0, keepdims=False).astype(F32)
-    tokens = own_image(patch_in, cls_in)
-    grad_rows = own_image(d_patch, d_cls) * keep
-
-    unit_one, std_one = unit_norm(tokens)
-    normed = (unit_one * vectors[0] + vectors[1]).astype(BF16)
-    head_biases = dot_nt(first[:, 3072:3080].T, order)
-    q_rot, k_rot, values, attended, log_sums = attention_forward(normed, first, head_biases, tables)
-    middle = tokens + (dot_nt(attended, out_w) + vectors[4])
-    unit_two, std_two = unit_norm(middle)
-    normed_two = (unit_two * vectors[5] + vectors[6]).astype(BF16)
-    gate = dot_nn(normed_two, gate_w) + ffn[0]
-    up = dot_nn(normed_two, up_w) + ffn[1]
-    silu = jax.nn.silu(gate)
-    unit_three, std_three = unit_norm(silu * up)
-    inner = (unit_three * ffn[2] + ffn[3]).astype(BF16)
-    result = middle + (dot_nt(inner, down_w) + vectors[7])
-    patch_out, cls_out = to_pair((result * keep).astype(BF16))
-
-    def weight_grad_halves(rows_in, grads):
-        near = dot_tn(rows_in[:, :512], grads).astype(BF16)
-        far = dot_tn(rows_in[:, 512:], grads).astype(BF16)
-        return near, far
-
-    def column_sum(rounded):
-        return jnp.sum(rounded.astype(F32), axis=0)
-
-    branch = grad_rows.astype(BF16)
-    down_grad = scatter_columns(*weight_grad_halves(branch, inner), third_split)
-    grad_inner = dot_nn(branch, down_w)
-    grad_mix = unit_norm_back(grad_inner * ffn[2], unit_three, std_three)
-    sigmoid = jax.nn.sigmoid(gate)
-    gate_low = (grad_mix * up * sigmoid * (1.0 + gate * (1.0 - sigmoid))).astype(BF16)
-    up_low = (grad_mix * silu).astype(BF16)
-    ffn_grads = sum_small(
-        jnp.stack(
-            [column_sum(gate_low), column_sum(up_low), jnp.sum(grad_inner * unit_three, axis=0), jnp.sum(grad_inner, axis=0)]
+    keep = jnp.full((8, 128), keep, F32)
+    ffn = jnp.pad(ffn_vectors.astype(F32), ((0, 4), (0, wide - hidden)))
+
+    z_one = g_low.along_z0()
+    z_low = g_low.along_z1()
+    g_high.along_z0(z_one)
+    xy_low = g_low.along_xy()
+    z_high = g_high.along_z1(z_low)
+    corner_low = g_low.corners(image_far)
+    z_one = g_gate.along_z0(z_high)
+    xy_high = g_high.along_xy(xy_low)
+    near_low = g_low.whole()
+    z_gate = g_gate.along_z1()
+
+    gate = near_low, g_low.far, image_rows, z_high, z_one
+    z_up = g_up.along_z0(gate)
+    vectors, head_biases = gathered_vectors(near_low, g_low.far, order)
+    tokens, normed = over_rows(
+        start_kernel, "start", [after(image_rows, gate)], [order, vectors], [(WIDTH, BF16), (WIDTH, BF16)],
+        flops=2_200_000_000,
+    )
+
+    def attend(block, gate):
+        group = g_low if block < 2 else g_high
+        return attention_forward(
+            after(normed, gate), group.near, group.far, head_biases, block, block % 2, tables
         )
-    )
-    gate_near, gate_far = weight_grad_halves(normed_two, gate_low)
-    up_near, up_far = weight_grad_halves(normed_two, up_low)
-    grad_two = dot_nt(gate_low, gate_w) + dot_nt(up_low, up_w)
-    grad_middle = grad_rows + unit_norm_back(grad_two * vectors[5], unit_two, std_two)
-    att_low = grad_middle.astype(BF16)
-    out_near, out_far = weight_grad_halves(att_low, attended)
-    pads = ((0, 0), (0, wide - hidden))
-    second_grad = scatter_columns(
-        joined(jnp.pad(gate_near, pads), out_near[:, :512], jnp.pad(up_near, pads), out_near[:, 512:], axis=1),
-        joined(jnp.pad(gate_far, pads), out_far[:, :512], jnp.pad(up_far, pads), out_far[:, 512:], axis=1),
-        half_two,
-    )
-    grad_attended = dot_nn(att_low, out_w).astype(BF16)
-    query_low, key_low, value_low = attention_backward(
-        q_rot, k_rot, values, grad_attended, attended, log_sums, tables
-    )
-    halves = [weight_grad_halves(normed, low) for low in (query_low, key_low, value_low)]
-    first_grad = scatter_columns(
-        joined(*[h[0] for h in halves], axis=1), joined(*[h[1] for h in halves], axis=1), 1536
-    )
-    grad_one = (
-        dot_nt(query_low, first[:, :1024])
-        + dot_nt(key_low, first[:, 1024:2048])
-        + dot_nt(value_low, first[:, 2048:3072])
-    )
-    grad_tokens = grad_middle + unit_norm_back(grad_one * vectors[0], unit_one, std_one)
+
+    gate = normed, xy_high, z_gate, z_up
+    corner_high = g_high.corners(gate)
+    xy_gate = g_gate.along_xy(gate)
+    z_up = g_up.along_z1(gate)
+    heads = [attend(0, gate)]
+
+    gate = heads[0][3], corner_high, xy_gate, z_up
+    near_high = g_high.whole(gate)
+    corner_gate = g_gate.corners(gate)
+    xy_up = g_up.along_xy(gate)
+    z_down = g_down.along_z0(gate)
+    heads.append(attend(1, gate))
+
+    gate = heads[1][3], g_high.far, corner_gate, z_down
+    near_gate = g_gate.whole(gate)
+    z_down = g_down.along_z1(gate)
+    heads.append(attend(2, gate))
+
+    gate = heads[2][3], xy_up, g_gate.far, z_down
+    corner_up = g_up.corners(gate)
+    xy_down = g_down.along_xy(gate)
+    heads.append(attend(3, gate))
+
+    gate = heads[3][3], corner_up
+    near_up = g_up.whole(gate)
+    out_w = [((w, (HALF, HALF), 3 + i)) for w in (near_high, g_high.far) for i in range(2)]
+    attended = [h[3] for h in heads]
+    middle, normed_two = over_rows(
+        middle_kernel, "middle", attended + [after(tokens, gate)], out_w + [vectors],
+        [(WIDTH, BF16), (WIDTH, BF16)], flops=2_200_000_000, step=520,
+    )
+
+    gate = normed_two, g_up.far, xy_down
+    corner_down = g_down.corners(gate)
+    grad_image_rows, grad_far = own_image(d_patch, d_cls, gate)
+    gate_up = [near_gate, g_gate.far, near_up, g_up.far]
+    gate_act, up_act, inner, stats = over_rows(
+        functools.partial(hidden_kernel, hidden=hidden), "hidden", [after(normed_two, gate)],
+        gate_up + [ffn], [(wide, BF16), (wide, BF16), (wide, BF16), (128, F32)], flops=12_000_000_000,
+    )
+
+    gate = inner, corner_down, grad_far
+    near_down = g_down.whole(gate)
+    down_w = [near_down, g_down.far]
+
+    branch, d_gate, d_up, wide_sums, branch_sums = over_rows(
+        functools.partial(hidden_back_kernel, hidden=hidden), "hidden_back",
+        [after(grad_image_rows, gate), gate_act, up_act, stats], [order, keep] + down_w + [ffn],
+        [(WIDTH, BF16), (wide, BF16), (wide, BF16)], [wide, WIDTH], flops=8_000_000_000,
+    )
+
+    ffn_sums = sum_over(wide_sums[:4, :hidden], BIT_CORE)
+    down_grads = weight_grads([(branch, inner)])
+    down = Scatter(*down_grads)
+
+    gate = down_grads, ffn_sums
+    down_stage = down.over_core(gate)
+    ffn_sums = sum_over(ffn_sums, BIT_X, gate)
+    (out_rows,) = over_rows(
+        result_kernel, "result", [inner, after(middle, gate)], down_w + [vectors, order, keep],
+        [(WIDTH, BF16)], flops=8_000_000_000, step=520,
+    )
+
+    gate = out_rows, down_stage, ffn_sums
+    down_stage = down.corners(gate)
+    ffn_sums = sum_over(ffn_sums, BIT_Y, gate)
+    outs = to_pair(after(out_rows, gate))
+    late = after(normed_two, gate)
+    second_grads = weight_grads([(late, d_gate), (late, d_up)])
+    second = Scatter(*second_grads)
+
+    gate = second_grads, down_stage, ffn_sums, outs
+    down_stage, second_stage = down.over_xy(gate), second.over_core(gate)
+    ffn_sums = sum_over(ffn_sums, BIT_Z0, gate)
+    att_low, *att_grads, middle_sums = over_rows(
+        middle_back_kernel, "middle_back", [d_gate, d_up, branch, after(middle, gate)],
+        gate_up + out_w + [vectors], [(WIDTH, BF16)] + [(HEAD_COLS, BF16)] * 4, [WIDTH],
+        flops=14_000_000_000, step=520,
+    )
+
+    def attend_back(block, gate):
+        return attention_backward(*heads[block], after(att_grads[block], gate), tables)
+
+    gate = att_low, down_stage, second_stage, ffn_sums
+    down_stage, second_stage = down.along_z1(gate), second.corners(gate)
+    ffn_grads = sum_over(ffn_sums, BIT_Z1, gate)
+    parts = [attend_back(0, gate)]
+
+    gate = parts[0][0], down_stage, second_stage, ffn_grads
+    down_grad, second_stage = down.along_z0(gate), second.over_xy(gate)
+    parts.append(attend_back(1, gate))
+
+    gate = parts[1][0], down_grad
+    parts.append(attend_back(2, gate))
+
+    gate = parts[2][0], second_stage
+    second_stage = second.along_z1(gate)
+    late, late_two = after(att_low, gate), after(normed, gate)
+    low_grads = weight_grads(
+        [(late, a) for a in attended] + [(late_two, g) for part in parts for g in part[:3]]
+    )
+    low = Scatter(*low_grads)
+
+    gate = low_grads
+    low_stage = low.over_core(gate)
+    parts.append(attend_back(3, gate))
+
+    gate = parts[3][0], low_stage, second_stage
+    low_stage = low.corners(gate)
+    gate_up_grad = second.along_z0(gate)
+    late = after(normed, gate)
+    high_grads = weight_grads([(late, g) for g in parts[3][:3]])
+    high = Scatter(*high_grads)
+
+    gate = high_grads, low_stage
+    low_stage, high_stage = low.over_xy(gate), high.over_core(gate)
+    grad_rows, first_sums = over_rows(
+        last_kernel, "last",
+        [g for part in parts for g in part[:3]] + [after(att_low, gate), tokens],
+        [(near_low, (HALF, 3 * HALF), 0), (g_low.far, (HALF, 3 * HALF), 0)]
+        + [(near_high, (HALF, 3 * HALF), 0), (g_high.far, (HALF, 3 * HALF), 0), vectors, order],
+        [(WIDTH, BF16)], [WIDTH], flops=9_000_000_000, step=520,
+    )
+    high.corners(grad_rows)
+    low.along_z1(grad_rows)
+    patch_grad, cls_grad = to_pair(grad_rows)
+    high.over_xy()
+    high.along_z1()
+    low_grad = low.along_z0()
+    high_grad = high.along_z0()
     head_sums = jnp.dot(
-        jnp.stack([column_sum(query_low), column_sum(value_low)]),
-        order.astype(F32),
-        precision=lax.Precision.HIGHEST,
+        joined(*[part[3][:2] for part in parts], axis=1), order.astype(F32), precision=lax.Precision.HIGHEST
     )
     vector_grads = scatter_small(
-        jnp.stack(
-            [
-                jnp.sum(grad_one * unit_one, axis=0),
-                jnp.sum(grad_one, axis=0),
-                head_sums[0],
-                head_sums[1],
-                column_sum(att_low),
-                jnp.sum(grad_two * unit_two, axis=0),
-                jnp.sum(grad_two, axis=0),
-                column_sum(branch),
-            ]
-        ).T
-    )
-    patch_grad, cls_grad = to_pair(grad_tokens.astype(BF16))
+        joined(first_sums[:2], head_sums, middle_sums[:3], branch_sums[:1]).T
+    )
+    blocks = [low_grad[:, WIDTH + i * HEAD_COLS :][:, :HEAD_COLS] for i in range(9)]
+    blocks += [high_grad[:, i * HEAD_COLS :][:, :HEAD_COLS] for i in range(3)]
+    query_grad, key_grad, value_grad = (joined(*blocks[i::3], axis=1) for i in range(3))
     return (
-        patch_out,
-        cls_out,
+        outs[0],
+        outs[1],
         patch_grad,
         cls_grad,
-        first_grad[:, :1024],
-        first_grad[:, 1024:2048],
-        first_grad[:, 2048:],
-        second_grad[:, :hidden],
-        second_grad[:, half_two : half_two + hidden],
-        joined(second_grad[:, wide:half_two], second_grad[:, half_two + wide :], axis=1).T,
-        down_grad.T,
+        query_grad,
+        key_grad,
+        value_grad,
+        gate_up_grad[:, :hidden],
+        gate_up_grad[:, wide : wide + hidden],
+        low_grad[:, :WIDTH].T,
+        down_grad[:, :hidden].T,
         vector_grads.T,
         ffn_grads,
     )

time: 922 us -> 651 us (0.71)
  matrix products: 196 us -> 1.88 us
  Pallas kernels: 109 us -> 301 us
  other arithmetic: 207 us -> 40 us
  waiting for transfers between devices: 254 us -> 192 us
  local copies, waits for them, and re-layouts: 87.6 us -> 31.3 us
  starting transfers between devices: 55.6 us -> 70.5 us
    dot_general x30 -> x1, matrix products: 196 us -> 1.88 us  [paired_device(): jnp.dot(joined(*[part[3][:2] for part in parts], axis=1), order.astype(F3...]
    pallas_call x1 -> x21, Pallas kernels: 50.1 us -> 244 us  [the longest x7 125 us: over_rows(): pl.pallas_call(kernel, grid=(ROWS // step,), in_specs=in_specs, out_specs...]
    concatenate x23 -> x22, other arithmetic: 130 us -> 10.6 us  [joined(): return jnp.concatenate(parts, axis=axis)]
    ppermute x57 -> x78, waiting for transfers between devices: 254 us -> 192 us  [swap_over(): return lax.ppermute(value, BOTH, [(i, i ^ bit) for i in range(count)])]
    reduce_sum x7 -> x0, other arithmetic: 38.7 us -> none  [the longest x4 31.7 us: column_sum(): return jnp.sum(rounded.astype(F32), axis=0)]
    ppermute x57 -> x78, starting transfers between devices: 55.6 us -> 70.5 us  [swap_over(): return lax.ppermute(value, BOTH, [(i, i ^ bit) for i in range(count)])]
    ppermute x5 -> x0, local copies, waits for them, and re-layouts: 14.1 us -> none  [swap_over(): return lax.ppermute(value, BOTH, [(i, i ^ bit) for i in range(count)])]
    slice x33 -> x36, local copies, waits for them, and re-layouts: 24.3 us -> 10.4 us  [the longest x2 1.6 us: paired_device(): high_heads = [w[:, HALF:] for w in (w_query, w_key, w_value)]]
  transfers between devices with their start and end apart: 57 -> 78, of which waited for: 24 -> 36; matrix products, arithmetic and copies ran while one was open for 23% -> 6% of each run, Pallas kernels for 5% -> 39%
where the time goes in v2:
time: 651 us; the launch traced here: 641 us
  Pallas kernels  301 us (46%)
  waiting for transfers between devices  192 us (29%)
  starting transfers between devices  70.5 us (11%)
  other arithmetic  40 us (6%)
  local copies, waits for them, and re-layouts  31.3 us (5%)
    ppermute x78, waiting for transfers between devices, swap_over(): return lax.ppermute(value, BOTH, [(i, i ^ bit) for i in range(count)])  192 us
    pallas_call x7, Pallas kernels, over_rows(): pl.pallas_call(kernel, grid=(ROWS // step,), in_specs=in_specs, out_specs...  125 us
    ppermute x78, starting transfers between devices, swap_over(): return lax.ppermute(value, BOTH, [(i, i ^ bit) for i in range(count)])  70.5 us
    pallas_call x4, Pallas kernels, attention_backward(): pl.pallas_call(functools.partial(attention_back_kernel, step=step), grid=...  56.9 us
    pallas_call x4, Pallas kernels, weight_grads(): pl.pallas_call(kernel, grid=(count,), in_specs=[pl.BlockSpec((ROWS, WIDTH...  56.2 us
    pallas_call x4, Pallas kernels, attention_forward(): pl.pallas_call(functools.partial(attention_kernel, step=step), grid=(1,),...  54.3 us
    convert_element_type x16, other arithmetic, rounded_sum(): return total.astype(BF16)  15.5 us
  transfers between devices with their start and end apart: 78, of which 36 were waited for; matrix products, arithmetic and copies ran while one was open for 6% of the time, Pallas kernels for 39%

profile of v2, /device:TPU:0, one launch (start us, length us, event | category | flops | bytes accessed | tf_op | source)
XLA Modules:
  0.0 640.7 jit_solution(5613381232989495920)
XLA Ops:
  0.7 3.0 collective-permute-start.15
  7.7 2.7 dynamic-slice_bitcast_fusion.3
  11.7 2.2 fusion.59.order_ref.refs_19_
  14.8 2.7 collective-permute-start.2
  18.9 7.5 %collective-permute-done.2 = bf16[64,1664]{1,0:T(8,128)(2,1)S(1)} collective-permute-done((bf16[64,1664]{1,0:T(8,128)(2,1)S(1)}, bf16[64,1664]{1,0:T(8,128)(2,1)S(1)}, u32[]{:S(2)}, u32[]{:S(2)}) %collective-permute-start.2) | collective-permute-done | bytes 213024 | tf_op jit(solution)/shard_map/ppermute | solution.py:432
  29.6 2.8 fusion.34
  32.4 5.8 collective-permute-done.4.refs_1_
  38.2 5.7 collective-permute-done.3.refs_2_
  46.1 2.7 collective-permute-start.9
  52.5 8.9 %collective-permute-done.9 = bf16[64,2560]{1,0:T(8,128)(2,1)S(1)} collective-permute-done((bf16[64,2560]{1,0:T(8,128)(2,1)S(1)}, bf16[64,2560]{1,0:T(8,128)(2,1)S(1)}, u32[]{:S(2)}, u32[]{:S(2)}) %collective-permute-start.9) | collective-permute-done | bytes 327712 | tf_op jit(solution)/shard_map/ppermute | solution.py:432
  64.1 3.7 collective-permute-done.10
  68.3 2.9 fusion.32.rows_ref
  71.2 14.9 %collective-permute-done.13 = bf16[64,2816]{1,0:T(8,128)(2,1)S(1)} collective-permute-done((bf16[64,2816]{1,0:T(8,128)(2,1)S(1)}, bf16[64,2816]{1,0:T(8,128)(2,1)S(1)}, u32[]{:S(2)}, u32[]{:S(2)}) %collective-permute-start.13) | collective-permute-done | bytes 360480 | tf_op jit(solution)/shard_map/ppermute | solution.py:432
  87.3 3.0 vectors.1
  90.4 7.7 %start.1 = (bf16[1040,1024]{1,0:T(8,128)(2,1)}, bf16[1040,1024]{1,0:T(8,128)(2,1)}) custom-call(bf16[1040,1024]{1,0:T(8,128)(2,1)} %fusion.32.rows_ref, bf16[1024,1024]{1,0:T(8,128)(2,1)} %fusion.59.order_ref.refs_19_, f32[8,1024]{1,0:T(8,128)} %get-tuple-element.183.vec_ref.refs_18_), custom_call_target="tpu_custom_call" | custom-call | flops 8800000000 | bytes 34078720 | tf_op jit(solution)/shard_map/start/pallas_call | solution.py:750
  105.1 13.5 %attention_forward.4 = (bf16[1040,256]{1,0:T(8,128)(2,1)S(1)}, bf16[1040,256]{1,0:T(8,128)(2,1)S(1)}, bf16[1040,256]{1,0:T(8,128)(2,1)S(1)}, bf16[1040,256]{1,0:T(8,128)(2,1)S(1)}, f32[8,1040]{1,0:T(8,128)S(1)}) custom-call(bf16[1040,1024]{1,0:T(8,128)(2,1)} %get-tuple-element.310.x_ref.refs_1_.refs_0_, bf16[512,1664]{1,0:T(8,128)(2,1)S(1)} %copy-done.3, ...), custom_call_target="tpu_custom_call" | custom-call | flops 30000001024 | bytes 28000000 | tf_op jit(solution)/shard_map/attention_forward/pallas_call | solution.py:629
  118.7 3.4 collective-permute-done.20
  123.3 1.8 collective-permute-start.24
  128.8 2.4 pack_rows.6.qn_ref.kn_ref.vn_ref.na_ref.nb_ref.refs_16_
  131.4 14.6 %attention_forward.5 = (bf16[1040,256]{1,0:T(8,128)(2,1)S(1)}, bf16[1040,256]{1,0:T(8,128)(2,1)S(1)}, bf16[1040,256]{1,0:T(8,128)(2,1)S(1)}, bf16[1040,256]{1,0:T(8,128)(2,1)S(1)}, f32[8,1040]{1,0:T(8,128)S(1)}) custom-call(bf16[1040,1024]{1,0:T(8,128)(2,1)} %get-tuple-element.310.x_ref.refs_1_.refs_0_, bf16[512,1664]{1,0:T(8,128)(2,1)S(1)} %copy-done.3, ...), custom_call_target="tpu_custom_call" | custom-call | flops 30000001024 | bytes 28000000 | tf_op jit(solution)/shard_map/attention_forward/pallas_call | solution.py:629
  149.2 2.4 copy-done.21
  151.5 13.1 %attention_forward.6 = (bf16[1040,256]{1,0:T(8,128)(2,1)S(1)}, bf16[1040,256]{1,0:T(8,128)(2,1)S(1)}, bf16[1040,256]{1,0:T(8,128)(2,1)S(1)}, bf16[1040,256]{1,0:T(8,128)(2,1)S(1)}, f32[8,1040]{1,0:T(8,128)S(1)}) custom-call(bf16[1040,1024]{1,0:T(8,128)(2,1)S(1)} %copy-done.21, bf16[512,2560]{1,0:T(8,128)(2,1)} %copy-done.7, ...), custom_call_target="tpu_custom_call" | custom-call | flops 30000001024 | bytes 28000000 | tf_op jit(solution)/shard_map/attention_forward/pallas_call | solution.py:629
  165.3 2.9 collective-permute-done.28
  168.3 1.7 collective-permute-start.30
  171.5 13.1 %attention_forward.7 = (bf16[1040,256]{1,0:T(8,128)(2,1)S(1)}, bf16[1040,256]{1,0:T(8,128)(2,1)S(1)}, bf16[1040,256]{1,0:T(8,128)(2,1)S(1)}, bf16[1040,256]{1,0:T(8,128)(2,1)S(1)}, f32[8,1040]{1,0:T(8,128)S(1)}) custom-call(bf16[1040,1024]{1,0:T(8,128)(2,1)S(1)} %copy-done.21, bf16[512,2560]{1,0:T(8,128)(2,1)} %copy-done.7, ...), custom_call_target="tpu_custom_call" | custom-call | flops 30000001024 | bytes 28000000 | tf_op jit(solution)/shard_map/attention_forward/pallas_call | solution.py:629
  185.5 2.3 copy-done.81
  190.7 7.7 %middle.1 = (bf16[1040,1024]{1,0:T(8,128)(2,1)}, bf16[1040,1024]{1,0:T(8,128)(2,1)}) custom-call(bf16[1040,256]{1,0:T(8,128)(2,1)} %copy-done.23, bf16[1040,256]{1,0:T(8,128)(2,1)} %copy-done.25, bf16[1040,256]{1,0:T(8,128)(2,1)} %copy-done.27, bf16[1040,256]{1,0:T(8,128)(2,1)} %copy-done.29, bf16[1040,1024]{1,0:T(8,128)(2,1)} %get-tuple-element.218.tokens_ref.refs_13_, ...), custom_call_target="tpu_custom_call" | custom-call | flops 8800000000 | bytes 76152832 | tf_op jit(solution)/shard_map/middle/pallas_call | solution.py:750
  198.4 8.9 %collective-permute-done.33.refs_1_ = bf16[128,2816]{1,0:T(8,128)(2,1)S(1)} collective-permute-done((bf16[128,2816]{1,0:T(8,128)(2,1)S(1)}, bf16[128,2816]{1,0:T(8,128)(2,1)S(1)}, u32[]{:S(2)}, u32[]{:S(2)}) %collective-permute-start.33) | collective-permute-done | bytes 720928 | tf_op jit(solution)/shard_map/ppermute | solution.py:432
  211.2 22.4 %hidden.1 = (bf16[1040,2816]{1,0:T(8,128)(2,1)}, bf16[1040,2816]{1,0:T(8,128)(2,1)}, bf16[1040,2816]{1,0:T(8,128)(2,1)}, f32[1040,128]{1,0:T(8,128)}) custom-call(bf16[1040,1024]{1,0:T(8,128)(2,1)} %get-tuple-element.254.x_ref.refs_0_, bf16[512,2816]{1,0:T(8,128)(2,1)} %copy-done.4, bf16[512,2816]{1,0:T(8,128)(2,1)} %collective-permute-done.27.gf_ref, ...), custom_call_target="tpu_custom_call" | custom-call | flops 48000000000 | bytes 127434752 | tf_op jit(solution)/shard_map/hidden/pallas_call | solution.py:750
  233.7 6.3 collective-permute-done.34
  243.3 3.0 fusion.33.d_ref
  247.8 29.5 %hidden_back.1 = (bf16[1040,1024]{1,0:T(8,128)(2,1)}, bf16[1040,2816]{1,0:T(8,128)(2,1)}, bf16[1040,2816]{1,0:T(8,128)(2,1)}, f32[8,2816]{1,0:T(8,128)}, f32[8,1024]{1,0:T(8,128)}) custom-call(bf16[1040,1024]{1,0:T(8,128)(2,1)} %fusion.33.d_ref, bf16[1040,2816]{1,0:T(8,128)(2,1)} %get-tuple-element.233.gate_ref, ...), custom_call_target="tpu_custom_call" | custom-call | flops 32000000000 | bytes 145211392 | tf_op jit(solution)/shard_map/hidden_back/pallas_call | solution.py:750
  279.9 12.7 %weight_grads.4 = (bf16[512,2816]{1,0:T(8,128)(2,1)S(1)}, bf16[512,2816]{1,0:T(8,128)(2,1)}) custom-call(bf16[1040,1024]{1,0:T(8,128)(2,1)S(1)} %copy-done.34, bf16[1040,2816]{1,0:T(8,128)(2,1)} %get-tuple-element.227.refs_1_.inner_ref), custom_call_target="tpu_custom_call" | custom-call | flops 23991418880 | bytes 46858240 | tf_op jit(solution)/shard_map/weight_grads/pallas_call | solution.py:965
  294.7 14.5 %result.1 = bf16[1040,1024]{1,0:T(8,128)(2,1)} custom-call(bf16[1040,2816]{1,0:T(8,128)(2,1)} %get-tuple-element.227.refs_1_.inner_ref, bf16[1040,1024]{1,0:T(8,128)(2,1)} %get-tuple-element.259.middle_ref, bf16[512,2816]{1,0:T(8,128)(2,1)} %copy-done.6, bf16[512,2816]{1,0:T(8,128)(2,1)} %collective-permute-done.37.far_ref, ...), custom_call_target="tpu_custom_call" | custom-call | flops 32000000000 | bytes 72073216 | tf_op jit(solution)/shard_map/result/pallas_call | solution.py:750
  309.3 2.6 add_convert_fusion.2
  315.7 24.3 %weight_grads.5 = (bf16[512,5632]{1,0:T(8,128)(2,1)}, bf16[512,5632]{1,0:T(8,128)(2,1)}) custom-call(bf16[1040,1024]{1,0:T(8,128)(2,1)S(1)} %copy-done.20, bf16[1040,2816]{1,0:T(8,128)(2,1)} %get-tuple-element.252.refs_1_.dgate_ref, bf16[1040,2816]{1,0:T(8,128)(2,1)} %get-tuple-element.253.refs_2_.dup_ref), custom_call_target="tpu_custom_call" | custom-call | flops 47982837760 | bytes 93716480 | tf_op jit(solution)/shard_map/weight_grads/pallas_call | solution.py:965
  341.1 24.5 %collective-permute-done.41 = bf16[528,1024]{1,0:T(8,128)(2,1)S(1)} collective-permute-done((bf16[528,1024]{1,0:T(8,128)(2,1)S(1)}, bf16[528,1024]{1,0:T(8,128)(2,1)S(1)}, u32[]{:S(2)}, u32[]{:S(2)}) %collective-permute-start.41) | collective-permute-done | bytes 1081376 | tf_op jit(solution)/shard_map/ppermute | solution.py:432
  369.0 26.4 %middle_back.1 = (bf16[1040,1024]{1,0:T(8,128)(2,1)}, bf16[1040,256]{1,0:T(8,128)(2,1)}, bf16[1040,256]{1,0:T(8,128)(2,1)}, bf16[1040,256]{1,0:T(8,128)(2,1)}, b...) custom-call(bf16[1040,2816]{1,0:T(8,128)(2,1)} %get-tuple-element.252.refs_1_.dgate_ref, ...), custom_call_target="tpu_custom_call" | custom-call | flops 56000000000 | bytes 169279488 | tf_op jit(solution)/shard_map/middle_back/pallas_call | solution.py:750
  397.2 5.7 add_convert_fusion
  403.6 2.5 collective-permute-start.49
  410.1 14.1 %attention_backward.4 = (bf16[1040,256]{1,0:T(8,128)(2,1)S(1)}, bf16[1040,256]{1,0:T(8,128)(2,1)S(1)}, bf16[1040,256]{1,0:T(8,128)(2,1)S(1)}, f32[8,256]{1,0:T(8,128)S(1)}) custom-call(bf16[1040,256]{1,0:T(8,128)(2,1)S(1)} %copy-done.55, bf16[1040,256]{1,0:T(8,128)(2,1)S(1)} %copy-done.57, bf16[1040,256]{1,0:T(8,128)(2,1)S(1)} %copy-done.59, ...), custom_call_target="tpu_custom_call" | custom-call | flops 51999997952 | bytes 20000000 | tf_op jit(solution)/shard_map/attention_backward/pallas_call | solution.py:720
  426.4 1.9 add_convert_fusion.7
  429.7 2.1 collective-permute-start.53
  431.9 14.2 %attention_backward.5 = (bf16[1040,256]{1,0:T(8,128)(2,1)S(1)}, bf16[1040,256]{1,0:T(8,128)(2,1)S(1)}, bf16[1040,256]{1,0:T(8,128)(2,1)S(1)}, f32[8,256]{1,0:T(8,128)S(1)}) custom-call(bf16[1040,256]{1,0:T(8,128)(2,1)S(1)} %copy-done.61, bf16[1040,256]{1,0:T(8,128)(2,1)S(1)} %copy-done.63, bf16[1040,256]{1,0:T(8,128)(2,1)S(1)} %copy-done.65, ...), custom_call_target="tpu_custom_call" | custom-call | flops 51999997952 | bytes 20000000 | tf_op jit(solution)/shard_map/attention_backward/pallas_call | solution.py:720
  449.0 14.4 %attention_backward.6 = (bf16[1040,256]{1,0:T(8,128)(2,1)S(1)}, bf16[1040,256]{1,0:T(8,128)(2,1)S(1)}, bf16[1040,256]{1,0:T(8,128)(2,1)S(1)}, f32[8,256]{1,0:T(8,128)S(1)}) custom-call(bf16[1040,256]{1,0:T(8,128)(2,1)S(1)} %copy-done.40, bf16[1040,256]{1,0:T(8,128)(2,1)S(1)} %copy-done.42, bf16[1040,256]{1,0:T(8,128)(2,1)S(1)} %copy-done.44, ...), custom_call_target="tpu_custom_call" | custom-call | flops 51999997952 | bytes 20000000 | tf_op jit(solution)/shard_map/attention_backward/pallas_call | solution.py:720
  463.4 15.0 %collective-permute-done.54 = bf16[128,5632]{1,0:T(8,128)(2,1)} collective-permute-done((bf16[128,5632]{1,0:T(8,128)(2,1)S(1)}, bf16[128,5632]{1,0:T(8,128)(2,1)}, u32[]{:S(2)}, u32[]{:S(2)}) %collective-permute-start.54) | collective-permute-done | bytes 1441824 | tf_op jit(solution)/shard_map/ppermute | solution.py:432
  479.5 2.7 add_convert_fusion.3
  483.0 16.0 %weight_grads.6 = (bf16[512,3328]{1,0:T(8,128)(2,1)}, bf16[512,3328]{1,0:T(8,128)(2,1)}) custom-call(bf16[1040,1024]{1,0:T(8,128)(2,1)} %get-tuple-element.314.refs_0_.refs_12_, bf16[1040,1024]{1,0:T(8,128)(2,1)} %get-tuple-element.310.x_ref.refs_1_.refs_0_, bf16[1040,256]{1,0:T(8,128)(2,1)S(1)} %copy-done.24, bf16[1040,256]{1,0:T(8,128)(2,1)S(1)} %copy-done.26, ...), custom_call_target="tpu_custom_call" | custom-call | flops 28353495040 | bytes 55377920 | tf_op jit(solution)/shard_map/weight_grads/pallas_call | solution.py:965
  499.2 14.2 %attention_backward.7 = (bf16[1040,256]{1,0:T(8,128)(2,1)S(1)}, bf16[1040,256]{1,0:T(8,128)(2,1)S(1)}, bf16[1040,256]{1,0:T(8,128)(2,1)S(1)}, f32[8,256]{1,0:T(8,128)S(1)}) custom-call(bf16[1040,256]{1,0:T(8,128)(2,1)S(1)} %get-tuple-element.293.q_ref, bf16[1040,256]{1,0:T(8,128)(2,1)S(1)} %copy-done.36, bf16[1040,256]{1,0:T(8,128)(2,1)S(1)} %copy-done.38, ...), custom_call_target="tpu_custom_call" | custom-call | flops 51999997952 | bytes 20000000 | tf_op jit(solution)/shard_map/attention_backward/pallas_call | solution.py:720
  513.7 1.9 fusion.37
  515.7 4.1 collective-permute-done.56
  522.4 3.1 weight_grads.7
  525.5 7.2 %collective-permute-done.59 = bf16[64,3328]{1,0:T(8,128)(2,1)S(1)} collective-permute-done((bf16[64,3328]{1,0:T(8,128)(2,1)S(1)}, bf16[64,3328]{1,0:T(8,128)(2,1)S(1)}, u32[]{:S(2)}, u32[]{:S(2)}) %collective-permute-start.59) | collective-permute-done | bytes 426016 | tf_op jit(solution)/shard_map/ppermute | solution.py:432
  533.8 17.3 %last.1 = (bf16[1040,1024]{1,0:T(8,128)(2,1)}, f32[8,1024]{1,0:T(8,128)}) custom-call(bf16[1040,256]{1,0:T(8,128)(2,1)} %copy-done.45, bf16[1040,256]{1,0:T(8,128)(2,1)} %copy-done.46, bf16[1040,256]{1,0:T(8,128)(2,1)} %copy-done.47, bf16[1040,256]{1,0:T(8,128)(2,1)} %copy-done.48, bf16[1040,256]{1,0:T(8,128)(2,1)} %copy-done.49, ...), custom_call_target="tpu_custom_call" | custom-call | flops 35999997952 | bytes 94371840 | tf_op jit(solution)/shard_map/last/pallas_call | solution.py:750
  555.1 1.9 collective-permute-done.74
  557.5 5.5 collective-permute-done.72
  563.2 2.1 collective-permute-start.76
  569.7 2.2 collective-permute-done.77
  574.9 13.1 %collective-permute-done.61 = bf16[128,3328]{1,0:T(8,128)(2,1)S(1)} collective-permute-done((bf16[128,3328]{1,0:T(8,128)(2,1)S(1)}, bf16[128,3328]{1,0:T(8,128)(2,1)S(1)}, u32[]{:S(2)}, u32[]{:S(2)}) %collective-permute-start.61) | collective-permute-done | bytes 852000 | tf_op jit(solution)/shard_map/ppermute | solution.py:432
  589.9 23.2 %collective-permute-done.67 = bf16[64,768]{1,0:T(8,128)(2,1)S(1)} collective-permute-done((bf16[64,768]{1,0:T(8,128)(2,1)S(1)}, bf16[64,768]{1,0:T(8,128)(2,1)S(1)}, u32[]{:S(2)}, u32[]{:S(2)}) %collective-permute-start.67) | collective-permute-done | bytes 98336 | tf_op jit(solution)/shard_map/ppermute | solution.py:432
  615.8 3.3 collective-permute-done.68
  622.8 3.9 collective-permute-done.70
  627.5 3.9 collective-permute-done.71
  631.7 5.8 collective-permute-done.64
  (477 shorter events, 105.1 us)
Async XLA Ops:
  0.7 13.3 %collective-permute-start.15 = (s32[512,2]{0,1:T(2,128)}, s32[512,2]{0,1:T(2,128)}, u32[]{:S(2)}, u32[]{:S(2)}) collective-permute-start(s32[512,2]{0,1:T(2,128)} %param.20), channel_id=1, source_target_pairs={{0,1},{1,0},{2,3},{3,2},{4,5},{5,4},{6,7},{7,6},{8,9},{9,8},{10,11... | collective-permute-start | bytes 12296 | tf_op jit(solution)/shard_map/ppermute | solution.py:432
  6.1 8.6 %collective-permute-start.1 = (bf16[32,1664]{1,0:T(8,128)(2,1)S(1)}, bf16[32,1664]{1,0:T(8,128)(2,1)S(1)}, u32[]{:S(2)}, u32[]{:S(2)}) collective-permute-start(bf16[32,1664]{1,0:T(8,128)(2,1)S(1)} %fusion.36), channel_id=1, source_target_pairs={{0,8},{1,9},{2,10},{3,11},{4,12},{5,13},{6,14},{7,15},{8,0},{9,1},... | collective-permute-start | bytes 319496 | tf_op jit(solution)/shard_map/ppermute | solution.py:432
  10.4 33.5 %collective-permute-start = (bf16[512,1024]{1,0:T(8,128)(2,1)S(1)}, bf16[512,1024]{1,0:T(8,128)(2,1)S(1)}, u32[]{:S(2)}, u32[]{:S(2)}) collective-permute-start(bf16[512,1024]{1,0:T(8,128)(2,1)S(1)} %get-tuple-element.352), channel_id=1, source_target_pairs={{0,1},{1,0},{2,3},{3,2},{4,5},{5,4},{6,7},{7,6},{8,9},{9,8},{10,11... | collective-permute-start | bytes 3145736 | tf_op jit(solution)/shard_map/ppermute | solution.py:432
  14.8 11.6 %collective-permute-start.2 = (bf16[64,1664]{1,0:T(8,128)(2,1)S(1)}, bf16[64,1664]{1,0:T(8,128)(2,1)S(1)}, u32[]{:S(2)}, u32[]{:S(2)}) collective-permute-start(bf16[64,1664]{1,0:T(8,128)(2,1)S(1)} %pad_maximum_fusion.12), channel_id=1, source_target_pairs={{0,16},{1,17},{2,18},{3,19},{4,20},{5,21},{6,22},{7,23},{8,24},{9,... | collective-permute-start | bytes 638984 | tf_op jit(solution)/shard_map/ppermute | solution.py:432
  18.4 27.7 %collective-permute-start.8 = (bf16[32,2560]{1,0:T(8,128)(2,1)S(1)}, bf16[32,2560]{1,0:T(8,128)(2,1)S(1)}, u32[]{:S(2)}, u32[]{:S(2)}) collective-permute-start(bf16[32,2560]{1,0:T(8,128)(2,1)S(1)} %pad_maximum_fusion.15), channel_id=1, source_target_pairs={{0,8},{1,9},{2,10},{3,11},{4,12},{5,13},{6,14},{7,15},{8,0},{9,1},... | collective-permute-start | bytes 491528 | tf_op jit(solution)/shard_map/ppermute | solution.py:432
  26.4 11.7 %collective-permute-start.4 = (bf16[128,1664]{1,0:T(8,128)(2,1)S(1)}, bf16[128,1664]{1,0:T(8,128)(2,1)S(1)}, u32[]{:S(2)}, u32[]{:S(2)}) collective-permute-start(bf16[128,1664]{1,0:T(8,128)(2,1)S(1)} %pad_maximum_fusion.7.refs_0_), channel_id=1, source_target_pairs={{0,4},{1,5},{2,6},{3,7},{4,0},{5,1},{6,2},{7,3},{8,12},{9,13},{10,... | collective-permute-start | bytes 1277960 | tf_op jit(solution)/shard_map/ppermute | solution.py:432
  28.1 15.8 %collective-permute-start.3 = (bf16[128,1664]{1,0:T(8,128)(2,1)S(1)}, bf16[128,1664]{1,0:T(8,128)(2,1)S(1)}, u32[]{:S(2)}, u32[]{:S(2)}) collective-permute-start(bf16[128,1664]{1,0:T(8,128)(2,1)S(1)} %pad_maximum_fusion.7.refs_0_), channel_id=1, source_target_pairs={{0,1},{1,0},{2,3},{3,2},{4,5},{5,4},{6,7},{7,6},{8,9},{9,8},{10,11... | collective-permute-start | bytes 1277960 | tf_op jit(solution)/shard_map/ppermute | solution.py:432
  46.1 15.3 %collective-permute-start.9 = (bf16[64,2560]{1,0:T(8,128)(2,1)S(1)}, bf16[64,2560]{1,0:T(8,128)(2,1)S(1)}, u32[]{:S(2)}, u32[]{:S(2)}) collective-permute-start(bf16[64,2560]{1,0:T(8,128)(2,1)S(1)} %pad_maximum_fusion.11), channel_id=1, source_target_pairs={{0,16},{1,17},{2,18},{3,19},{4,20},{5,21},{6,22},{7,23},{8,24},{9,... | collective-permute-start | bytes 983048 | tf_op jit(solution)/shard_map/ppermute | solution.py:432
  51.5 34.6 %collective-permute-start.7 = (bf16[512,1664]{1,0:T(8,128)(2,1)S(1)}, bf16[512,1664]{1,0:T(8,128)(2,1)S(1)}, u32[]{:S(2)}, u32[]{:S(2)}) collective-permute-start(bf16[512,1664]{1,0:T(8,128)(2,1)S(1)} %pack_rows.5.near_ref.qn_ref.kn_ref.vn_ref.refs_14_), channel_id=1, source_target_pairs={{0,2},{1,3},{2,0},{3,1},{4,6},{5,7},{6,4},{7,5},{8,10},{9,11},{10,... | collective-permute-start | bytes 5111816 | tf_op jit(solution)/shard_map/ppermute | solution.py:432
  61.4 6.5 %collective-permute-start.10 = (bf16[32,2816]{1,0:T(8,128)(2,1)S(1)}, bf16[32,2816]{1,0:T(8,128)(2,1)S(1)}, u32[]{:S(2)}, u32[]{:S(2)}) collective-permute-start(bf16[32,2816]{1,0:T(8,128)(2,1)S(1)} %pad.33), channel_id=1, source_target_pairs={{0,8},{1,9},{2,10},{3,11},{4,12},{5,13},{6,14},{7,15},{8,0},{9,1},... | collective-permute-start | bytes 540680 | tf_op jit(solution)/shard_map/ppermute | solution.py:432
  62.1 35.9 %collective-permute-start.12 = (bf16[128,2560]{1,0:T(8,128)(2,1)}, bf16[128,2560]{1,0:T(8,128)(2,1)S(1)}, u32[]{:S(2)}, u32[]{:S(2)}) collective-permute-start(bf16[128,2560]{1,0:T(8,128)(2,1)} %constant_dynamic-update-slice_fusion.refs_0_), channel_id=1, source_target_pairs={{0,4},{1,5},{2,6},{3,7},{4,0},{5,1},{6,2},{7,3},{8,12},{9,13},{10,... | collective-permute-start | bytes 1966088 | tf_op jit(solution)/shard_map/ppermute | solution.py:432
  62.7 35.3 %collective-permute-start.11 = (bf16[128,2560]{1,0:T(8,128)(2,1)}, bf16[128,2560]{1,0:T(8,128)(2,1)}, u32[]{:S(2)}, u32[]{:S(2)}) collective-permute-start(bf16[128,2560]{1,0:T(8,128)(2,1)} %constant_dynamic-update-slice_fusion.refs_0_), channel_id=1, source_target_pairs={{0,1},{1,0},{2,3},{3,2},{4,5},{5,4},{6,7},{7,6},{8,9},{9,8},{10,11... | collective-permute-start | bytes 1966088 | tf_op jit(solution)/shard_map/ppermute | solution.py:432
  67.9 18.2 %collective-permute-start.13 = (bf16[64,2816]{1,0:T(8,128)(2,1)S(1)}, bf16[64,2816]{1,0:T(8,128)(2,1)S(1)}, u32[]{:S(2)}, u32[]{:S(2)}) collective-permute-start(bf16[64,2816]{1,0:T(8,128)(2,1)S(1)} %pad_maximum_fusion.8), channel_id=1, source_target_pairs={{0,16},{1,17},{2,18},{3,19},{4,20},{5,21},{6,22},{7,23},{8,24},{9,... | collective-permute-start | bytes 1081352 | tf_op jit(solution)/shard_map/ppermute | solution.py:432
  87.3 10.7 %collective-permute-start.14 = (bf16[32,2816]{1,0:T(8,128)(2,1)S(1)}, bf16[32,2816]{1,0:T(8,128)(2,1)}, u32[]{:S(2)}, u32[]{:S(2)}) collective-permute-start(bf16[32,2816]{1,0:T(8,128)(2,1)S(1)} %pad.34), channel_id=1, source_target_pairs={{0,8},{1,9},{2,10},{3,11},{4,12},{5,13},{6,14},{7,15},{8,0},{9,1},... | collective-permute-start | bytes 540680 | tf_op jit(solution)/shard_map/ppermute | solution.py:432
  98.1 25.2 %collective-permute-start.19 = (bf16[128,2816]{1,0:T(8,128)(2,1)S(1)}, bf16[128,2816]{1,0:T(8,128)(2,1)S(1)}, u32[]{:S(2)}, u32[]{:S(2)}) collective-permute-start(bf16[128,2816]{1,0:T(8,128)(2,1)S(1)} %pad_maximum_fusion.4.refs_0_), channel_id=1, source_target_pairs={{0,4},{1,5},{2,6},{3,7},{4,0},{5,1},{6,2},{7,3},{8,12},{9,13},{10,... | collective-permute-start | bytes 2162696 | tf_op jit(solution)/shard_map/ppermute | solution.py:432
  98.5 24.8 %collective-permute-start.18 = (bf16[128,2816]{1,0:T(8,128)(2,1)S(1)}, bf16[128,2816]{1,0:T(8,128)(2,1)S(1)}, u32[]{:S(2)}, u32[]{:S(2)}) collective-permute-start(bf16[128,2816]{1,0:T(8,128)(2,1)S(1)} %pad_maximum_fusion.4.refs_0_), channel_id=1, source_target_pairs={{0,1},{1,0},{2,3},{3,2},{4,5},{5,4},{6,7},{7,6},{8,9},{9,8},{10,11... | collective-permute-start | bytes 2162696 | tf_op jit(solution)/shard_map/ppermute | solution.py:432
  102.1 21.1 %collective-permute-start.17 = (bf16[64,2560]{1,0:T(8,128)(2,1)S(1)}, bf16[64,2560]{1,0:T(8,128)(2,1)S(1)}, u32[]{:S(2)}, u32[]{:S(2)}) collective-permute-start(bf16[64,2560]{1,0:T(8,128)(2,1)S(1)} %slice.349), channel_id=1, source_target_pairs={{0,4},{1,5},{2,6},{3,7},{4,0},{5,1},{6,2},{7,3},{8,12},{9,13},{10,... | collective-permute-start | bytes 983048 | tf_op jit(solution)/shard_map/ppermute | solution.py:432
  103.7 19.6 %collective-permute-start.16 = (bf16[64,2560]{1,0:T(8,128)(2,1)S(1)}, bf16[64,2560]{1,0:T(8,128)(2,1)S(1)}, u32[]{:S(2)}, u32[]{:S(2)}) collective-permute-start(bf16[64,2560]{1,0:T(8,128)(2,1)S(1)} %slice.348), channel_id=1, source_target_pairs={{0,1},{1,0},{2,3},{3,2},{4,5},{5,4},{6,7},{7,6},{8,9},{9,8},{10,11... | collective-permute-start | bytes 983048 | tf_op jit(solution)/shard_map/ppermute | solution.py:432
  104.2 17.8 %collective-permute-start.20 = (bf16[64,2816]{1,0:T(8,128)(2,1)S(1)}, bf16[64,2816]{1,0:T(8,128)(2,1)S(1)}, u32[]{:S(2)}, u32[]{:S(2)}) collective-permute-start(bf16[64,2816]{1,0:T(8,128)(2,1)S(1)} %pad_maximum_fusion.9), channel_id=1, source_target_pairs={{0,16},{1,17},{2,18},{3,19},{4,20},{5,21},{6,22},{7,23},{8,24},{9,... | collective-permute-start | bytes 1081352 | tf_op jit(solution)/shard_map/ppermute | solution.py:432
  123.3 24.3 %collective-permute-start.24 = (bf16[32,2816]{1,0:T(8,128)(2,1)S(1)}, bf16[32,2816]{1,0:T(8,128)(2,1)S(1)}, u32[]{:S(2)}, u32[]{:S(2)}) collective-permute-start(bf16[32,2816]{1,0:T(8,128)(2,1)S(1)} %pad.36), channel_id=1, source_target_pairs={{0,8},{1,9},{2,10},{3,11},{4,12},{5,13},{6,14},{7,15},{8,0},{9,1},... | collective-permute-start | bytes 540680 | tf_op jit(solution)/shard_map/ppermute | solution.py:432
  125.2 23.0 %collective-permute-start.23 = (bf16[64,2816]{1,0:T(8,128)(2,1)S(1)}, bf16[64,2816]{1,0:T(8,128)(2,1)S(1)}, u32[]{:S(2)}, u32[]{:S(2)}) collective-permute-start(bf16[64,2816]{1,0:T(8,128)(2,1)S(1)} %slice.351), channel_id=1, source_target_pairs={{0,4},{1,5},{2,6},{3,7},{4,0},{5,1},{6,2},{7,3},{8,12},{9,13},{10,... | collective-permute-start | bytes 1081352 | tf_op jit(solution)/shard_map/ppermute | solution.py:432
  126.9 21.3 %collective-permute-start.22 = (bf16[64,2816]{1,0:T(8,128)(2,1)S(1)}, bf16[64,2816]{1,0:T(8,128)(2,1)S(1)}, u32[]{:S(2)}, u32[]{:S(2)}) collective-permute-start(bf16[64,2816]{1,0:T(8,128)(2,1)S(1)} %slice.350), channel_id=1, source_target_pairs={{0,1},{1,0},{2,3},{3,2},{4,5},{5,4},{6,7},{7,6},{8,9},{9,8},{10,11... | collective-permute-start | bytes 1081352 | tf_op jit(solution)/shard_map/ppermute | solution.py:432
  128.4 36.3 %collective-permute-start.26 = (bf16[128,2816]{1,0:T(8,128)(2,1)S(1)}, bf16[128,2816]{1,0:T(8,128)(2,1)S(1)}, u32[]{:S(2)}, u32[]{:S(2)}) collective-permute-start(bf16[128,2816]{1,0:T(8,128)(2,1)S(1)} %constant_dynamic-update-slice_fusion.4.refs_0_), channel_id=1, source_target_pairs={{0,4},{1,5},{2,6},{3,7},{4,0},{5,1},{6,2},{7,3},{8,12},{9,13},{10,... | collective-permute-start | bytes 2162696 | tf_op jit(solution)/shard_map/ppermute | solution.py:432
  131.3 16.9 %collective-permute-start.21 = (bf16[512,2560]{1,0:T(8,128)(2,1)S(1)}, bf16[512,2560]{1,0:T(8,128)(2,1)}, u32[]{:S(2)}, u32[]{:S(2)}) collective-permute-start(bf16[512,2560]{1,0:T(8,128)(2,1)S(1)} %pack_rows.6.qn_ref.kn_ref.vn_ref.na_ref.nb_ref.refs_16_), channel_id=1, source_target_pairs={{0,2},{1,3},{2,0},{3,1},{4,6},{5,7},{6,4},{7,5},{8,10},{9,11},{10,... | collective-permute-start | bytes 7864328 | tf_op jit(solution)/shard_map/ppermute | solution.py:432
  147.6 17.8 %collective-permute-start.25 = (bf16[128,2816]{1,0:T(8,128)(2,1)S(1)}, bf16[128,2816]{1,0:T(8,128)(2,1)S(1)}, u32[]{:S(2)}, u32[]{:S(2)}) collective-permute-start(bf16[128,2816]{1,0:T(8,128)(2,1)S(1)} %constant_dynamic-update-slice_fusion.4.refs_0_), channel_id=1, source_target_pairs={{0,1},{1,0},{2,3},{3,2},{4,5},{5,4},{6,7},{7,6},{8,9},{9,8},{10,11... | collective-permute-start | bytes 2162696 | tf_op jit(solution)/shard_map/ppermute | solution.py:432
  148.9 19.4 %collective-permute-start.27 = (bf16[512,2816]{1,0:T(8,128)(2,1)S(1)}, bf16[512,2816]{1,0:T(8,128)(2,1)}, u32[]{:S(2)}, u32[]{:S(2)}) collective-permute-start(bf16[512,2816]{1,0:T(8,128)(2,1)S(1)} %pack_rows.7.gn_ref), channel_id=1, source_target_pairs={{0,2},{1,3},{2,0},{3,1},{4,6},{5,7},{6,4},{7,5},{8,10},{9,11},{10,... | collective-permute-start | bytes 8650760 | tf_op jit(solution)/shard_map/ppermute | solution.py:432
  149.0 19.2 %collective-permute-start.28 = (bf16[64,2816]{1,0:T(8,128)(2,1)S(1)}, bf16[64,2816]{1,0:T(8,128)(2,1)S(1)}, u32[]{:S(2)}, u32[]{:S(2)}) collective-permute-start(bf16[64,2816]{1,0:T(8,128)(2,1)S(1)} %pad_maximum_fusion.10), channel_id=1, source_target_pairs={{0,16},{1,17},{2,18},{3,19},{4,20},{5,21},{6,22},{7,23},{8,24},{9,... | collective-permute-start | bytes 1081352 | tf_op jit(solution)/shard_map/ppermute | solution.py:432
  168.3 16.3 %collective-permute-start.30 = (bf16[64,2816]{1,0:T(8,128)(2,1)S(1)}, bf16[64,2816]{1,0:T(8,128)(2,1)S(1)}, u32[]{:S(2)}, u32[]{:S(2)}) collective-permute-start(bf16[64,2816]{1,0:T(8,128)(2,1)S(1)} %slice.353), channel_id=1, source_target_pairs={{0,4},{1,5},{2,6},{3,7},{4,0},{5,1},{6,2},{7,3},{8,12},{9,13},{10,... | collective-permute-start | bytes 1081352 | tf_op jit(solution)/shard_map/ppermute | solution.py:432
  170.0 14.6 %collective-permute-start.29 = (bf16[64,2816]{1,0:T(8,128)(2,1)S(1)}, bf16[64,2816]{1,0:T(8,128)(2,1)S(1)}, u32[]{:S(2)}, u32[]{:S(2)}) collective-permute-start(bf16[64,2816]{1,0:T(8,128)(2,1)S(1)} %slice.352), channel_id=1, source_target_pairs={{0,1},{1,0},{2,3},{3,2},{4,5},{5,4},{6,7},{7,6},{8,9},{9,8},{10,11... | collective-permute-start | bytes 1081352 | tf_op jit(solution)/shard_map/ppermute | solution.py:432
  185.4 22.0 %collective-permute-start.31 = (bf16[512,2816]{1,0:T(8,128)(2,1)S(1)}, bf16[512,2816]{1,0:T(8,128)(2,1)}, u32[]{:S(2)}, u32[]{:S(2)}) collective-permute-start(bf16[512,2816]{1,0:T(8,128)(2,1)S(1)} %pack_rows.8.un_ref), channel_id=1, source_target_pairs={{0,2},{1,3},{2,0},{3,1},{4,6},{5,7},{6,4},{7,5},{8,10},{9,11},{10,... | collective-permute-start | bytes 8650760 | tf_op jit(solution)/shard_map/ppermute | solution.py:432
  189.7 17.6 %collective-permute-start.33 = (bf16[128,2816]{1,0:T(8,128)(2,1)S(1)}, bf16[128,2816]{1,0:T(8,128)(2,1)S(1)}, u32[]{:S(2)}, u32[]{:S(2)}) collective-permute-start(bf16[128,2816]{1,0:T(8,128)(2,1)S(1)} %constant_dynamic-update-slice_fusion.6.refs_0_), channel_id=1, source_target_pairs={{0,4},{1,5},{2,6},{3,7},{4,0},{5,1},{6,2},{7,3},{8,12},{9,13},{10,... | collective-permute-start | bytes 2162696 | tf_op jit(solution)/shard_map/ppermute | solution.py:432
  190.2 17.3 %collective-permute-start.32 = (bf16[128,2816]{1,0:T(8,128)(2,1)S(1)}, bf16[128,2816]{1,0:T(8,128)(2,1)S(1)}, u32[]{:S(2)}, u32[]{:S(2)}) collective-permute-start(bf16[128,2816]{1,0:T(8,128)(2,1)S(1)} %constant_dynamic-update-slice_fusion.6.refs_0_), channel_id=1, source_target_pairs={{0,1},{1,0},{2,3},{3,2},{4,5},{5,4},{6,7},{7,6},{8,9},{9,8},{10,11... | collective-permute-start | bytes 2162696 | tf_op jit(solution)/shard_map/ppermute | solution.py:432
  207.6 26.1 %collective-permute-start.36 = (bf16[64,2816]{1,0:T(8,128)(2,1)S(1)}, bf16[64,2816]{1,0:T(8,128)(2,1)S(1)}, u32[]{:S(2)}, u32[]{:S(2)}) collective-permute-start(bf16[64,2816]{1,0:T(8,128)(2,1)S(1)} %slice.355), channel_id=1, source_target_pairs={{0,4},{1,5},{2,6},{3,7},{4,0},{5,1},{6,2},{7,3},{8,12},{9,13},{10,... | collective-permute-start | bytes 1081352 | tf_op jit(solution)/shard_map/ppermute | solution.py:432
  209.2 24.5 %collective-permute-start.35 = (bf16[64,2816]{1,0:T(8,128)(2,1)S(1)}, bf16[64,2816]{1,0:T(8,128)(2,1)S(1)}, u32[]{:S(2)}, u32[]{:S(2)}) collective-permute-start(bf16[64,2816]{1,0:T(8,128)(2,1)S(1)} %slice.354), channel_id=1, source_target_pairs={{0,1},{1,0},{2,3},{3,2},{4,5},{5,4},{6,7},{7,6},{8,9},{9,8},{10,11... | collective-permute-start | bytes 1081352 | tf_op jit(solution)/shard_map/ppermute | solution.py:432
  209.8 30.3 %collective-permute-start.34 = (bf16[512,1024]{1,0:T(8,128)(2,1)S(1)}, bf16[512,1024]{1,0:T(8,128)(2,1)S(1)}, u32[]{:S(2)}, u32[]{:S(2)}) collective-permute-start(bf16[512,1024]{1,0:T(8,128)(2,1)S(1)} %get-tuple-element.229), channel_id=1, source_target_pairs={{0,1},{1,0},{2,3},{3,2},{4,5},{5,4},{6,7},{7,6},{8,9},{9,8},{10,11... | collective-permute-start | bytes 3145736 | tf_op jit(solution)/shard_map/ppermute | solution.py:432
  278.2 15.8 %collective-permute-start.38 = (f32[4,2730]{1,0:T(4,128)S(1)}, f32[4,2730]{1,0:T(4,128)S(1)}, u32[]{:S(2)}, u32[]{:S(2)}) collective-permute-start(f32[4,2730]{1,0:T(4,128)S(1)} %slice.356), channel_id=1, source_target_pairs={{0,2},{1,3},{2,0},{3,1},{4,6},{5,7},{6,4},{7,5},{8,10},{9,11},{10,... | collective-permute-start | bytes 131048 | tf_op jit(solution)/shard_map/ppermute | solution.py:432
  294.0 15.2 %collective-permute-start.40 = (f32[4,2730]{1,0:T(4,128)S(1)}, f32[4,2730]{1,0:T(4,128)S(1)}, u32[]{:S(2)}, u32[]{:S(2)}) collective-permute-start(f32[4,2730]{1,0:T(4,128)S(1)} %add.236), channel_id=1, source_target_pairs={{0,1},{1,0},{2,3},{3,2},{4,5},{5,4},{6,7},{7,6},{8,9},{9,8},{10,11... | collective-permute-start | bytes 131048 | tf_op jit(solution)/shard_map/ppermute | solution.py:432
  294.6 14.6 %collective-permute-start.39 = (bf16[512,2816]{1,0:T(8,128)(2,1)}, bf16[512,2816]{1,0:T(8,128)(2,1)}, u32[]{:S(2)}, u32[]{:S(2)}) collective-permute-start(bf16[512,2816]{1,0:T(8,128)(2,1)} %get-tuple-element.246), channel_id=1, source_target_pairs={{0,2},{1,3},{2,0},{3,1},{4,6},{5,7},{6,4},{7,5},{8,10},{9,11},{10,... | collective-permute-start | bytes 8650760 | tf_op jit(solution)/shard_map/ppermute | solution.py:432
  311.9 28.8 %collective-permute-start.44 = (f32[4,2730]{1,0:T(4,128)S(1)}, f32[4,2730]{1,0:T(4,128)S(1)}, u32[]{:S(2)}, u32[]{:S(2)}) collective-permute-start(f32[4,2730]{1,0:T(4,128)S(1)} %add.238), channel_id=1, source_target_pairs={{0,4},{1,5},{2,6},{3,7},{4,0},{5,1},{6,2},{7,3},{8,12},{9,13},{10,... | collective-permute-start | bytes 131048 | tf_op jit(solution)/shard_map/ppermute | solution.py:432
  312.7 28.1 %collective-permute-start.43 = (bf16[64,2816]{1,0:T(8,128)(2,1)S(1)}, bf16[64,2816]{1,0:T(8,128)(2,1)S(1)}, u32[]{:S(2)}, u32[]{:S(2)}) collective-permute-start(bf16[64,2816]{1,0:T(8,128)(2,1)S(1)} %get-tuple-element.345), channel_id=1, source_target_pairs={{0,1},{1,0},{2,3},{3,2},{4,5},{5,4},{6,7},{7,6},{8,9},{9,8},{10,11... | collective-permute-start | bytes 1081352 | tf_op jit(solution)/shard_map/ppermute | solution.py:432
  314.2 26.6 %collective-permute-start.42 = (bf16[64,2816]{1,0:T(8,128)(2,1)S(1)}, bf16[64,2816]{1,0:T(8,128)(2,1)S(1)}, u32[]{:S(2)}, u32[]{:S(2)}) collective-permute-start(bf16[64,2816]{1,0:T(8,128)(2,1)S(1)} %get-tuple-element.347), channel_id=1, source_target_pairs={{0,4},{1,5},{2,6},{3,7},{4,0},{5,1},{6,2},{7,3},{8,12},{9,13},{10,... | collective-permute-start | bytes 1081352 | tf_op jit(solution)/shard_map/ppermute | solution.py:432
  340.1 25.4 %collective-permute-start.41 = (bf16[528,1024]{1,0:T(8,128)(2,1)S(1)}, bf16[528,1024]{1,0:T(8,128)(2,1)S(1)}, u32[]{:S(2)}, u32[]{:S(2)}) collective-permute-start(bf16[528,1024]{1,0:T(8,128)(2,1)S(1)} %slice.358), channel_id=1, source_target_pairs={{0,1},{1,0},{2,3},{3,2},{4,5},{5,4},{6,7},{7,6},{8,9},{9,8},{10,11... | collective-permute-start | bytes 3244040 | tf_op jit(solution)/shard_map/ppermute | solution.py:432
  367.9 28.9 %collective-permute-start.48 = (f32[4,2730]{1,0:T(4,128)S(1)}, f32[4,2730]{1,0:T(4,128)S(1)}, u32[]{:S(2)}, u32[]{:S(2)}) collective-permute-start(f32[4,2730]{1,0:T(4,128)S(1)} %add.241), channel_id=1, source_target_pairs={{0,8},{1,9},{2,10},{3,11},{4,12},{5,13},{6,14},{7,15},{8,0},{9,1},... | collective-permute-start | bytes 131048 | tf_op jit(solution)/shard_map/ppermute | solution.py:432
  367.9 29.0 %collective-permute-start.45 = (bf16[128,2816]{1,0:T(8,128)(2,1)S(1)}, bf16[128,2816]{1,0:T(8,128)(2,1)S(1)}, u32[]{:S(2)}, u32[]{:S(2)}) collective-permute-start(bf16[128,2816]{1,0:T(8,128)(2,1)S(1)} %pad_maximum_fusion.6), channel_id=1, source_target_pairs={{0,4},{1,5},{2,6},{3,7},{4,0},{5,1},{6,2},{7,3},{8,12},{9,13},{10,... | collective-permute-start | bytes 2162696 | tf_op jit(solution)/shard_map/ppermute | solution.py:432
  368.5 28.4 %collective-permute-start.46 = (bf16[128,2816]{1,0:T(8,128)(2,1)S(1)}, bf16[128,2816]{1,0:T(8,128)(2,1)S(1)}, u32[]{:S(2)}, u32[]{:S(2)}) collective-permute-start(bf16[128,2816]{1,0:T(8,128)(2,1)S(1)} %pad_maximum_fusion.5), channel_id=1, source_target_pairs={{0,1},{1,0},{2,3},{3,2},{4,5},{5,4},{6,7},{7,6},{8,9},{9,8},{10,11... | collective-permute-start | bytes 2162696 | tf_op jit(solution)/shard_map/ppermute | solution.py:432
  369.0 28.1 %collective-permute-start.47 = (bf16[512,5632]{1,0:T(8,128)(2,1)}, bf16[512,5632]{1,0:T(8,128)(2,1)}, u32[]{:S(2)}, u32[]{:S(2)}) collective-permute-start(bf16[512,5632]{1,0:T(8,128)(2,1)} %get-tuple-element.264), channel_id=1, source_target_pairs={{0,2},{1,3},{2,0},{3,1},{4,6},{5,7},{6,4},{7,5},{8,10},{9,11},{10,... | collective-permute-start | bytes 17301512 | tf_op jit(solution)/shard_map/ppermute | solution.py:432
  403.0 21.9 %collective-permute-start.52 = (f32[4,2730]{1,0:T(4,128)S(1)}, f32[4,2730]{1,0:T(4,128)S(1)}, u32[]{:S(2)}, u32[]{:S(2)}) collective-permute-start(f32[4,2730]{1,0:T(4,128)S(1)} %add.245), channel_id=1, source_target_pairs={{0,16},{1,17},{2,18},{3,19},{4,20},{5,21},{6,22},{7,23},{8,24},{9,... | collective-permute-start | bytes 131048 | tf_op jit(solution)/shard_map/ppermute | solution.py:432
  403.6 22.0 %collective-permute-start.49 = (bf16[64,2816]{1,0:T(8,128)(2,1)S(1)}, bf16[64,2816]{1,0:T(8,128)(2,1)S(1)}, u32[]{:S(2)}, u32[]{:S(2)}) collective-permute-start(bf16[64,2816]{1,0:T(8,128)(2,1)S(1)} %slice.370), channel_id=1, source_target_pairs={{0,16},{1,17},{2,18},{3,19},{4,20},{5,21},{6,22},{7,23},{8,24},{9,... | collective-permute-start | bytes 1081352 | tf_op jit(solution)/shard_map/ppermute | solution.py:432
  407.1 18.6 %collective-permute-start.51 = (bf16[64,5632]{1,0:T(8,128)(2,1)}, bf16[64,5632]{1,0:T(8,128)(2,1)S(1)}, u32[]{:S(2)}, u32[]{:S(2)}) collective-permute-start(bf16[64,5632]{1,0:T(8,128)(2,1)} %get-tuple-element.333), channel_id=1, source_target_pairs={{0,1},{1,0},{2,3},{3,2},{4,5},{5,4},{6,7},{7,6},{8,9},{9,8},{10,11... | collective-permute-start | bytes 2162696 | tf_op jit(solution)/shard_map/ppermute | solution.py:432
  408.6 17.8 %collective-permute-start.50 = (bf16[64,5632]{1,0:T(8,128)(2,1)S(1)}, bf16[64,5632]{1,0:T(8,128)(2,1)}, u32[]{:S(2)}, u32[]{:S(2)}) collective-permute-start(bf16[64,5632]{1,0:T(8,128)(2,1)S(1)} %get-tuple-element.335), channel_id=1, source_target_pairs={{0,4},{1,5},{2,6},{3,7},{4,0},{5,1},{6,2},{7,3},{8,12},{9,13},{10,... | collective-permute-start | bytes 2162696 | tf_op jit(solution)/shard_map/ppermute | solution.py:432
  429.7 18.5 %collective-permute-start.53 = (bf16[32,2816]{1,0:T(8,128)(2,1)S(1)}, bf16[32,2816]{1,0:T(8,128)(2,1)S(1)}, u32[]{:S(2)}, u32[]{:S(2)}) collective-permute-start(bf16[32,2816]{1,0:T(8,128)(2,1)S(1)} %slice.378), channel_id=1, source_target_pairs={{0,8},{1,9},{2,10},{3,11},{4,12},{5,13},{6,14},{7,15},{8,0},{9,1},... | collective-permute-start | bytes 540680 | tf_op jit(solution)/shard_map/ppermute | solution.py:432
  446.1 32.3 %collective-permute-start.54 = (bf16[128,5632]{1,0:T(8,128)(2,1)S(1)}, bf16[128,5632]{1,0:T(8,128)(2,1)}, u32[]{:S(2)}, u32[]{:S(2)}) collective-permute-start(bf16[128,5632]{1,0:T(8,128)(2,1)S(1)} %pad_maximum_fusion.1), channel_id=1, source_target_pairs={{0,4},{1,5},{2,6},{3,7},{4,0},{5,1},{6,2},{7,3},{8,12},{9,13},{10,... | collective-permute-start | bytes 4325384 | tf_op jit(solution)/shard_map/ppermute | solution.py:432
  447.6 31.8 %collective-permute-start.55 = (bf16[128,5632]{1,0:T(8,128)(2,1)S(1)}, bf16[128,5632]{1,0:T(8,128)(2,1)}, u32[]{:S(2)}, u32[]{:S(2)}) collective-permute-start(bf16[128,5632]{1,0:T(8,128)(2,1)S(1)} %copy-done.83), channel_id=1, source_target_pairs={{0,1},{1,0},{2,3},{3,2},{4,5},{5,4},{6,7},{7,6},{8,9},{9,8},{10,11... | collective-permute-start | bytes 4325384 | tf_op jit(solution)/shard_map/ppermute | solution.py:432
  482.3 33.3 %collective-permute-start.57 = (bf16[64,5632]{1,0:T(8,128)(2,1)S(1)}, bf16[64,5632]{1,0:T(8,128)(2,1)S(1)}, u32[]{:S(2)}, u32[]{:S(2)}) collective-permute-start(bf16[64,5632]{1,0:T(8,128)(2,1)S(1)} %slice.381), channel_id=1, source_target_pairs={{0,16},{1,17},{2,18},{3,19},{4,20},{5,21},{6,22},{7,23},{8,24},{9,... | collective-permute-start | bytes 2162696 | tf_op jit(solution)/shard_map/ppermute | solution.py:432
  520.8 11.9 %collective-permute-start.59 = (bf16[64,3328]{1,0:T(8,128)(2,1)S(1)}, bf16[64,3328]{1,0:T(8,128)(2,1)S(1)}, u32[]{:S(2)}, u32[]{:S(2)}) collective-permute-start(bf16[64,3328]{1,0:T(8,128)(2,1)S(1)} %get-tuple-element.339), channel_id=1, source_target_pairs={{0,1},{1,0},{2,3},{3,2},{4,5},{5,4},{6,7},{7,6},{8,9},{9,8},{10,11... | collective-permute-start | bytes 1277960 | tf_op jit(solution)/shard_map/ppermute | solution.py:432
  521.8 11.6 %collective-permute-start.58 = (bf16[64,3328]{1,0:T(8,128)(2,1)S(1)}, bf16[64,3328]{1,0:T(8,128)(2,1)S(1)}, u32[]{:S(2)}, u32[]{:S(2)}) collective-permute-start(bf16[64,3328]{1,0:T(8,128)(2,1)S(1)} %get-tuple-element.341), channel_id=1, source_target_pairs={{0,4},{1,5},{2,6},{3,7},{4,0},{5,1},{6,2},{7,3},{8,12},{9,13},{10,... | collective-permute-start | bytes 1277960 | tf_op jit(solution)/shard_map/ppermute | solution.py:432
  552.1 10.9 %collective-permute-start.72 = (bf16[32,5632]{1,0:T(8,128)(2,1)S(1)}, bf16[32,5632]{1,0:T(8,128)(2,1)S(1)}, u32[]{:S(2)}, u32[]{:S(2)}) collective-permute-start(bf16[32,5632]{1,0:T(8,128)(2,1)S(1)} %slice.422), channel_id=1, source_target_pairs={{0,8},{1,9},{2,10},{3,11},{4,12},{5,13},{6,14},{7,15},{8,0},{9,1},... | collective-permute-start | bytes 1081352 | tf_op jit(solution)/shard_map/ppermute | solution.py:432
  563.1 9.4 %collective-permute-start.65 = (bf16[512,768]{1,0:T(8,128)(2,1)S(1)}, bf16[512,768]{1,0:T(8,128)(2,1)S(1)}, u32[]{:S(2)}, u32[]{:S(2)}) collective-permute-start(bf16[512,768]{1,0:T(8,128)(2,1)S(1)} %get-tuple-element.319), channel_id=1, source_target_pairs={{0,2},{1,3},{2,0},{3,1},{4,6},{5,7},{6,4},{7,5},{8,10},{9,11},{10,... | collective-permute-start | bytes 2359304 | tf_op jit(solution)/shard_map/ppermute | solution.py:432
  566.3 21.8 %collective-permute-start.61 = (bf16[128,3328]{1,0:T(8,128)(2,1)S(1)}, bf16[128,3328]{1,0:T(8,128)(2,1)S(1)}, u32[]{:S(2)}, u32[]{:S(2)}) collective-permute-start(bf16[128,3328]{1,0:T(8,128)(2,1)S(1)} %pad_maximum_fusion.3), channel_id=1, source_target_pairs={{0,4},{1,5},{2,6},{3,7},{4,0},{5,1},{6,2},{7,3},{8,12},{9,13},{10,... | collective-permute-start | bytes 2555912 | tf_op jit(solution)/shard_map/ppermute | solution.py:432
  567.1 21.8 %collective-permute-start.62 = (bf16[128,3328]{1,0:T(8,128)(2,1)S(1)}, bf16[128,3328]{1,0:T(8,128)(2,1)S(1)}, u32[]{:S(2)}, u32[]{:S(2)}) collective-permute-start(bf16[128,3328]{1,0:T(8,128)(2,1)S(1)} %pad_maximum_fusion.2), channel_id=1, source_target_pairs={{0,1},{1,0},{2,3},{3,2},{4,5},{5,4},{6,7},{7,6},{8,9},{9,8},{10,11... | collective-permute-start | bytes 2555912 | tf_op jit(solution)/shard_map/ppermute | solution.py:432
  568.8 46.9 %collective-permute-start.60 = (bf16[528,1024]{1,0:T(8,128)(2,1)S(1)}, bf16[528,1024]{1,0:T(8,128)(2,1)S(1)}, u32[]{:S(2)}, u32[]{:S(2)}) collective-permute-start(bf16[528,1024]{1,0:T(8,128)(2,1)S(1)} %slice.389), channel_id=1, source_target_pairs={{0,1},{1,0},{2,3},{3,2},{4,5},{5,4},{6,7},{7,6},{8,9},{9,8},{10,11... | collective-permute-start | bytes 3244040 | tf_op jit(solution)/shard_map/ppermute | solution.py:432
  572.7 40.4 %collective-permute-start.67 = (bf16[64,768]{1,0:T(8,128)(2,1)S(1)}, bf16[64,768]{1,0:T(8,128)(2,1)S(1)}, u32[]{:S(2)}, u32[]{:S(2)}) collective-permute-start(bf16[64,768]{1,0:T(8,128)(2,1)S(1)} %get-tuple-element.355), channel_id=1, source_target_pairs={{0,1},{1,0},{2,3},{3,2},{4,5},{5,4},{6,7},{7,6},{8,9},{9,8},{10,11... | collective-permute-start | bytes 294920 | tf_op jit(solution)/shard_map/ppermute | solution.py:432
  573.7 39.4 %collective-permute-start.66 = (bf16[64,768]{1,0:T(8,128)(2,1)S(1)}, bf16[64,768]{1,0:T(8,128)(2,1)S(1)}, u32[]{:S(2)}, u32[]{:S(2)}) collective-permute-start(bf16[64,768]{1,0:T(8,128)(2,1)S(1)} %get-tuple-element.357), channel_id=1, source_target_pairs={{0,4},{1,5},{2,6},{3,7},{4,0},{5,1},{6,2},{7,3},{8,12},{9,13},{10,... | collective-permute-start | bytes 294920 | tf_op jit(solution)/shard_map/ppermute | solution.py:432
  589.2 42.2 %collective-permute-start.63 = (bf16[64,3328]{1,0:T(8,128)(2,1)S(1)}, bf16[64,3328]{1,0:T(8,128)(2,1)S(1)}, u32[]{:S(2)}, u32[]{:S(2)}) collective-permute-start(bf16[64,3328]{1,0:T(8,128)(2,1)S(1)} %slice.395), channel_id=1, source_target_pairs={{0,16},{1,17},{2,18},{3,19},{4,20},{5,21},{6,22},{7,23},{8,24},{9,... | collective-permute-start | bytes 1277960 | tf_op jit(solution)/shard_map/ppermute | solution.py:432
  (125 other events, 1572.5 us)

commit v3 on v2

--- a/solution.py
+++ b/solution.py
@@ -414,7 +414,7 @@
 
 
 BOTH = ("dp", "ctx")
-BIT_X, BIT_CORE, BIT_Y, BIT_Z0, BIT_Z1 = 1, 2, 4, 8, 16
+BIT_X, BIT_CORE, BIT_Y, BIT_Z0, BIT_Z1 = 1, 2, 4, 16, 8
 ROWS = 1040
 KEYS = 1024
 WIDTH = 1024
@@ -427,7 +427,11 @@
 BF16 = jnp.bfloat16
 
 
+SENT = []
+
+
 def swap_over(value, bit):
+    SENT.append(value)
     count = lax.axis_size(BOTH)
     return lax.ppermute(value, BOTH, [(i, i ^ bit) for i in range(count)])
 
@@ -438,6 +442,12 @@
 
 def after(value, *deps):
     return lax.optimization_barrier((value,) + deps)[0]
+
+
+def ready(value, *deps):
+    corners = [sum(v[0:1, 0:1].astype(F32) for v in SENT)] if SENT else []
+    SENT.clear()
+    return after(value, *deps, *corners)
 
 
 def dot_nn(a, b):
@@ -523,24 +533,35 @@
 
 
 class Scatter:
-    def __init__(self, near, far):
-        self.near, self.far = near, far
-
-    def over_core(self, *deps):
-        self.total = rounded_sum(self.near, swap_over(after(self.far, *deps), BIT_CORE))
+    def over_core(self, far, *deps):
+        return swap_over(after(far, *deps), BIT_CORE)
+
+    def corner(self, total, *deps):
+        self.total = after(total, *deps)
+        self.to_x = rounded_sum(self.total[256:384], swap_over(self.total[384:], BIT_Y))
+        self.to_y = self.total[128:256]
+        return self.to_x
+
+    def corners(self, total, *deps):
+        self.total = total = after(total, *deps)
+        from_x, from_y = swap_over(total[384:448], BIT_X), swap_over(total[448:512], BIT_Y)
+        self.to_y = joined(rounded_sum(total[128:192], from_x), total[192:256])
+        self.to_x = joined(total[256:320], rounded_sum(total[320:384], from_y))
+        return self.to_x, self.to_y
+
+    def sides(self, *deps):
+        to_x, to_y = after((self.to_x, self.to_y), *deps)
+        self.total = rounded_sum(self.total[:128], swap_over(to_y, BIT_Y), swap_over(to_x, BIT_X))
         return self.total
 
-    def corners(self, *deps):
+    def over_x(self, *deps):
         total = after(self.total, *deps)
-        from_x, from_y = swap_over(total[384:448], BIT_X), swap_over(total[448:512], BIT_Y)
-        to_y = joined(rounded_sum(total[128:192], from_x), total[192:256])
-        to_x = joined(total[256:320], rounded_sum(total[320:384], from_y))
-        self.sides = to_x, to_y
-        return self.sides
-
-    def over_xy(self, *deps):
-        to_x, to_y = after(self.sides, *deps)
-        self.total = rounded_sum(self.total[:128], swap_over(to_y, BIT_Y), swap_over(to_x, BIT_X))
+        self.total = rounded_sum(total[:256], swap_over(total[256:], BIT_X))
+        return self.total
+
+    def over_y(self, *deps):
+        total = after(self.total, *deps)
+        self.total = rounded_sum(total[:128], swap_over(total[128:], BIT_Y))
         return self.total
 
     def along_z1(self, *deps):
@@ -553,11 +574,6 @@
         return total[:32].astype(F32) + swap_over(total[32:], BIT_Z0).astype(F32)
 
 
-def sum_over(value, bit, *deps):
-    value = after(value, *deps)
-    return value + swap_over(value, bit)
-
-
 def scatter_small(value):
     for rows, bit in ((512, BIT_CORE), (256, BIT_X), (128, BIT_Y), (64, BIT_Z1), (32, BIT_Z0)):
         value = value[:rows] + swap_over(value[rows:], bit)
@@ -575,7 +591,7 @@
 
 def attention_kernel(
     x_ref, qn_ref, qf_ref, kn_ref, kf_ref, vn_ref, vf_ref, b_ref, c_ref, s1_ref, s2_ref,
-    q_ref, k_ref, v_ref, o_ref, l_ref, stat_ref, *, step
+    q_ref, k_ref, v_ref, o_ref, l_ref
 ):
     def project(near_ref, far_ref):
         return dot_nn(x_ref[:, :HALF], near_ref[...]) + dot_nn(x_ref[:, HALF:], far_ref[...])
@@ -588,37 +604,31 @@
     lane = lax.broadcasted_iota(jnp.int32, (1, 128), 1)
     low_half = lane < 64
 
-    def tile(i, carry):
-        rows = pl.ds(pl.multiple_of(i * step, 16), step)
-        stats = jnp.zeros((step, 128), F32)
-        for pair in range(2):
-            cols = slice(pair * 128, pair * 128 + 128)
-            q_pair = q_ref[rows, cols]
-            k_pair, v_pair = k_ref[0:KEYS, cols], v_ref[0:KEYS, cols]
-            k_class = k_ref[KEYS : KEYS + 16, cols].astype(F32)[0:1]
-            v_class = v_ref[KEYS : KEYS + 16, cols].astype(F32)[0:1]
-            product = q_pair.astype(F32) * k_class
-            outs = []
-            for h in range(2):
-                own = low_half if h == 0 else ~low_half
-                scores = dot_nt(jnp.where(own, q_pair, jnp.zeros_like(q_pair)), k_pair)
-                class_score = jnp.sum(jnp.where(own, product, 0.0), axis=1, keepdims=True)
-                peak = jnp.maximum(jnp.max(scores, axis=1, keepdims=True), class_score)
-                p = jnp.exp2(scores - peak)
-                class_p = jnp.exp2(class_score - peak)
-                total = jnp.sum(p, axis=1, keepdims=True) + class_p
-                out = dot_nn(p.astype(BF16), v_pair) + class_p * v_class
-                outs.append(out * (1.0 / total))
-                stats = jnp.where(lane == pair * 2 + h, peak + jnp.log2(total), stats)
-            o_ref[rows, cols] = jnp.where(low_half, outs[0], outs[1]).astype(BF16)
-        stat_ref[rows, :] = stats
-        return carry
-
-    lax.fori_loop(0, ROWS // step, tile, 0)
-    l_ref[...] = stat_ref[...].T[0:8, :]
-
-
-def attention_forward(x, near, far, biases, head_block, at, tables, step=STEP):
+    stats = jnp.zeros((ROWS, 128), F32)
+    for pair in range(2):
+        cols = slice(pair * 128, pair * 128 + 128)
+        q_pair = q_ref[:, cols]
+        k_pair, v_pair = k_ref[0:KEYS, cols], v_ref[0:KEYS, cols]
+        k_class = k_ref[KEYS : KEYS + 16, cols].astype(F32)[0:1]
+        v_class = v_ref[KEYS : KEYS + 16, cols].astype(F32)[0:1]
+        product = q_pair.astype(F32) * k_class
+        outs = []
+        for h in range(2):
+            own = low_half if h == 0 else ~low_half
+            scores = dot_nt(jnp.where(own, q_pair, jnp.zeros_like(q_pair)), k_pair)
+            class_score = jnp.sum(jnp.where(own, product, 0.0), axis=1, keepdims=True)
+            peak = jnp.maximum(jnp.max(scores, axis=1, keepdims=True), class_score)
+            p = jnp.exp2(scores - peak)
+            class_p = jnp.exp2(class_score - peak)
+            total = jnp.sum(p, axis=1, keepdims=True) + class_p
+            out = dot_nn(p.astype(BF16), v_pair) + class_p * v_class
+            outs.append(out * (1.0 / total))
+            stats = jnp.where(lane == pair * 2 + h, peak + jnp.log2(total), stats)
+        o_ref[:, cols] = jnp.where(low_half, outs[0], outs[1]).astype(BF16)
+    l_ref[...] = stats.T[0:8, :]
+
+
+def attention_forward(x, near, far, biases, head_block, at, tables):
     def block(index):
         return pl.BlockSpec((HALF, HEAD_COLS), lambda j: (0, index))
 
@@ -627,7 +637,7 @@
 
     out = pl.BlockSpec((ROWS, HEAD_COLS), lambda j: (0, 0))
     return pl.pallas_call(
-        functools.partial(attention_kernel, step=step),
+        attention_kernel,
         grid=(1,),
         in_specs=[whole(x)]
         + [block(at + first) for first in (0, 0, 2, 2, 4, 4)]
@@ -635,8 +645,7 @@
         + [whole(t) for t in tables],
         out_specs=[out] * 4 + [pl.BlockSpec((8, ROWS), lambda j: (0, 0))],
         out_shape=[jax.ShapeDtypeStruct((ROWS, HEAD_COLS), BF16)] * 4 + [jax.ShapeDtypeStruct((8, ROWS), F32)],
-        scratch_shapes=[pltpu.VMEM((ROWS, 128), F32)],
-        compiler_params=pltpu.CompilerParams(vmem_limit_bytes=48 << 20),
+        compiler_params=pltpu.CompilerParams(vmem_limit_bytes=56 << 20),
         cost_estimate=cost_of(flops=7_500_000_000, bytes_accessed=7_000_000, transcendentals=4_300_000),
         name="attention_forward",
     )(x, near, far, near, far, near, far, biases, *tables)
@@ -644,7 +653,7 @@
 
 def attention_back_kernel(
     q_ref, k_ref, v_ref, g_ref, o_ref, l_ref, c_ref, s1_ref, s2_ref,
-    dq_ref, dk_ref, dv_ref, sum_ref, dq_sum, dk_sum, dv_sum, delta_ref, *, step
+    dq_ref, dk_ref, dv_ref, sum_ref, dq_turned, dk_sum, dv_sum, delta_ref, k_turned, *, step
 ):
     lane = lax.broadcasted_iota(jnp.int32, (1, 128), 1)
     low_half = lane < 64
@@ -658,31 +667,41 @@
             deltas = jnp.where(lane == pair * 2 + h, delta, deltas)
     delta_ref[...] = deltas.T[0:8, :]
     real_key = lax.broadcasted_iota(jnp.int32, (ROWS, 1), 0) <= KEYS
-    dk_sum[...] = jnp.zeros_like(dk_sum)
-    dv_sum[...] = jnp.zeros_like(dv_sum)
+    class_key = lax.broadcasted_iota(jnp.int32, (ROWS - KEYS, 1), 0) == 0
+    k_turned[...] = k_ref[...].T
     for t in range(KEYS // step):
         rows = pl.ds(t * step, step)
         for pair in range(2):
             cols = slice(pair * 128, pair * 128 + 128)
             q_pair, g_pair = q_ref[rows, cols], g_ref[rows, cols]
             k_pair, v_pair = k_ref[:, cols], v_ref[:, cols]
-            dqs, dk, dv = [], None, None
+            dk, dv = None, None
             for h in range(2):
                 own = low_half if h == 0 else ~low_half
                 head = pair * 2 + h
                 q_head = jnp.where(own, q_pair, jnp.zeros_like(q_pair))
                 g_head = jnp.where(own, g_pair, jnp.zeros_like(g_pair))
                 scores = dot_nt(k_pair, q_head)
-                p = jnp.where(real_key, jnp.exp2(scores - l_ref[head : head + 1, rows]), 0.0)
+                log_sums = l_ref[head : head + 1, rows]
+                p = jnp.concatenate(
+                    [
+                        jnp.exp2(scores[:KEYS] - log_sums),
+                        jnp.where(class_key, jnp.exp2(scores[KEYS:] - log_sums), 0.0),
+                    ],
+                    axis=0,
+                )
                 gp = dot_nt(v_pair, g_head)
                 ds = (p * (gp - delta_ref[head : head + 1, rows])).astype(BF16)
                 dv_part, dk_part = dot_nn(p.astype(BF16), g_head), dot_nn(ds, q_head)
                 dv = dv_part if dv is None else dv + dv_part
                 dk = dk_part if dk is None else dk + dk_part
-                dqs.append(dot_tn(ds, k_pair))
-            dq_sum[rows, cols] = jnp.where(low_half, dqs[0], dqs[1])
-            dk_sum[:, cols] += dk
-            dv_sum[:, cols] += dv
+                own_rows = slice(head * 64, head * 64 + 64)
+                dq_turned[own_rows, rows] = dot_nn(k_turned[own_rows, :], ds)
+            if t == 0:
+                dk_sum[:, cols], dv_sum[:, cols] = dk, dv
+            else:
+                dk_sum[:, cols] += dk
+                dv_sum[:, cols] += dv
     q_class = q_ref[KEYS : KEYS + 16, :][0:1].astype(F32)
     g_class = g_ref[KEYS : KEYS + 16, :][0:1].astype(F32)
     shape = (128, HEAD_COLS)
@@ -696,16 +715,16 @@
         delta_class = jnp.where(lane == head, delta_ref[head : head + 1, KEYS : KEYS + 1], delta_class)
     p = jnp.where(real_key & (lane < 4), jnp.exp2(scores - log_class), 0.0)
     ds = (p * (gp - delta_class)).astype(BF16)
-    dv_sum[...] += dot_nn(p.astype(BF16), g_diag)
-    dk_sum[...] += dot_nn(ds, q_diag)
+    dv = dv_sum[...] + dot_nn(p.astype(BF16), g_diag)
+    dk = dk_sum[...] + dot_nn(ds, q_diag)
     dq_class = jnp.sum(jnp.where(own, dot_tn(ds, k_ref[...]), 0.0), axis=0, keepdims=True)
     first = lax.broadcasted_iota(jnp.int32, (16, 1), 0) == 0
-    dq_sum[KEYS : KEYS + 16, :] = jnp.where(first, dq_class, 0.0)
+    dq = jnp.concatenate([dq_turned[...].T, jnp.where(first, dq_class, 0.0)], axis=0)
     c, s1, s2 = twice(c_ref[...]), twice(s1_ref[...]), twice(s2_ref[...])
-    dq = (rotate_lanes(dq_sum[...], c, -s1, -s2) * 0.125).astype(BF16)
-    dv = dv_sum[...].astype(BF16)
+    dq = (rotate_lanes(dq, c, -s1, -s2) * 0.125).astype(BF16)
+    dv = dv.astype(BF16)
     dq_ref[...] = dq
-    dk_ref[...] = (rotate_lanes(dk_sum[...], c, -s1, -s2) * (1.0 / LOG2E)).astype(BF16)
+    dk_ref[...] = (rotate_lanes(dk, c, -s1, -s2) * (1.0 / LOG2E)).astype(BF16)
     dv_ref[...] = dv
     sum_ref[0:1, :] = jnp.sum(dq.astype(F32), axis=0, keepdims=True)
     sum_ref[1:2, :] = jnp.sum(dv.astype(F32), axis=0, keepdims=True)
@@ -724,7 +743,9 @@
         out_specs=[block] * 3 + [pl.BlockSpec((8, HEAD_COLS), lambda j: (0, 0))],
         out_shape=[jax.ShapeDtypeStruct((ROWS, HEAD_COLS), BF16)] * 3
         + [jax.ShapeDtypeStruct((8, HEAD_COLS), F32)],
-        scratch_shapes=[pltpu.VMEM((ROWS, HEAD_COLS), F32)] * 3 + [pltpu.VMEM((8, ROWS), F32)],
+        scratch_shapes=[pltpu.VMEM((HEAD_COLS, KEYS), F32)]
+        + [pltpu.VMEM((ROWS, HEAD_COLS), F32)] * 2
+        + [pltpu.VMEM((8, ROWS), F32), pltpu.VMEM((HEAD_COLS, ROWS), BF16)],
         compiler_params=pltpu.CompilerParams(vmem_limit_bytes=48 << 20),
         cost_estimate=cost_of(
             flops=13_000_000_000, bytes_accessed=5_000_000, transcendentals=4_300_000
@@ -733,8 +754,14 @@
     )(q, k, v, g, o, log_sums, *tables)
 
 
-def over_rows(kernel, name, tiled, held, outs, sums=(), flops=0, step=STEP):
-    in_specs = [pl.BlockSpec((step, a.shape[1]), lambda i: (i, 0)) for a in tiled]
+def over_rows(kernel, name, tiled, held, outs, sums=(), flops=0, step=STEP, only=None):
+    rows = ROWS if only is None else step
+    if only is None:
+        in_specs = [pl.BlockSpec((step, a.shape[1]), lambda i: (i, 0)) for a in tiled]
+    else:
+        in_specs = [
+            pl.BlockSpec((pl.Element(step), pl.Element(a.shape[1])), lambda i: (only, 0)) for a in tiled
+        ]
     held = [h if isinstance(h, tuple) else (h, h.shape, 0) for h in held]
     in_specs += [
         pl.BlockSpec(shape, lambda i, column=column: (0, column), pipeline_mode=pl.Buffered(1))
@@ -743,13 +770,13 @@
     held = [h[0] for h in held]
     out_specs = [pl.BlockSpec((step, n), lambda i: (i, 0)) for n, _ in outs]
     out_specs += [pl.BlockSpec((8, n), lambda i: (0, 0)) for n in sums]
-    out_shape = [jax.ShapeDtypeStruct((ROWS, n), t) for n, t in outs]
+    out_shape = [jax.ShapeDtypeStruct((rows, n), t) for n, t in outs]
     out_shape += [jax.ShapeDtypeStruct((8, n), F32) for n in sums]
     moved = sum(a.size * a.dtype.itemsize for a in list(tiled) + list(held))
     moved += sum(s.size * s.dtype.itemsize for s in out_shape)
     return pl.pallas_call(
         kernel,
-        grid=(ROWS // step,),
+        grid=(rows // step,),
         in_specs=in_specs,
         out_specs=out_specs,
         out_shape=out_shape,
@@ -923,59 +950,76 @@
     add_sums(sum_ref, g_one * unit, g_one)
 
 
-def weight_grads(pairs, tile=HEAD_COLS):
-    sources = []
-    for x, _ in pairs:
+def weight_grads(half, steps, received=None):
+    sources, arrays = [], []
+    for x, gs in steps:
         if not any(x is s for s in sources):
             sources.append(x)
-    starts, count = [], 0
-    for x, g in pairs:
-        starts.append(count)
-        count += g.shape[1] // tile
-    ends = starts[1:] + [count]
+        for g, _, _ in gs:
+            if not any(g is a for a in arrays):
+                arrays.append(g)
+    tile = sum(width for _, width, _ in steps[0][1])
+    refs_of, specs, operands = [], [], []
+    for j, (x, gs) in enumerate(steps):
+        mine = []
+        for g, width, at in gs:
+            found = next((i for i, o in enumerate(operands) if o[0] is g and o[1] == width), None)
+            if found is None:
+                operands.append((g, width, {}))
+                found = len(operands) - 1
+            operands[found][2][j] = at
+            mine.append(found)
+        refs_of.append(mine)
+    for g, width, places in operands:
+        known = sorted(places.items())
+
+        def index(j, known=known):
+            at = known[0][1]
+            for step, place in known[1:]:
+                at = jnp.where(j >= step, place, at)
+            return 0, at
+
+        specs.append(pl.BlockSpec((ROWS, width), index))
+    plus = [] if received is None else [received]
 
     def kernel(*refs):
-        xs, gs = refs[: len(sources)], refs[len(sources) : len(sources) + len(pairs)]
-        near_ref, far_ref, turned, last = refs[len(sources) + len(pairs) :]
-        j = pl.program_id(0)
-        for s, x in enumerate(sources):
-            begin = min(a for a, (px, _) in zip(starts, pairs) if px is x)
-
-            @pl.when(j == begin)
-            def _(s=s):
-                turned[...] = xs[s][0:KEYS, :].T
-                last[...] = xs[s][KEYS : KEYS + 16, :].astype(F32).T
-
-        for i in range(len(pairs)):
-
-            @pl.when((j >= starts[i]) & (j < ends[i]))
-            def _(i=i):
-                main = dot_nn(turned[...], gs[i][0:KEYS, :])
-                row = gs[i][KEYS : KEYS + 16, :].astype(F32)[0:1]
-                out = (main + last[:, 0:1] * row).astype(BF16)
-                near_ref[...] = out[:HALF]
-                far_ref[...] = out[HALF:]
-
-    def g_spec(i):
-        blocks = ends[i] - starts[i]
-        return pl.BlockSpec((ROWS, tile), lambda j: (0, jnp.clip(j - starts[i], 0, blocks - 1)))
-
-    out = pl.BlockSpec((HALF, tile), lambda j: (0, j))
-    columns = count * tile
+        xs, gs = refs[: len(sources)], refs[len(sources) : len(sources) + len(operands)]
+        out_ref, turned, last = refs[-3:]
+        step = pl.program_id(0)
+        for j, (x, _) in enumerate(steps):
+            source = next(i for i, s in enumerate(sources) if s is x)
+            fresh = j == 0 or steps[j - 1][0] is not x
+
+            @pl.when(step == j)
+            def _(j=j, source=source, fresh=fresh):
+                if fresh:
+                    turned[...] = xs[source][0:KEYS, :].T
+                    last[...] = xs[source][KEYS:ROWS, :].astype(F32).T
+                parts = [gs[r] for r in refs_of[j]]
+                main = jnp.concatenate([p[0:KEYS, :] for p in parts], axis=1)
+                row = jnp.concatenate([p[KEYS:ROWS, :].astype(F32)[0:1] for p in parts], axis=1)
+                out = dot_nn(turned[...], main) + last[:, 0:1] * row
+                if plus:
+                    out = out + refs[len(sources) + len(operands)][...].astype(F32)
+                out_ref[...] = out.astype(BF16)
+
+    block = pl.BlockSpec((HALF, tile), lambda j: (0, j))
+    columns = len(steps) * tile
     return pl.pallas_call(
         kernel,
-        grid=(count,),
-        in_specs=[pl.BlockSpec((ROWS, WIDTH), lambda j: (0, 0), pipeline_mode=pl.Buffered(1)) for _ in sources]
-        + [g_spec(i) for i in range(len(pairs))],
-        out_specs=[out, out],
-        out_shape=[jax.ShapeDtypeStruct((HALF, columns), BF16)] * 2,
-        scratch_shapes=[pltpu.VMEM((WIDTH, KEYS), BF16), pltpu.VMEM((WIDTH, 16), F32)],
+        grid=(len(steps),),
+        in_specs=[pl.BlockSpec((ROWS, HALF), lambda j: (0, half), pipeline_mode=pl.Buffered(1)) for _ in sources]
+        + specs
+        + [block] * len(plus),
+        out_specs=block,
+        out_shape=jax.ShapeDtypeStruct((HALF, columns), BF16),
+        scratch_shapes=[pltpu.VMEM((HALF, KEYS), BF16), pltpu.VMEM((HALF, ROWS - KEYS), F32)],
         compiler_params=pltpu.CompilerParams(vmem_limit_bytes=48 << 20),
         cost_estimate=cost_of(
-            flops=2 * ROWS * WIDTH * columns, bytes_accessed=4 * ROWS * columns, transcendentals=0
+            flops=ROWS * WIDTH * columns, bytes_accessed=3 * ROWS * columns, transcendentals=0
         ),
         name="weight_grads",
-    )(*sources, *[g for _, g in pairs])
+    )(*sources, *[g for g, _, _ in operands], *plus)
 
 
 def pair_tables(coords):
@@ -1007,6 +1051,7 @@
     patch_in, cls_in, d_patch, d_cls, image_valid, patch_coords,
     w_query, w_key, w_value, w_gate, w_up, w_out, w_down, layer_vectors, ffn_vectors,
 ):
+    SENT.clear()
     me, pos = lax.axis_index(BOTH), lax.axis_index("ctx")
     hidden = w_gate.shape[1]
     wide = (hidden + 255) // 256 * 256
@@ -1019,8 +1064,8 @@
         class_row = lax.dynamic_index_in_dim(classes, pos, 0)
         return joined(near, far, jnp.pad(class_row, ((0, ROWS - KEYS - 1), (0, 0)))), far
 
-    def to_pair(rows):
-        near, far = rows[:512], swap_over(rows[512:], BIT_X)
+    def to_pair(rows, far):
+        near = rows[:512]
         is_first = pos == 0
         near_class, far_class = rows[KEYS], far[512]
         patches = jnp.where(is_first, jnp.stack([near, far[:512]]), jnp.stack([far[:512], near]))
@@ -1052,52 +1097,52 @@
     corner_low = g_low.corners(image_far)
     z_one = g_gate.along_z0(z_high)
     xy_high = g_high.along_xy(xy_low)
-    near_low = g_low.whole()
-    z_gate = g_gate.along_z1()
-
-    gate = near_low, g_low.far, image_rows, z_high, z_one
-    z_up = g_up.along_z0(gate)
+    near_low = g_low.whole(z_high)
+
+    gate = near_low, g_low.far, image_rows, z_one
+    z_gate = g_gate.along_z1(gate)
     vectors, head_biases = gathered_vectors(near_low, g_low.far, order)
     tokens, normed = over_rows(
-        start_kernel, "start", [after(image_rows, gate)], [order, vectors], [(WIDTH, BF16), (WIDTH, BF16)],
+        start_kernel, "start", [ready(image_rows, gate)], [order, vectors], [(WIDTH, BF16), (WIDTH, BF16)],
         flops=2_200_000_000,
     )
 
     def attend(block, gate):
         group = g_low if block < 2 else g_high
         return attention_forward(
-            after(normed, gate), group.near, group.far, head_biases, block, block % 2, tables
+            ready(normed, gate), group.near, group.far, head_biases, block, block % 2, tables
         )
 
-    gate = normed, xy_high, z_gate, z_up
+    gate = normed, xy_high, z_gate
+    z_up = g_up.along_z0(gate)
     corner_high = g_high.corners(gate)
     xy_gate = g_gate.along_xy(gate)
-    z_up = g_up.along_z1(gate)
     heads = [attend(0, gate)]
 
     gate = heads[0][3], corner_high, xy_gate, z_up
     near_high = g_high.whole(gate)
     corner_gate = g_gate.corners(gate)
+    z_up = g_up.along_z1(gate)
+    heads.append(attend(1, gate))
+
+    gate = heads[1][3], g_high.far, corner_gate, z_up
+    near_gate = g_gate.whole(gate)
     xy_up = g_up.along_xy(gate)
     z_down = g_down.along_z0(gate)
-    heads.append(attend(1, gate))
-
-    gate = heads[1][3], g_high.far, corner_gate, z_down
-    near_gate = g_gate.whole(gate)
-    z_down = g_down.along_z1(gate)
     heads.append(attend(2, gate))
 
     gate = heads[2][3], xy_up, g_gate.far, z_down
     corner_up = g_up.corners(gate)
+    z_down = g_down.along_z1(gate)
+    heads.append(attend(3, gate))
+
+    gate = heads[3][3], corner_up, z_down
+    near_up = g_up.whole(gate)
     xy_down = g_down.along_xy(gate)
-    heads.append(attend(3, gate))
-
-    gate = heads[3][3], corner_up
-    near_up = g_up.whole(gate)
     out_w = [((w, (HALF, HALF), 3 + i)) for w in (near_high, g_high.far) for i in range(2)]
     attended = [h[3] for h in heads]
     middle, normed_two = over_rows(
-        middle_kernel, "middle", attended + [after(tokens, gate)], out_w + [vectors],
+        middle_kernel, "middle", attended + [ready(tokens, gate)], out_w + [vectors],
         [(WIDTH, BF16), (WIDTH, BF16)], flops=2_200_000_000, step=520,
     )
 
@@ -1106,107 +1151,141 @@
     grad_image_rows, grad_far = own_image(d_patch, d_cls, gate)
     gate_up = [near_gate, g_gate.far, near_up, g_up.far]
     gate_act, up_act, inner, stats = over_rows(
-        functools.partial(hidden_kernel, hidden=hidden), "hidden", [after(normed_two, gate)],
+        functools.partial(hidden_kernel, hidden=hidden), "hidden", [ready(normed_two, gate)],
         gate_up + [ffn], [(wide, BF16), (wide, BF16), (wide, BF16), (128, F32)], flops=12_000_000_000,
     )
 
     gate = inner, corner_down, grad_far
     near_down = g_down.whole(gate)
     down_w = [near_down, g_down.far]
-
+    (out_rows,) = over_rows(
+        result_kernel, "result", [inner, ready(middle, gate)], down_w + [vectors, order, keep],
+        [(WIDTH, BF16)], flops=8_000_000_000, step=520,
+    )
+
+    gate = out_rows
+    far_rows = swap_over(after(out_rows, gate)[HALF:], BIT_X)
     branch, d_gate, d_up, wide_sums, branch_sums = over_rows(
         functools.partial(hidden_back_kernel, hidden=hidden), "hidden_back",
-        [after(grad_image_rows, gate), gate_act, up_act, stats], [order, keep] + down_w + [ffn],
+        [ready(grad_image_rows, gate), gate_act, up_act, stats], [order, keep] + down_w + [ffn],
         [(WIDTH, BF16), (wide, BF16), (wide, BF16)], [wide, WIDTH], flops=8_000_000_000,
     )
 
-    ffn_sums = sum_over(wide_sums[:4, :hidden], BIT_CORE)
-    down_grads = weight_grads([(branch, inner)])
-    down = Scatter(*down_grads)
-
-    gate = down_grads, ffn_sums
-    down_stage = down.over_core(gate)
-    ffn_sums = sum_over(ffn_sums, BIT_X, gate)
-    (out_rows,) = over_rows(
-        result_kernel, "result", [inner, after(middle, gate)], down_w + [vectors, order, keep],
-        [(WIDTH, BF16)], flops=8_000_000_000, step=520,
-    )
-
-    gate = out_rows, down_stage, ffn_sums
-    down_stage = down.corners(gate)
-    ffn_sums = sum_over(ffn_sums, BIT_Y, gate)
-    outs = to_pair(after(out_rows, gate))
-    late = after(normed_two, gate)
-    second_grads = weight_grads([(late, d_gate), (late, d_up)])
-    second = Scatter(*second_grads)
-
-    gate = second_grads, down_stage, ffn_sums, outs
-    down_stage, second_stage = down.over_xy(gate), second.over_core(gate)
-    ffn_sums = sum_over(ffn_sums, BIT_Z0, gate)
+    gate = wide_sums, far_rows
+    outs = to_pair(out_rows, far_rows)
+    all_sums = lax.all_gather(wide_sums, BOTH)
+    part_width = wide // 2
+    down, second, low, high = Scatter(), Scatter(), Scatter(), Scatter()
+    late = ready(normed_two, gate)
+    second_steps = [(late, [(g, part_width, i)]) for g in (d_gate, d_up) for i in range(2)]
+    second_far = weight_grads(1, second_steps)
+
+    gate = second_far
+    second_stage = second.over_core(second_far, gate)
+    late = ready(branch, gate)
+    down_steps = [(late, [(inner, part_width, i)]) for i in range(2)]
+    down_far = weight_grads(1, down_steps)
+
+    gate = down_far, second_stage
+    down_stage = down.over_core(down_far, gate)
+    late = ready(normed_two, gate)
+    second_total = weight_grads(0, [(late, gs) for _, gs in second_steps], second_stage)
+
+    gate = second_total, down_stage
+    second_stage = second.corners(second_total, gate)
+    late = ready(branch, gate)
+    down_total = weight_grads(0, [(late, gs) for _, gs in down_steps], down_stage)
+
+    gate = down_total, second_stage
+    second_stage = second.sides(gate)
     att_low, *att_grads, middle_sums = over_rows(
-        middle_back_kernel, "middle_back", [d_gate, d_up, branch, after(middle, gate)],
+        middle_back_kernel, "middle_back", [d_gate, d_up, branch, ready(middle, gate)],
         gate_up + out_w + [vectors], [(WIDTH, BF16)] + [(HEAD_COLS, BF16)] * 4, [WIDTH],
         flops=14_000_000_000, step=520,
     )
 
     def attend_back(block, gate):
-        return attention_backward(*heads[block], after(att_grads[block], gate), tables)
-
-    gate = att_low, down_stage, second_stage, ffn_sums
-    down_stage, second_stage = down.along_z1(gate), second.corners(gate)
-    ffn_grads = sum_over(ffn_sums, BIT_Z1, gate)
+        return attention_backward(*heads[block], ready(att_grads[block], gate), tables)
+
+    gate = att_low, second_stage
+    second_stage, down_stage = second.along_z1(gate), down.corners(down_total, gate)
     parts = [attend_back(0, gate)]
 
-    gate = parts[0][0], down_stage, second_stage, ffn_grads
-    down_grad, second_stage = down.along_z0(gate), second.over_xy(gate)
+    gate = parts[0][0], second_stage, down_stage
+    gate_up_grad, down_stage = second.along_z0(gate), down.sides(gate)
     parts.append(attend_back(1, gate))
 
-    gate = parts[1][0], down_grad
+    def pieces(*arrays):
+        return [(a, HEAD_COLS, 0) for a in arrays]
+
+    gate = parts[1][0], gate_up_grad, down_stage
+    down_stage = down.along_z1(gate)
+    late, late_two = ready((att_low, normed), gate)
+    grads = [g for part in parts for g in part[:3]]
+    low_steps = [(late, pieces(*attended[2 * i : 2 * i + 2])) for i in range(2)]
+    low_steps += [(late_two, pieces(*grads[2 * i : 2 * i + 2])) for i in range(3)]
+    low_far = weight_grads(1, low_steps)
+
+    gate = low_far, down_stage
+    low_stage, down_grad = low.over_core(low_far, gate), down.along_z0(gate)
     parts.append(attend_back(2, gate))
 
-    gate = parts[2][0], second_stage
-    second_stage = second.along_z1(gate)
-    late, late_two = after(att_low, gate), after(normed, gate)
-    low_grads = weight_grads(
-        [(late, a) for a in attended] + [(late_two, g) for part in parts for g in part[:3]]
-    )
-    low = Scatter(*low_grads)
-
-    gate = low_grads
-    low_stage = low.over_core(gate)
+    gate = parts[2][0], low_stage, down_grad
+    late, late_two = ready((att_low, normed), gate)
+    low_total = weight_grads(
+        0, [(late if i < 2 else late_two, gs) for i, (_, gs) in enumerate(low_steps)], low_stage
+    )
+
+    gate = low_total
+    low_stage = low.corner(low_total, gate)
     parts.append(attend_back(3, gate))
 
-    gate = parts[3][0], low_stage, second_stage
-    low_stage = low.corners(gate)
-    gate_up_grad = second.along_z0(gate)
-    late = after(normed, gate)
-    high_grads = weight_grads([(late, g) for g in parts[3][:3]])
-    high = Scatter(*high_grads)
-
-    gate = high_grads, low_stage
-    low_stage, high_stage = low.over_xy(gate), high.over_core(gate)
-    grad_rows, first_sums = over_rows(
-        last_kernel, "last",
-        [g for part in parts for g in part[:3]] + [after(att_low, gate), tokens],
-        [(near_low, (HALF, 3 * HALF), 0), (g_low.far, (HALF, 3 * HALF), 0)]
-        + [(near_high, (HALF, 3 * HALF), 0), (g_high.far, (HALF, 3 * HALF), 0), vectors, order],
-        [(WIDTH, BF16)], [WIDTH], flops=9_000_000_000, step=520,
-    )
-    high.corners(grad_rows)
-    low.along_z1(grad_rows)
-    patch_grad, cls_grad = to_pair(grad_rows)
-    high.over_xy()
+    gate = parts[3][0], low_stage
+    low_stage = low.sides(gate)
+    late = ready(normed, gate)
+    grads = [g for part in parts[2:] for g in part[:3]]
+    high_steps = [(late, pieces(*grads[2 * i : 2 * i + 2])) for i in range(3)]
+    high_far = weight_grads(1, high_steps)
+    high_stage = high.over_core(high_far)
+
+    def last_rows(gate, first, count):
+        return over_rows(
+            last_kernel, "last",
+            [g for part in parts for g in part[:3]] + [ready(att_low, gate), tokens],
+            [(near_low, (HALF, 3 * HALF), 0), (g_low.far, (HALF, 3 * HALF), 0)]
+            + [(near_high, (HALF, 3 * HALF), 0), (g_high.far, (HALF, 3 * HALF), 0), vectors, order],
+            [(WIDTH, BF16)], [WIDTH], flops=4_500_000_000, step=count, only=first,
+        )
+
+    far_part, far_sums = last_rows(high_far, HALF, ROWS - HALF)
+
+    gate = far_part, high_stage, low_stage
+    low_stage = low.along_z1(gate)
+    late = ready(normed, gate)
+    high_total = weight_grads(0, [(late, gs) for _, gs in high_steps], high_stage)
+
+    gate = high_total
+    high.total = high_total
+    high_stage = high.over_x(gate)
+    near_part, near_sums = last_rows(gate, 0, HALF)
+
+    gate = near_part, low_stage, high_stage
+    far_rows = swap_over(after(far_part, gate), BIT_X)
+    high.over_y(gate)
+    low_grad = low.along_z0(gate)
+    first_sums = far_sums + after(near_sums, gate)
     high.along_z1()
-    low_grad = low.along_z0()
     high_grad = high.along_z0()
+    patch_grad, cls_grad = to_pair(joined(near_part, far_part), far_rows)
+    ffn_grads = jnp.sum(after(all_sums, parts[1][0]), axis=0)[:4, :hidden]
     head_sums = jnp.dot(
         joined(*[part[3][:2] for part in parts], axis=1), order.astype(F32), precision=lax.Precision.HIGHEST
     )
     vector_grads = scatter_small(
         joined(first_sums[:2], head_sums, middle_sums[:3], branch_sums[:1]).T
     )
-    blocks = [low_grad[:, WIDTH + i * HEAD_COLS :][:, :HEAD_COLS] for i in range(9)]
-    blocks += [high_grad[:, i * HEAD_COLS :][:, :HEAD_COLS] for i in range(3)]
+    blocks = [low_grad[:, WIDTH + i * HEAD_COLS :][:, :HEAD_COLS] for i in range(6)]
+    blocks += [high_grad[:, i * HEAD_COLS :][:, :HEAD_COLS] for i in range(6)]
     query_grad, key_grad, value_grad = (joined(*blocks[i::3], axis=1) for i in range(3))
     return (
         outs[0],

time: 651 us -> 616 us (0.946)
  waiting for transfers between devices: 192 us -> 159 us
  between operations: 3.98 us -> 16.9 us
  other arithmetic: 40 us -> 29.9 us
    ppermute x78 -> x70, waiting for transfers between devices: 192 us -> 159 us  [swap_over(): return lax.ppermute(value, BOTH, [(i, i ^ bit) for i in range(count)])]
    convert_element_type x16 -> x12, other arithmetic: 15.5 us -> 7.6 us  [rounded_sum(): return total.astype(BF16)]
    pallas_call x4, Pallas kernels: 56.9 us -> 49.9 us  [attention_backward(): pl.pallas_call(functools.partial(attention_back_kernel, step=step), grid=...]
    pallas_call x15 -> x20, Pallas kernels: 236 us -> 240 us  [the longest x8 131 us: over_rows(): pl.pallas_call(kernel, grid=(rows // step,), in_specs=in_specs, out_specs...]
    ppermute x78 -> x70, starting transfers between devices: 70.5 us -> 69.5 us  [swap_over(): return lax.ppermute(value, BOTH, [(i, i ^ bit) for i in range(count)])]
  transfers between devices with their start and end apart: 78 -> 71, of which waited for: 36 -> 35; matrix products, arithmetic and copies ran while one was open for 6% -> 9% of each run, Pallas kernels for 39% -> 44%
where the time goes in v3:
time: 616 us; the launch traced here: 610 us
  Pallas kernels  299 us (49%)
  waiting for transfers between devices  159 us (26%)
  starting transfers between devices  69.6 us (11%)
  local copies, waits for them, and re-layouts  34.3 us (6%)
  other arithmetic  29.9 us (5%)
  between operations  16.9 us (3%)
    ppermute x70, waiting for transfers between devices, swap_over(): return lax.ppermute(value, BOTH, [(i, i ^ bit) for i in range(count)])  159 us
    pallas_call x8, Pallas kernels, over_rows(): pl.pallas_call(kernel, grid=(rows // step,), in_specs=in_specs, out_specs...  131 us
    ppermute x70, starting transfers between devices, swap_over(): return lax.ppermute(value, BOTH, [(i, i ^ bit) for i in range(count)])  69.5 us
    pallas_call x8, Pallas kernels, weight_grads(): pl.pallas_call(kernel, grid=(len(steps),), in_specs=[pl.BlockSpec((ROWS,...  59.7 us
    pallas_call x4, Pallas kernels, attention_backward(): pl.pallas_call(functools.partial(attention_back_kernel, step=step), grid=...  49.9 us
    pallas_call x4, Pallas kernels, attention_forward(): pl.pallas_call(attention_kernel, grid=(1,), in_specs=[whole(x)] + [block(...  49.2 us
  transfers between devices with their start and end apart: 71, of which 35 were waited for; matrix products, arithmetic and copies ran while one was open for 9% of the time, Pallas kernels for 44%

profile of v3, /device:TPU:0, one launch (start us, length us, event | category | flops | bytes accessed | tf_op | source)
XLA Modules:
  0.0 610.2 jit_solution(12218742771394052466)
XLA Ops:
  7.3 3.0 collective-permute-start.14
  12.7 2.7 collective-permute-start.1
  15.4 2.7 dynamic-slice_bitcast_fusion.3
  18.8 2.2 fusion.59.order_ref.refs_19_
  23.4 1.9 collective-permute-start.7
  25.4 5.0 collective-permute-done.2
  33.8 4.8 collective-permute-done.4.refs_1_
  38.6 13.0 %collective-permute-done.3.refs_2_ = bf16[128,1664]{1,0:T(8,128)(2,1)S(1)} collective-permute-done((bf16[128,1664]{1,0:T(8,128)(2,1)S(1)}, bf16[128,1664]{1,0:T(8,128)(2,1)S(1)}, u32[]{:S(2)}, u32[]{:S(2)}) %collective-permute-start.3) | collective-permute-done | bytes 426016 | tf_op jit(solution)/shard_map/ppermute | solution.py:436
  54.1 3.4 collective-permute-done.6.refs_4_
  59.3 2.8 fusion.34
  65.0 9.6 %collective-permute-done.10 = bf16[32,2816]{1,0:T(8,128)(2,1)S(1)} collective-permute-done((bf16[32,2816]{1,0:T(8,128)(2,1)S(1)}, bf16[32,2816]{1,0:T(8,128)(2,1)S(1)}, u32[]{:S(2)}, u32[]{:S(2)}) %collective-permute-start.10) | collective-permute-done | bytes 180256 | tf_op jit(solution)/shard_map/ppermute | solution.py:436
  77.4 3.0 vectors.1
  80.5 8.0 %start.1 = (bf16[1040,1024]{1,0:T(8,128)(2,1)}, bf16[1040,1024]{1,0:T(8,128)(2,1)}) custom-call(bf16[1040,1024]{1,0:T(8,128)(2,1)} %fusion.32.rows_ref, bf16[1024,1024]{1,0:T(8,128)(2,1)} %fusion.59.order_ref.refs_19_, f32[8,1024]{1,0:T(8,128)} %get-tuple-element.183.vec_ref.refs_18_), custom_call_target="tpu_custom_call" | custom-call | flops 8800000000 | bytes 34078720 | tf_op jit(solution)/shard_map/start/pallas_call | solution.py:777
  89.7 1.8 collective-permute-start.19
  94.7 11.7 %attention_forward.4 = (bf16[1040,256]{1,0:T(8,128)(2,1)}, bf16[1040,256]{1,0:T(8,128)(2,1)}, bf16[1040,256]{1,0:T(8,128)(2,1)}, bf16[1040,256]{1,0:T(8,128)(2,1)}, f32[8,1040]{1,0:T(8,128)}) custom-call(bf16[1040,1024]{1,0:T(8,128)(2,1)} %get-tuple-element.313.x_ref.refs_1_.refs_0_, bf16[512,1664]{1,0:T(8,128)(2,1)} %copy-done.2, ...), custom_call_target="tpu_custom_call" | custom-call | flops 30000001024 | bytes 28000000 | tf_op jit(solution)/shard_map/attention_forward/pallas_call | solution.py:639
  106.4 7.0 %collective-permute-done.16.refs_4_ = bf16[64,2560]{1,0:T(8,128)(2,1)S(1)} collective-permute-done((bf16[64,2560]{1,0:T(8,128)(2,1)S(1)}, bf16[64,2560]{1,0:T(8,128)(2,1)S(1)}, u32[]{:S(2)}, u32[]{:S(2)}) %collective-permute-start.16) | collective-permute-done | bytes 327712 | tf_op jit(solution)/shard_map/ppermute | solution.py:436
  117.6 2.4 pack_rows.6.qn_ref.kn_ref.vn_ref.na_ref.nb_ref.refs_16_
  120.1 12.6 %attention_forward.5 = (bf16[1040,256]{1,0:T(8,128)(2,1)}, bf16[1040,256]{1,0:T(8,128)(2,1)}, bf16[1040,256]{1,0:T(8,128)(2,1)}, bf16[1040,256]{1,0:T(8,128)(2,1)}, f32[8,1040]{1,0:T(8,128)}) custom-call(bf16[1040,1024]{1,0:T(8,128)(2,1)} %get-tuple-element.313.x_ref.refs_1_.refs_0_, bf16[512,1664]{1,0:T(8,128)(2,1)} %copy-done.2, ...), custom_call_target="tpu_custom_call" | custom-call | flops 30000001024 | bytes 28000000 | tf_op jit(solution)/shard_map/attention_forward/pallas_call | solution.py:639
  139.9 12.7 %attention_forward.6 = (bf16[1040,256]{1,0:T(8,128)(2,1)}, bf16[1040,256]{1,0:T(8,128)(2,1)}, bf16[1040,256]{1,0:T(8,128)(2,1)}, bf16[1040,256]{1,0:T(8,128)(2,1)}, f32[8,1040]{1,0:T(8,128)}) custom-call(bf16[1040,1024]{1,0:T(8,128)(2,1)} %get-tuple-element.313.x_ref.refs_1_.refs_0_, bf16[512,2560]{1,0:T(8,128)(2,1)} %copy-done.6, ...), custom_call_target="tpu_custom_call" | custom-call | flops 30000001024 | bytes 28000000 | tf_op jit(solution)/shard_map/attention_forward/pallas_call | solution.py:639
  156.9 12.2 %attention_forward.7 = (bf16[1040,256]{1,0:T(8,128)(2,1)}, bf16[1040,256]{1,0:T(8,128)(2,1)}, bf16[1040,256]{1,0:T(8,128)(2,1)}, bf16[1040,256]{1,0:T(8,128)(2,1)}, f32[8,1040]{1,0:T(8,128)}) custom-call(bf16[1040,1024]{1,0:T(8,128)(2,1)} %get-tuple-element.313.x_ref.refs_1_.refs_0_, bf16[512,2560]{1,0:T(8,128)(2,1)} %copy-done.6, ...), custom_call_target="tpu_custom_call" | custom-call | flops 30000001024 | bytes 28000000 | tf_op jit(solution)/shard_map/attention_forward/pallas_call | solution.py:639
  174.8 7.3 %middle.1 = (bf16[1040,1024]{1,0:T(8,128)(2,1)}, bf16[1040,1024]{1,0:T(8,128)(2,1)}) custom-call(bf16[1040,256]{1,0:T(8,128)(2,1)} %get-tuple-element.189.a0_ref.o_ref.refs_2_, bf16[1040,256]{1,0:T(8,128)(2,1)} %get-tuple-element.195.a1_ref.o_ref.refs_3_, bf16[1040,256]{1,0:T(8,128)(2,1)} %get-tuple-element.205.a2_ref.refs_4_.o_ref, ...), custom_call_target="tpu_custom_call" | custom-call | flops 8800000000 | bytes 76152832 | tf_op jit(solution)/shard_map/middle/pallas_call | solution.py:777
  182.1 9.1 %collective-permute-done.33.refs_1_ = bf16[128,2816]{1,0:T(8,128)(2,1)S(1)} collective-permute-done((bf16[128,2816]{1,0:T(8,128)(2,1)S(1)}, bf16[128,2816]{1,0:T(8,128)(2,1)S(1)}, u32[]{:S(2)}, u32[]{:S(2)}) %collective-permute-start.33) | collective-permute-done | bytes 720928 | tf_op jit(solution)/shard_map/ppermute | solution.py:436
  195.2 22.5 %hidden.1 = (bf16[1040,2816]{1,0:T(8,128)(2,1)}, bf16[1040,2816]{1,0:T(8,128)(2,1)}, bf16[1040,2816]{1,0:T(8,128)(2,1)}, f32[1040,128]{1,0:T(8,128)}) custom-call(bf16[1040,1024]{1,0:T(8,128)(2,1)} %get-tuple-element.254.x_ref.refs_0_, bf16[512,2816]{1,0:T(8,128)(2,1)} %copy-done.3, bf16[512,2816]{1,0:T(8,128)(2,1)} %collective-permute-done.26.gf_ref, ...), custom_call_target="tpu_custom_call" | custom-call | flops 48000000000 | bytes 127434752 | tf_op jit(solution)/shard_map/hidden/pallas_call | solution.py:777
  217.7 7.0 %collective-permute-done.36 = bf16[512,1024]{1,0:T(8,128)(2,1)S(1)} collective-permute-done((bf16[512,1024]{1,0:T(8,128)(2,1)S(1)}, bf16[512,1024]{1,0:T(8,128)(2,1)S(1)}, u32[]{:S(2)}, u32[]{:S(2)}) %collective-permute-start.36) | collective-permute-done | bytes 1048608 | tf_op jit(solution)/shard_map/ppermute | solution.py:436
  228.4 2.3 collective-permute-done.37.far_ref
  232.9 14.5 %result.1 = bf16[1040,1024]{1,0:T(8,128)(2,1)} custom-call(bf16[1040,2816]{1,0:T(8,128)(2,1)} %get-tuple-element.228.inner_ref.refs_1_, bf16[1040,1024]{1,0:T(8,128)(2,1)} %get-tuple-element.258.middle_ref, bf16[512,2816]{1,0:T(8,128)(2,1)} %copy-done.5, bf16[512,2816]{1,0:T(8,128)(2,1)} %copy-done.99, f32[8,1024]{1,0:T(8,128)} %get-tuple-element.183.vec_ref.refs_18_, ...), custom_call_target="tpu_custom_call" | custom-call | flops 32000000000 | bytes 72073216 | tf_op jit(solution)/shard_map/result/pallas_call | solution.py:777
  250.0 29.6 %hidden_back.1 = (bf16[1040,1024]{1,0:T(8,128)(2,1)}, bf16[1040,2816]{1,0:T(8,128)(2,1)}, bf16[1040,2816]{1,0:T(8,128)(2,1)}, f32[8,2816]{1,0:T(8,128)}, f32[8,1024]{1,0:T(8,128)}) custom-call(bf16[1040,1024]{1,0:T(8,128)(2,1)} %fusion.33.d_ref, bf16[1040,2816]{1,0:T(8,128)(2,1)} %get-tuple-element.244.gate_ref, ...), custom_call_target="tpu_custom_call" | custom-call | flops 32000000000 | bytes 145211392 | tf_op jit(solution)/shard_map/hidden_back/pallas_call | solution.py:777
  280.6 12.2 %weight_grads.8 = bf16[512,5632]{1,0:T(8,128)(2,1)} custom-call(bf16[1040,1024]{1,0:T(8,128)(2,1)S(1)} %copy-done.14, bf16[1040,2816]{1,0:T(8,128)(2,1)} %get-tuple-element.247.refs_1_.dgate_ref, bf16[1040,2816]{1,0:T(8,128)(2,1)} %get-tuple-element.248.refs_2_.dup_ref), custom_call_target="tpu_custom_call" | custom-call | flops 23991418880 | bytes 70287360 | tf_op jit(solution)/shard_map/weight_grads/pallas_call | solution.py:1008
  292.9 5.8 weight_grads.9
  298.7 3.9 collective-permute-done.39.refs_3_
  305.4 2.3 slice_bitcast_fusion.2
  309.4 12.9 %weight_grads.10 = bf16[512,5632]{1,0:T(8,128)(2,1)} custom-call(bf16[1040,1024]{1,0:T(8,128)(2,1)S(1)} %copy-done.15, bf16[1040,2816]{1,0:T(8,128)(2,1)} %get-tuple-element.247.refs_1_.dgate_ref, bf16[1040,2816]{1,0:T(8,128)(2,1)} %get-tuple-element.248.refs_2_.dup_ref, bf16[512,5632]{1,0:T(8,128)(2,1)} %collective-permute-done.39.refs_3_), custom_call_target="tpu_custom_call" | custom-call | flops 23991418880 | bytes 70287360 | tf_op jit(solution)/shard_map/weight_grads/pallas_call | solution.py:1008
  322.2 2.1 fusion.60
  325.9 6.8 %weight_grads.11 = bf16[512,2816]{1,0:T(8,128)(2,1)S(1)} custom-call(bf16[1040,1024]{1,0:T(8,128)(2,1)S(1)} %copy-done.17, bf16[1040,2816]{1,0:T(8,128)(2,1)} %get-tuple-element.228.inner_ref.refs_1_, bf16[512,2816]{1,0:T(8,128)(2,1)} %collective-permute-done.40.refs_2_), custom_call_target="tpu_custom_call" | custom-call | flops 11995709440 | bytes 35143680 | tf_op jit(solution)/shard_map/weight_grads/pallas_call | solution.py:1008
  332.7 12.7 %collective-permute-done.42 = bf16[64,5632]{1,0:T(8,128)(2,1)S(1)} collective-permute-done((bf16[64,5632]{1,0:T(8,128)(2,1)S(1)}, bf16[64,5632]{1,0:T(8,128)(2,1)S(1)}, u32[]{:S(2)}, u32[]{:S(2)}) %collective-permute-start.42) | collective-permute-done | bytes 720928 | tf_op jit(solution)/shard_map/ppermute | solution.py:436
  348.7 26.4 %middle_back.1 = (bf16[1040,1024]{1,0:T(8,128)(2,1)}, bf16[1040,256]{1,0:T(8,128)(2,1)}, bf16[1040,256]{1,0:T(8,128)(2,1)}, bf16[1040,256]{1,0:T(8,128)(2,1)}, b...) custom-call(bf16[1040,2816]{1,0:T(8,128)(2,1)} %get-tuple-element.247.refs_1_.dgate_ref, ...), custom_call_target="tpu_custom_call" | custom-call | flops 56000000000 | bytes 169279488 | tf_op jit(solution)/shard_map/middle_back/pallas_call | solution.py:777
  376.6 6.5 %collective-permute-done.43 = bf16[128,5632]{1,0:T(8,128)(2,1)S(1)} collective-permute-done((bf16[128,5632]{1,0:T(8,128)(2,1)S(1)}, bf16[128,5632]{1,0:T(8,128)(2,1)S(1)}, u32[]{:S(2)}, u32[]{:S(2)}) %collective-permute-start.43) | collective-permute-done | bytes 1441824 | tf_op jit(solution)/shard_map/ppermute | solution.py:436
  383.1 2.3 add_convert_fusion
  387.7 12.7 %attention_backward.4 = (bf16[1040,256]{1,0:T(8,128)(2,1)S(1)}, bf16[1040,256]{1,0:T(8,128)(2,1)S(1)}, bf16[1040,256]{1,0:T(8,128)(2,1)S(1)}, f32[8,256]{1,0:T(8,128)S(1)}) custom-call(bf16[1040,256]{1,0:T(8,128)(2,1)S(1)} %copy-done.49, bf16[1040,256]{1,0:T(8,128)(2,1)S(1)} %copy-done.50, bf16[1040,256]{1,0:T(8,128)(2,1)S(1)} %copy-done.51, ...), custom_call_target="tpu_custom_call" | custom-call | flops 51999997952 | bytes 20000000 | tf_op jit(solution)/shard_map/attention_backward/pallas_call | solution.py:739
  403.9 14.5 %collective-permute-done.45 = bf16[64,5632]{1,0:T(8,128)(2,1)S(1)} collective-permute-done((bf16[64,5632]{1,0:T(8,128)(2,1)S(1)}, bf16[64,5632]{1,0:T(8,128)(2,1)S(1)}, u32[]{:S(2)}, u32[]{:S(2)}) %collective-permute-start.45) | collective-permute-done | bytes 720928 | tf_op jit(solution)/shard_map/ppermute | solution.py:436
  418.6 2.4 collective-permute-start.48
  421.0 12.4 %attention_backward.5 = (bf16[1040,256]{1,0:T(8,128)(2,1)S(1)}, bf16[1040,256]{1,0:T(8,128)(2,1)S(1)}, bf16[1040,256]{1,0:T(8,128)(2,1)S(1)}, f32[8,256]{1,0:T(8,128)S(1)}) custom-call(bf16[1040,256]{1,0:T(8,128)(2,1)S(1)} %copy-done.46, bf16[1040,256]{1,0:T(8,128)(2,1)S(1)} %copy-done.47, bf16[1040,256]{1,0:T(8,128)(2,1)S(1)} %copy-done.48, ...), custom_call_target="tpu_custom_call" | custom-call | flops 51999997952 | bytes 20000000 | tf_op jit(solution)/shard_map/attention_backward/pallas_call | solution.py:739
  436.8 12.7 %collective-permute-done.49 = bf16[128,2816]{1,0:T(8,128)(2,1)S(1)} collective-permute-done((bf16[128,2816]{1,0:T(8,128)(2,1)S(1)}, bf16[128,2816]{1,0:T(8,128)(2,1)S(1)}, u32[]{:S(2)}, u32[]{:S(2)}) %collective-permute-start.49) | collective-permute-done | bytes 720928 | tf_op jit(solution)/shard_map/ppermute | solution.py:436
  450.8 1.8 collective-permute-start.51
  452.6 6.6 %weight_grads.12 = bf16[512,2560]{1,0:T(8,128)(2,1)} custom-call(bf16[1040,1024]{1,0:T(8,128)(2,1)} %get-tuple-element.314.refs_0_.refs_12_, bf16[1040,1024]{1,0:T(8,128)(2,1)} %get-tuple-element.313.x_ref.refs_1_.refs_0_, bf16[1040,256]{1,0:T(8,128)(2,1)S(1)} %copy-done.30, bf16[1040,256]{1,0:T(8,128)(2,1)S(1)} %copy-done.31, ...), custom_call_target="tpu_custom_call" | custom-call | flops 10905190400 | bytes 31948800 | tf_op jit(solution)/shard_map/weight_grads/pallas_call | solution.py:1008
  460.3 12.6 %attention_backward.6 = (bf16[1040,256]{1,0:T(8,128)(2,1)S(1)}, bf16[1040,256]{1,0:T(8,128)(2,1)S(1)}, bf16[1040,256]{1,0:T(8,128)(2,1)S(1)}, f32[8,256]{1,0:T(8,128)S(1)}) custom-call(bf16[1040,256]{1,0:T(8,128)(2,1)S(1)} %copy-done.40, bf16[1040,256]{1,0:T(8,128)(2,1)S(1)} %copy-done.41, bf16[1040,256]{1,0:T(8,128)(2,1)S(1)} %copy-done.42, ...), custom_call_target="tpu_custom_call" | custom-call | flops 51999997952 | bytes 20000000 | tf_op jit(solution)/shard_map/attention_backward/pallas_call | solution.py:739
  473.9 7.6 %weight_grads.13 = bf16[512,2560]{1,0:T(8,128)(2,1)} custom-call(bf16[1040,1024]{1,0:T(8,128)(2,1)} %get-tuple-element.314.refs_0_.refs_12_, bf16[1040,1024]{1,0:T(8,128)(2,1)} %get-tuple-element.313.x_ref.refs_1_.refs_0_, bf16[1040,256]{1,0:T(8,128)(2,1)S(1)} %copy-done.30, bf16[1040,256]{1,0:T(8,128)(2,1)S(1)} %copy-done.31, ...), custom_call_target="tpu_custom_call" | custom-call | flops 10905190400 | bytes 31948800 | tf_op jit(solution)/shard_map/weight_grads/pallas_call | solution.py:1008
  481.6 12.2 %attention_backward.7 = (bf16[1040,256]{1,0:T(8,128)(2,1)S(1)}, bf16[1040,256]{1,0:T(8,128)(2,1)S(1)}, bf16[1040,256]{1,0:T(8,128)(2,1)S(1)}, f32[8,256]{1,0:T(8,128)S(1)}) custom-call(bf16[1040,256]{1,0:T(8,128)(2,1)S(1)} %copy-done.43, bf16[1040,256]{1,0:T(8,128)(2,1)S(1)} %copy-done.44, bf16[1040,256]{1,0:T(8,128)(2,1)S(1)} %copy-done.45, ...), custom_call_target="tpu_custom_call" | custom-call | flops 51999997952 | bytes 20000000 | tf_op jit(solution)/shard_map/attention_backward/pallas_call | solution.py:739
  494.7 1.9 fusion.37
  496.6 14.6 %collective-permute-done.54 = bf16[128,2560]{1,0:T(8,128)(2,1)S(1)} collective-permute-done((bf16[128,2560]{1,0:T(8,128)(2,1)S(1)}, bf16[128,2560]{1,0:T(8,128)(2,1)S(1)}, u32[]{:S(2)}, u32[]{:S(2)}) %collective-permute-start.54) | collective-permute-done | bytes 655392 | tf_op jit(solution)/shard_map/ppermute | solution.py:436
  512.2 3.6 weight_grads.14
  517.9 11.4 %last.2 = (bf16[528,1024]{1,0:T(8,128)(2,1)}, f32[8,1024]{1,0:T(8,128)}) custom-call(bf16[1040,256]{1,0:T(8,128)(2,1)} %copy-done.34, bf16[1040,256]{1,0:T(8,128)(2,1)} %copy-done.35, bf16[1040,256]{1,0:T(8,128)(2,1)} %copy-done.36, bf16[1040,256]{1,0:T(8,128)(2,1)} %copy-done.37, bf16[1040,256]{1,0:T(8,128)(2,1)} %copy-done.38, ...), custom_call_target="tpu_custom_call" | custom-call | flops 17999998976 | bytes 90177536 | tf_op jit(solution)/shard_map/last/pallas_call | solution.py:777
  529.3 3.2 collective-permute-done.56
  534.3 4.3 weight_grads.15
  538.7 2.3 collective-permute-start.58
  542.7 11.2 %last.3 = (bf16[512,1024]{1,0:T(8,128)(2,1)}, f32[8,1024]{1,0:T(8,128)}) custom-call(bf16[1040,256]{1,0:T(8,128)(2,1)} %copy-done.34, bf16[1040,256]{1,0:T(8,128)(2,1)} %copy-done.35, bf16[1040,256]{1,0:T(8,128)(2,1)} %copy-done.36, bf16[1040,256]{1,0:T(8,128)(2,1)} %copy-done.37, bf16[1040,256]{1,0:T(8,128)(2,1)} %copy-done.38, ...), custom_call_target="tpu_custom_call" | custom-call | flops 17999998976 | bytes 90046464 | tf_op jit(solution)/shard_map/last/pallas_call | solution.py:777
  554.0 4.9 collective-permute-done.59
  567.0 2.0 reduce_sum.9
  570.9 2.4 collective-permute-done.68
  575.3 1.9 collective-permute-start.61
  579.9 3.4 collective-permute-done.61
  583.4 1.9 collective-permute-done.62
  586.5 5.8 collective-permute-done.63
  593.5 5.2 collective-permute-done.64
  (437 shorter events, 109.5 us)
Async XLA Ops:
  7.2 559.8 %all-gather.3.cloned.1.call-start = ((), (), s32[]{:S(2)}) async-start(), calls=%async_computation | async-start | bytes 2973696 | tf_op jit(solution)/shard_map/all_gather | solution.py:1176
  7.3 16.1 %collective-permute-start.14 = (s32[512,2]{0,1:T(2,128)}, s32[512,2]{0,1:T(2,128)S(1)}, u32[]{:S(2)}, u32[]{:S(2)}) collective-permute-start(s32[512,2]{0,1:T(2,128)} %param.20), channel_id=1, source_target_pairs={{0,1},{1,0},{2,3},{3,2},{4,5},{5,4},{6,7},{7,6},{8,9},{9,8},{10,11... | collective-permute-start | bytes 12296 | tf_op jit(solution)/shard_map/ppermute | solution.py:436
  12.7 8.3 %collective-permute-start.1 = (bf16[32,1664]{1,0:T(8,128)(2,1)S(1)}, bf16[32,1664]{1,0:T(8,128)(2,1)S(1)}, u32[]{:S(2)}, u32[]{:S(2)}) collective-permute-start(bf16[32,1664]{1,0:T(8,128)(2,1)S(1)} %fusion.36), channel_id=1, source_target_pairs={{0,16},{1,17},{2,18},{3,19},{4,20},{5,21},{6,22},{7,23},{8,24},{9,... | collective-permute-start | bytes 319496 | tf_op jit(solution)/shard_map/ppermute | solution.py:436
  18.1 33.5 %collective-permute-start = (bf16[512,1024]{1,0:T(8,128)(2,1)S(1)}, bf16[512,1024]{1,0:T(8,128)(2,1)S(1)}, u32[]{:S(2)}, u32[]{:S(2)}) collective-permute-start(bf16[512,1024]{1,0:T(8,128)(2,1)S(1)} %get-tuple-element.348), channel_id=1, source_target_pairs={{0,1},{1,0},{2,3},{3,2},{4,5},{5,4},{6,7},{7,6},{8,9},{9,8},{10,11... | collective-permute-start | bytes 3145736 | tf_op jit(solution)/shard_map/ppermute | solution.py:436
  21.0 9.3 %collective-permute-start.2 = (bf16[64,1664]{1,0:T(8,128)(2,1)S(1)}, bf16[64,1664]{1,0:T(8,128)(2,1)S(1)}, u32[]{:S(2)}, u32[]{:S(2)}) collective-permute-start(bf16[64,1664]{1,0:T(8,128)(2,1)S(1)} %pad_maximum_fusion.9), channel_id=1, source_target_pairs={{0,8},{1,9},{2,10},{3,11},{4,12},{5,13},{6,14},{7,15},{8,0},{9,1},... | collective-permute-start | bytes 638984 | tf_op jit(solution)/shard_map/ppermute | solution.py:436
  23.4 9.8 %collective-permute-start.7 = (bf16[32,2560]{1,0:T(8,128)(2,1)S(1)}, bf16[32,2560]{1,0:T(8,128)(2,1)S(1)}, u32[]{:S(2)}, u32[]{:S(2)}) collective-permute-start(bf16[32,2560]{1,0:T(8,128)(2,1)S(1)} %pad_maximum_fusion.10), channel_id=1, source_target_pairs={{0,16},{1,17},{2,18},{3,19},{4,20},{5,21},{6,22},{7,23},{8,24},{9,... | collective-permute-start | bytes 491528 | tf_op jit(solution)/shard_map/ppermute | solution.py:436
  30.4 8.2 %collective-permute-start.4 = (bf16[128,1664]{1,0:T(8,128)(2,1)S(1)}, bf16[128,1664]{1,0:T(8,128)(2,1)S(1)}, u32[]{:S(2)}, u32[]{:S(2)}) collective-permute-start(bf16[128,1664]{1,0:T(8,128)(2,1)S(1)} %pad_maximum_fusion.4.refs_0_), channel_id=1, source_target_pairs={{0,4},{1,5},{2,6},{3,7},{4,0},{5,1},{6,2},{7,3},{8,12},{9,13},{10,... | collective-permute-start | bytes 1277960 | tf_op jit(solution)/shard_map/ppermute | solution.py:436
  32.0 19.6 %collective-permute-start.3 = (bf16[128,1664]{1,0:T(8,128)(2,1)S(1)}, bf16[128,1664]{1,0:T(8,128)(2,1)S(1)}, u32[]{:S(2)}, u32[]{:S(2)}) collective-permute-start(bf16[128,1664]{1,0:T(8,128)(2,1)S(1)} %pad_maximum_fusion.4.refs_0_), channel_id=1, source_target_pairs={{0,1},{1,0},{2,3},{3,2},{4,5},{5,4},{6,7},{7,6},{8,9},{9,8},{10,11... | collective-permute-start | bytes 1277960 | tf_op jit(solution)/shard_map/ppermute | solution.py:436
  33.3 20.8 %collective-permute-start.8 = (bf16[64,2560]{1,0:T(8,128)(2,1)S(1)}, bf16[64,2560]{1,0:T(8,128)(2,1)S(1)}, u32[]{:S(2)}, u32[]{:S(2)}) collective-permute-start(bf16[64,2560]{1,0:T(8,128)(2,1)S(1)} %pad_maximum_fusion.8), channel_id=1, source_target_pairs={{0,8},{1,9},{2,10},{3,11},{4,12},{5,13},{6,14},{7,15},{8,0},{9,1},... | collective-permute-start | bytes 983048 | tf_op jit(solution)/shard_map/ppermute | solution.py:436
  59.2 17.0 %collective-permute-start.9 = (bf16[512,1664]{1,0:T(8,128)(2,1)S(1)}, bf16[512,1664]{1,0:T(8,128)(2,1)S(1)}, u32[]{:S(2)}, u32[]{:S(2)}) collective-permute-start(bf16[512,1664]{1,0:T(8,128)(2,1)S(1)} %pack_rows.5.near_ref.qn_ref.kn_ref.vn_ref.refs_14_), channel_id=1, source_target_pairs={{0,2},{1,3},{2,0},{3,1},{4,6},{5,7},{6,4},{7,5},{8,10},{9,11},{10,... | collective-permute-start | bytes 5111816 | tf_op jit(solution)/shard_map/ppermute | solution.py:436
  62.9 11.7 %collective-permute-start.10 = (bf16[32,2816]{1,0:T(8,128)(2,1)S(1)}, bf16[32,2816]{1,0:T(8,128)(2,1)S(1)}, u32[]{:S(2)}, u32[]{:S(2)}) collective-permute-start(bf16[32,2816]{1,0:T(8,128)(2,1)S(1)} %pad.33), channel_id=1, source_target_pairs={{0,16},{1,17},{2,18},{3,19},{4,20},{5,21},{6,22},{7,23},{8,24},{9,... | collective-permute-start | bytes 540680 | tf_op jit(solution)/shard_map/ppermute | solution.py:436
  64.0 24.6 %collective-permute-start.12 = (bf16[128,2560]{1,0:T(8,128)(2,1)}, bf16[128,2560]{1,0:T(8,128)(2,1)S(1)}, u32[]{:S(2)}, u32[]{:S(2)}) collective-permute-start(bf16[128,2560]{1,0:T(8,128)(2,1)} %constant_dynamic-update-slice_fusion.refs_0_), channel_id=1, source_target_pairs={{0,4},{1,5},{2,6},{3,7},{4,0},{5,1},{6,2},{7,3},{8,12},{9,13},{10,... | collective-permute-start | bytes 1966088 | tf_op jit(solution)/shard_map/ppermute | solution.py:436
  64.5 24.1 %collective-permute-start.11 = (bf16[128,2560]{1,0:T(8,128)(2,1)}, bf16[128,2560]{1,0:T(8,128)(2,1)S(1)}, u32[]{:S(2)}, u32[]{:S(2)}) collective-permute-start(bf16[128,2560]{1,0:T(8,128)(2,1)} %constant_dynamic-update-slice_fusion.refs_0_), channel_id=1, source_target_pairs={{0,1},{1,0},{2,3},{3,2},{4,5},{5,4},{6,7},{7,6},{8,9},{9,8},{10,11... | collective-permute-start | bytes 1966088 | tf_op jit(solution)/shard_map/ppermute | solution.py:436
  77.4 11.1 %collective-permute-start.13 = (bf16[64,2816]{1,0:T(8,128)(2,1)S(1)}, bf16[64,2816]{1,0:T(8,128)(2,1)S(1)}, u32[]{:S(2)}, u32[]{:S(2)}) collective-permute-start(bf16[64,2816]{1,0:T(8,128)(2,1)S(1)} %pad_maximum_fusion.5), channel_id=1, source_target_pairs={{0,8},{1,9},{2,10},{3,11},{4,12},{5,13},{6,14},{7,15},{8,0},{9,1},... | collective-permute-start | bytes 1081352 | tf_op jit(solution)/shard_map/ppermute | solution.py:436
  88.6 25.0 %collective-permute-start.18 = (bf16[128,2816]{1,0:T(8,128)(2,1)S(1)}, bf16[128,2816]{1,0:T(8,128)(2,1)S(1)}, u32[]{:S(2)}, u32[]{:S(2)}) collective-permute-start(bf16[128,2816]{1,0:T(8,128)(2,1)S(1)} %constant_dynamic-update-slice_fusion.4.refs_0_), channel_id=1, source_target_pairs={{0,4},{1,5},{2,6},{3,7},{4,0},{5,1},{6,2},{7,3},{8,12},{9,13},{10,... | collective-permute-start | bytes 2162696 | tf_op jit(solution)/shard_map/ppermute | solution.py:436
  89.2 24.5 %collective-permute-start.17 = (bf16[128,2816]{1,0:T(8,128)(2,1)S(1)}, bf16[128,2816]{1,0:T(8,128)(2,1)S(1)}, u32[]{:S(2)}, u32[]{:S(2)}) collective-permute-start(bf16[128,2816]{1,0:T(8,128)(2,1)S(1)} %constant_dynamic-update-slice_fusion.4.refs_0_), channel_id=1, source_target_pairs={{0,1},{1,0},{2,3},{3,2},{4,5},{5,4},{6,7},{7,6},{8,9},{9,8},{10,11... | collective-permute-start | bytes 2162696 | tf_op jit(solution)/shard_map/ppermute | solution.py:436
  89.7 16.7 %collective-permute-start.19 = (bf16[32,2816]{1,0:T(8,128)(2,1)S(1)}, bf16[32,2816]{1,0:T(8,128)(2,1)S(1)}, u32[]{:S(2)}, u32[]{:S(2)}) collective-permute-start(bf16[32,2816]{1,0:T(8,128)(2,1)S(1)} %copy-done.74), channel_id=1, source_target_pairs={{0,16},{1,17},{2,18},{3,19},{4,20},{5,21},{6,22},{7,23},{8,24},{9,... | collective-permute-start | bytes 540680 | tf_op jit(solution)/shard_map/ppermute | solution.py:436
  91.6 21.9 %collective-permute-start.16 = (bf16[64,2560]{1,0:T(8,128)(2,1)S(1)}, bf16[64,2560]{1,0:T(8,128)(2,1)S(1)}, u32[]{:S(2)}, u32[]{:S(2)}) collective-permute-start(bf16[64,2560]{1,0:T(8,128)(2,1)S(1)} %slice.407), channel_id=1, source_target_pairs={{0,4},{1,5},{2,6},{3,7},{4,0},{5,1},{6,2},{7,3},{8,12},{9,13},{10,... | collective-permute-start | bytes 983048 | tf_op jit(solution)/shard_map/ppermute | solution.py:436
  93.2 20.5 %collective-permute-start.15 = (bf16[64,2560]{1,0:T(8,128)(2,1)S(1)}, bf16[64,2560]{1,0:T(8,128)(2,1)S(1)}, u32[]{:S(2)}, u32[]{:S(2)}) collective-permute-start(bf16[64,2560]{1,0:T(8,128)(2,1)S(1)} %slice.406), channel_id=1, source_target_pairs={{0,1},{1,0},{2,3},{3,2},{4,5},{5,4},{6,7},{7,6},{8,9},{9,8},{10,11... | collective-permute-start | bytes 983048 | tf_op jit(solution)/shard_map/ppermute | solution.py:436
  113.7 21.6 %collective-permute-start.22 = (bf16[64,2816]{1,0:T(8,128)(2,1)S(1)}, bf16[64,2816]{1,0:T(8,128)(2,1)S(1)}, u32[]{:S(2)}, u32[]{:S(2)}) collective-permute-start(bf16[64,2816]{1,0:T(8,128)(2,1)S(1)} %slice.409), channel_id=1, source_target_pairs={{0,4},{1,5},{2,6},{3,7},{4,0},{5,1},{6,2},{7,3},{8,12},{9,13},{10,... | collective-permute-start | bytes 1081352 | tf_op jit(solution)/shard_map/ppermute | solution.py:436
  115.3 20.0 %collective-permute-start.21 = (bf16[64,2816]{1,0:T(8,128)(2,1)S(1)}, bf16[64,2816]{1,0:T(8,128)(2,1)S(1)}, u32[]{:S(2)}, u32[]{:S(2)}) collective-permute-start(bf16[64,2816]{1,0:T(8,128)(2,1)S(1)} %slice.408), channel_id=1, source_target_pairs={{0,1},{1,0},{2,3},{3,2},{4,5},{5,4},{6,7},{7,6},{8,9},{9,8},{10,11... | collective-permute-start | bytes 1081352 | tf_op jit(solution)/shard_map/ppermute | solution.py:436
  115.8 17.7 %collective-permute-start.23 = (bf16[64,2816]{1,0:T(8,128)(2,1)S(1)}, bf16[64,2816]{1,0:T(8,128)(2,1)}, u32[]{:S(2)}, u32[]{:S(2)}) collective-permute-start(bf16[64,2816]{1,0:T(8,128)(2,1)S(1)} %pad_maximum_fusion.6), channel_id=1, source_target_pairs={{0,8},{1,9},{2,10},{3,11},{4,12},{5,13},{6,14},{7,15},{8,0},{9,1},... | collective-permute-start | bytes 1081352 | tf_op jit(solution)/shard_map/ppermute | solution.py:436
  120.1 15.2 %collective-permute-start.20 = (bf16[512,2560]{1,0:T(8,128)(2,1)S(1)}, bf16[512,2560]{1,0:T(8,128)(2,1)}, u32[]{:S(2)}, u32[]{:S(2)}) collective-permute-start(bf16[512,2560]{1,0:T(8,128)(2,1)S(1)} %pack_rows.6.qn_ref.kn_ref.vn_ref.na_ref.nb_ref.refs_16_), channel_id=1, source_target_pairs={{0,2},{1,3},{2,0},{3,1},{4,6},{5,7},{6,4},{7,5},{8,10},{9,11},{10,... | collective-permute-start | bytes 7864328 | tf_op jit(solution)/shard_map/ppermute | solution.py:436
  135.3 18.0 %collective-permute-start.25 = (bf16[128,2816]{1,0:T(8,128)(2,1)}, bf16[128,2816]{1,0:T(8,128)(2,1)S(1)}, u32[]{:S(2)}, u32[]{:S(2)}) collective-permute-start(bf16[128,2816]{1,0:T(8,128)(2,1)} %constant_dynamic-update-slice_fusion.6.refs_0_), channel_id=1, source_target_pairs={{0,4},{1,5},{2,6},{3,7},{4,0},{5,1},{6,2},{7,3},{8,12},{9,13},{10,... | collective-permute-start | bytes 2162696 | tf_op jit(solution)/shard_map/ppermute | solution.py:436
  135.9 17.6 %collective-permute-start.24 = (bf16[128,2816]{1,0:T(8,128)(2,1)}, bf16[128,2816]{1,0:T(8,128)(2,1)S(1)}, u32[]{:S(2)}, u32[]{:S(2)}) collective-permute-start(bf16[128,2816]{1,0:T(8,128)(2,1)} %constant_dynamic-update-slice_fusion.6.refs_0_), channel_id=1, source_target_pairs={{0,1},{1,0},{2,3},{3,2},{4,5},{5,4},{6,7},{7,6},{8,9},{9,8},{10,11... | collective-permute-start | bytes 2162696 | tf_op jit(solution)/shard_map/ppermute | solution.py:436
  137.4 15.3 %collective-permute-start.27 = (bf16[32,2816]{1,0:T(8,128)(2,1)S(1)}, bf16[32,2816]{1,0:T(8,128)(2,1)S(1)}, u32[]{:S(2)}, u32[]{:S(2)}) collective-permute-start(bf16[32,2816]{1,0:T(8,128)(2,1)S(1)} %pad.36), channel_id=1, source_target_pairs={{0,16},{1,17},{2,18},{3,19},{4,20},{5,21},{6,22},{7,23},{8,24},{9,... | collective-permute-start | bytes 540680 | tf_op jit(solution)/shard_map/ppermute | solution.py:436
  139.8 13.6 %collective-permute-start.26 = (bf16[512,2816]{1,0:T(8,128)(2,1)S(1)}, bf16[512,2816]{1,0:T(8,128)(2,1)}, u32[]{:S(2)}, u32[]{:S(2)}) collective-permute-start(bf16[512,2816]{1,0:T(8,128)(2,1)S(1)} %pack_rows.7.gn_ref), channel_id=1, source_target_pairs={{0,2},{1,3},{2,0},{3,1},{4,6},{5,7},{6,4},{7,5},{8,10},{9,11},{10,... | collective-permute-start | bytes 8650760 | tf_op jit(solution)/shard_map/ppermute | solution.py:436
  153.5 15.5 %collective-permute-start.29 = (bf16[64,2816]{1,0:T(8,128)(2,1)S(1)}, bf16[64,2816]{1,0:T(8,128)(2,1)S(1)}, u32[]{:S(2)}, u32[]{:S(2)}) collective-permute-start(bf16[64,2816]{1,0:T(8,128)(2,1)S(1)} %slice.411), channel_id=1, source_target_pairs={{0,4},{1,5},{2,6},{3,7},{4,0},{5,1},{6,2},{7,3},{8,12},{9,13},{10,... | collective-permute-start | bytes 1081352 | tf_op jit(solution)/shard_map/ppermute | solution.py:436
  155.1 13.9 %collective-permute-start.28 = (bf16[64,2816]{1,0:T(8,128)(2,1)S(1)}, bf16[64,2816]{1,0:T(8,128)(2,1)S(1)}, u32[]{:S(2)}, u32[]{:S(2)}) collective-permute-start(bf16[64,2816]{1,0:T(8,128)(2,1)S(1)} %slice.410), channel_id=1, source_target_pairs={{0,1},{1,0},{2,3},{3,2},{4,5},{5,4},{6,7},{7,6},{8,9},{9,8},{10,11... | collective-permute-start | bytes 1081352 | tf_op jit(solution)/shard_map/ppermute | solution.py:436
  156.6 12.5 %collective-permute-start.30 = (bf16[64,2816]{1,0:T(8,128)(2,1)S(1)}, bf16[64,2816]{1,0:T(8,128)(2,1)S(1)}, u32[]{:S(2)}, u32[]{:S(2)}) collective-permute-start(bf16[64,2816]{1,0:T(8,128)(2,1)S(1)} %pad_maximum_fusion.7), channel_id=1, source_target_pairs={{0,8},{1,9},{2,10},{3,11},{4,12},{5,13},{6,14},{7,15},{8,0},{9,1},... | collective-permute-start | bytes 1081352 | tf_op jit(solution)/shard_map/ppermute | solution.py:436
  170.7 20.8 %collective-permute-start.31 = (bf16[512,2816]{1,0:T(8,128)(2,1)S(1)}, bf16[512,2816]{1,0:T(8,128)(2,1)}, u32[]{:S(2)}, u32[]{:S(2)}) collective-permute-start(bf16[512,2816]{1,0:T(8,128)(2,1)S(1)} %pack_rows.8.un_ref), channel_id=1, source_target_pairs={{0,2},{1,3},{2,0},{3,1},{4,6},{5,7},{6,4},{7,5},{8,10},{9,11},{10,... | collective-permute-start | bytes 8650760 | tf_op jit(solution)/shard_map/ppermute | solution.py:436
  173.0 18.2 %collective-permute-start.33 = (bf16[128,2816]{1,0:T(8,128)(2,1)S(1)}, bf16[128,2816]{1,0:T(8,128)(2,1)S(1)}, u32[]{:S(2)}, u32[]{:S(2)}) collective-permute-start(bf16[128,2816]{1,0:T(8,128)(2,1)S(1)} %constant_dynamic-update-slice_fusion.8.refs_0_), channel_id=1, source_target_pairs={{0,4},{1,5},{2,6},{3,7},{4,0},{5,1},{6,2},{7,3},{8,12},{9,13},{10,... | collective-permute-start | bytes 2162696 | tf_op jit(solution)/shard_map/ppermute | solution.py:436
  173.6 17.9 %collective-permute-start.32 = (bf16[128,2816]{1,0:T(8,128)(2,1)S(1)}, bf16[128,2816]{1,0:T(8,128)(2,1)S(1)}, u32[]{:S(2)}, u32[]{:S(2)}) collective-permute-start(bf16[128,2816]{1,0:T(8,128)(2,1)S(1)} %constant_dynamic-update-slice_fusion.8.refs_0_), channel_id=1, source_target_pairs={{0,1},{1,0},{2,3},{3,2},{4,5},{5,4},{6,7},{7,6},{8,9},{9,8},{10,11... | collective-permute-start | bytes 2162696 | tf_op jit(solution)/shard_map/ppermute | solution.py:436
  191.6 26.1 %collective-permute-start.35 = (bf16[64,2816]{1,0:T(8,128)(2,1)S(1)}, bf16[64,2816]{1,0:T(8,128)(2,1)S(1)}, u32[]{:S(2)}, u32[]{:S(2)}) collective-permute-start(bf16[64,2816]{1,0:T(8,128)(2,1)S(1)} %slice.413), channel_id=1, source_target_pairs={{0,4},{1,5},{2,6},{3,7},{4,0},{5,1},{6,2},{7,3},{8,12},{9,13},{10,... | collective-permute-start | bytes 1081352 | tf_op jit(solution)/shard_map/ppermute | solution.py:436
  193.2 24.5 %collective-permute-start.34 = (bf16[64,2816]{1,0:T(8,128)(2,1)S(1)}, bf16[64,2816]{1,0:T(8,128)(2,1)S(1)}, u32[]{:S(2)}, u32[]{:S(2)}) collective-permute-start(bf16[64,2816]{1,0:T(8,128)(2,1)S(1)} %slice.412), channel_id=1, source_target_pairs={{0,1},{1,0},{2,3},{3,2},{4,5},{5,4},{6,7},{7,6},{8,9},{9,8},{10,11... | collective-permute-start | bytes 1081352 | tf_op jit(solution)/shard_map/ppermute | solution.py:436
  194.4 30.3 %collective-permute-start.36 = (bf16[512,1024]{1,0:T(8,128)(2,1)S(1)}, bf16[512,1024]{1,0:T(8,128)(2,1)S(1)}, u32[]{:S(2)}, u32[]{:S(2)}) collective-permute-start(bf16[512,1024]{1,0:T(8,128)(2,1)S(1)} %get-tuple-element.232), channel_id=1, source_target_pairs={{0,1},{1,0},{2,3},{3,2},{4,5},{5,4},{6,7},{7,6},{8,9},{9,8},{10,11... | collective-permute-start | bytes 3145736 | tf_op jit(solution)/shard_map/ppermute | solution.py:436
  248.7 30.9 %collective-permute-start.38 = (bf16[528,1024]{1,0:T(8,128)(2,1)S(1)}, bf16[528,1024]{1,0:T(8,128)(2,1)S(1)}, u32[]{:S(2)}, u32[]{:S(2)}) collective-permute-start(bf16[528,1024]{1,0:T(8,128)(2,1)S(1)} %slice.415), channel_id=1, source_target_pairs={{0,1},{1,0},{2,3},{3,2},{4,5},{5,4},{6,7},{7,6},{8,9},{9,8},{10,11... | collective-permute-start | bytes 3244040 | tf_op jit(solution)/shard_map/ppermute | solution.py:436
  292.8 9.8 %collective-permute-start.39 = (bf16[512,5632]{1,0:T(8,128)(2,1)}, bf16[512,5632]{1,0:T(8,128)(2,1)}, u32[]{:S(2)}, u32[]{:S(2)}) collective-permute-start(bf16[512,5632]{1,0:T(8,128)(2,1)} %weight_grads.8), channel_id=1, source_target_pairs={{0,2},{1,3},{2,0},{3,1},{4,6},{5,7},{6,4},{7,5},{8,10},{9,11},{10,... | collective-permute-start | bytes 17301512 | tf_op jit(solution)/shard_map/ppermute | solution.py:436
  302.6 19.6 %collective-permute-start.40 = (bf16[512,2816]{1,0:T(8,128)(2,1)S(1)}, bf16[512,2816]{1,0:T(8,128)(2,1)}, u32[]{:S(2)}, u32[]{:S(2)}) collective-permute-start(bf16[512,2816]{1,0:T(8,128)(2,1)S(1)} %weight_grads.9), channel_id=1, source_target_pairs={{0,2},{1,3},{2,0},{3,1},{4,6},{5,7},{6,4},{7,5},{8,10},{9,11},{10,... | collective-permute-start | bytes 8650760 | tf_op jit(solution)/shard_map/ppermute | solution.py:436
  324.3 21.0 %collective-permute-start.42 = (bf16[64,5632]{1,0:T(8,128)(2,1)S(1)}, bf16[64,5632]{1,0:T(8,128)(2,1)S(1)}, u32[]{:S(2)}, u32[]{:S(2)}) collective-permute-start(bf16[64,5632]{1,0:T(8,128)(2,1)S(1)} %get-tuple-element.333), channel_id=1, source_target_pairs={{0,1},{1,0},{2,3},{3,2},{4,5},{5,4},{6,7},{7,6},{8,9},{9,8},{10,11... | collective-permute-start | bytes 2162696 | tf_op jit(solution)/shard_map/ppermute | solution.py:436
  325.2 20.1 %collective-permute-start.41 = (bf16[64,5632]{1,0:T(8,128)(2,1)S(1)}, bf16[64,5632]{1,0:T(8,128)(2,1)S(1)}, u32[]{:S(2)}, u32[]{:S(2)}) collective-permute-start(bf16[64,5632]{1,0:T(8,128)(2,1)S(1)} %get-tuple-element.335), channel_id=1, source_target_pairs={{0,4},{1,5},{2,6},{3,7},{4,0},{5,1},{6,2},{7,3},{8,12},{9,13},{10,... | collective-permute-start | bytes 2162696 | tf_op jit(solution)/shard_map/ppermute | solution.py:436
  347.2 35.8 %collective-permute-start.43 = (bf16[128,5632]{1,0:T(8,128)(2,1)S(1)}, bf16[128,5632]{1,0:T(8,128)(2,1)S(1)}, u32[]{:S(2)}, u32[]{:S(2)}) collective-permute-start(bf16[128,5632]{1,0:T(8,128)(2,1)S(1)} %pad_maximum_fusion.1), channel_id=1, source_target_pairs={{0,4},{1,5},{2,6},{3,7},{4,0},{5,1},{6,2},{7,3},{8,12},{9,13},{10,... | collective-permute-start | bytes 4325384 | tf_op jit(solution)/shard_map/ppermute | solution.py:436
  348.3 34.8 %collective-permute-start.44 = (bf16[128,5632]{1,0:T(8,128)(2,1)S(1)}, bf16[128,5632]{1,0:T(8,128)(2,1)}, u32[]{:S(2)}, u32[]{:S(2)}) collective-permute-start(bf16[128,5632]{1,0:T(8,128)(2,1)S(1)} %pad_maximum_fusion), channel_id=1, source_target_pairs={{0,1},{1,0},{2,3},{3,2},{4,5},{5,4},{6,7},{7,6},{8,9},{9,8},{10,11... | collective-permute-start | bytes 4325384 | tf_op jit(solution)/shard_map/ppermute | solution.py:436
  385.5 17.2 %collective-permute-start.47 = (bf16[64,2816]{1,0:T(8,128)(2,1)S(1)}, bf16[64,2816]{1,0:T(8,128)(2,1)S(1)}, u32[]{:S(2)}, u32[]{:S(2)}) collective-permute-start(bf16[64,2816]{1,0:T(8,128)(2,1)S(1)} %get-tuple-element.339), channel_id=1, source_target_pairs={{0,1},{1,0},{2,3},{3,2},{4,5},{5,4},{6,7},{7,6},{8,9},{9,8},{10,11... | collective-permute-start | bytes 1081352 | tf_op jit(solution)/shard_map/ppermute | solution.py:436
  387.0 15.7 %collective-permute-start.46 = (bf16[64,2816]{1,0:T(8,128)(2,1)S(1)}, bf16[64,2816]{1,0:T(8,128)(2,1)S(1)}, u32[]{:S(2)}, u32[]{:S(2)}) collective-permute-start(bf16[64,2816]{1,0:T(8,128)(2,1)S(1)} %get-tuple-element.341), channel_id=1, source_target_pairs={{0,4},{1,5},{2,6},{3,7},{4,0},{5,1},{6,2},{7,3},{8,12},{9,13},{10,... | collective-permute-start | bytes 1081352 | tf_op jit(solution)/shard_map/ppermute | solution.py:436
  401.1 17.2 %collective-permute-start.45 = (bf16[64,5632]{1,0:T(8,128)(2,1)S(1)}, bf16[64,5632]{1,0:T(8,128)(2,1)S(1)}, u32[]{:S(2)}, u32[]{:S(2)}) collective-permute-start(bf16[64,5632]{1,0:T(8,128)(2,1)S(1)} %slice.427), channel_id=1, source_target_pairs={{0,8},{1,9},{2,10},{3,11},{4,12},{5,13},{6,14},{7,15},{8,0},{9,1},... | collective-permute-start | bytes 2162696 | tf_op jit(solution)/shard_map/ppermute | solution.py:436
  418.6 17.2 %collective-permute-start.48 = (bf16[32,5632]{1,0:T(8,128)(2,1)S(1)}, bf16[32,5632]{1,0:T(8,128)(2,1)S(1)}, u32[]{:S(2)}, u32[]{:S(2)}) collective-permute-start(bf16[32,5632]{1,0:T(8,128)(2,1)S(1)} %slice.435), channel_id=1, source_target_pairs={{0,16},{1,17},{2,18},{3,19},{4,20},{5,21},{6,22},{7,23},{8,24},{9,... | collective-permute-start | bytes 1081352 | tf_op jit(solution)/shard_map/ppermute | solution.py:436
  433.5 15.9 %collective-permute-start.49 = (bf16[128,2816]{1,0:T(8,128)(2,1)S(1)}, bf16[128,2816]{1,0:T(8,128)(2,1)S(1)}, u32[]{:S(2)}, u32[]{:S(2)}) collective-permute-start(bf16[128,2816]{1,0:T(8,128)(2,1)S(1)} %pad_maximum_fusion.3), channel_id=1, source_target_pairs={{0,4},{1,5},{2,6},{3,7},{4,0},{5,1},{6,2},{7,3},{8,12},{9,13},{10,... | collective-permute-start | bytes 2162696 | tf_op jit(solution)/shard_map/ppermute | solution.py:436
  434.9 15.5 %collective-permute-start.50 = (bf16[128,2816]{1,0:T(8,128)(2,1)S(1)}, bf16[128,2816]{1,0:T(8,128)(2,1)S(1)}, u32[]{:S(2)}, u32[]{:S(2)}) collective-permute-start(bf16[128,2816]{1,0:T(8,128)(2,1)S(1)} %copy-done.73), channel_id=1, source_target_pairs={{0,1},{1,0},{2,3},{3,2},{4,5},{5,4},{6,7},{7,6},{8,9},{9,8},{10,11... | collective-permute-start | bytes 2162696 | tf_op jit(solution)/shard_map/ppermute | solution.py:436
  450.8 8.4 %collective-permute-start.51 = (bf16[64,2816]{1,0:T(8,128)(2,1)S(1)}, bf16[64,2816]{1,0:T(8,128)(2,1)S(1)}, u32[]{:S(2)}, u32[]{:S(2)}) collective-permute-start(bf16[64,2816]{1,0:T(8,128)(2,1)S(1)} %slice.438), channel_id=1, source_target_pairs={{0,8},{1,9},{2,10},{3,11},{4,12},{5,13},{6,14},{7,15},{8,0},{9,1},... | collective-permute-start | bytes 1081352 | tf_op jit(solution)/shard_map/ppermute | solution.py:436
  459.2 13.7 %collective-permute-start.53 = (bf16[32,2816]{1,0:T(8,128)(2,1)S(1)}, bf16[32,2816]{1,0:T(8,128)(2,1)S(1)}, u32[]{:S(2)}, u32[]{:S(2)}) collective-permute-start(bf16[32,2816]{1,0:T(8,128)(2,1)S(1)} %slice.440), channel_id=1, source_target_pairs={{0,16},{1,17},{2,18},{3,19},{4,20},{5,21},{6,22},{7,23},{8,24},{9,... | collective-permute-start | bytes 540680 | tf_op jit(solution)/shard_map/ppermute | solution.py:436
  460.2 13.6 %collective-permute-start.52 = (bf16[512,2560]{1,0:T(8,128)(2,1)}, bf16[512,2560]{1,0:T(8,128)(2,1)}, u32[]{:S(2)}, u32[]{:S(2)}) collective-permute-start(bf16[512,2560]{1,0:T(8,128)(2,1)} %weight_grads.12), channel_id=1, source_target_pairs={{0,2},{1,3},{2,0},{3,1},{4,6},{5,7},{6,4},{7,5},{8,10},{9,11},{10,... | collective-permute-start | bytes 7864328 | tf_op jit(solution)/shard_map/ppermute | solution.py:436
  494.0 17.2 %collective-permute-start.54 = (bf16[128,2560]{1,0:T(8,128)(2,1)S(1)}, bf16[128,2560]{1,0:T(8,128)(2,1)S(1)}, u32[]{:S(2)}, u32[]{:S(2)}) collective-permute-start(bf16[128,2560]{1,0:T(8,128)(2,1)S(1)} %get-tuple-element.344), channel_id=1, source_target_pairs={{0,4},{1,5},{2,6},{3,7},{4,0},{5,1},{6,2},{7,3},{8,12},{9,13},{10,... | collective-permute-start | bytes 1966088 | tf_op jit(solution)/shard_map/ppermute | solution.py:436
  515.9 16.5 %collective-permute-start.56 = (bf16[128,2560]{1,0:T(8,128)(2,1)S(1)}, bf16[128,2560]{1,0:T(8,128)(2,1)}, u32[]{:S(2)}, u32[]{:S(2)}) collective-permute-start(bf16[128,2560]{1,0:T(8,128)(2,1)S(1)} %get-tuple-element.311), channel_id=1, source_target_pairs={{0,4},{1,5},{2,6},{3,7},{4,0},{5,1},{6,2},{7,3},{8,12},{9,13},{10,... | collective-permute-start | bytes 1966088 | tf_op jit(solution)/shard_map/ppermute | solution.py:436
  516.4 16.3 %collective-permute-start.57 = (bf16[128,2560]{1,0:T(8,128)(2,1)}, bf16[128,2560]{1,0:T(8,128)(2,1)}, u32[]{:S(2)}, u32[]{:S(2)}) collective-permute-start(bf16[128,2560]{1,0:T(8,128)(2,1)} %add_convert_fusion.7), channel_id=1, source_target_pairs={{0,1},{1,0},{2,3},{3,2},{4,5},{5,4},{6,7},{7,6},{8,9},{9,8},{10,11... | collective-permute-start | bytes 1966088 | tf_op jit(solution)/shard_map/ppermute | solution.py:436
  517.9 16.3 %collective-permute-start.55 = (bf16[512,1536]{1,0:T(8,128)(2,1)S(1)}, bf16[512,1536]{1,0:T(8,128)(2,1)}, u32[]{:S(2)}, u32[]{:S(2)}) collective-permute-start(bf16[512,1536]{1,0:T(8,128)(2,1)S(1)} %weight_grads.14), channel_id=1, source_target_pairs={{0,2},{1,3},{2,0},{3,1},{4,6},{5,7},{6,4},{7,5},{8,10},{9,11},{10,... | collective-permute-start | bytes 4718600 | tf_op jit(solution)/shard_map/ppermute | solution.py:436
  538.7 15.2 %collective-permute-start.58 = (bf16[64,2560]{1,0:T(8,128)(2,1)S(1)}, bf16[64,2560]{1,0:T(8,128)(2,1)S(1)}, u32[]{:S(2)}, u32[]{:S(2)}) collective-permute-start(bf16[64,2560]{1,0:T(8,128)(2,1)S(1)} %slice.446), channel_id=1, source_target_pairs={{0,8},{1,9},{2,10},{3,11},{4,12},{5,13},{6,14},{7,15},{8,0},{9,1},... | collective-permute-start | bytes 983048 | tf_op jit(solution)/shard_map/ppermute | solution.py:436
  541.1 17.8 %collective-permute-start.59 = (bf16[256,1536]{1,0:T(8,128)(2,1)S(1)}, bf16[256,1536]{1,0:T(8,128)(2,1)S(1)}, u32[]{:S(2)}, u32[]{:S(2)}) collective-permute-start(bf16[256,1536]{1,0:T(8,128)(2,1)S(1)} %slice.448), channel_id=1, source_target_pairs={{0,1},{1,0},{2,3},{3,2},{4,5},{5,4},{6,7},{7,6},{8,9},{9,8},{10,11... | collective-permute-start | bytes 2359304 | tf_op jit(solution)/shard_map/ppermute | solution.py:436
  573.4 5.9 collective-permute-start.69
  575.3 8.0 %collective-permute-start.61 = (bf16[32,2560]{1,0:T(8,128)(2,1)S(1)}, bf16[32,2560]{1,0:T(8,128)(2,1)S(1)}, u32[]{:S(2)}, u32[]{:S(2)}) collective-permute-start(bf16[32,2560]{1,0:T(8,128)(2,1)S(1)} %slice.453), channel_id=1, source_target_pairs={{0,16},{1,17},{2,18},{3,19},{4,20},{5,21},{6,22},{7,23},{8,24},{9,... | collective-permute-start | bytes 491528 | tf_op jit(solution)/shard_map/ppermute | solution.py:436
  577.2 8.1 %collective-permute-start.62 = (bf16[128,1536]{1,0:T(8,128)(2,1)S(1)}, bf16[128,1536]{1,0:T(8,128)(2,1)S(1)}, u32[]{:S(2)}, u32[]{:S(2)}) collective-permute-start(bf16[128,1536]{1,0:T(8,128)(2,1)S(1)} %slice.457), channel_id=1, source_target_pairs={{0,4},{1,5},{2,6},{3,7},{4,0},{5,1},{6,2},{7,3},{8,12},{9,13},{10,... | collective-permute-start | bytes 1179656 | tf_op jit(solution)/shard_map/ppermute | solution.py:436
  577.8 23.0 %collective-permute-start.60 = (bf16[528,1024]{1,0:T(8,128)(2,1)S(1)}, bf16[528,1024]{1,0:T(8,128)(2,1)S(1)}, u32[]{:S(2)}, u32[]{:S(2)}) collective-permute-start(bf16[528,1024]{1,0:T(8,128)(2,1)S(1)} %copy-done.98), channel_id=1, source_target_pairs={{0,1},{1,0},{2,3},{3,2},{4,5},{5,4},{6,7},{7,6},{8,9},{9,8},{10,11... | collective-permute-start | bytes 3244040 | tf_op jit(solution)/shard_map/ppermute | solution.py:436
  585.4 6.8 %collective-permute-start.63 = (bf16[64,1536]{1,0:T(8,128)(2,1)S(1)}, bf16[64,1536]{1,0:T(8,128)(2,1)S(1)}, u32[]{:S(2)}, u32[]{:S(2)}) collective-permute-start(bf16[64,1536]{1,0:T(8,128)(2,1)S(1)} %slice.505), channel_id=1, source_target_pairs={{0,8},{1,9},{2,10},{3,11},{4,12},{5,13},{6,14},{7,15},{8,0},{9,1},... | collective-permute-start | bytes 589832 | tf_op jit(solution)/shard_map/ppermute | solution.py:436
  592.3 6.4 %collective-permute-start.64 = (bf16[32,1536]{1,0:T(8,128)(2,1)S(1)}, bf16[32,1536]{1,0:T(8,128)(2,1)S(1)}, u32[]{:S(2)}, u32[]{:S(2)}) collective-permute-start(bf16[32,1536]{1,0:T(8,128)(2,1)S(1)} %slice.507), channel_id=1, source_target_pairs={{0,16},{1,17},{2,18},{3,19},{4,20},{5,21},{6,22},{7,23},{8,24},{9,... | collective-permute-start | bytes 294920 | tf_op jit(solution)/shard_map/ppermute | solution.py:436
  (108 other events, 1826.1 us)
Sparse Core Ops, SparseCore 0:
  302.9 60.7 all-gather.2

commit v4 on v3

--- a/solution.py
+++ b/solution.py
@@ -431,6 +431,7 @@
 
 
 def swap_over(value, bit):
+    value = lax.optimization_barrier(value)
     SENT.append(value)
     count = lax.axis_size(BOTH)
     return lax.ppermute(value, BOTH, [(i, i ^ bit) for i in range(count)])
@@ -554,14 +555,15 @@
         self.total = rounded_sum(self.total[:128], swap_over(to_y, BIT_Y), swap_over(to_x, BIT_X))
         return self.total
 
+    def over_y(self, *deps):
+        total = after(self.total, *deps)
+        kept, sent = joined(total[:128], total[256:384]), joined(total[128:256], total[384:])
+        self.total = rounded_sum(kept, swap_over(sent, BIT_Y))
+        return self.total
+
     def over_x(self, *deps):
         total = after(self.total, *deps)
-        self.total = rounded_sum(total[:256], swap_over(total[256:], BIT_X))
-        return self.total
-
-    def over_y(self, *deps):
-        total = after(self.total, *deps)
-        self.total = rounded_sum(total[:128], swap_over(total[128:], BIT_Y))
+        self.total = rounded_sum(total[:128], swap_over(total[128:], BIT_X))
         return self.total
 
     def along_z1(self, *deps):
@@ -1172,7 +1174,7 @@
     )
 
     gate = wide_sums, far_rows
-    outs = to_pair(out_rows, far_rows)
+    outs = to_pair(after(out_rows, far_rows), far_rows)
     all_sums = lax.all_gather(wide_sums, BOTH)
     part_width = wide // 2
     down, second, low, high = Scatter(), Scatter(), Scatter(), Scatter()
@@ -1266,23 +1268,24 @@
 
     gate = high_total
     high.total = high_total
-    high_stage = high.over_x(gate)
+    far_rows = swap_over(after(far_part, gate), BIT_X)
+    high_stage = high.over_y(gate)
     near_part, near_sums = last_rows(gate, 0, HALF)
 
     gate = near_part, low_stage, high_stage
-    far_rows = swap_over(after(far_part, gate), BIT_X)
-    high.over_y(gate)
     low_grad = low.along_z0(gate)
-    first_sums = far_sums + after(near_sums, gate)
+    high.over_x(gate, far_rows)
     high.along_z1()
     high_grad = high.along_z0()
-    patch_grad, cls_grad = to_pair(joined(near_part, far_part), far_rows)
-    ffn_grads = jnp.sum(after(all_sums, parts[1][0]), axis=0)[:4, :hidden]
+    sums = [far_sums, near_sums, middle_sums, branch_sums] + [part[3] for part in parts]
+    far_sums, near_sums, middle_sums, branch_sums, *head_sums = after(sums, far_rows)
+    patch_grad, cls_grad = to_pair(after(joined(near_part, far_part), far_rows), far_rows)
+    ffn_grads = jnp.sum(after(all_sums, far_rows), axis=0)[:4, :hidden]
     head_sums = jnp.dot(
-        joined(*[part[3][:2] for part in parts], axis=1), order.astype(F32), precision=lax.Precision.HIGHEST
+        joined(*[part[:2] for part in head_sums], axis=1), order.astype(F32), precision=lax.Precision.HIGHEST
     )
     vector_grads = scatter_small(
-        joined(first_sums[:2], head_sums, middle_sums[:3], branch_sums[:1]).T
+        joined((far_sums + near_sums)[:2], head_sums, middle_sums[:3], branch_sums[:1]).T
     )
     blocks = [low_grad[:, WIDTH + i * HEAD_COLS :][:, :HEAD_COLS] for i in range(6)]
     blocks += [high_grad[:, i * HEAD_COLS :][:, :HEAD_COLS] for i in range(6)]

time: 616 us -> 593 us (0.963)
  waiting for transfers between devices: 159 us -> 145 us
  starting transfers between devices: 69.6 us -> 63 us
    ppermute x70, waiting for transfers between devices: 159 us -> 145 us  [swap_over(): return lax.ppermute(value, BOTH, [(i, i ^ bit) for i in range(count)])]
    ppermute x70, starting transfers between devices: 69.5 us -> 63 us  [swap_over(): return lax.ppermute(value, BOTH, [(i, i ^ bit) for i in range(count)])]
  transfers between devices with their start and end apart: 71 -> 71, of which waited for: 35 -> 33; matrix products, arithmetic and copies ran while one was open for 9% -> 9% of each run, Pallas kernels for 44% -> 45%
where the time goes in v4:
time: 593 us; the launch traced here: 588 us
  Pallas kernels  297 us (50%)
  waiting for transfers between devices  145 us (24%)
  starting transfers between devices  63 us (11%)
  local copies, waits for them, and re-layouts  34.6 us (6%)
  other arithmetic  29.2 us (5%)
  between operations  16.8 us (3%)
    ppermute x70, waiting for transfers between devices, swap_over(): return lax.ppermute(value, BOTH, [(i, i ^ bit) for i in range(count)])  145 us
    pallas_call x8, Pallas kernels, over_rows(): pl.pallas_call(kernel, grid=(rows // step,), in_specs=in_specs, out_specs...  131 us
    ppermute x70, starting transfers between devices, swap_over(): return lax.ppermute(value, BOTH, [(i, i ^ bit) for i in range(count)])  63 us
    pallas_call x8, Pallas kernels, weight_grads(): pl.pallas_call(kernel, grid=(len(steps),), in_specs=[pl.BlockSpec((ROWS,...  59.8 us
    pallas_call x4, Pallas kernels, attention_backward(): pl.pallas_call(functools.partial(attention_back_kernel, step=step), grid=...  50.1 us
    pallas_call x4, Pallas kernels, attention_forward(): pl.pallas_call(attention_kernel, grid=(1,), in_specs=[whole(x)] + [block(...  47.5 us
    unnamed x188, local copies, waits for them, and re-layouts  12.2 us
  transfers between devices with their start and end apart: 71, of which 33 were waited for; matrix products, arithmetic and copies ran while one was open for 9% of the time, Pallas kernels for 45%

profile of v4, /device:TPU:0, one launch (start us, length us, event | category | flops | bytes accessed | tf_op | source)
XLA Modules:
  0.0 587.8 jit_solution(1531424648726328532)
XLA Ops:
  7.3 3.0 collective-permute-start.14
  12.7 2.7 collective-permute-start.1
  15.4 2.7 dynamic-slice_bitcast_fusion.3
  18.8 2.2 fusion.59.order_ref.refs_19_
  21.0 1.6 collective-permute-start.2
  24.1 1.9 collective-permute-start.7
  26.0 3.4 collective-permute-done.2
  33.9 3.8 collective-permute-done.4.refs_1_
  37.6 14.1 %collective-permute-done.3.refs_2_ = bf16[128,1664]{1,0:T(8,128)(2,1)S(1)} collective-permute-done((bf16[128,1664]{1,0:T(8,128)(2,1)S(1)}, bf16[128,1664]{1,0:T(8,128)(2,1)S(1)}, u32[]{:S(2)}, u32[]{:S(2)}) %collective-permute-start.3) | collective-permute-done | bytes 426016 | tf_op jit(solution)/shard_map/ppermute | solution.py:437
  54.2 3.4 collective-permute-done.6.refs_4_
  59.5 2.8 fusion.34
  65.1 9.6 %collective-permute-done.10 = bf16[32,2816]{1,0:T(8,128)(2,1)S(1)} collective-permute-done((bf16[32,2816]{1,0:T(8,128)(2,1)S(1)}, bf16[32,2816]{1,0:T(8,128)(2,1)S(1)}, u32[]{:S(2)}, u32[]{:S(2)}) %collective-permute-start.10) | collective-permute-done | bytes 180256 | tf_op jit(solution)/shard_map/ppermute | solution.py:437
  78.4 3.0 vectors.1
  81.4 8.0 %start.1 = (bf16[1040,1024]{1,0:T(8,128)(2,1)}, bf16[1040,1024]{1,0:T(8,128)(2,1)}) custom-call(bf16[1040,1024]{1,0:T(8,128)(2,1)} %fusion.32.rows_ref, bf16[1024,1024]{1,0:T(8,128)(2,1)} %fusion.59.order_ref.refs_19_, f32[8,1024]{1,0:T(8,128)} %get-tuple-element.192.vec_ref.refs_18_), custom_call_target="tpu_custom_call" | custom-call | flops 8800000000 | bytes 34078720 | tf_op jit(solution)/shard_map/start/pallas_call | solution.py:779
  96.4 11.7 %attention_forward.4 = (bf16[1040,256]{1,0:T(8,128)(2,1)}, bf16[1040,256]{1,0:T(8,128)(2,1)}, bf16[1040,256]{1,0:T(8,128)(2,1)}, bf16[1040,256]{1,0:T(8,128)(2,1)}, f32[8,1040]{1,0:T(8,128)}) custom-call(bf16[1040,1024]{1,0:T(8,128)(2,1)} %get-tuple-element.323.x_ref.refs_1_.refs_0_, bf16[512,1664]{1,0:T(8,128)(2,1)} %copy-done.2, ...), custom_call_target="tpu_custom_call" | custom-call | flops 30000001024 | bytes 28000000 | tf_op jit(solution)/shard_map/attention_forward/pallas_call | solution.py:641
  108.1 7.2 %collective-permute-done.16.refs_4_ = bf16[64,2560]{1,0:T(8,128)(2,1)S(1)} collective-permute-done((bf16[64,2560]{1,0:T(8,128)(2,1)S(1)}, bf16[64,2560]{1,0:T(8,128)(2,1)S(1)}, u32[]{:S(2)}, u32[]{:S(2)}) %collective-permute-start.16) | collective-permute-done | bytes 327712 | tf_op jit(solution)/shard_map/ppermute | solution.py:437
  115.6 2.6 pack_rows.6.qn_ref.kn_ref.vn_ref.na_ref.nb_ref.refs_16_
  121.0 11.7 %attention_forward.5 = (bf16[1040,256]{1,0:T(8,128)(2,1)}, bf16[1040,256]{1,0:T(8,128)(2,1)}, bf16[1040,256]{1,0:T(8,128)(2,1)}, bf16[1040,256]{1,0:T(8,128)(2,1)}, f32[8,1040]{1,0:T(8,128)}) custom-call(bf16[1040,1024]{1,0:T(8,128)(2,1)} %get-tuple-element.323.x_ref.refs_1_.refs_0_, bf16[512,1664]{1,0:T(8,128)(2,1)} %copy-done.2, ...), custom_call_target="tpu_custom_call" | custom-call | flops 30000001024 | bytes 28000000 | tf_op jit(solution)/shard_map/attention_forward/pallas_call | solution.py:641
  138.9 1.7 collective-permute-start.27
  140.6 11.8 %attention_forward.6 = (bf16[1040,256]{1,0:T(8,128)(2,1)}, bf16[1040,256]{1,0:T(8,128)(2,1)}, bf16[1040,256]{1,0:T(8,128)(2,1)}, bf16[1040,256]{1,0:T(8,128)(2,1)}, f32[8,1040]{1,0:T(8,128)}) custom-call(bf16[1040,1024]{1,0:T(8,128)(2,1)} %get-tuple-element.323.x_ref.refs_1_.refs_0_, bf16[512,2560]{1,0:T(8,128)(2,1)} %copy-done.6, ...), custom_call_target="tpu_custom_call" | custom-call | flops 30000001024 | bytes 28000000 | tf_op jit(solution)/shard_map/attention_forward/pallas_call | solution.py:641
  158.6 12.2 %attention_forward.7 = (bf16[1040,256]{1,0:T(8,128)(2,1)}, bf16[1040,256]{1,0:T(8,128)(2,1)}, bf16[1040,256]{1,0:T(8,128)(2,1)}, bf16[1040,256]{1,0:T(8,128)(2,1)}, f32[8,1040]{1,0:T(8,128)}) custom-call(bf16[1040,1024]{1,0:T(8,128)(2,1)} %get-tuple-element.323.x_ref.refs_1_.refs_0_, bf16[512,2560]{1,0:T(8,128)(2,1)} %copy-done.6, ...), custom_call_target="tpu_custom_call" | custom-call | flops 30000001024 | bytes 28000000 | tf_op jit(solution)/shard_map/attention_forward/pallas_call | solution.py:641
  174.9 7.2 %middle.1 = (bf16[1040,1024]{1,0:T(8,128)(2,1)}, bf16[1040,1024]{1,0:T(8,128)(2,1)}) custom-call(bf16[1040,256]{1,0:T(8,128)(2,1)} %get-tuple-element.198.a0_ref.o_ref.refs_2_, bf16[1040,256]{1,0:T(8,128)(2,1)} %get-tuple-element.204.a1_ref.o_ref.refs_3_, bf16[1040,256]{1,0:T(8,128)(2,1)} %get-tuple-element.214.a2_ref.refs_4_.o_ref, ...), custom_call_target="tpu_custom_call" | custom-call | flops 8800000000 | bytes 76152832 | tf_op jit(solution)/shard_map/middle/pallas_call | solution.py:779
  182.2 9.8 %collective-permute-done.33.refs_1_ = bf16[128,2816]{1,0:T(8,128)(2,1)S(1)} collective-permute-done((bf16[128,2816]{1,0:T(8,128)(2,1)S(1)}, bf16[128,2816]{1,0:T(8,128)(2,1)S(1)}, u32[]{:S(2)}, u32[]{:S(2)}) %collective-permute-start.33) | collective-permute-done | bytes 720928 | tf_op jit(solution)/shard_map/ppermute | solution.py:437
  195.9 22.5 %hidden.1 = (bf16[1040,2816]{1,0:T(8,128)(2,1)}, bf16[1040,2816]{1,0:T(8,128)(2,1)}, bf16[1040,2816]{1,0:T(8,128)(2,1)}, f32[1040,128]{1,0:T(8,128)}) custom-call(bf16[1040,1024]{1,0:T(8,128)(2,1)} %get-tuple-element.264.x_ref.refs_0_, bf16[512,2816]{1,0:T(8,128)(2,1)} %copy-done.3, bf16[512,2816]{1,0:T(8,128)(2,1)} %collective-permute-done.26.gf_ref, ...), custom_call_target="tpu_custom_call" | custom-call | flops 48000000000 | bytes 127434752 | tf_op jit(solution)/shard_map/hidden/pallas_call | solution.py:779
  218.4 6.9 %collective-permute-done.36 = bf16[512,1024]{1,0:T(8,128)(2,1)S(1)} collective-permute-done((bf16[512,1024]{1,0:T(8,128)(2,1)S(1)}, bf16[512,1024]{1,0:T(8,128)(2,1)S(1)}, u32[]{:S(2)}, u32[]{:S(2)}) %collective-permute-start.36) | collective-permute-done | bytes 1048608 | tf_op jit(solution)/shard_map/ppermute | solution.py:437
  230.1 2.2 collective-permute-done.37.far_ref
  234.5 14.6 %result.1 = bf16[1040,1024]{1,0:T(8,128)(2,1)} custom-call(bf16[1040,2816]{1,0:T(8,128)(2,1)} %get-tuple-element.237.inner_ref.refs_1_, bf16[1040,1024]{1,0:T(8,128)(2,1)} %get-tuple-element.268.middle_ref, bf16[512,2816]{1,0:T(8,128)(2,1)} %copy-done.5, bf16[512,2816]{1,0:T(8,128)(2,1)} %copy-done.87, f32[8,1024]{1,0:T(8,128)} %get-tuple-element.192.vec_ref.refs_18_, ...), custom_call_target="tpu_custom_call" | custom-call | flops 32000000000 | bytes 72073216 | tf_op jit(solution)/shard_map/result/pallas_call | solution.py:779
  250.9 29.6 %hidden_back.1 = (bf16[1040,1024]{1,0:T(8,128)(2,1)}, bf16[1040,2816]{1,0:T(8,128)(2,1)}, bf16[1040,2816]{1,0:T(8,128)(2,1)}, f32[8,2816]{1,0:T(8,128)}, f32[8,1024]{1,0:T(8,128)}) custom-call(bf16[1040,1024]{1,0:T(8,128)(2,1)} %fusion.33.d_ref, bf16[1040,2816]{1,0:T(8,128)(2,1)} %get-tuple-element.254.gate_ref, ...), custom_call_target="tpu_custom_call" | custom-call | flops 32000000000 | bytes 145211392 | tf_op jit(solution)/shard_map/hidden_back/pallas_call | solution.py:779
  280.6 12.1 %weight_grads.8 = bf16[512,5632]{1,0:T(8,128)(2,1)} custom-call(bf16[1040,1024]{1,0:T(8,128)(2,1)S(1)} %copy-done.12, bf16[1040,2816]{1,0:T(8,128)(2,1)} %get-tuple-element.257.refs_1_.dgate_ref, bf16[1040,2816]{1,0:T(8,128)(2,1)} %get-tuple-element.258.refs_2_.dup_ref), custom_call_target="tpu_custom_call" | custom-call | flops 23991418880 | bytes 70287360 | tf_op jit(solution)/shard_map/weight_grads/pallas_call | solution.py:1010
  294.4 5.8 weight_grads.9
  300.2 2.3 collective-permute-done.39.refs_3_
  307.0 12.9 %weight_grads.10 = bf16[512,5632]{1,0:T(8,128)(2,1)} custom-call(bf16[1040,1024]{1,0:T(8,128)(2,1)S(1)} %copy-done.12, bf16[1040,2816]{1,0:T(8,128)(2,1)} %get-tuple-element.257.refs_1_.dgate_ref, bf16[1040,2816]{1,0:T(8,128)(2,1)} %get-tuple-element.258.refs_2_.dup_ref, bf16[512,5632]{1,0:T(8,128)(2,1)} %collective-permute-done.39.refs_3_), custom_call_target="tpu_custom_call" | custom-call | flops 23991418880 | bytes 70287360 | tf_op jit(solution)/shard_map/weight_grads/pallas_call | solution.py:1010
  319.9 3.0 fusion.60
  325.1 6.8 %weight_grads.11 = bf16[512,2816]{1,0:T(8,128)(2,1)S(1)} custom-call(bf16[1040,1024]{1,0:T(8,128)(2,1)S(1)} %copy-done.13, bf16[1040,2816]{1,0:T(8,128)(2,1)} %get-tuple-element.237.inner_ref.refs_1_, bf16[512,2816]{1,0:T(8,128)(2,1)} %copy-done.88), custom_call_target="tpu_custom_call" | custom-call | flops 11995709440 | bytes 35143680 | tf_op jit(solution)/shard_map/weight_grads/pallas_call | solution.py:1010
  331.9 14.7 %collective-permute-done.42 = bf16[64,5632]{1,0:T(8,128)(2,1)S(1)} collective-permute-done((bf16[64,5632]{1,0:T(8,128)(2,1)S(1)}, bf16[64,5632]{1,0:T(8,128)(2,1)S(1)}, u32[]{:S(2)}, u32[]{:S(2)}) %collective-permute-start.42) | collective-permute-done | bytes 720928 | tf_op jit(solution)/shard_map/ppermute | solution.py:437
  347.6 1.8 add_convert_fusion.4
  350.9 26.4 %middle_back.1 = (bf16[1040,1024]{1,0:T(8,128)(2,1)}, bf16[1040,256]{1,0:T(8,128)(2,1)}, bf16[1040,256]{1,0:T(8,128)(2,1)}, bf16[1040,256]{1,0:T(8,128)(2,1)}, b...) custom-call(bf16[1040,2816]{1,0:T(8,128)(2,1)} %get-tuple-element.257.refs_1_.dgate_ref, ...), custom_call_target="tpu_custom_call" | custom-call | flops 56000000000 | bytes 169279488 | tf_op jit(solution)/shard_map/middle_back/pallas_call | solution.py:779
  377.4 5.0 collective-permute-done.44
  382.9 2.4 add_convert_fusion
  388.1 12.7 %attention_backward.4 = (bf16[1040,256]{1,0:T(8,128)(2,1)S(1)}, bf16[1040,256]{1,0:T(8,128)(2,1)S(1)}, bf16[1040,256]{1,0:T(8,128)(2,1)S(1)}, f32[8,256]{1,0:T(8,128)S(1)}) custom-call(bf16[1040,256]{1,0:T(8,128)(2,1)S(1)} %copy-done.45, bf16[1040,256]{1,0:T(8,128)(2,1)S(1)} %copy-done.46, bf16[1040,256]{1,0:T(8,128)(2,1)S(1)} %copy-done.47, ...), custom_call_target="tpu_custom_call" | custom-call | flops 51999997952 | bytes 20000000 | tf_op jit(solution)/shard_map/attention_backward/pallas_call | solution.py:741
  404.3 12.5 %attention_backward.5 = (bf16[1040,256]{1,0:T(8,128)(2,1)S(1)}, bf16[1040,256]{1,0:T(8,128)(2,1)S(1)}, bf16[1040,256]{1,0:T(8,128)(2,1)S(1)}, f32[8,256]{1,0:T(8,128)S(1)}) custom-call(bf16[1040,256]{1,0:T(8,128)(2,1)S(1)} %copy-done.42, bf16[1040,256]{1,0:T(8,128)(2,1)S(1)} %copy-done.43, bf16[1040,256]{1,0:T(8,128)(2,1)S(1)} %copy-done.44, ...), custom_call_target="tpu_custom_call" | custom-call | flops 51999997952 | bytes 20000000 | tf_op jit(solution)/shard_map/attention_backward/pallas_call | solution.py:741
  419.4 6.6 %weight_grads.12 = bf16[512,2560]{1,0:T(8,128)(2,1)} custom-call(bf16[1040,1024]{1,0:T(8,128)(2,1)} %get-tuple-element.324.refs_0_.refs_12_, bf16[1040,1024]{1,0:T(8,128)(2,1)} %get-tuple-element.323.x_ref.refs_1_.refs_0_, bf16[1040,256]{1,0:T(8,128)(2,1)S(1)} %copy-done.26, bf16[1040,256]{1,0:T(8,128)(2,1)S(1)} %copy-done.27, ...), custom_call_target="tpu_custom_call" | custom-call | flops 10905190400 | bytes 31948800 | tf_op jit(solution)/shard_map/weight_grads/pallas_call | solution.py:1010
  426.1 2.8 collective-permute-done.51
  429.6 12.7 %attention_backward.6 = (bf16[1040,256]{1,0:T(8,128)(2,1)S(1)}, bf16[1040,256]{1,0:T(8,128)(2,1)S(1)}, bf16[1040,256]{1,0:T(8,128)(2,1)S(1)}, f32[8,256]{1,0:T(8,128)S(1)}) custom-call(bf16[1040,256]{1,0:T(8,128)(2,1)S(1)} %copy-done.39, bf16[1040,256]{1,0:T(8,128)(2,1)S(1)} %copy-done.40, bf16[1040,256]{1,0:T(8,128)(2,1)S(1)} %copy-done.41, ...), custom_call_target="tpu_custom_call" | custom-call | flops 51999997952 | bytes 20000000 | tf_op jit(solution)/shard_map/attention_backward/pallas_call | solution.py:741
  444.7 7.6 %weight_grads.13 = bf16[512,2560]{1,0:T(8,128)(2,1)} custom-call(bf16[1040,1024]{1,0:T(8,128)(2,1)} %get-tuple-element.324.refs_0_.refs_12_, bf16[1040,1024]{1,0:T(8,128)(2,1)} %get-tuple-element.323.x_ref.refs_1_.refs_0_, bf16[1040,256]{1,0:T(8,128)(2,1)S(1)} %copy-done.26, bf16[1040,256]{1,0:T(8,128)(2,1)S(1)} %copy-done.27, ...), custom_call_target="tpu_custom_call" | custom-call | flops 10905190400 | bytes 31948800 | tf_op jit(solution)/shard_map/weight_grads/pallas_call | solution.py:1010
  455.2 12.3 %attention_backward.7 = (bf16[1040,256]{1,0:T(8,128)(2,1)S(1)}, bf16[1040,256]{1,0:T(8,128)(2,1)S(1)}, bf16[1040,256]{1,0:T(8,128)(2,1)S(1)}, f32[8,256]{1,0:T(8,128)S(1)}) custom-call(bf16[1040,256]{1,0:T(8,128)(2,1)S(1)} %copy-done.36, bf16[1040,256]{1,0:T(8,128)(2,1)S(1)} %copy-done.37, bf16[1040,256]{1,0:T(8,128)(2,1)S(1)} %copy-done.38, ...), custom_call_target="tpu_custom_call" | custom-call | flops 51999997952 | bytes 20000000 | tf_op jit(solution)/shard_map/attention_backward/pallas_call | solution.py:741
  467.4 3.5 collective-permute-done.54
  472.2 3.7 weight_grads.14
  475.9 1.7 collective-permute-start.57
  478.2 11.4 %last.2 = (bf16[528,1024]{1,0:T(8,128)(2,1)}, f32[8,1024]{1,0:T(8,128)}) custom-call(bf16[1040,256]{1,0:T(8,128)(2,1)} %copy-done.30, bf16[1040,256]{1,0:T(8,128)(2,1)} %copy-done.31, bf16[1040,256]{1,0:T(8,128)(2,1)} %copy-done.32, bf16[1040,256]{1,0:T(8,128)(2,1)} %copy-done.33, bf16[1040,256]{1,0:T(8,128)(2,1)} %copy-done.34, ...), custom_call_target="tpu_custom_call" | custom-call | flops 17999998976 | bytes 90177536 | tf_op jit(solution)/shard_map/last/pallas_call | solution.py:779
  489.6 3.1 collective-permute-done.57
  495.4 4.3 weight_grads.15
  500.9 1.7 collective-permute-start.60
  502.6 11.2 %last.3 = (bf16[512,1024]{1,0:T(8,128)(2,1)}, f32[8,1024]{1,0:T(8,128)}) custom-call(bf16[1040,256]{1,0:T(8,128)(2,1)} %copy-done.30, bf16[1040,256]{1,0:T(8,128)(2,1)} %copy-done.31, bf16[1040,256]{1,0:T(8,128)(2,1)} %copy-done.32, bf16[1040,256]{1,0:T(8,128)(2,1)} %copy-done.33, bf16[1040,256]{1,0:T(8,128)(2,1)} %copy-done.34, ...), custom_call_target="tpu_custom_call" | custom-call | flops 17999998976 | bytes 90046464 | tf_op jit(solution)/shard_map/last/pallas_call | solution.py:779
  513.9 4.9 collective-permute-done.60
  519.1 2.3 collective-permute-start.61
  522.5 4.7 collective-permute-done.61
  527.9 16.7 %collective-permute-done.58 = bf16[528,1024]{1,0:T(8,128)(2,1)S(1)} collective-permute-done((bf16[528,1024]{1,0:T(8,128)(2,1)S(1)}, bf16[528,1024]{1,0:T(8,128)(2,1)S(1)}, u32[]{:S(2)}, u32[]{:S(2)}) %collective-permute-start.58) | collective-permute-done | bytes 1081376 | tf_op jit(solution)/shard_map/ppermute | solution.py:437
  546.2 1.9 fusion.37
  552.2 7.8 %collective-permute-done.66 = f32[256,8]{0,1:T(8,128)S(1)} collective-permute-done((f32[256,8]{0,1:T(8,128)S(1)}, f32[256,8]{0,1:T(8,128)S(1)}, u32[]{:S(2)}, u32[]{:S(2)}) %collective-permute-start.66) | collective-permute-done | bytes 8224 | tf_op jit(solution)/shard_map/ppermute | solution.py:437
  561.6 2.0 reduce_sum.9
  564.2 1.6 collective-permute-start.68
  569.0 3.1 collective-permute-done.63
  573.2 5.5 collective-permute-done.64
  (420 shorter events, 105.7 us)
Async XLA Ops:
  7.2 554.3 %all-gather.3.cloned.1.call-start = ((), (), s32[]{:S(2)}) async-start(), calls=%async_computation | async-start | bytes 2973696 | tf_op jit(solution)/shard_map/all_gather | solution.py:1178
  7.3 16.8 %collective-permute-start.14 = (s32[512,2]{0,1:T(2,128)}, s32[512,2]{0,1:T(2,128)S(1)}, u32[]{:S(2)}, u32[]{:S(2)}) collective-permute-start(s32[512,2]{0,1:T(2,128)} %param.20), channel_id=1, source_target_pairs={{0,1},{1,0},{2,3},{3,2},{4,5},{5,4},{6,7},{7,6},{8,9},{9,8},{10,11... | collective-permute-start | bytes 12296 | tf_op jit(solution)/shard_map/ppermute | solution.py:437
  12.7 8.2 %collective-permute-start.1 = (bf16[32,1664]{1,0:T(8,128)(2,1)S(1)}, bf16[32,1664]{1,0:T(8,128)(2,1)S(1)}, u32[]{:S(2)}, u32[]{:S(2)}) collective-permute-start(bf16[32,1664]{1,0:T(8,128)(2,1)S(1)} %fusion.36), channel_id=1, source_target_pairs={{0,16},{1,17},{2,18},{3,19},{4,20},{5,21},{6,22},{7,23},{8,24},{9,... | collective-permute-start | bytes 319496 | tf_op jit(solution)/shard_map/ppermute | solution.py:437
  18.0 33.7 %collective-permute-start = (bf16[512,1024]{1,0:T(8,128)(2,1)}, bf16[512,1024]{1,0:T(8,128)(2,1)S(1)}, u32[]{:S(2)}, u32[]{:S(2)}) collective-permute-start(bf16[512,1024]{1,0:T(8,128)(2,1)} %get-tuple-element.366), channel_id=1, source_target_pairs={{0,1},{1,0},{2,3},{3,2},{4,5},{5,4},{6,7},{7,6},{8,9},{9,8},{10,11... | collective-permute-start | bytes 3145736 | tf_op jit(solution)/shard_map/ppermute | solution.py:437
  21.0 8.4 %collective-permute-start.2 = (bf16[64,1664]{1,0:T(8,128)(2,1)S(1)}, bf16[64,1664]{1,0:T(8,128)(2,1)S(1)}, u32[]{:S(2)}, u32[]{:S(2)}) collective-permute-start(bf16[64,1664]{1,0:T(8,128)(2,1)S(1)} %pad_maximum_fusion.11), channel_id=1, source_target_pairs={{0,8},{1,9},{2,10},{3,11},{4,12},{5,13},{6,14},{7,15},{8,0},{9,1},... | collective-permute-start | bytes 638984 | tf_op jit(solution)/shard_map/ppermute | solution.py:437
  24.1 9.7 %collective-permute-start.7 = (bf16[32,2560]{1,0:T(8,128)(2,1)S(1)}, bf16[32,2560]{1,0:T(8,128)(2,1)S(1)}, u32[]{:S(2)}, u32[]{:S(2)}) collective-permute-start(bf16[32,2560]{1,0:T(8,128)(2,1)S(1)} %pad_maximum_fusion.12), channel_id=1, source_target_pairs={{0,16},{1,17},{2,18},{3,19},{4,20},{5,21},{6,22},{7,23},{8,24},{9,... | collective-permute-start | bytes 491528 | tf_op jit(solution)/shard_map/ppermute | solution.py:437
  29.4 8.2 %collective-permute-start.4 = (bf16[128,1664]{1,0:T(8,128)(2,1)S(1)}, bf16[128,1664]{1,0:T(8,128)(2,1)S(1)}, u32[]{:S(2)}, u32[]{:S(2)}) collective-permute-start(bf16[128,1664]{1,0:T(8,128)(2,1)S(1)} %pad_maximum_fusion.6.refs_0_), channel_id=1, source_target_pairs={{0,4},{1,5},{2,6},{3,7},{4,0},{5,1},{6,2},{7,3},{8,12},{9,13},{10,... | collective-permute-start | bytes 1277960 | tf_op jit(solution)/shard_map/ppermute | solution.py:437
  31.0 20.7 %collective-permute-start.3 = (bf16[128,1664]{1,0:T(8,128)(2,1)S(1)}, bf16[128,1664]{1,0:T(8,128)(2,1)S(1)}, u32[]{:S(2)}, u32[]{:S(2)}) collective-permute-start(bf16[128,1664]{1,0:T(8,128)(2,1)S(1)} %pad_maximum_fusion.6.refs_0_), channel_id=1, source_target_pairs={{0,1},{1,0},{2,3},{3,2},{4,5},{5,4},{6,7},{7,6},{8,9},{9,8},{10,11... | collective-permute-start | bytes 1277960 | tf_op jit(solution)/shard_map/ppermute | solution.py:437
  33.8 20.5 %collective-permute-start.8 = (bf16[64,2560]{1,0:T(8,128)(2,1)S(1)}, bf16[64,2560]{1,0:T(8,128)(2,1)S(1)}, u32[]{:S(2)}, u32[]{:S(2)}) collective-permute-start(bf16[64,2560]{1,0:T(8,128)(2,1)S(1)} %pad_maximum_fusion.10), channel_id=1, source_target_pairs={{0,8},{1,9},{2,10},{3,11},{4,12},{5,13},{6,14},{7,15},{8,0},{9,1},... | collective-permute-start | bytes 983048 | tf_op jit(solution)/shard_map/ppermute | solution.py:437
  59.4 17.7 %collective-permute-start.9 = (bf16[512,1664]{1,0:T(8,128)(2,1)S(1)}, bf16[512,1664]{1,0:T(8,128)(2,1)S(1)}, u32[]{:S(2)}, u32[]{:S(2)}) collective-permute-start(bf16[512,1664]{1,0:T(8,128)(2,1)S(1)} %pack_rows.5.near_ref.qn_ref.kn_ref.vn_ref.refs_14_), channel_id=1, source_target_pairs={{0,2},{1,3},{2,0},{3,1},{4,6},{5,7},{6,4},{7,5},{8,10},{9,11},{10,... | collective-permute-start | bytes 5111816 | tf_op jit(solution)/shard_map/ppermute | solution.py:437
  63.0 11.7 %collective-permute-start.10 = (bf16[32,2816]{1,0:T(8,128)(2,1)S(1)}, bf16[32,2816]{1,0:T(8,128)(2,1)S(1)}, u32[]{:S(2)}, u32[]{:S(2)}) collective-permute-start(bf16[32,2816]{1,0:T(8,128)(2,1)S(1)} %pad.33), channel_id=1, source_target_pairs={{0,16},{1,17},{2,18},{3,19},{4,20},{5,21},{6,22},{7,23},{8,24},{9,... | collective-permute-start | bytes 540680 | tf_op jit(solution)/shard_map/ppermute | solution.py:437
  64.1 26.4 %collective-permute-start.12 = (bf16[128,2560]{1,0:T(8,128)(2,1)}, bf16[128,2560]{1,0:T(8,128)(2,1)S(1)}, u32[]{:S(2)}, u32[]{:S(2)}) collective-permute-start(bf16[128,2560]{1,0:T(8,128)(2,1)} %constant_dynamic-update-slice_fusion.refs_0_), channel_id=1, source_target_pairs={{0,4},{1,5},{2,6},{3,7},{4,0},{5,1},{6,2},{7,3},{8,12},{9,13},{10,... | collective-permute-start | bytes 1966088 | tf_op jit(solution)/shard_map/ppermute | solution.py:437
  64.6 25.9 %collective-permute-start.11 = (bf16[128,2560]{1,0:T(8,128)(2,1)}, bf16[128,2560]{1,0:T(8,128)(2,1)}, u32[]{:S(2)}, u32[]{:S(2)}) collective-permute-start(bf16[128,2560]{1,0:T(8,128)(2,1)} %constant_dynamic-update-slice_fusion.refs_0_), channel_id=1, source_target_pairs={{0,1},{1,0},{2,3},{3,2},{4,5},{5,4},{6,7},{7,6},{8,9},{9,8},{10,11... | collective-permute-start | bytes 1966088 | tf_op jit(solution)/shard_map/ppermute | solution.py:437
  77.1 13.3 %collective-permute-start.13 = (bf16[64,2816]{1,0:T(8,128)(2,1)}, bf16[64,2816]{1,0:T(8,128)(2,1)S(1)}, u32[]{:S(2)}, u32[]{:S(2)}) collective-permute-start(bf16[64,2816]{1,0:T(8,128)(2,1)} %pad_maximum_fusion.7), channel_id=1, source_target_pairs={{0,8},{1,9},{2,10},{3,11},{4,12},{5,13},{6,14},{7,15},{8,0},{9,1},... | collective-permute-start | bytes 1081352 | tf_op jit(solution)/shard_map/ppermute | solution.py:437
  90.5 25.0 %collective-permute-start.18 = (bf16[128,2816]{1,0:T(8,128)(2,1)S(1)}, bf16[128,2816]{1,0:T(8,128)(2,1)S(1)}, u32[]{:S(2)}, u32[]{:S(2)}) collective-permute-start(bf16[128,2816]{1,0:T(8,128)(2,1)S(1)} %constant_dynamic-update-slice_fusion.4.refs_0_), channel_id=1, source_target_pairs={{0,4},{1,5},{2,6},{3,7},{4,0},{5,1},{6,2},{7,3},{8,12},{9,13},{10,... | collective-permute-start | bytes 2162696 | tf_op jit(solution)/shard_map/ppermute | solution.py:437
  91.1 24.5 %collective-permute-start.17 = (bf16[128,2816]{1,0:T(8,128)(2,1)S(1)}, bf16[128,2816]{1,0:T(8,128)(2,1)S(1)}, u32[]{:S(2)}, u32[]{:S(2)}) collective-permute-start(bf16[128,2816]{1,0:T(8,128)(2,1)S(1)} %constant_dynamic-update-slice_fusion.4.refs_0_), channel_id=1, source_target_pairs={{0,1},{1,0},{2,3},{3,2},{4,5},{5,4},{6,7},{7,6},{8,9},{9,8},{10,11... | collective-permute-start | bytes 2162696 | tf_op jit(solution)/shard_map/ppermute | solution.py:437
  91.6 16.5 %collective-permute-start.19 = (bf16[32,2816]{1,0:T(8,128)(2,1)S(1)}, bf16[32,2816]{1,0:T(8,128)(2,1)S(1)}, u32[]{:S(2)}, u32[]{:S(2)}) collective-permute-start(bf16[32,2816]{1,0:T(8,128)(2,1)S(1)} %copy-done.66), channel_id=1, source_target_pairs={{0,16},{1,17},{2,18},{3,19},{4,20},{5,21},{6,22},{7,23},{8,24},{9,... | collective-permute-start | bytes 540680 | tf_op jit(solution)/shard_map/ppermute | solution.py:437
  93.2 22.1 %collective-permute-start.16 = (bf16[64,2560]{1,0:T(8,128)(2,1)S(1)}, bf16[64,2560]{1,0:T(8,128)(2,1)S(1)}, u32[]{:S(2)}, u32[]{:S(2)}) collective-permute-start(bf16[64,2560]{1,0:T(8,128)(2,1)S(1)} %slice.395), channel_id=1, source_target_pairs={{0,4},{1,5},{2,6},{3,7},{4,0},{5,1},{6,2},{7,3},{8,12},{9,13},{10,... | collective-permute-start | bytes 983048 | tf_op jit(solution)/shard_map/ppermute | solution.py:437
  94.9 20.7 %collective-permute-start.15 = (bf16[64,2560]{1,0:T(8,128)(2,1)S(1)}, bf16[64,2560]{1,0:T(8,128)(2,1)S(1)}, u32[]{:S(2)}, u32[]{:S(2)}) collective-permute-start(bf16[64,2560]{1,0:T(8,128)(2,1)S(1)} %slice.394), channel_id=1, source_target_pairs={{0,1},{1,0},{2,3},{3,2},{4,5},{5,4},{6,7},{7,6},{8,9},{9,8},{10,11... | collective-permute-start | bytes 983048 | tf_op jit(solution)/shard_map/ppermute | solution.py:437
  118.3 16.0 %collective-permute-start.22 = (bf16[64,2816]{1,0:T(8,128)(2,1)S(1)}, bf16[64,2816]{1,0:T(8,128)(2,1)S(1)}, u32[]{:S(2)}, u32[]{:S(2)}) collective-permute-start(bf16[64,2816]{1,0:T(8,128)(2,1)S(1)} %slice.397), channel_id=1, source_target_pairs={{0,4},{1,5},{2,6},{3,7},{4,0},{5,1},{6,2},{7,3},{8,12},{9,13},{10,... | collective-permute-start | bytes 1081352 | tf_op jit(solution)/shard_map/ppermute | solution.py:437
  119.9 14.4 %collective-permute-start.21 = (bf16[64,2816]{1,0:T(8,128)(2,1)S(1)}, bf16[64,2816]{1,0:T(8,128)(2,1)S(1)}, u32[]{:S(2)}, u32[]{:S(2)}) collective-permute-start(bf16[64,2816]{1,0:T(8,128)(2,1)S(1)} %slice.396), channel_id=1, source_target_pairs={{0,1},{1,0},{2,3},{3,2},{4,5},{5,4},{6,7},{7,6},{8,9},{9,8},{10,11... | collective-permute-start | bytes 1081352 | tf_op jit(solution)/shard_map/ppermute | solution.py:437
  120.4 13.1 %collective-permute-start.23 = (bf16[64,2816]{1,0:T(8,128)(2,1)S(1)}, bf16[64,2816]{1,0:T(8,128)(2,1)S(1)}, u32[]{:S(2)}, u32[]{:S(2)}) collective-permute-start(bf16[64,2816]{1,0:T(8,128)(2,1)S(1)} %pad_maximum_fusion.8), channel_id=1, source_target_pairs={{0,8},{1,9},{2,10},{3,11},{4,12},{5,13},{6,14},{7,15},{8,0},{9,1},... | collective-permute-start | bytes 1081352 | tf_op jit(solution)/shard_map/ppermute | solution.py:437
  121.0 14.0 %collective-permute-start.20 = (bf16[512,2560]{1,0:T(8,128)(2,1)S(1)}, bf16[512,2560]{1,0:T(8,128)(2,1)}, u32[]{:S(2)}, u32[]{:S(2)}) collective-permute-start(bf16[512,2560]{1,0:T(8,128)(2,1)S(1)} %pack_rows.6.qn_ref.kn_ref.vn_ref.na_ref.nb_ref.refs_16_), channel_id=1, source_target_pairs={{0,2},{1,3},{2,0},{3,1},{4,6},{5,7},{6,4},{7,5},{8,10},{9,11},{10,... | collective-permute-start | bytes 7864328 | tf_op jit(solution)/shard_map/ppermute | solution.py:437
  135.0 18.8 %collective-permute-start.25 = (bf16[128,2816]{1,0:T(8,128)(2,1)}, bf16[128,2816]{1,0:T(8,128)(2,1)S(1)}, u32[]{:S(2)}, u32[]{:S(2)}) collective-permute-start(bf16[128,2816]{1,0:T(8,128)(2,1)} %constant_dynamic-update-slice_fusion.6.refs_0_), channel_id=1, source_target_pairs={{0,4},{1,5},{2,6},{3,7},{4,0},{5,1},{6,2},{7,3},{8,12},{9,13},{10,... | collective-permute-start | bytes 2162696 | tf_op jit(solution)/shard_map/ppermute | solution.py:437
  135.5 18.5 %collective-permute-start.24 = (bf16[128,2816]{1,0:T(8,128)(2,1)}, bf16[128,2816]{1,0:T(8,128)(2,1)S(1)}, u32[]{:S(2)}, u32[]{:S(2)}) collective-permute-start(bf16[128,2816]{1,0:T(8,128)(2,1)} %constant_dynamic-update-slice_fusion.6.refs_0_), channel_id=1, source_target_pairs={{0,1},{1,0},{2,3},{3,2},{4,5},{5,4},{6,7},{7,6},{8,9},{9,8},{10,11... | collective-permute-start | bytes 2162696 | tf_op jit(solution)/shard_map/ppermute | solution.py:437
  138.9 13.5 %collective-permute-start.27 = (bf16[32,2816]{1,0:T(8,128)(2,1)S(1)}, bf16[32,2816]{1,0:T(8,128)(2,1)S(1)}, u32[]{:S(2)}, u32[]{:S(2)}) collective-permute-start(bf16[32,2816]{1,0:T(8,128)(2,1)S(1)} %copy-done.65), channel_id=1, source_target_pairs={{0,16},{1,17},{2,18},{3,19},{4,20},{5,21},{6,22},{7,23},{8,24},{9,... | collective-permute-start | bytes 540680 | tf_op jit(solution)/shard_map/ppermute | solution.py:437
  140.6 13.4 %collective-permute-start.26 = (bf16[512,2816]{1,0:T(8,128)(2,1)S(1)}, bf16[512,2816]{1,0:T(8,128)(2,1)}, u32[]{:S(2)}, u32[]{:S(2)}) collective-permute-start(bf16[512,2816]{1,0:T(8,128)(2,1)S(1)} %pack_rows.7.gn_ref), channel_id=1, source_target_pairs={{0,2},{1,3},{2,0},{3,1},{4,6},{5,7},{6,4},{7,5},{8,10},{9,11},{10,... | collective-permute-start | bytes 8650760 | tf_op jit(solution)/shard_map/ppermute | solution.py:437
  154.0 16.7 %collective-permute-start.29 = (bf16[64,2816]{1,0:T(8,128)(2,1)S(1)}, bf16[64,2816]{1,0:T(8,128)(2,1)S(1)}, u32[]{:S(2)}, u32[]{:S(2)}) collective-permute-start(bf16[64,2816]{1,0:T(8,128)(2,1)S(1)} %slice.399), channel_id=1, source_target_pairs={{0,4},{1,5},{2,6},{3,7},{4,0},{5,1},{6,2},{7,3},{8,12},{9,13},{10,... | collective-permute-start | bytes 1081352 | tf_op jit(solution)/shard_map/ppermute | solution.py:437
  155.6 15.2 %collective-permute-start.28 = (bf16[64,2816]{1,0:T(8,128)(2,1)S(1)}, bf16[64,2816]{1,0:T(8,128)(2,1)S(1)}, u32[]{:S(2)}, u32[]{:S(2)}) collective-permute-start(bf16[64,2816]{1,0:T(8,128)(2,1)S(1)} %slice.398), channel_id=1, source_target_pairs={{0,1},{1,0},{2,3},{3,2},{4,5},{5,4},{6,7},{7,6},{8,9},{9,8},{10,11... | collective-permute-start | bytes 1081352 | tf_op jit(solution)/shard_map/ppermute | solution.py:437
  157.1 13.7 %collective-permute-start.30 = (bf16[64,2816]{1,0:T(8,128)(2,1)S(1)}, bf16[64,2816]{1,0:T(8,128)(2,1)S(1)}, u32[]{:S(2)}, u32[]{:S(2)}) collective-permute-start(bf16[64,2816]{1,0:T(8,128)(2,1)S(1)} %pad_maximum_fusion.9), channel_id=1, source_target_pairs={{0,8},{1,9},{2,10},{3,11},{4,12},{5,13},{6,14},{7,15},{8,0},{9,1},... | collective-permute-start | bytes 1081352 | tf_op jit(solution)/shard_map/ppermute | solution.py:437
  172.4 19.8 %collective-permute-start.31 = (bf16[512,2816]{1,0:T(8,128)(2,1)S(1)}, bf16[512,2816]{1,0:T(8,128)(2,1)}, u32[]{:S(2)}, u32[]{:S(2)}) collective-permute-start(bf16[512,2816]{1,0:T(8,128)(2,1)S(1)} %pack_rows.8.un_ref), channel_id=1, source_target_pairs={{0,2},{1,3},{2,0},{3,1},{4,6},{5,7},{6,4},{7,5},{8,10},{9,11},{10,... | collective-permute-start | bytes 8650760 | tf_op jit(solution)/shard_map/ppermute | solution.py:437
  173.8 18.2 %collective-permute-start.33 = (bf16[128,2816]{1,0:T(8,128)(2,1)S(1)}, bf16[128,2816]{1,0:T(8,128)(2,1)S(1)}, u32[]{:S(2)}, u32[]{:S(2)}) collective-permute-start(bf16[128,2816]{1,0:T(8,128)(2,1)S(1)} %constant_dynamic-update-slice_fusion.8.refs_0_), channel_id=1, source_target_pairs={{0,4},{1,5},{2,6},{3,7},{4,0},{5,1},{6,2},{7,3},{8,12},{9,13},{10,... | collective-permute-start | bytes 2162696 | tf_op jit(solution)/shard_map/ppermute | solution.py:437
  174.4 17.8 %collective-permute-start.32 = (bf16[128,2816]{1,0:T(8,128)(2,1)S(1)}, bf16[128,2816]{1,0:T(8,128)(2,1)S(1)}, u32[]{:S(2)}, u32[]{:S(2)}) collective-permute-start(bf16[128,2816]{1,0:T(8,128)(2,1)S(1)} %constant_dynamic-update-slice_fusion.8.refs_0_), channel_id=1, source_target_pairs={{0,1},{1,0},{2,3},{3,2},{4,5},{5,4},{6,7},{7,6},{8,9},{9,8},{10,11... | collective-permute-start | bytes 2162696 | tf_op jit(solution)/shard_map/ppermute | solution.py:437
  192.3 26.1 %collective-permute-start.35 = (bf16[64,2816]{1,0:T(8,128)(2,1)S(1)}, bf16[64,2816]{1,0:T(8,128)(2,1)S(1)}, u32[]{:S(2)}, u32[]{:S(2)}) collective-permute-start(bf16[64,2816]{1,0:T(8,128)(2,1)S(1)} %slice.401), channel_id=1, source_target_pairs={{0,4},{1,5},{2,6},{3,7},{4,0},{5,1},{6,2},{7,3},{8,12},{9,13},{10,... | collective-permute-start | bytes 1081352 | tf_op jit(solution)/shard_map/ppermute | solution.py:437
  193.9 24.5 %collective-permute-start.34 = (bf16[64,2816]{1,0:T(8,128)(2,1)S(1)}, bf16[64,2816]{1,0:T(8,128)(2,1)S(1)}, u32[]{:S(2)}, u32[]{:S(2)}) collective-permute-start(bf16[64,2816]{1,0:T(8,128)(2,1)S(1)} %slice.400), channel_id=1, source_target_pairs={{0,1},{1,0},{2,3},{3,2},{4,5},{5,4},{6,7},{7,6},{8,9},{9,8},{10,11... | collective-permute-start | bytes 1081352 | tf_op jit(solution)/shard_map/ppermute | solution.py:437
  194.4 30.9 %collective-permute-start.36 = (bf16[512,1024]{1,0:T(8,128)(2,1)S(1)}, bf16[512,1024]{1,0:T(8,128)(2,1)S(1)}, u32[]{:S(2)}, u32[]{:S(2)}) collective-permute-start(bf16[512,1024]{1,0:T(8,128)(2,1)S(1)} %get-tuple-element.241), channel_id=1, source_target_pairs={{0,1},{1,0},{2,3},{3,2},{4,5},{5,4},{6,7},{7,6},{8,9},{9,8},{10,11... | collective-permute-start | bytes 3145736 | tf_op jit(solution)/shard_map/ppermute | solution.py:437
  250.3 30.2 %collective-permute-start.38 = (bf16[528,1024]{1,0:T(8,128)(2,1)S(1)}, bf16[528,1024]{1,0:T(8,128)(2,1)S(1)}, u32[]{:S(2)}, u32[]{:S(2)}) collective-permute-start(bf16[528,1024]{1,0:T(8,128)(2,1)S(1)} %slice.402), channel_id=1, source_target_pairs={{0,1},{1,0},{2,3},{3,2},{4,5},{5,4},{6,7},{7,6},{8,9},{9,8},{10,11... | collective-permute-start | bytes 3244040 | tf_op jit(solution)/shard_map/ppermute | solution.py:437
  292.7 9.8 %collective-permute-start.39 = (bf16[512,5632]{1,0:T(8,128)(2,1)}, bf16[512,5632]{1,0:T(8,128)(2,1)}, u32[]{:S(2)}, u32[]{:S(2)}) collective-permute-start(bf16[512,5632]{1,0:T(8,128)(2,1)} %weight_grads.8), channel_id=1, source_target_pairs={{0,2},{1,3},{2,0},{3,1},{4,6},{5,7},{6,4},{7,5},{8,10},{9,11},{10,... | collective-permute-start | bytes 17301512 | tf_op jit(solution)/shard_map/ppermute | solution.py:437
  302.5 17.4 %collective-permute-start.40 = (bf16[512,2816]{1,0:T(8,128)(2,1)S(1)}, bf16[512,2816]{1,0:T(8,128)(2,1)S(1)}, u32[]{:S(2)}, u32[]{:S(2)}) collective-permute-start(bf16[512,2816]{1,0:T(8,128)(2,1)S(1)} %weight_grads.9), channel_id=1, source_target_pairs={{0,2},{1,3},{2,0},{3,1},{4,6},{5,7},{6,4},{7,5},{8,10},{9,11},{10,... | collective-permute-start | bytes 8650760 | tf_op jit(solution)/shard_map/ppermute | solution.py:437
  322.9 23.6 %collective-permute-start.42 = (bf16[64,5632]{1,0:T(8,128)(2,1)S(1)}, bf16[64,5632]{1,0:T(8,128)(2,1)S(1)}, u32[]{:S(2)}, u32[]{:S(2)}) collective-permute-start(bf16[64,5632]{1,0:T(8,128)(2,1)S(1)} %get-tuple-element.351), channel_id=1, source_target_pairs={{0,1},{1,0},{2,3},{3,2},{4,5},{5,4},{6,7},{7,6},{8,9},{9,8},{10,11... | collective-permute-start | bytes 2162696 | tf_op jit(solution)/shard_map/ppermute | solution.py:437
  324.4 23.2 %collective-permute-start.41 = (bf16[64,5632]{1,0:T(8,128)(2,1)S(1)}, bf16[64,5632]{1,0:T(8,128)(2,1)S(1)}, u32[]{:S(2)}, u32[]{:S(2)}) collective-permute-start(bf16[64,5632]{1,0:T(8,128)(2,1)S(1)} %get-tuple-element.353), channel_id=1, source_target_pairs={{0,4},{1,5},{2,6},{3,7},{4,0},{5,1},{6,2},{7,3},{8,12},{9,13},{10,... | collective-permute-start | bytes 2162696 | tf_op jit(solution)/shard_map/ppermute | solution.py:437
  349.6 32.8 %collective-permute-start.44 = (bf16[128,5632]{1,0:T(8,128)(2,1)S(1)}, bf16[128,5632]{1,0:T(8,128)(2,1)S(1)}, u32[]{:S(2)}, u32[]{:S(2)}) collective-permute-start(bf16[128,5632]{1,0:T(8,128)(2,1)S(1)} %pad_maximum_fusion.1), channel_id=1, source_target_pairs={{0,1},{1,0},{2,3},{3,2},{4,5},{5,4},{6,7},{7,6},{8,9},{9,8},{10,11... | collective-permute-start | bytes 4325384 | tf_op jit(solution)/shard_map/ppermute | solution.py:437
  350.3 32.6 %collective-permute-start.43 = (bf16[128,5632]{1,0:T(8,128)(2,1)S(1)}, bf16[128,5632]{1,0:T(8,128)(2,1)}, u32[]{:S(2)}, u32[]{:S(2)}) collective-permute-start(bf16[128,5632]{1,0:T(8,128)(2,1)S(1)} %pad_maximum_fusion.2), channel_id=1, source_target_pairs={{0,4},{1,5},{2,6},{3,7},{4,0},{5,1},{6,2},{7,3},{8,12},{9,13},{10,... | collective-permute-start | bytes 4325384 | tf_op jit(solution)/shard_map/ppermute | solution.py:437
  385.4 16.2 %collective-permute-start.45 = (bf16[64,5632]{1,0:T(8,128)(2,1)S(1)}, bf16[64,5632]{1,0:T(8,128)(2,1)S(1)}, u32[]{:S(2)}, u32[]{:S(2)}) collective-permute-start(bf16[64,5632]{1,0:T(8,128)(2,1)S(1)} %slice.415), channel_id=1, source_target_pairs={{0,8},{1,9},{2,10},{3,11},{4,12},{5,13},{6,14},{7,15},{8,0},{9,1},... | collective-permute-start | bytes 2162696 | tf_op jit(solution)/shard_map/ppermute | solution.py:437
  386.0 15.0 %collective-permute-start.47 = (bf16[64,2816]{1,0:T(8,128)(2,1)S(1)}, bf16[64,2816]{1,0:T(8,128)(2,1)S(1)}, u32[]{:S(2)}, u32[]{:S(2)}) collective-permute-start(bf16[64,2816]{1,0:T(8,128)(2,1)S(1)} %get-tuple-element.357), channel_id=1, source_target_pairs={{0,1},{1,0},{2,3},{3,2},{4,5},{5,4},{6,7},{7,6},{8,9},{9,8},{10,11... | collective-permute-start | bytes 1081352 | tf_op jit(solution)/shard_map/ppermute | solution.py:437
  387.4 13.6 %collective-permute-start.46 = (bf16[64,2816]{1,0:T(8,128)(2,1)S(1)}, bf16[64,2816]{1,0:T(8,128)(2,1)S(1)}, u32[]{:S(2)}, u32[]{:S(2)}) collective-permute-start(bf16[64,2816]{1,0:T(8,128)(2,1)S(1)} %get-tuple-element.359), channel_id=1, source_target_pairs={{0,4},{1,5},{2,6},{3,7},{4,0},{5,1},{6,2},{7,3},{8,12},{9,13},{10,... | collective-permute-start | bytes 1081352 | tf_op jit(solution)/shard_map/ppermute | solution.py:437
  401.8 16.2 %collective-permute-start.48 = (bf16[32,5632]{1,0:T(8,128)(2,1)S(1)}, bf16[32,5632]{1,0:T(8,128)(2,1)S(1)}, u32[]{:S(2)}, u32[]{:S(2)}) collective-permute-start(bf16[32,5632]{1,0:T(8,128)(2,1)S(1)} %slice.423), channel_id=1, source_target_pairs={{0,16},{1,17},{2,18},{3,19},{4,20},{5,21},{6,22},{7,23},{8,24},{9,... | collective-permute-start | bytes 1081352 | tf_op jit(solution)/shard_map/ppermute | solution.py:437
  402.4 16.6 %collective-permute-start.50 = (bf16[128,2816]{1,0:T(8,128)(2,1)S(1)}, bf16[128,2816]{1,0:T(8,128)(2,1)S(1)}, u32[]{:S(2)}, u32[]{:S(2)}) collective-permute-start(bf16[128,2816]{1,0:T(8,128)(2,1)S(1)} %pad_maximum_fusion.4), channel_id=1, source_target_pairs={{0,1},{1,0},{2,3},{3,2},{4,5},{5,4},{6,7},{7,6},{8,9},{9,8},{10,11... | collective-permute-start | bytes 2162696 | tf_op jit(solution)/shard_map/ppermute | solution.py:437
  403.3 15.7 %collective-permute-start.49 = (bf16[128,2816]{1,0:T(8,128)(2,1)S(1)}, bf16[128,2816]{1,0:T(8,128)(2,1)S(1)}, u32[]{:S(2)}, u32[]{:S(2)}) collective-permute-start(bf16[128,2816]{1,0:T(8,128)(2,1)S(1)} %pad_maximum_fusion.5), channel_id=1, source_target_pairs={{0,4},{1,5},{2,6},{3,7},{4,0},{5,1},{6,2},{7,3},{8,12},{9,13},{10,... | collective-permute-start | bytes 2162696 | tf_op jit(solution)/shard_map/ppermute | solution.py:437
  419.3 9.6 %collective-permute-start.51 = (bf16[64,2816]{1,0:T(8,128)(2,1)S(1)}, bf16[64,2816]{1,0:T(8,128)(2,1)S(1)}, u32[]{:S(2)}, u32[]{:S(2)}) collective-permute-start(bf16[64,2816]{1,0:T(8,128)(2,1)S(1)} %slice.426), channel_id=1, source_target_pairs={{0,8},{1,9},{2,10},{3,11},{4,12},{5,13},{6,14},{7,15},{8,0},{9,1},... | collective-permute-start | bytes 1081352 | tf_op jit(solution)/shard_map/ppermute | solution.py:437
  429.0 13.3 %collective-permute-start.53 = (bf16[32,2816]{1,0:T(8,128)(2,1)S(1)}, bf16[32,2816]{1,0:T(8,128)(2,1)S(1)}, u32[]{:S(2)}, u32[]{:S(2)}) collective-permute-start(bf16[32,2816]{1,0:T(8,128)(2,1)S(1)} %slice.428), channel_id=1, source_target_pairs={{0,16},{1,17},{2,18},{3,19},{4,20},{5,21},{6,22},{7,23},{8,24},{9,... | collective-permute-start | bytes 540680 | tf_op jit(solution)/shard_map/ppermute | solution.py:437
  429.5 13.7 %collective-permute-start.52 = (bf16[512,2560]{1,0:T(8,128)(2,1)}, bf16[512,2560]{1,0:T(8,128)(2,1)S(1)}, u32[]{:S(2)}, u32[]{:S(2)}) collective-permute-start(bf16[512,2560]{1,0:T(8,128)(2,1)} %weight_grads.12), channel_id=1, source_target_pairs={{0,2},{1,3},{2,0},{3,1},{4,6},{5,7},{6,4},{7,5},{8,10},{9,11},{10,... | collective-permute-start | bytes 7864328 | tf_op jit(solution)/shard_map/ppermute | solution.py:437
  453.8 17.2 %collective-permute-start.54 = (bf16[128,2560]{1,0:T(8,128)(2,1)S(1)}, bf16[128,2560]{1,0:T(8,128)(2,1)S(1)}, u32[]{:S(2)}, u32[]{:S(2)}) collective-permute-start(bf16[128,2560]{1,0:T(8,128)(2,1)S(1)} %get-tuple-element.362), channel_id=1, source_target_pairs={{0,4},{1,5},{2,6},{3,7},{4,0},{5,1},{6,2},{7,3},{8,12},{9,13},{10,... | collective-permute-start | bytes 1966088 | tf_op jit(solution)/shard_map/ppermute | solution.py:437
  475.9 16.7 %collective-permute-start.57 = (bf16[128,2560]{1,0:T(8,128)(2,1)}, bf16[128,2560]{1,0:T(8,128)(2,1)}, u32[]{:S(2)}, u32[]{:S(2)}) collective-permute-start(bf16[128,2560]{1,0:T(8,128)(2,1)} %add_convert_fusion.7), channel_id=1, source_target_pairs={{0,1},{1,0},{2,3},{3,2},{4,5},{5,4},{6,7},{7,6},{8,9},{9,8},{10,11... | collective-permute-start | bytes 1966088 | tf_op jit(solution)/shard_map/ppermute | solution.py:437
  477.7 16.1 %collective-permute-start.56 = (bf16[128,2560]{1,0:T(8,128)(2,1)S(1)}, bf16[128,2560]{1,0:T(8,128)(2,1)}, u32[]{:S(2)}, u32[]{:S(2)}) collective-permute-start(bf16[128,2560]{1,0:T(8,128)(2,1)S(1)} %get-tuple-element.321), channel_id=1, source_target_pairs={{0,4},{1,5},{2,6},{3,7},{4,0},{5,1},{6,2},{7,3},{8,12},{9,13},{10,... | collective-permute-start | bytes 1966088 | tf_op jit(solution)/shard_map/ppermute | solution.py:437
  478.2 17.2 %collective-permute-start.55 = (bf16[512,1536]{1,0:T(8,128)(2,1)S(1)}, bf16[512,1536]{1,0:T(8,128)(2,1)}, u32[]{:S(2)}, u32[]{:S(2)}) collective-permute-start(bf16[512,1536]{1,0:T(8,128)(2,1)S(1)} %weight_grads.14), channel_id=1, source_target_pairs={{0,2},{1,3},{2,0},{3,1},{4,6},{5,7},{6,4},{7,5},{8,10},{9,11},{10,... | collective-permute-start | bytes 4718600 | tf_op jit(solution)/shard_map/ppermute | solution.py:437
  499.8 14.0 %collective-permute-start.59 = (bf16[64,2560]{1,0:T(8,128)(2,1)S(1)}, bf16[64,2560]{1,0:T(8,128)(2,1)S(1)}, u32[]{:S(2)}, u32[]{:S(2)}) collective-permute-start(bf16[64,2560]{1,0:T(8,128)(2,1)S(1)} %slice.438), channel_id=1, source_target_pairs={{0,8},{1,9},{2,10},{3,11},{4,12},{5,13},{6,14},{7,15},{8,0},{9,1},... | collective-permute-start | bytes 983048 | tf_op jit(solution)/shard_map/ppermute | solution.py:437
  500.9 17.9 %collective-permute-start.60 = (bf16[256,1536]{1,0:T(8,128)(2,1)S(1)}, bf16[256,1536]{1,0:T(8,128)(2,1)S(1)}, u32[]{:S(2)}, u32[]{:S(2)}) collective-permute-start(bf16[256,1536]{1,0:T(8,128)(2,1)S(1)} %pad_maximum_fusion.3), channel_id=1, source_target_pairs={{0,4},{1,5},{2,6},{3,7},{4,0},{5,1},{6,2},{7,3},{8,12},{9,13},{10,... | collective-permute-start | bytes 2359304 | tf_op jit(solution)/shard_map/ppermute | solution.py:437
  519.1 8.1 %collective-permute-start.61 = (bf16[32,2560]{1,0:T(8,128)(2,1)S(1)}, bf16[32,2560]{1,0:T(8,128)(2,1)S(1)}, u32[]{:S(2)}, u32[]{:S(2)}) collective-permute-start(bf16[32,2560]{1,0:T(8,128)(2,1)S(1)} %slice.444), channel_id=1, source_target_pairs={{0,16},{1,17},{2,18},{3,19},{4,20},{5,21},{6,22},{7,23},{8,24},{9,... | collective-permute-start | bytes 491528 | tf_op jit(solution)/shard_map/ppermute | solution.py:437
  521.6 23.0 %collective-permute-start.58 = (bf16[528,1024]{1,0:T(8,128)(2,1)S(1)}, bf16[528,1024]{1,0:T(8,128)(2,1)S(1)}, u32[]{:S(2)}, u32[]{:S(2)}) collective-permute-start(bf16[528,1024]{1,0:T(8,128)(2,1)S(1)} %copy-done.59), channel_id=1, source_target_pairs={{0,1},{1,0},{2,3},{3,2},{4,5},{5,4},{6,7},{7,6},{8,9},{9,8},{10,11... | collective-permute-start | bytes 3244040 | tf_op jit(solution)/shard_map/ppermute | solution.py:437
  548.2 17.7 %collective-permute-start.62 = (bf16[128,1536]{1,0:T(8,128)(2,1)S(1)}, bf16[128,1536]{1,0:T(8,128)(2,1)S(1)}, u32[]{:S(2)}, u32[]{:S(2)}) collective-permute-start(bf16[128,1536]{1,0:T(8,128)(2,1)S(1)} %slice.448), channel_id=1, source_target_pairs={{0,1},{1,0},{2,3},{3,2},{4,5},{5,4},{6,7},{7,6},{8,9},{9,8},{10,11... | collective-permute-start | bytes 1179656 | tf_op jit(solution)/shard_map/ppermute | solution.py:437
  549.6 10.3 %collective-permute-start.66 = (f32[256,8]{0,1:T(8,128)S(1)}, f32[256,8]{0,1:T(8,128)S(1)}, u32[]{:S(2)}, u32[]{:S(2)}) collective-permute-start(f32[256,8]{0,1:T(8,128)S(1)} %slice.516), channel_id=1, source_target_pairs={{0,1},{1,0},{2,3},{3,2},{4,5},{5,4},{6,7},{7,6},{8,9},{9,8},{10,11... | collective-permute-start | bytes 24584 | tf_op jit(solution)/shard_map/ppermute | solution.py:437
  566.0 6.1 %collective-permute-start.63 = (bf16[64,1536]{1,0:T(8,128)(2,1)S(1)}, bf16[64,1536]{1,0:T(8,128)(2,1)S(1)}, u32[]{:S(2)}, u32[]{:S(2)}) collective-permute-start(bf16[64,1536]{1,0:T(8,128)(2,1)S(1)} %slice.494), channel_id=1, source_target_pairs={{0,8},{1,9},{2,10},{3,11},{4,12},{5,13},{6,14},{7,15},{8,0},{9,1},... | collective-permute-start | bytes 589832 | tf_op jit(solution)/shard_map/ppermute | solution.py:437
  572.2 6.5 %collective-permute-start.64 = (bf16[32,1536]{1,0:T(8,128)(2,1)S(1)}, bf16[32,1536]{1,0:T(8,128)(2,1)S(1)}, u32[]{:S(2)}, u32[]{:S(2)}) collective-permute-start(bf16[32,1536]{1,0:T(8,128)(2,1)S(1)} %slice.496), channel_id=1, source_target_pairs={{0,16},{1,17},{2,18},{3,19},{4,20},{5,21},{6,22},{7,23},{8,24},{9,... | collective-permute-start | bytes 294920 | tf_op jit(solution)/shard_map/ppermute | solution.py:437
  (98 other events, 1471.4 us)
Sparse Core Ops, SparseCore 0:
  292.9 60.6 all-gather.2

commit v5 on v4

--- a/solution.py
+++ b/solution.py
@@ -1093,16 +1093,17 @@
 
     z_one = g_low.along_z0()
     z_low = g_low.along_z1()
-    g_high.along_z0(z_one)
+    z_one = g_high.along_z0(z_one)
+    z_one = g_gate.along_z0(z_one)
     xy_low = g_low.along_xy()
     z_high = g_high.along_z1(z_low)
     corner_low = g_low.corners(image_far)
-    z_one = g_gate.along_z0(z_high)
     xy_high = g_high.along_xy(xy_low)
     near_low = g_low.whole(z_high)
 
-    gate = near_low, g_low.far, image_rows, z_one
+    gate = near_low, g_low.far, image_rows, z_one, xy_high
     z_gate = g_gate.along_z1(gate)
+    corner_high = g_high.corners(gate)
     vectors, head_biases = gathered_vectors(near_low, g_low.far, order)
     tokens, normed = over_rows(
         start_kernel, "start", [ready(image_rows, gate)], [order, vectors], [(WIDTH, BF16), (WIDTH, BF16)],
@@ -1115,14 +1116,13 @@
             ready(normed, gate), group.near, group.far, head_biases, block, block % 2, tables
         )
 
-    gate = normed, xy_high, z_gate
+    gate = normed, z_gate, corner_high
     z_up = g_up.along_z0(gate)
-    corner_high = g_high.corners(gate)
+    near_high = g_high.whole(gate)
     xy_gate = g_gate.along_xy(gate)
     heads = [attend(0, gate)]
 
-    gate = heads[0][3], corner_high, xy_gate, z_up
-    near_high = g_high.whole(gate)
+    gate = heads[0][3], xy_gate, z_up
     corner_gate = g_gate.corners(gate)
     z_up = g_up.along_z1(gate)
     heads.append(attend(1, gate))
@@ -1272,9 +1272,9 @@
     high_stage = high.over_y(gate)
     near_part, near_sums = last_rows(gate, 0, HALF)
 
-    gate = near_part, low_stage, high_stage
+    gate = near_part, low_stage, high_stage, far_rows
     low_grad = low.along_z0(gate)
-    high.over_x(gate, far_rows)
+    high.over_x(gate)
     high.along_z1()
     high_grad = high.along_z0()
     sums = [far_sums, near_sums, middle_sums, branch_sums] + [part[3] for part in parts]

time: 593 us -> 579 us (0.976)
  waiting for transfers between devices: 145 us -> 119 us
  other arithmetic: 29.2 us -> 35.7 us
    ppermute x70, waiting for transfers between devices: 145 us -> 119 us  [swap_over(): return lax.ppermute(value, BOTH, [(i, i ^ bit) for i in range(count)])]
    unnamed x188 -> x186, local copies, waits for them, and re-layouts: 12.2 us -> 14.6 us
  transfers between devices with their start and end apart: 71 -> 71, of which waited for: 33 -> 33; matrix products, arithmetic and copies ran while one was open for 9% -> 10% of each run, Pallas kernels for 45% -> 47%
where the time goes in v5:
time: 579 us; the launch traced here: 573 us
  Pallas kernels  295 us (51%)
  waiting for transfers between devices  119 us (21%)
  starting transfers between devices  64.3 us (11%)
  local copies, waits for them, and re-layouts  39.6 us (7%)
  other arithmetic  35.7 us (6%)
  between operations  16.7 us (3%)
    pallas_call x8, Pallas kernels, over_rows(): pl.pallas_call(kernel, grid=(rows // step,), in_specs=in_specs, out_specs...  130 us
    ppermute x70, waiting for transfers between devices, swap_over(): return lax.ppermute(value, BOTH, [(i, i ^ bit) for i in range(count)])  119 us
    ppermute x70, starting transfers between devices, swap_over(): return lax.ppermute(value, BOTH, [(i, i ^ bit) for i in range(count)])  64.2 us
    pallas_call x8, Pallas kernels, weight_grads(): pl.pallas_call(kernel, grid=(len(steps),), in_specs=[pl.BlockSpec((ROWS,...  59.7 us
    pallas_call x4, Pallas kernels, attention_backward(): pl.pallas_call(functools.partial(attention_back_kernel, step=step), grid=...  50.2 us
    pallas_call x4, Pallas kernels, attention_forward(): pl.pallas_call(attention_kernel, grid=(1,), in_specs=[whole(x)] + [block(...  47.7 us
    unnamed x186, local copies, waits for them, and re-layouts  14.6 us
  transfers between devices with their start and end apart: 71, of which 33 were waited for; matrix products, arithmetic and copies ran while one was open for 10% of the time, Pallas kernels for 47%

profile of v5, /device:TPU:0, one launch (start us, length us, event | category | flops | bytes accessed | tf_op | source)
XLA Modules:
  0.0 572.6 jit_solution(13079505523261851877)
XLA Ops:
  7.3 3.0 collective-permute-start.16
  12.6 2.7 collective-permute-start.1
  15.3 1.7 dynamic-slice_bitcast_fusion.3
  19.7 2.9 fusion.59.order_ref.refs_19_
  31.4 1.8 collective-permute-start.3
  33.1 4.5 collective-permute-done.7
  37.7 2.2 collective-permute-done.4.refs_1_
  39.9 10.7 %collective-permute-done.3.refs_2_ = bf16[128,1664]{1,0:T(8,128)(2,1)S(1)} collective-permute-done((bf16[128,1664]{1,0:T(8,128)(2,1)S(1)}, bf16[128,1664]{1,0:T(8,128)(2,1)S(1)}, u32[]{:S(2)}, u32[]{:S(2)}) %collective-permute-start.3) | collective-permute-done | bytes 426016 | tf_op jit(solution)/shard_map/ppermute | solution.py:437
  53.1 3.4 collective-permute-done.6.refs_4_
  58.3 2.8 fusion.34
  62.6 10.2 %collective-permute-done.10 = bf16[32,2816]{1,0:T(8,128)(2,1)S(1)} collective-permute-done((bf16[32,2816]{1,0:T(8,128)(2,1)S(1)}, bf16[32,2816]{1,0:T(8,128)(2,1)S(1)}, u32[]{:S(2)}, u32[]{:S(2)}) %collective-permute-start.10) | collective-permute-done | bytes 180256 | tf_op jit(solution)/shard_map/ppermute | solution.py:437
  72.8 2.9 fusion.32.rows_ref
  75.7 2.7 collective-permute-done.12.refs_1_
  83.9 3.0 vectors.1
  86.9 7.6 %start.1 = (bf16[1040,1024]{1,0:T(8,128)(2,1)}, bf16[1040,1024]{1,0:T(8,128)(2,1)}) custom-call(bf16[1040,1024]{1,0:T(8,128)(2,1)} %fusion.32.rows_ref, bf16[1024,1024]{1,0:T(8,128)(2,1)} %fusion.59.order_ref.refs_19_, f32[8,1024]{1,0:T(8,128)} %get-tuple-element.193.vec_ref.refs_18_), custom_call_target="tpu_custom_call" | custom-call | flops 8800000000 | bytes 34078720 | tf_op jit(solution)/shard_map/start/pallas_call | solution.py:779
  103.4 2.6 collective-permute-start.19
  106.1 11.8 %attention_forward.4 = (bf16[1040,256]{1,0:T(8,128)(2,1)}, bf16[1040,256]{1,0:T(8,128)(2,1)}, bf16[1040,256]{1,0:T(8,128)(2,1)}, bf16[1040,256]{1,0:T(8,128)(2,1)}, f32[8,1040]{1,0:T(8,128)}) custom-call(bf16[1040,1024]{1,0:T(8,128)(2,1)} %get-tuple-element.323.x_ref.refs_1_.refs_0_, bf16[512,1664]{1,0:T(8,128)(2,1)} %copy-done.2, ...), custom_call_target="tpu_custom_call" | custom-call | flops 30000001024 | bytes 28000000 | tf_op jit(solution)/shard_map/attention_forward/pallas_call | solution.py:641
  120.5 11.9 %attention_forward.5 = (bf16[1040,256]{1,0:T(8,128)(2,1)}, bf16[1040,256]{1,0:T(8,128)(2,1)}, bf16[1040,256]{1,0:T(8,128)(2,1)}, bf16[1040,256]{1,0:T(8,128)(2,1)}, f32[8,1040]{1,0:T(8,128)}) custom-call(bf16[1040,1024]{1,0:T(8,128)(2,1)} %get-tuple-element.323.x_ref.refs_1_.refs_0_, bf16[512,1664]{1,0:T(8,128)(2,1)} %copy-done.2, ...), custom_call_target="tpu_custom_call" | custom-call | flops 30000001024 | bytes 28000000 | tf_op jit(solution)/shard_map/attention_forward/pallas_call | solution.py:641
  139.3 11.8 %attention_forward.6 = (bf16[1040,256]{1,0:T(8,128)(2,1)}, bf16[1040,256]{1,0:T(8,128)(2,1)}, bf16[1040,256]{1,0:T(8,128)(2,1)}, bf16[1040,256]{1,0:T(8,128)(2,1)}, f32[8,1040]{1,0:T(8,128)}) custom-call(bf16[1040,1024]{1,0:T(8,128)(2,1)} %get-tuple-element.323.x_ref.refs_1_.refs_0_, bf16[512,2560]{1,0:T(8,128)(2,1)} %copy-done.6, ...), custom_call_target="tpu_custom_call" | custom-call | flops 30000001024 | bytes 28000000 | tf_op jit(solution)/shard_map/attention_forward/pallas_call | solution.py:641
  157.6 12.2 %attention_forward.7 = (bf16[1040,256]{1,0:T(8,128)(2,1)}, bf16[1040,256]{1,0:T(8,128)(2,1)}, bf16[1040,256]{1,0:T(8,128)(2,1)}, bf16[1040,256]{1,0:T(8,128)(2,1)}, f32[8,1040]{1,0:T(8,128)}) custom-call(bf16[1040,1024]{1,0:T(8,128)(2,1)} %get-tuple-element.323.x_ref.refs_1_.refs_0_, bf16[512,2560]{1,0:T(8,128)(2,1)} %copy-done.6, ...), custom_call_target="tpu_custom_call" | custom-call | flops 30000001024 | bytes 28000000 | tf_op jit(solution)/shard_map/attention_forward/pallas_call | solution.py:641
  174.0 7.2 %middle.1 = (bf16[1040,1024]{1,0:T(8,128)(2,1)}, bf16[1040,1024]{1,0:T(8,128)(2,1)}) custom-call(bf16[1040,256]{1,0:T(8,128)(2,1)} %get-tuple-element.200.a0_ref.o_ref.refs_2_, bf16[1040,256]{1,0:T(8,128)(2,1)} %get-tuple-element.204.a1_ref.o_ref.refs_3_, bf16[1040,256]{1,0:T(8,128)(2,1)} %get-tuple-element.214.a2_ref.refs_4_.o_ref, ...), custom_call_target="tpu_custom_call" | custom-call | flops 8800000000 | bytes 76152832 | tf_op jit(solution)/shard_map/middle/pallas_call | solution.py:779
  181.2 9.8 %collective-permute-done.33.refs_1_ = bf16[128,2816]{1,0:T(8,128)(2,1)S(1)} collective-permute-done((bf16[128,2816]{1,0:T(8,128)(2,1)S(1)}, bf16[128,2816]{1,0:T(8,128)(2,1)S(1)}, u32[]{:S(2)}, u32[]{:S(2)}) %collective-permute-start.33) | collective-permute-done | bytes 720928 | tf_op jit(solution)/shard_map/ppermute | solution.py:437
  194.9 22.5 %hidden.1 = (bf16[1040,2816]{1,0:T(8,128)(2,1)}, bf16[1040,2816]{1,0:T(8,128)(2,1)}, bf16[1040,2816]{1,0:T(8,128)(2,1)}, f32[1040,128]{1,0:T(8,128)}) custom-call(bf16[1040,1024]{1,0:T(8,128)(2,1)} %get-tuple-element.264.x_ref.refs_0_, bf16[512,2816]{1,0:T(8,128)(2,1)} %copy-done.3, bf16[512,2816]{1,0:T(8,128)(2,1)} %collective-permute-done.26.gf_ref, ...), custom_call_target="tpu_custom_call" | custom-call | flops 48000000000 | bytes 127434752 | tf_op jit(solution)/shard_map/hidden/pallas_call | solution.py:779
  217.4 6.9 %collective-permute-done.36 = bf16[512,1024]{1,0:T(8,128)(2,1)S(1)} collective-permute-done((bf16[512,1024]{1,0:T(8,128)(2,1)S(1)}, bf16[512,1024]{1,0:T(8,128)(2,1)S(1)}, u32[]{:S(2)}, u32[]{:S(2)}) %collective-permute-start.36) | collective-permute-done | bytes 1048608 | tf_op jit(solution)/shard_map/ppermute | solution.py:437
  229.1 2.2 collective-permute-done.37.far_ref
  233.5 14.5 %result.1 = bf16[1040,1024]{1,0:T(8,128)(2,1)} custom-call(bf16[1040,2816]{1,0:T(8,128)(2,1)} %get-tuple-element.237.inner_ref.refs_1_, bf16[1040,1024]{1,0:T(8,128)(2,1)} %get-tuple-element.268.middle_ref, bf16[512,2816]{1,0:T(8,128)(2,1)} %copy-done.5, bf16[512,2816]{1,0:T(8,128)(2,1)} %copy-done.86, f32[8,1024]{1,0:T(8,128)} %get-tuple-element.193.vec_ref.refs_18_, ...), custom_call_target="tpu_custom_call" | custom-call | flops 32000000000 | bytes 72073216 | tf_op jit(solution)/shard_map/result/pallas_call | solution.py:779
  250.0 29.6 %hidden_back.1 = (bf16[1040,1024]{1,0:T(8,128)(2,1)}, bf16[1040,2816]{1,0:T(8,128)(2,1)}, bf16[1040,2816]{1,0:T(8,128)(2,1)}, f32[8,2816]{1,0:T(8,128)}, f32[8,1024]{1,0:T(8,128)}) custom-call(bf16[1040,1024]{1,0:T(8,128)(2,1)} %fusion.33.d_ref, bf16[1040,2816]{1,0:T(8,128)(2,1)} %get-tuple-element.254.gate_ref, ...), custom_call_target="tpu_custom_call" | custom-call | flops 32000000000 | bytes 145211392 | tf_op jit(solution)/shard_map/hidden_back/pallas_call | solution.py:779
  279.6 12.0 %weight_grads.8 = bf16[512,5632]{1,0:T(8,128)(2,1)} custom-call(bf16[1040,1024]{1,0:T(8,128)(2,1)S(1)} %copy-done.20, bf16[1040,2816]{1,0:T(8,128)(2,1)} %get-tuple-element.257.refs_1_.dgate_ref, bf16[1040,2816]{1,0:T(8,128)(2,1)} %get-tuple-element.258.refs_2_.dup_ref), custom_call_target="tpu_custom_call" | custom-call | flops 23991418880 | bytes 70287360 | tf_op jit(solution)/shard_map/weight_grads/pallas_call | solution.py:1010
  293.3 5.8 %weight_grads.9 = bf16[512,2816]{1,0:T(8,128)(2,1)S(1)} custom-call(bf16[1040,1024]{1,0:T(8,128)(2,1)S(1)} %copy-done.21, bf16[1040,2816]{1,0:T(8,128)(2,1)} %get-tuple-element.237.inner_ref.refs_1_), custom_call_target="tpu_custom_call" | custom-call | flops 11995709440 | bytes 35143680 | tf_op jit(solution)/shard_map/weight_grads/pallas_call | solution.py:1010
  299.2 2.3 collective-permute-done.39.refs_3_
  306.0 12.9 %weight_grads.10 = bf16[512,5632]{1,0:T(8,128)(2,1)} custom-call(bf16[1040,1024]{1,0:T(8,128)(2,1)S(1)} %copy-done.20, bf16[1040,2816]{1,0:T(8,128)(2,1)} %get-tuple-element.257.refs_1_.dgate_ref, bf16[1040,2816]{1,0:T(8,128)(2,1)} %get-tuple-element.258.refs_2_.dup_ref, bf16[512,5632]{1,0:T(8,128)(2,1)} %collective-permute-done.39.refs_3_), custom_call_target="tpu_custom_call" | custom-call | flops 23991418880 | bytes 70287360 | tf_op jit(solution)/shard_map/weight_grads/pallas_call | solution.py:1010
  318.8 3.0 fusion.60
  323.9 6.8 %weight_grads.11 = bf16[512,2816]{1,0:T(8,128)(2,1)S(1)} custom-call(bf16[1040,1024]{1,0:T(8,128)(2,1)S(1)} %copy-done.21, bf16[1040,2816]{1,0:T(8,128)(2,1)} %get-tuple-element.237.inner_ref.refs_1_, bf16[512,2816]{1,0:T(8,128)(2,1)} %copy-done.87), custom_call_target="tpu_custom_call" | custom-call | flops 11995709440 | bytes 35143680 | tf_op jit(solution)/shard_map/weight_grads/pallas_call | solution.py:1010
  330.7 14.7 %collective-permute-done.42 = bf16[64,5632]{1,0:T(8,128)(2,1)S(1)} collective-permute-done((bf16[64,5632]{1,0:T(8,128)(2,1)S(1)}, bf16[64,5632]{1,0:T(8,128)(2,1)S(1)}, u32[]{:S(2)}, u32[]{:S(2)}) %collective-permute-start.42) | collective-permute-done | bytes 720928 | tf_op jit(solution)/shard_map/ppermute | solution.py:437
  346.7 1.8 add_convert_fusion.4
  349.8 26.4 %middle_back.1 = (bf16[1040,1024]{1,0:T(8,128)(2,1)}, bf16[1040,256]{1,0:T(8,128)(2,1)}, bf16[1040,256]{1,0:T(8,128)(2,1)}, bf16[1040,256]{1,0:T(8,128)(2,1)}, b...) custom-call(bf16[1040,2816]{1,0:T(8,128)(2,1)} %get-tuple-element.257.refs_1_.dgate_ref, ...), custom_call_target="tpu_custom_call" | custom-call | flops 56000000000 | bytes 169279488 | tf_op jit(solution)/shard_map/middle_back/pallas_call | solution.py:779
  376.3 5.3 collective-permute-done.44
  381.9 2.4 add_convert_fusion
  387.0 12.7 %attention_backward.4 = (bf16[1040,256]{1,0:T(8,128)(2,1)S(1)}, bf16[1040,256]{1,0:T(8,128)(2,1)S(1)}, bf16[1040,256]{1,0:T(8,128)(2,1)S(1)}, f32[8,256]{1,0:T(8,128)S(1)}) custom-call(bf16[1040,256]{1,0:T(8,128)(2,1)S(1)} %copy-done.53, bf16[1040,256]{1,0:T(8,128)(2,1)S(1)} %copy-done.54, bf16[1040,256]{1,0:T(8,128)(2,1)S(1)} %copy-done.55, ...), custom_call_target="tpu_custom_call" | custom-call | flops 51999997952 | bytes 20000000 | tf_op jit(solution)/shard_map/attention_backward/pallas_call | solution.py:741
  403.1 12.5 %attention_backward.5 = (bf16[1040,256]{1,0:T(8,128)(2,1)S(1)}, bf16[1040,256]{1,0:T(8,128)(2,1)S(1)}, bf16[1040,256]{1,0:T(8,128)(2,1)S(1)}, f32[8,256]{1,0:T(8,128)S(1)}) custom-call(bf16[1040,256]{1,0:T(8,128)(2,1)S(1)} %copy-done.50, bf16[1040,256]{1,0:T(8,128)(2,1)S(1)} %copy-done.51, bf16[1040,256]{1,0:T(8,128)(2,1)S(1)} %copy-done.52, ...), custom_call_target="tpu_custom_call" | custom-call | flops 51999997952 | bytes 20000000 | tf_op jit(solution)/shard_map/attention_backward/pallas_call | solution.py:741
  418.6 6.6 %weight_grads.12 = bf16[512,2560]{1,0:T(8,128)(2,1)} custom-call(bf16[1040,1024]{1,0:T(8,128)(2,1)} %get-tuple-element.324.refs_0_.refs_12_, bf16[1040,1024]{1,0:T(8,128)(2,1)} %get-tuple-element.323.x_ref.refs_1_.refs_0_, bf16[1040,256]{1,0:T(8,128)(2,1)S(1)} %copy-done.34, bf16[1040,256]{1,0:T(8,128)(2,1)S(1)} %copy-done.35, ...), custom_call_target="tpu_custom_call" | custom-call | flops 10905190400 | bytes 31948800 | tf_op jit(solution)/shard_map/weight_grads/pallas_call | solution.py:1010
  425.2 3.0 collective-permute-done.51
  428.6 12.7 %attention_backward.6 = (bf16[1040,256]{1,0:T(8,128)(2,1)S(1)}, bf16[1040,256]{1,0:T(8,128)(2,1)S(1)}, bf16[1040,256]{1,0:T(8,128)(2,1)S(1)}, f32[8,256]{1,0:T(8,128)S(1)}) custom-call(bf16[1040,256]{1,0:T(8,128)(2,1)S(1)} %copy-done.47, bf16[1040,256]{1,0:T(8,128)(2,1)S(1)} %copy-done.48, bf16[1040,256]{1,0:T(8,128)(2,1)S(1)} %copy-done.49, ...), custom_call_target="tpu_custom_call" | custom-call | flops 51999997952 | bytes 20000000 | tf_op jit(solution)/shard_map/attention_backward/pallas_call | solution.py:741
  443.8 7.6 %weight_grads.13 = bf16[512,2560]{1,0:T(8,128)(2,1)} custom-call(bf16[1040,1024]{1,0:T(8,128)(2,1)} %get-tuple-element.324.refs_0_.refs_12_, bf16[1040,1024]{1,0:T(8,128)(2,1)} %get-tuple-element.323.x_ref.refs_1_.refs_0_, bf16[1040,256]{1,0:T(8,128)(2,1)S(1)} %copy-done.34, bf16[1040,256]{1,0:T(8,128)(2,1)S(1)} %copy-done.35, ...), custom_call_target="tpu_custom_call" | custom-call | flops 10905190400 | bytes 31948800 | tf_op jit(solution)/shard_map/weight_grads/pallas_call | solution.py:1010
  451.4 2.2 fusion.62
  455.1 12.3 %attention_backward.7 = (bf16[1040,256]{1,0:T(8,128)(2,1)S(1)}, bf16[1040,256]{1,0:T(8,128)(2,1)S(1)}, bf16[1040,256]{1,0:T(8,128)(2,1)S(1)}, f32[8,256]{1,0:T(8,128)S(1)}) custom-call(bf16[1040,256]{1,0:T(8,128)(2,1)S(1)} %copy-done.44, bf16[1040,256]{1,0:T(8,128)(2,1)S(1)} %copy-done.45, bf16[1040,256]{1,0:T(8,128)(2,1)S(1)} %copy-done.46, ...), custom_call_target="tpu_custom_call" | custom-call | flops 51999997952 | bytes 20000000 | tf_op jit(solution)/shard_map/attention_backward/pallas_call | solution.py:741
  467.5 3.3 collective-permute-done.54
  471.9 3.7 weight_grads.14
  475.7 1.9 collective-permute-start.57
  477.9 11.4 %last.2 = (bf16[528,1024]{1,0:T(8,128)(2,1)}, f32[8,1024]{1,0:T(8,128)}) custom-call(bf16[1040,256]{1,0:T(8,128)(2,1)} %copy-done.38, bf16[1040,256]{1,0:T(8,128)(2,1)} %copy-done.39, bf16[1040,256]{1,0:T(8,128)(2,1)} %copy-done.40, bf16[1040,256]{1,0:T(8,128)(2,1)} %copy-done.41, bf16[1040,256]{1,0:T(8,128)(2,1)} %copy-done.42, ...), custom_call_target="tpu_custom_call" | custom-call | flops 17999998976 | bytes 90177536 | tf_op jit(solution)/shard_map/last/pallas_call | solution.py:779
  489.3 3.2 collective-permute-done.57
  495.7 4.3 weight_grads.15
  503.7 11.2 %last.3 = (bf16[512,1024]{1,0:T(8,128)(2,1)}, f32[8,1024]{1,0:T(8,128)}) custom-call(bf16[1040,256]{1,0:T(8,128)(2,1)} %copy-done.38, bf16[1040,256]{1,0:T(8,128)(2,1)} %copy-done.39, bf16[1040,256]{1,0:T(8,128)(2,1)} %copy-done.40, bf16[1040,256]{1,0:T(8,128)(2,1)} %copy-done.41, bf16[1040,256]{1,0:T(8,128)(2,1)} %copy-done.42, ...), custom_call_target="tpu_custom_call" | custom-call | flops 17999998976 | bytes 90046464 | tf_op jit(solution)/shard_map/last/pallas_call | solution.py:779
  514.9 1.7 pad_maximum_fusion
  517.7 7.8 %collective-permute-done.58 = bf16[528,1024]{1,0:T(8,128)(2,1)S(1)} collective-permute-done((bf16[528,1024]{1,0:T(8,128)(2,1)}, bf16[528,1024]{1,0:T(8,128)(2,1)S(1)}, u32[]{:S(2)}, u32[]{:S(2)}) %collective-permute-start.58) | collective-permute-done | bytes 1081376 | tf_op jit(solution)/shard_map/ppermute | solution.py:437
  525.5 1.9 fusion.37
  531.1 2.0 reduce_sum.9
  533.7 2.8 collective-permute-start.61
  538.1 2.8 collective-permute-done.67
  541.0 1.7 collective-permute-start.68
  546.2 3.0 collective-permute-done.69
  550.0 1.7 collective-permute-start.63
  552.4 4.4 collective-permute-done.63
  556.9 6.5 %collective-permute-done.64 = bf16[32,1536]{1,0:T(8,128)(2,1)S(1)} collective-permute-done((bf16[32,1536]{1,0:T(8,128)(2,1)S(1)}, bf16[32,1536]{1,0:T(8,128)(2,1)S(1)}, u32[]{:S(2)}, u32[]{:S(2)}) %collective-permute-start.64) | collective-permute-done | bytes 98336 | tf_op jit(solution)/shard_map/ppermute | solution.py:437
  (418 shorter events, 112.8 us)
Async XLA Ops:
  7.2 523.9 %all-gather.3.cloned.1.call-start = ((), (), s32[]{:S(2)}) async-start(), calls=%async_computation | async-start | bytes 2973696 | tf_op jit(solution)/shard_map/all_gather | solution.py:1178
  7.3 20.5 %collective-permute-start.16 = (s32[512,2]{0,1:T(2,128)}, s32[512,2]{0,1:T(2,128)}, u32[]{:S(2)}, u32[]{:S(2)}) collective-permute-start(s32[512,2]{0,1:T(2,128)} %param.20), channel_id=1, source_target_pairs={{0,1},{1,0},{2,3},{3,2},{4,5},{5,4},{6,7},{7,6},{8,9},{9,8},{10,11... | collective-permute-start | bytes 12296 | tf_op jit(solution)/shard_map/ppermute | solution.py:437
  12.6 10.0 %collective-permute-start.1 = (bf16[32,1664]{1,0:T(8,128)(2,1)S(1)}, bf16[32,1664]{1,0:T(8,128)(2,1)}, u32[]{:S(2)}, u32[]{:S(2)}) collective-permute-start(bf16[32,1664]{1,0:T(8,128)(2,1)S(1)} %fusion.36), channel_id=1, source_target_pairs={{0,16},{1,17},{2,18},{3,19},{4,20},{5,21},{6,22},{7,23},{8,24},{9,... | collective-permute-start | bytes 319496 | tf_op jit(solution)/shard_map/ppermute | solution.py:437
  17.0 33.5 %collective-permute-start = (bf16[512,1024]{1,0:T(8,128)(2,1)S(1)}, bf16[512,1024]{1,0:T(8,128)(2,1)S(1)}, u32[]{:S(2)}, u32[]{:S(2)}) collective-permute-start(bf16[512,1024]{1,0:T(8,128)(2,1)S(1)} %get-tuple-element.366), channel_id=1, source_target_pairs={{0,1},{1,0},{2,3},{3,2},{4,5},{5,4},{6,7},{7,6},{8,9},{9,8},{10,11... | collective-permute-start | bytes 3145736 | tf_op jit(solution)/shard_map/ppermute | solution.py:437
  23.5 6.2 %collective-permute-start.2 = (bf16[64,1664]{1,0:T(8,128)(2,1)S(1)}, bf16[64,1664]{1,0:T(8,128)(2,1)S(1)}, u32[]{:S(2)}, u32[]{:S(2)}) collective-permute-start(bf16[64,1664]{1,0:T(8,128)(2,1)S(1)} %pad_maximum_fusion.11), channel_id=1, source_target_pairs={{0,8},{1,9},{2,10},{3,11},{4,12},{5,13},{6,14},{7,15},{8,0},{9,1},... | collective-permute-start | bytes 638984 | tf_op jit(solution)/shard_map/ppermute | solution.py:437
  28.5 9.1 %collective-permute-start.7 = (bf16[32,2560]{1,0:T(8,128)(2,1)S(1)}, bf16[32,2560]{1,0:T(8,128)(2,1)S(1)}, u32[]{:S(2)}, u32[]{:S(2)}) collective-permute-start(bf16[32,2560]{1,0:T(8,128)(2,1)S(1)} %pad_maximum_fusion.12), channel_id=1, source_target_pairs={{0,16},{1,17},{2,18},{3,19},{4,20},{5,21},{6,22},{7,23},{8,24},{9,... | collective-permute-start | bytes 491528 | tf_op jit(solution)/shard_map/ppermute | solution.py:437
  29.8 10.1 %collective-permute-start.4 = (bf16[128,1664]{1,0:T(8,128)(2,1)S(1)}, bf16[128,1664]{1,0:T(8,128)(2,1)S(1)}, u32[]{:S(2)}, u32[]{:S(2)}) collective-permute-start(bf16[128,1664]{1,0:T(8,128)(2,1)S(1)} %pad_maximum_fusion.6.refs_0_), channel_id=1, source_target_pairs={{0,4},{1,5},{2,6},{3,7},{4,0},{5,1},{6,2},{7,3},{8,12},{9,13},{10,... | collective-permute-start | bytes 1277960 | tf_op jit(solution)/shard_map/ppermute | solution.py:437
  31.4 19.2 %collective-permute-start.3 = (bf16[128,1664]{1,0:T(8,128)(2,1)S(1)}, bf16[128,1664]{1,0:T(8,128)(2,1)S(1)}, u32[]{:S(2)}, u32[]{:S(2)}) collective-permute-start(bf16[128,1664]{1,0:T(8,128)(2,1)S(1)} %pad_maximum_fusion.6.refs_0_), channel_id=1, source_target_pairs={{0,1},{1,0},{2,3},{3,2},{4,5},{5,4},{6,7},{7,6},{8,9},{9,8},{10,11... | collective-permute-start | bytes 1277960 | tf_op jit(solution)/shard_map/ppermute | solution.py:437
  37.6 15.5 %collective-permute-start.8 = (bf16[64,2560]{1,0:T(8,128)(2,1)S(1)}, bf16[64,2560]{1,0:T(8,128)(2,1)S(1)}, u32[]{:S(2)}, u32[]{:S(2)}) collective-permute-start(bf16[64,2560]{1,0:T(8,128)(2,1)S(1)} %pad_maximum_fusion.10), channel_id=1, source_target_pairs={{0,8},{1,9},{2,10},{3,11},{4,12},{5,13},{6,14},{7,15},{8,0},{9,1},... | collective-permute-start | bytes 983048 | tf_op jit(solution)/shard_map/ppermute | solution.py:437
  58.2 20.4 %collective-permute-start.9 = (bf16[512,1664]{1,0:T(8,128)(2,1)S(1)}, bf16[512,1664]{1,0:T(8,128)(2,1)S(1)}, u32[]{:S(2)}, u32[]{:S(2)}) collective-permute-start(bf16[512,1664]{1,0:T(8,128)(2,1)S(1)} %pack_rows.5.near_ref.qn_ref.kn_ref.vn_ref.refs_14_), channel_id=1, source_target_pairs={{0,2},{1,3},{2,0},{3,1},{4,6},{5,7},{6,4},{7,5},{8,10},{9,11},{10,... | collective-permute-start | bytes 5111816 | tf_op jit(solution)/shard_map/ppermute | solution.py:437
  61.1 11.7 %collective-permute-start.10 = (bf16[32,2816]{1,0:T(8,128)(2,1)S(1)}, bf16[32,2816]{1,0:T(8,128)(2,1)S(1)}, u32[]{:S(2)}, u32[]{:S(2)}) collective-permute-start(bf16[32,2816]{1,0:T(8,128)(2,1)S(1)} %pad.33), channel_id=1, source_target_pairs={{0,16},{1,17},{2,18},{3,19},{4,20},{5,21},{6,22},{7,23},{8,24},{9,... | collective-permute-start | bytes 540680 | tf_op jit(solution)/shard_map/ppermute | solution.py:437
  61.5 16.9 %collective-permute-start.12 = (bf16[128,2560]{1,0:T(8,128)(2,1)S(1)}, bf16[128,2560]{1,0:T(8,128)(2,1)S(1)}, u32[]{:S(2)}, u32[]{:S(2)}) collective-permute-start(bf16[128,2560]{1,0:T(8,128)(2,1)S(1)} %constant_dynamic-update-slice_fusion.refs_0_), channel_id=1, source_target_pairs={{0,4},{1,5},{2,6},{3,7},{4,0},{5,1},{6,2},{7,3},{8,12},{9,13},{10,... | collective-permute-start | bytes 1966088 | tf_op jit(solution)/shard_map/ppermute | solution.py:437
  62.1 16.5 %collective-permute-start.11 = (bf16[128,2560]{1,0:T(8,128)(2,1)S(1)}, bf16[128,2560]{1,0:T(8,128)(2,1)S(1)}, u32[]{:S(2)}, u32[]{:S(2)}) collective-permute-start(bf16[128,2560]{1,0:T(8,128)(2,1)S(1)} %constant_dynamic-update-slice_fusion.refs_0_), channel_id=1, source_target_pairs={{0,1},{1,0},{2,3},{3,2},{4,5},{5,4},{6,7},{7,6},{8,9},{9,8},{10,11... | collective-permute-start | bytes 1966088 | tf_op jit(solution)/shard_map/ppermute | solution.py:437
  80.2 15.3 %collective-permute-start.15 = (bf16[64,2560]{1,0:T(8,128)(2,1)}, bf16[64,2560]{1,0:T(8,128)(2,1)S(1)}, u32[]{:S(2)}, u32[]{:S(2)}) collective-permute-start(bf16[64,2560]{1,0:T(8,128)(2,1)} %slice.393), channel_id=1, source_target_pairs={{0,4},{1,5},{2,6},{3,7},{4,0},{5,1},{6,2},{7,3},{8,12},{9,13},{10,... | collective-permute-start | bytes 983048 | tf_op jit(solution)/shard_map/ppermute | solution.py:437
  81.8 14.5 %collective-permute-start.14 = (bf16[64,2560]{1,0:T(8,128)(2,1)}, bf16[64,2560]{1,0:T(8,128)(2,1)S(1)}, u32[]{:S(2)}, u32[]{:S(2)}) collective-permute-start(bf16[64,2560]{1,0:T(8,128)(2,1)} %slice.392), channel_id=1, source_target_pairs={{0,1},{1,0},{2,3},{3,2},{4,5},{5,4},{6,7},{7,6},{8,9},{9,8},{10,11... | collective-permute-start | bytes 983048 | tf_op jit(solution)/shard_map/ppermute | solution.py:437
  82.3 12.2 %collective-permute-start.13 = (bf16[64,2816]{1,0:T(8,128)(2,1)S(1)}, bf16[64,2816]{1,0:T(8,128)(2,1)}, u32[]{:S(2)}, u32[]{:S(2)}) collective-permute-start(bf16[64,2816]{1,0:T(8,128)(2,1)S(1)} %pad_maximum_fusion.7), channel_id=1, source_target_pairs={{0,8},{1,9},{2,10},{3,11},{4,12},{5,13},{6,14},{7,15},{8,0},{9,1},... | collective-permute-start | bytes 1081352 | tf_op jit(solution)/shard_map/ppermute | solution.py:437
  97.0 20.8 %collective-permute-start.18 = (bf16[128,2816]{1,0:T(8,128)(2,1)S(1)}, bf16[128,2816]{1,0:T(8,128)(2,1)S(1)}, u32[]{:S(2)}, u32[]{:S(2)}) collective-permute-start(bf16[128,2816]{1,0:T(8,128)(2,1)S(1)} %constant_dynamic-update-slice_fusion.4.refs_0_), channel_id=1, source_target_pairs={{0,4},{1,5},{2,6},{3,7},{4,0},{5,1},{6,2},{7,3},{8,12},{9,13},{10,... | collective-permute-start | bytes 2162696 | tf_op jit(solution)/shard_map/ppermute | solution.py:437
  97.5 20.3 %collective-permute-start.17 = (bf16[128,2816]{1,0:T(8,128)(2,1)S(1)}, bf16[128,2816]{1,0:T(8,128)(2,1)S(1)}, u32[]{:S(2)}, u32[]{:S(2)}) collective-permute-start(bf16[128,2816]{1,0:T(8,128)(2,1)S(1)} %constant_dynamic-update-slice_fusion.4.refs_0_), channel_id=1, source_target_pairs={{0,1},{1,0},{2,3},{3,2},{4,5},{5,4},{6,7},{7,6},{8,9},{9,8},{10,11... | collective-permute-start | bytes 2162696 | tf_op jit(solution)/shard_map/ppermute | solution.py:437
  103.4 14.4 %collective-permute-start.19 = (bf16[32,2816]{1,0:T(8,128)(2,1)S(1)}, bf16[32,2816]{1,0:T(8,128)(2,1)S(1)}, u32[]{:S(2)}, u32[]{:S(2)}) collective-permute-start(bf16[32,2816]{1,0:T(8,128)(2,1)S(1)} %copy-done.70), channel_id=1, source_target_pairs={{0,16},{1,17},{2,18},{3,19},{4,20},{5,21},{6,22},{7,23},{8,24},{9,... | collective-permute-start | bytes 540680 | tf_op jit(solution)/shard_map/ppermute | solution.py:437
  106.0 28.7 %collective-permute-start.20 = (bf16[512,2560]{1,0:T(8,128)(2,1)S(1)}, bf16[512,2560]{1,0:T(8,128)(2,1)}, u32[]{:S(2)}, u32[]{:S(2)}) collective-permute-start(bf16[512,2560]{1,0:T(8,128)(2,1)S(1)} %pack_rows.6.qn_ref.kn_ref.vn_ref.na_ref.nb_ref.refs_16_), channel_id=1, source_target_pairs={{0,2},{1,3},{2,0},{3,1},{4,6},{5,7},{6,4},{7,5},{8,10},{9,11},{10,... | collective-permute-start | bytes 7864328 | tf_op jit(solution)/shard_map/ppermute | solution.py:437
  118.0 16.0 %collective-permute-start.22 = (bf16[64,2816]{1,0:T(8,128)(2,1)S(1)}, bf16[64,2816]{1,0:T(8,128)(2,1)S(1)}, u32[]{:S(2)}, u32[]{:S(2)}) collective-permute-start(bf16[64,2816]{1,0:T(8,128)(2,1)S(1)} %slice.397), channel_id=1, source_target_pairs={{0,4},{1,5},{2,6},{3,7},{4,0},{5,1},{6,2},{7,3},{8,12},{9,13},{10,... | collective-permute-start | bytes 1081352 | tf_op jit(solution)/shard_map/ppermute | solution.py:437
  119.5 14.5 %collective-permute-start.21 = (bf16[64,2816]{1,0:T(8,128)(2,1)S(1)}, bf16[64,2816]{1,0:T(8,128)(2,1)S(1)}, u32[]{:S(2)}, u32[]{:S(2)}) collective-permute-start(bf16[64,2816]{1,0:T(8,128)(2,1)S(1)} %slice.396), channel_id=1, source_target_pairs={{0,1},{1,0},{2,3},{3,2},{4,5},{5,4},{6,7},{7,6},{8,9},{9,8},{10,11... | collective-permute-start | bytes 1081352 | tf_op jit(solution)/shard_map/ppermute | solution.py:437
  120.1 13.2 %collective-permute-start.23 = (bf16[64,2816]{1,0:T(8,128)(2,1)S(1)}, bf16[64,2816]{1,0:T(8,128)(2,1)S(1)}, u32[]{:S(2)}, u32[]{:S(2)}) collective-permute-start(bf16[64,2816]{1,0:T(8,128)(2,1)S(1)} %pad_maximum_fusion.8), channel_id=1, source_target_pairs={{0,8},{1,9},{2,10},{3,11},{4,12},{5,13},{6,14},{7,15},{8,0},{9,1},... | collective-permute-start | bytes 1081352 | tf_op jit(solution)/shard_map/ppermute | solution.py:437
  134.7 17.9 %collective-permute-start.25 = (bf16[128,2816]{1,0:T(8,128)(2,1)}, bf16[128,2816]{1,0:T(8,128)(2,1)S(1)}, u32[]{:S(2)}, u32[]{:S(2)}) collective-permute-start(bf16[128,2816]{1,0:T(8,128)(2,1)} %constant_dynamic-update-slice_fusion.6.refs_0_), channel_id=1, source_target_pairs={{0,4},{1,5},{2,6},{3,7},{4,0},{5,1},{6,2},{7,3},{8,12},{9,13},{10,... | collective-permute-start | bytes 2162696 | tf_op jit(solution)/shard_map/ppermute | solution.py:437
  135.2 17.6 %collective-permute-start.24 = (bf16[128,2816]{1,0:T(8,128)(2,1)}, bf16[128,2816]{1,0:T(8,128)(2,1)S(1)}, u32[]{:S(2)}, u32[]{:S(2)}) collective-permute-start(bf16[128,2816]{1,0:T(8,128)(2,1)} %constant_dynamic-update-slice_fusion.6.refs_0_), channel_id=1, source_target_pairs={{0,1},{1,0},{2,3},{3,2},{4,5},{5,4},{6,7},{7,6},{8,9},{9,8},{10,11... | collective-permute-start | bytes 2162696 | tf_op jit(solution)/shard_map/ppermute | solution.py:437
  138.4 12.7 %collective-permute-start.27 = (bf16[32,2816]{1,0:T(8,128)(2,1)S(1)}, bf16[32,2816]{1,0:T(8,128)(2,1)S(1)}, u32[]{:S(2)}, u32[]{:S(2)}) collective-permute-start(bf16[32,2816]{1,0:T(8,128)(2,1)S(1)} %pad.36), channel_id=1, source_target_pairs={{0,16},{1,17},{2,18},{3,19},{4,20},{5,21},{6,22},{7,23},{8,24},{9,... | collective-permute-start | bytes 540680 | tf_op jit(solution)/shard_map/ppermute | solution.py:437
  139.3 13.5 %collective-permute-start.26 = (bf16[512,2816]{1,0:T(8,128)(2,1)S(1)}, bf16[512,2816]{1,0:T(8,128)(2,1)}, u32[]{:S(2)}, u32[]{:S(2)}) collective-permute-start(bf16[512,2816]{1,0:T(8,128)(2,1)S(1)} %pack_rows.7.gn_ref), channel_id=1, source_target_pairs={{0,2},{1,3},{2,0},{3,1},{4,6},{5,7},{6,4},{7,5},{8,10},{9,11},{10,... | collective-permute-start | bytes 8650760 | tf_op jit(solution)/shard_map/ppermute | solution.py:437
  152.9 16.9 %collective-permute-start.29 = (bf16[64,2816]{1,0:T(8,128)(2,1)S(1)}, bf16[64,2816]{1,0:T(8,128)(2,1)S(1)}, u32[]{:S(2)}, u32[]{:S(2)}) collective-permute-start(bf16[64,2816]{1,0:T(8,128)(2,1)S(1)} %slice.399), channel_id=1, source_target_pairs={{0,4},{1,5},{2,6},{3,7},{4,0},{5,1},{6,2},{7,3},{8,12},{9,13},{10,... | collective-permute-start | bytes 1081352 | tf_op jit(solution)/shard_map/ppermute | solution.py:437
  154.5 15.3 %collective-permute-start.28 = (bf16[64,2816]{1,0:T(8,128)(2,1)S(1)}, bf16[64,2816]{1,0:T(8,128)(2,1)S(1)}, u32[]{:S(2)}, u32[]{:S(2)}) collective-permute-start(bf16[64,2816]{1,0:T(8,128)(2,1)S(1)} %slice.398), channel_id=1, source_target_pairs={{0,1},{1,0},{2,3},{3,2},{4,5},{5,4},{6,7},{7,6},{8,9},{9,8},{10,11... | collective-permute-start | bytes 1081352 | tf_op jit(solution)/shard_map/ppermute | solution.py:437
  156.0 13.8 %collective-permute-start.30 = (bf16[64,2816]{1,0:T(8,128)(2,1)S(1)}, bf16[64,2816]{1,0:T(8,128)(2,1)S(1)}, u32[]{:S(2)}, u32[]{:S(2)}) collective-permute-start(bf16[64,2816]{1,0:T(8,128)(2,1)S(1)} %pad_maximum_fusion.9), channel_id=1, source_target_pairs={{0,8},{1,9},{2,10},{3,11},{4,12},{5,13},{6,14},{7,15},{8,0},{9,1},... | collective-permute-start | bytes 1081352 | tf_op jit(solution)/shard_map/ppermute | solution.py:437
  171.5 19.8 %collective-permute-start.31 = (bf16[512,2816]{1,0:T(8,128)(2,1)S(1)}, bf16[512,2816]{1,0:T(8,128)(2,1)}, u32[]{:S(2)}, u32[]{:S(2)}) collective-permute-start(bf16[512,2816]{1,0:T(8,128)(2,1)S(1)} %pack_rows.8.un_ref), channel_id=1, source_target_pairs={{0,2},{1,3},{2,0},{3,1},{4,6},{5,7},{6,4},{7,5},{8,10},{9,11},{10,... | collective-permute-start | bytes 8650760 | tf_op jit(solution)/shard_map/ppermute | solution.py:437
  172.9 18.2 %collective-permute-start.33 = (bf16[128,2816]{1,0:T(8,128)(2,1)S(1)}, bf16[128,2816]{1,0:T(8,128)(2,1)S(1)}, u32[]{:S(2)}, u32[]{:S(2)}) collective-permute-start(bf16[128,2816]{1,0:T(8,128)(2,1)S(1)} %constant_dynamic-update-slice_fusion.8.refs_0_), channel_id=1, source_target_pairs={{0,4},{1,5},{2,6},{3,7},{4,0},{5,1},{6,2},{7,3},{8,12},{9,13},{10,... | collective-permute-start | bytes 2162696 | tf_op jit(solution)/shard_map/ppermute | solution.py:437
  173.4 17.8 %collective-permute-start.32 = (bf16[128,2816]{1,0:T(8,128)(2,1)S(1)}, bf16[128,2816]{1,0:T(8,128)(2,1)S(1)}, u32[]{:S(2)}, u32[]{:S(2)}) collective-permute-start(bf16[128,2816]{1,0:T(8,128)(2,1)S(1)} %constant_dynamic-update-slice_fusion.8.refs_0_), channel_id=1, source_target_pairs={{0,1},{1,0},{2,3},{3,2},{4,5},{5,4},{6,7},{7,6},{8,9},{9,8},{10,11... | collective-permute-start | bytes 2162696 | tf_op jit(solution)/shard_map/ppermute | solution.py:437
  191.3 26.1 %collective-permute-start.35 = (bf16[64,2816]{1,0:T(8,128)(2,1)S(1)}, bf16[64,2816]{1,0:T(8,128)(2,1)S(1)}, u32[]{:S(2)}, u32[]{:S(2)}) collective-permute-start(bf16[64,2816]{1,0:T(8,128)(2,1)S(1)} %slice.401), channel_id=1, source_target_pairs={{0,4},{1,5},{2,6},{3,7},{4,0},{5,1},{6,2},{7,3},{8,12},{9,13},{10,... | collective-permute-start | bytes 1081352 | tf_op jit(solution)/shard_map/ppermute | solution.py:437
  192.9 24.5 %collective-permute-start.34 = (bf16[64,2816]{1,0:T(8,128)(2,1)S(1)}, bf16[64,2816]{1,0:T(8,128)(2,1)S(1)}, u32[]{:S(2)}, u32[]{:S(2)}) collective-permute-start(bf16[64,2816]{1,0:T(8,128)(2,1)S(1)} %slice.400), channel_id=1, source_target_pairs={{0,1},{1,0},{2,3},{3,2},{4,5},{5,4},{6,7},{7,6},{8,9},{9,8},{10,11... | collective-permute-start | bytes 1081352 | tf_op jit(solution)/shard_map/ppermute | solution.py:437
  193.5 30.9 %collective-permute-start.36 = (bf16[512,1024]{1,0:T(8,128)(2,1)S(1)}, bf16[512,1024]{1,0:T(8,128)(2,1)S(1)}, u32[]{:S(2)}, u32[]{:S(2)}) collective-permute-start(bf16[512,1024]{1,0:T(8,128)(2,1)S(1)} %get-tuple-element.241), channel_id=1, source_target_pairs={{0,1},{1,0},{2,3},{3,2},{4,5},{5,4},{6,7},{7,6},{8,9},{9,8},{10,11... | collective-permute-start | bytes 3145736 | tf_op jit(solution)/shard_map/ppermute | solution.py:437
  249.4 30.2 %collective-permute-start.38 = (bf16[528,1024]{1,0:T(8,128)(2,1)S(1)}, bf16[528,1024]{1,0:T(8,128)(2,1)S(1)}, u32[]{:S(2)}, u32[]{:S(2)}) collective-permute-start(bf16[528,1024]{1,0:T(8,128)(2,1)S(1)} %slice.402), channel_id=1, source_target_pairs={{0,1},{1,0},{2,3},{3,2},{4,5},{5,4},{6,7},{7,6},{8,9},{9,8},{10,11... | collective-permute-start | bytes 3244040 | tf_op jit(solution)/shard_map/ppermute | solution.py:437
  291.6 9.8 %collective-permute-start.39 = (bf16[512,5632]{1,0:T(8,128)(2,1)}, bf16[512,5632]{1,0:T(8,128)(2,1)}, u32[]{:S(2)}, u32[]{:S(2)}) collective-permute-start(bf16[512,5632]{1,0:T(8,128)(2,1)} %weight_grads.8), channel_id=1, source_target_pairs={{0,2},{1,3},{2,0},{3,1},{4,6},{5,7},{6,4},{7,5},{8,10},{9,11},{10,... | collective-permute-start | bytes 17301512 | tf_op jit(solution)/shard_map/ppermute | solution.py:437
  301.5 17.4 %collective-permute-start.40 = (bf16[512,2816]{1,0:T(8,128)(2,1)S(1)}, bf16[512,2816]{1,0:T(8,128)(2,1)S(1)}, u32[]{:S(2)}, u32[]{:S(2)}) collective-permute-start(bf16[512,2816]{1,0:T(8,128)(2,1)S(1)} %weight_grads.9), channel_id=1, source_target_pairs={{0,2},{1,3},{2,0},{3,1},{4,6},{5,7},{6,4},{7,5},{8,10},{9,11},{10,... | collective-permute-start | bytes 8650760 | tf_op jit(solution)/shard_map/ppermute | solution.py:437
  321.8 23.6 %collective-permute-start.42 = (bf16[64,5632]{1,0:T(8,128)(2,1)S(1)}, bf16[64,5632]{1,0:T(8,128)(2,1)S(1)}, u32[]{:S(2)}, u32[]{:S(2)}) collective-permute-start(bf16[64,5632]{1,0:T(8,128)(2,1)S(1)} %get-tuple-element.351), channel_id=1, source_target_pairs={{0,1},{1,0},{2,3},{3,2},{4,5},{5,4},{6,7},{7,6},{8,9},{9,8},{10,11... | collective-permute-start | bytes 2162696 | tf_op jit(solution)/shard_map/ppermute | solution.py:437
  323.4 23.2 %collective-permute-start.41 = (bf16[64,5632]{1,0:T(8,128)(2,1)S(1)}, bf16[64,5632]{1,0:T(8,128)(2,1)S(1)}, u32[]{:S(2)}, u32[]{:S(2)}) collective-permute-start(bf16[64,5632]{1,0:T(8,128)(2,1)S(1)} %get-tuple-element.353), channel_id=1, source_target_pairs={{0,4},{1,5},{2,6},{3,7},{4,0},{5,1},{6,2},{7,3},{8,12},{9,13},{10,... | collective-permute-start | bytes 2162696 | tf_op jit(solution)/shard_map/ppermute | solution.py:437
  348.6 32.9 %collective-permute-start.44 = (bf16[128,5632]{1,0:T(8,128)(2,1)S(1)}, bf16[128,5632]{1,0:T(8,128)(2,1)S(1)}, u32[]{:S(2)}, u32[]{:S(2)}) collective-permute-start(bf16[128,5632]{1,0:T(8,128)(2,1)S(1)} %pad_maximum_fusion.1), channel_id=1, source_target_pairs={{0,1},{1,0},{2,3},{3,2},{4,5},{5,4},{6,7},{7,6},{8,9},{9,8},{10,11... | collective-permute-start | bytes 4325384 | tf_op jit(solution)/shard_map/ppermute | solution.py:437
  349.2 32.7 %collective-permute-start.43 = (bf16[128,5632]{1,0:T(8,128)(2,1)S(1)}, bf16[128,5632]{1,0:T(8,128)(2,1)}, u32[]{:S(2)}, u32[]{:S(2)}) collective-permute-start(bf16[128,5632]{1,0:T(8,128)(2,1)S(1)} %pad_maximum_fusion.2), channel_id=1, source_target_pairs={{0,4},{1,5},{2,6},{3,7},{4,0},{5,1},{6,2},{7,3},{8,12},{9,13},{10,... | collective-permute-start | bytes 4325384 | tf_op jit(solution)/shard_map/ppermute | solution.py:437
  384.4 16.3 %collective-permute-start.45 = (bf16[64,5632]{1,0:T(8,128)(2,1)S(1)}, bf16[64,5632]{1,0:T(8,128)(2,1)S(1)}, u32[]{:S(2)}, u32[]{:S(2)}) collective-permute-start(bf16[64,5632]{1,0:T(8,128)(2,1)S(1)} %slice.415), channel_id=1, source_target_pairs={{0,8},{1,9},{2,10},{3,11},{4,12},{5,13},{6,14},{7,15},{8,0},{9,1},... | collective-permute-start | bytes 2162696 | tf_op jit(solution)/shard_map/ppermute | solution.py:437
  384.9 14.9 %collective-permute-start.47 = (bf16[64,2816]{1,0:T(8,128)(2,1)S(1)}, bf16[64,2816]{1,0:T(8,128)(2,1)S(1)}, u32[]{:S(2)}, u32[]{:S(2)}) collective-permute-start(bf16[64,2816]{1,0:T(8,128)(2,1)S(1)} %get-tuple-element.357), channel_id=1, source_target_pairs={{0,1},{1,0},{2,3},{3,2},{4,5},{5,4},{6,7},{7,6},{8,9},{9,8},{10,11... | collective-permute-start | bytes 1081352 | tf_op jit(solution)/shard_map/ppermute | solution.py:437
  386.3 13.5 %collective-permute-start.46 = (bf16[64,2816]{1,0:T(8,128)(2,1)S(1)}, bf16[64,2816]{1,0:T(8,128)(2,1)S(1)}, u32[]{:S(2)}, u32[]{:S(2)}) collective-permute-start(bf16[64,2816]{1,0:T(8,128)(2,1)S(1)} %get-tuple-element.359), channel_id=1, source_target_pairs={{0,4},{1,5},{2,6},{3,7},{4,0},{5,1},{6,2},{7,3},{8,12},{9,13},{10,... | collective-permute-start | bytes 1081352 | tf_op jit(solution)/shard_map/ppermute | solution.py:437
  400.9 16.3 %collective-permute-start.48 = (bf16[32,5632]{1,0:T(8,128)(2,1)S(1)}, bf16[32,5632]{1,0:T(8,128)(2,1)S(1)}, u32[]{:S(2)}, u32[]{:S(2)}) collective-permute-start(bf16[32,5632]{1,0:T(8,128)(2,1)S(1)} %slice.423), channel_id=1, source_target_pairs={{0,16},{1,17},{2,18},{3,19},{4,20},{5,21},{6,22},{7,23},{8,24},{9,... | collective-permute-start | bytes 1081352 | tf_op jit(solution)/shard_map/ppermute | solution.py:437
  401.0 17.2 %collective-permute-start.50 = (bf16[128,2816]{1,0:T(8,128)(2,1)S(1)}, bf16[128,2816]{1,0:T(8,128)(2,1)S(1)}, u32[]{:S(2)}, u32[]{:S(2)}) collective-permute-start(bf16[128,2816]{1,0:T(8,128)(2,1)S(1)} %pad_maximum_fusion.4), channel_id=1, source_target_pairs={{0,1},{1,0},{2,3},{3,2},{4,5},{5,4},{6,7},{7,6},{8,9},{9,8},{10,11... | collective-permute-start | bytes 2162696 | tf_op jit(solution)/shard_map/ppermute | solution.py:437
  402.5 15.7 %collective-permute-start.49 = (bf16[128,2816]{1,0:T(8,128)(2,1)S(1)}, bf16[128,2816]{1,0:T(8,128)(2,1)S(1)}, u32[]{:S(2)}, u32[]{:S(2)}) collective-permute-start(bf16[128,2816]{1,0:T(8,128)(2,1)S(1)} %pad_maximum_fusion.5), channel_id=1, source_target_pairs={{0,4},{1,5},{2,6},{3,7},{4,0},{5,1},{6,2},{7,3},{8,12},{9,13},{10,... | collective-permute-start | bytes 2162696 | tf_op jit(solution)/shard_map/ppermute | solution.py:437
  418.4 9.7 %collective-permute-start.51 = (bf16[64,2816]{1,0:T(8,128)(2,1)S(1)}, bf16[64,2816]{1,0:T(8,128)(2,1)S(1)}, u32[]{:S(2)}, u32[]{:S(2)}) collective-permute-start(bf16[64,2816]{1,0:T(8,128)(2,1)S(1)} %slice.426), channel_id=1, source_target_pairs={{0,8},{1,9},{2,10},{3,11},{4,12},{5,13},{6,14},{7,15},{8,0},{9,1},... | collective-permute-start | bytes 1081352 | tf_op jit(solution)/shard_map/ppermute | solution.py:437
  428.2 13.1 %collective-permute-start.53 = (bf16[32,2816]{1,0:T(8,128)(2,1)S(1)}, bf16[32,2816]{1,0:T(8,128)(2,1)S(1)}, u32[]{:S(2)}, u32[]{:S(2)}) collective-permute-start(bf16[32,2816]{1,0:T(8,128)(2,1)S(1)} %slice.428), channel_id=1, source_target_pairs={{0,16},{1,17},{2,18},{3,19},{4,20},{5,21},{6,22},{7,23},{8,24},{9,... | collective-permute-start | bytes 540680 | tf_op jit(solution)/shard_map/ppermute | solution.py:437
  428.6 13.7 %collective-permute-start.52 = (bf16[512,2560]{1,0:T(8,128)(2,1)}, bf16[512,2560]{1,0:T(8,128)(2,1)S(1)}, u32[]{:S(2)}, u32[]{:S(2)}) collective-permute-start(bf16[512,2560]{1,0:T(8,128)(2,1)} %weight_grads.12), channel_id=1, source_target_pairs={{0,2},{1,3},{2,0},{3,1},{4,6},{5,7},{6,4},{7,5},{8,10},{9,11},{10,... | collective-permute-start | bytes 7864328 | tf_op jit(solution)/shard_map/ppermute | solution.py:437
  453.6 17.1 %collective-permute-start.54 = (bf16[128,2560]{1,0:T(8,128)(2,1)S(1)}, bf16[128,2560]{1,0:T(8,128)(2,1)S(1)}, u32[]{:S(2)}, u32[]{:S(2)}) collective-permute-start(bf16[128,2560]{1,0:T(8,128)(2,1)S(1)} %get-tuple-element.362), channel_id=1, source_target_pairs={{0,4},{1,5},{2,6},{3,7},{4,0},{5,1},{6,2},{7,3},{8,12},{9,13},{10,... | collective-permute-start | bytes 1966088 | tf_op jit(solution)/shard_map/ppermute | solution.py:437
  475.7 16.8 %collective-permute-start.57 = (bf16[128,2560]{1,0:T(8,128)(2,1)}, bf16[128,2560]{1,0:T(8,128)(2,1)S(1)}, u32[]{:S(2)}, u32[]{:S(2)}) collective-permute-start(bf16[128,2560]{1,0:T(8,128)(2,1)} %add_convert_fusion.7), channel_id=1, source_target_pairs={{0,1},{1,0},{2,3},{3,2},{4,5},{5,4},{6,7},{7,6},{8,9},{9,8},{10,11... | collective-permute-start | bytes 1966088 | tf_op jit(solution)/shard_map/ppermute | solution.py:437
  477.6 16.4 %collective-permute-start.56 = (bf16[128,2560]{1,0:T(8,128)(2,1)}, bf16[128,2560]{1,0:T(8,128)(2,1)}, u32[]{:S(2)}, u32[]{:S(2)}) collective-permute-start(bf16[128,2560]{1,0:T(8,128)(2,1)} %get-tuple-element.321), channel_id=1, source_target_pairs={{0,4},{1,5},{2,6},{3,7},{4,0},{5,1},{6,2},{7,3},{8,12},{9,13},{10,... | collective-permute-start | bytes 1966088 | tf_op jit(solution)/shard_map/ppermute | solution.py:437
  477.9 17.7 %collective-permute-start.55 = (bf16[512,1536]{1,0:T(8,128)(2,1)S(1)}, bf16[512,1536]{1,0:T(8,128)(2,1)}, u32[]{:S(2)}, u32[]{:S(2)}) collective-permute-start(bf16[512,1536]{1,0:T(8,128)(2,1)S(1)} %weight_grads.14), channel_id=1, source_target_pairs={{0,2},{1,3},{2,0},{3,1},{4,6},{5,7},{6,4},{7,5},{8,10},{9,11},{10,... | collective-permute-start | bytes 4718600 | tf_op jit(solution)/shard_map/ppermute | solution.py:437
  500.0 16.6 %collective-permute-start.59 = (bf16[64,2560]{1,0:T(8,128)(2,1)S(1)}, bf16[64,2560]{1,0:T(8,128)(2,1)}, u32[]{:S(2)}, u32[]{:S(2)}) collective-permute-start(bf16[64,2560]{1,0:T(8,128)(2,1)S(1)} %slice.438), channel_id=1, source_target_pairs={{0,8},{1,9},{2,10},{3,11},{4,12},{5,13},{6,14},{7,15},{8,0},{9,1},... | collective-permute-start | bytes 983048 | tf_op jit(solution)/shard_map/ppermute | solution.py:437
  500.9 24.6 %collective-permute-start.58 = (bf16[528,1024]{1,0:T(8,128)(2,1)}, bf16[528,1024]{1,0:T(8,128)(2,1)S(1)}, u32[]{:S(2)}, u32[]{:S(2)}) collective-permute-start(bf16[528,1024]{1,0:T(8,128)(2,1)} %get-tuple-element.326), channel_id=1, source_target_pairs={{0,1},{1,0},{2,3},{3,2},{4,5},{5,4},{6,7},{7,6},{8,9},{9,8},{10,11... | collective-permute-start | bytes 3244040 | tf_op jit(solution)/shard_map/ppermute | solution.py:437
  502.1 27.0 %collective-permute-start.60 = (bf16[256,1536]{1,0:T(8,128)(2,1)S(1)}, bf16[256,1536]{1,0:T(8,128)(2,1)S(1)}, u32[]{:S(2)}, u32[]{:S(2)}) collective-permute-start(bf16[256,1536]{1,0:T(8,128)(2,1)S(1)} %pad_maximum_fusion.3), channel_id=1, source_target_pairs={{0,4},{1,5},{2,6},{3,7},{4,0},{5,1},{6,2},{7,3},{8,12},{9,13},{10,... | collective-permute-start | bytes 2359304 | tf_op jit(solution)/shard_map/ppermute | solution.py:437
  530.3 7.0 %collective-permute-start.66 = (f32[256,8]{0,1:T(8,128)S(1)}, f32[256,8]{0,1:T(8,128)S(1)}, u32[]{:S(2)}, u32[]{:S(2)}) collective-permute-start(f32[256,8]{0,1:T(8,128)S(1)} %slice.516), channel_id=1, source_target_pairs={{0,1},{1,0},{2,3},{3,2},{4,5},{5,4},{6,7},{7,6},{8,9},{9,8},{10,11... | collective-permute-start | bytes 24584 | tf_op jit(solution)/shard_map/ppermute | solution.py:437
  533.7 16.1 %collective-permute-start.61 = (bf16[32,2560]{1,0:T(8,128)(2,1)S(1)}, bf16[32,2560]{1,0:T(8,128)(2,1)S(1)}, u32[]{:S(2)}, u32[]{:S(2)}) collective-permute-start(bf16[32,2560]{1,0:T(8,128)(2,1)S(1)} %slice.444), channel_id=1, source_target_pairs={{0,16},{1,17},{2,18},{3,19},{4,20},{5,21},{6,22},{7,23},{8,24},{9,... | collective-permute-start | bytes 491528 | tf_op jit(solution)/shard_map/ppermute | solution.py:437
  536.5 13.3 %collective-permute-start.62 = (bf16[128,1536]{1,0:T(8,128)(2,1)S(1)}, bf16[128,1536]{1,0:T(8,128)(2,1)S(1)}, u32[]{:S(2)}, u32[]{:S(2)}) collective-permute-start(bf16[128,1536]{1,0:T(8,128)(2,1)S(1)} %slice.448), channel_id=1, source_target_pairs={{0,1},{1,0},{2,3},{3,2},{4,5},{5,4},{6,7},{7,6},{8,9},{9,8},{10,11... | collective-permute-start | bytes 1179656 | tf_op jit(solution)/shard_map/ppermute | solution.py:437
  550.0 6.8 %collective-permute-start.63 = (bf16[64,1536]{1,0:T(8,128)(2,1)S(1)}, bf16[64,1536]{1,0:T(8,128)(2,1)S(1)}, u32[]{:S(2)}, u32[]{:S(2)}) collective-permute-start(bf16[64,1536]{1,0:T(8,128)(2,1)S(1)} %slice.494), channel_id=1, source_target_pairs={{0,8},{1,9},{2,10},{3,11},{4,12},{5,13},{6,14},{7,15},{8,0},{9,1},... | collective-permute-start | bytes 589832 | tf_op jit(solution)/shard_map/ppermute | solution.py:437
  556.8 6.6 %collective-permute-start.64 = (bf16[32,1536]{1,0:T(8,128)(2,1)S(1)}, bf16[32,1536]{1,0:T(8,128)(2,1)S(1)}, u32[]{:S(2)}, u32[]{:S(2)}) collective-permute-start(bf16[32,1536]{1,0:T(8,128)(2,1)S(1)} %slice.496), channel_id=1, source_target_pairs={{0,16},{1,17},{2,18},{3,19},{4,20},{5,21},{6,22},{7,23},{8,24},{9,... | collective-permute-start | bytes 294920 | tf_op jit(solution)/shard_map/ppermute | solution.py:437
  (97 other events, 1171.2 us)
Sparse Core Ops, SparseCore 0:
  291.9 59.9 all-gather.2

commit v6 on v5

--- a/solution.py
+++ b/solution.py
@@ -1099,7 +1099,7 @@
     z_high = g_high.along_z1(z_low)
     corner_low = g_low.corners(image_far)
     xy_high = g_high.along_xy(xy_low)
-    near_low = g_low.whole(z_high)
+    near_low = g_low.whole(z_high, z_one)
 
     gate = near_low, g_low.far, image_rows, z_one, xy_high
     z_gate = g_gate.along_z1(gate)

time: 579 us -> 576 us (level)
  waiting for transfers between devices: 119 us -> 110 us
  starting transfers between devices: 64.3 us -> 70.2 us
    ppermute x70, waiting for transfers between devices: 119 us -> 110 us  [swap_over(): return lax.ppermute(value, BOTH, [(i, i ^ bit) for i in range(count)])]
    ppermute x70, starting transfers between devices: 64.2 us -> 70.1 us  [swap_over(): return lax.ppermute(value, BOTH, [(i, i ^ bit) for i in range(count)])]
  transfers between devices with their start and end apart: 71 -> 71, of which waited for: 33 -> 29; matrix products, arithmetic and copies ran while one was open for 10% -> 10% of each run, Pallas kernels for 47% -> 47%
where the time goes in v6:
time: 576 us; the launch traced here: 570 us
  Pallas kernels  296 us (51%)
  waiting for transfers between devices  110 us (19%)
  starting transfers between devices  70.2 us (12%)
  local copies, waits for them, and re-layouts  39.6 us (7%)
  other arithmetic  35.8 us (6%)
  between operations  16.7 us (3%)
    pallas_call x8, Pallas kernels, over_rows(): pl.pallas_call(kernel, grid=(rows // step,), in_specs=in_specs, out_specs...  130 us
    ppermute x70, waiting for transfers between devices, swap_over(): return lax.ppermute(value, BOTH, [(i, i ^ bit) for i in range(count)])  110 us
    ppermute x70, starting transfers between devices, swap_over(): return lax.ppermute(value, BOTH, [(i, i ^ bit) for i in range(count)])  70.1 us
    pallas_call x8, Pallas kernels, weight_grads(): pl.pallas_call(kernel, grid=(len(steps),), in_specs=[pl.BlockSpec((ROWS,...  59.6 us
    pallas_call x4, Pallas kernels, attention_backward(): pl.pallas_call(functools.partial(attention_back_kernel, step=step), grid=...  50.2 us
    pallas_call x4, Pallas kernels, attention_forward(): pl.pallas_call(attention_kernel, grid=(1,), in_specs=[whole(x)] + [block(...  48.2 us
    unnamed x186, local copies, waits for them, and re-layouts  14.6 us
  transfers between devices with their start and end apart: 71, of which 29 were waited for; matrix products, arithmetic and copies ran while one was open for 10% of the time, Pallas kernels for 47%

profile of v6, /device:TPU:0, one launch (start us, length us, event | category | flops | bytes accessed | tf_op | source)
XLA Modules:
  0.0 570.0 jit_solution(17383570697750207741)
XLA Ops:
  7.3 3.0 collective-permute-start.16
  12.6 2.7 collective-permute-start.1
  15.3 1.7 dynamic-slice_bitcast_fusion.3
  19.7 2.9 fusion.59.order_ref.refs_19_
  31.4 1.8 collective-permute-start.3
  33.1 4.5 collective-permute-done.7
  39.9 10.7 %collective-permute-done.3.refs_2_ = bf16[128,1664]{1,0:T(8,128)(2,1)S(1)} collective-permute-done((bf16[128,1664]{1,0:T(8,128)(2,1)S(1)}, bf16[128,1664]{1,0:T(8,128)(2,1)S(1)}, u32[]{:S(2)}, u32[]{:S(2)}) %collective-permute-start.3) | collective-permute-done | bytes 426016 | tf_op jit(solution)/shard_map/ppermute | solution.py:437
  53.1 3.4 collective-permute-done.6.refs_4_
  58.3 2.8 fusion.34
  62.3 2.9 fusion.32.rows_ref
  65.2 13.2 %collective-permute-done.12.refs_1_ = bf16[128,2560]{1,0:T(8,128)(2,1)S(1)} collective-permute-done((bf16[128,2560]{1,0:T(8,128)(2,1)S(1)}, bf16[128,2560]{1,0:T(8,128)(2,1)S(1)}, u32[]{:S(2)}, u32[]{:S(2)}) %collective-permute-start.12) | collective-permute-done | bytes 655392 | tf_op jit(solution)/shard_map/ppermute | solution.py:437
  83.8 3.0 vectors.1
  86.8 7.6 %start.1 = (bf16[1040,1024]{1,0:T(8,128)(2,1)}, bf16[1040,1024]{1,0:T(8,128)(2,1)}) custom-call(bf16[1040,1024]{1,0:T(8,128)(2,1)} %fusion.32.rows_ref, bf16[1024,1024]{1,0:T(8,128)(2,1)} %fusion.59.order_ref.refs_19_, f32[8,1024]{1,0:T(8,128)} %get-tuple-element.193.vec_ref.refs_18_), custom_call_target="tpu_custom_call" | custom-call | flops 8800000000 | bytes 34078720 | tf_op jit(solution)/shard_map/start/pallas_call | solution.py:779
  103.7 12.3 %attention_forward.4 = (bf16[1040,256]{1,0:T(8,128)(2,1)}, bf16[1040,256]{1,0:T(8,128)(2,1)}, bf16[1040,256]{1,0:T(8,128)(2,1)}, bf16[1040,256]{1,0:T(8,128)(2,1)}, f32[8,1040]{1,0:T(8,128)}) custom-call(bf16[1040,1024]{1,0:T(8,128)(2,1)} %get-tuple-element.323.x_ref.refs_1_.refs_0_, bf16[512,1664]{1,0:T(8,128)(2,1)} %copy-done.2, ...), custom_call_target="tpu_custom_call" | custom-call | flops 30000001024 | bytes 28000000 | tf_op jit(solution)/shard_map/attention_forward/pallas_call | solution.py:641
  118.7 11.9 %attention_forward.5 = (bf16[1040,256]{1,0:T(8,128)(2,1)}, bf16[1040,256]{1,0:T(8,128)(2,1)}, bf16[1040,256]{1,0:T(8,128)(2,1)}, bf16[1040,256]{1,0:T(8,128)(2,1)}, f32[8,1040]{1,0:T(8,128)}) custom-call(bf16[1040,1024]{1,0:T(8,128)(2,1)} %get-tuple-element.323.x_ref.refs_1_.refs_0_, bf16[512,1664]{1,0:T(8,128)(2,1)} %copy-done.2, ...), custom_call_target="tpu_custom_call" | custom-call | flops 30000001024 | bytes 28000000 | tf_op jit(solution)/shard_map/attention_forward/pallas_call | solution.py:641
  136.6 2.2 collective-permute-start.27
  138.8 11.8 %attention_forward.6 = (bf16[1040,256]{1,0:T(8,128)(2,1)}, bf16[1040,256]{1,0:T(8,128)(2,1)}, bf16[1040,256]{1,0:T(8,128)(2,1)}, bf16[1040,256]{1,0:T(8,128)(2,1)}, f32[8,1040]{1,0:T(8,128)}) custom-call(bf16[1040,1024]{1,0:T(8,128)(2,1)} %get-tuple-element.323.x_ref.refs_1_.refs_0_, bf16[512,2560]{1,0:T(8,128)(2,1)} %copy-done.6, ...), custom_call_target="tpu_custom_call" | custom-call | flops 30000001024 | bytes 28000000 | tf_op jit(solution)/shard_map/attention_forward/pallas_call | solution.py:641
  155.3 12.2 %attention_forward.7 = (bf16[1040,256]{1,0:T(8,128)(2,1)}, bf16[1040,256]{1,0:T(8,128)(2,1)}, bf16[1040,256]{1,0:T(8,128)(2,1)}, bf16[1040,256]{1,0:T(8,128)(2,1)}, f32[8,1040]{1,0:T(8,128)}) custom-call(bf16[1040,1024]{1,0:T(8,128)(2,1)} %get-tuple-element.323.x_ref.refs_1_.refs_0_, bf16[512,2560]{1,0:T(8,128)(2,1)} %copy-done.6, ...), custom_call_target="tpu_custom_call" | custom-call | flops 30000001024 | bytes 28000000 | tf_op jit(solution)/shard_map/attention_forward/pallas_call | solution.py:641
  171.7 7.2 %middle.1 = (bf16[1040,1024]{1,0:T(8,128)(2,1)}, bf16[1040,1024]{1,0:T(8,128)(2,1)}) custom-call(bf16[1040,256]{1,0:T(8,128)(2,1)} %get-tuple-element.200.a0_ref.o_ref.refs_2_, bf16[1040,256]{1,0:T(8,128)(2,1)} %get-tuple-element.204.a1_ref.o_ref.refs_3_, bf16[1040,256]{1,0:T(8,128)(2,1)} %get-tuple-element.214.a2_ref.refs_4_.o_ref, ...), custom_call_target="tpu_custom_call" | custom-call | flops 8800000000 | bytes 76152832 | tf_op jit(solution)/shard_map/middle/pallas_call | solution.py:779
  179.0 9.8 %collective-permute-done.33.refs_1_ = bf16[128,2816]{1,0:T(8,128)(2,1)S(1)} collective-permute-done((bf16[128,2816]{1,0:T(8,128)(2,1)S(1)}, bf16[128,2816]{1,0:T(8,128)(2,1)S(1)}, u32[]{:S(2)}, u32[]{:S(2)}) %collective-permute-start.33) | collective-permute-done | bytes 720928 | tf_op jit(solution)/shard_map/ppermute | solution.py:437
  192.6 22.5 %hidden.1 = (bf16[1040,2816]{1,0:T(8,128)(2,1)}, bf16[1040,2816]{1,0:T(8,128)(2,1)}, bf16[1040,2816]{1,0:T(8,128)(2,1)}, f32[1040,128]{1,0:T(8,128)}) custom-call(bf16[1040,1024]{1,0:T(8,128)(2,1)} %get-tuple-element.264.x_ref.refs_0_, bf16[512,2816]{1,0:T(8,128)(2,1)} %copy-done.3, bf16[512,2816]{1,0:T(8,128)(2,1)} %collective-permute-done.26.gf_ref, ...), custom_call_target="tpu_custom_call" | custom-call | flops 48000000000 | bytes 127434752 | tf_op jit(solution)/shard_map/hidden/pallas_call | solution.py:779
  215.1 6.9 %collective-permute-done.36 = bf16[512,1024]{1,0:T(8,128)(2,1)S(1)} collective-permute-done((bf16[512,1024]{1,0:T(8,128)(2,1)S(1)}, bf16[512,1024]{1,0:T(8,128)(2,1)S(1)}, u32[]{:S(2)}, u32[]{:S(2)}) %collective-permute-start.36) | collective-permute-done | bytes 1048608 | tf_op jit(solution)/shard_map/ppermute | solution.py:437
  226.8 2.2 collective-permute-done.37.far_ref
  231.2 14.5 %result.1 = bf16[1040,1024]{1,0:T(8,128)(2,1)} custom-call(bf16[1040,2816]{1,0:T(8,128)(2,1)} %get-tuple-element.237.inner_ref.refs_1_, bf16[1040,1024]{1,0:T(8,128)(2,1)} %get-tuple-element.268.middle_ref, bf16[512,2816]{1,0:T(8,128)(2,1)} %copy-done.5, bf16[512,2816]{1,0:T(8,128)(2,1)} %copy-done.86, f32[8,1024]{1,0:T(8,128)} %get-tuple-element.193.vec_ref.refs_18_, ...), custom_call_target="tpu_custom_call" | custom-call | flops 32000000000 | bytes 72073216 | tf_op jit(solution)/shard_map/result/pallas_call | solution.py:779
  247.8 29.6 %hidden_back.1 = (bf16[1040,1024]{1,0:T(8,128)(2,1)}, bf16[1040,2816]{1,0:T(8,128)(2,1)}, bf16[1040,2816]{1,0:T(8,128)(2,1)}, f32[8,2816]{1,0:T(8,128)}, f32[8,1024]{1,0:T(8,128)}) custom-call(bf16[1040,1024]{1,0:T(8,128)(2,1)} %fusion.33.d_ref, bf16[1040,2816]{1,0:T(8,128)(2,1)} %get-tuple-element.254.gate_ref, ...), custom_call_target="tpu_custom_call" | custom-call | flops 32000000000 | bytes 145211392 | tf_op jit(solution)/shard_map/hidden_back/pallas_call | solution.py:779
  277.4 12.0 %weight_grads.8 = bf16[512,5632]{1,0:T(8,128)(2,1)} custom-call(bf16[1040,1024]{1,0:T(8,128)(2,1)S(1)} %copy-done.20, bf16[1040,2816]{1,0:T(8,128)(2,1)} %get-tuple-element.257.refs_1_.dgate_ref, bf16[1040,2816]{1,0:T(8,128)(2,1)} %get-tuple-element.258.refs_2_.dup_ref), custom_call_target="tpu_custom_call" | custom-call | flops 23991418880 | bytes 70287360 | tf_op jit(solution)/shard_map/weight_grads/pallas_call | solution.py:1010
  291.1 5.8 %weight_grads.9 = bf16[512,2816]{1,0:T(8,128)(2,1)S(1)} custom-call(bf16[1040,1024]{1,0:T(8,128)(2,1)S(1)} %copy-done.21, bf16[1040,2816]{1,0:T(8,128)(2,1)} %get-tuple-element.237.inner_ref.refs_1_), custom_call_target="tpu_custom_call" | custom-call | flops 11995709440 | bytes 35143680 | tf_op jit(solution)/shard_map/weight_grads/pallas_call | solution.py:1010
  296.9 2.3 collective-permute-done.39.refs_3_
  303.7 12.8 %weight_grads.10 = bf16[512,5632]{1,0:T(8,128)(2,1)} custom-call(bf16[1040,1024]{1,0:T(8,128)(2,1)S(1)} %copy-done.20, bf16[1040,2816]{1,0:T(8,128)(2,1)} %get-tuple-element.257.refs_1_.dgate_ref, bf16[1040,2816]{1,0:T(8,128)(2,1)} %get-tuple-element.258.refs_2_.dup_ref, bf16[512,5632]{1,0:T(8,128)(2,1)} %collective-permute-done.39.refs_3_), custom_call_target="tpu_custom_call" | custom-call | flops 23991418880 | bytes 70287360 | tf_op jit(solution)/shard_map/weight_grads/pallas_call | solution.py:1010
  316.5 3.0 fusion.60
  321.6 6.8 %weight_grads.11 = bf16[512,2816]{1,0:T(8,128)(2,1)S(1)} custom-call(bf16[1040,1024]{1,0:T(8,128)(2,1)S(1)} %copy-done.21, bf16[1040,2816]{1,0:T(8,128)(2,1)} %get-tuple-element.237.inner_ref.refs_1_, bf16[512,2816]{1,0:T(8,128)(2,1)} %copy-done.87), custom_call_target="tpu_custom_call" | custom-call | flops 11995709440 | bytes 35143680 | tf_op jit(solution)/shard_map/weight_grads/pallas_call | solution.py:1010
  328.5 14.6 %collective-permute-done.42 = bf16[64,5632]{1,0:T(8,128)(2,1)S(1)} collective-permute-done((bf16[64,5632]{1,0:T(8,128)(2,1)S(1)}, bf16[64,5632]{1,0:T(8,128)(2,1)S(1)}, u32[]{:S(2)}, u32[]{:S(2)}) %collective-permute-start.42) | collective-permute-done | bytes 720928 | tf_op jit(solution)/shard_map/ppermute | solution.py:437
  344.3 1.8 add_convert_fusion.4
  347.5 26.4 %middle_back.1 = (bf16[1040,1024]{1,0:T(8,128)(2,1)}, bf16[1040,256]{1,0:T(8,128)(2,1)}, bf16[1040,256]{1,0:T(8,128)(2,1)}, bf16[1040,256]{1,0:T(8,128)(2,1)}, b...) custom-call(bf16[1040,2816]{1,0:T(8,128)(2,1)} %get-tuple-element.257.refs_1_.dgate_ref, ...), custom_call_target="tpu_custom_call" | custom-call | flops 56000000000 | bytes 169279488 | tf_op jit(solution)/shard_map/middle_back/pallas_call | solution.py:779
  374.0 4.7 collective-permute-done.44
  379.5 2.4 add_convert_fusion
  384.3 12.7 %attention_backward.4 = (bf16[1040,256]{1,0:T(8,128)(2,1)S(1)}, bf16[1040,256]{1,0:T(8,128)(2,1)S(1)}, bf16[1040,256]{1,0:T(8,128)(2,1)S(1)}, f32[8,256]{1,0:T(8,128)S(1)}) custom-call(bf16[1040,256]{1,0:T(8,128)(2,1)S(1)} %copy-done.53, bf16[1040,256]{1,0:T(8,128)(2,1)S(1)} %copy-done.54, bf16[1040,256]{1,0:T(8,128)(2,1)S(1)} %copy-done.55, ...), custom_call_target="tpu_custom_call" | custom-call | flops 51999997952 | bytes 20000000 | tf_op jit(solution)/shard_map/attention_backward/pallas_call | solution.py:741
  398.4 2.5 collective-permute-start.48
  400.9 1.9 collective-permute-start.50
  402.9 12.5 %attention_backward.5 = (bf16[1040,256]{1,0:T(8,128)(2,1)S(1)}, bf16[1040,256]{1,0:T(8,128)(2,1)S(1)}, bf16[1040,256]{1,0:T(8,128)(2,1)S(1)}, f32[8,256]{1,0:T(8,128)S(1)}) custom-call(bf16[1040,256]{1,0:T(8,128)(2,1)S(1)} %copy-done.50, bf16[1040,256]{1,0:T(8,128)(2,1)S(1)} %copy-done.51, bf16[1040,256]{1,0:T(8,128)(2,1)S(1)} %copy-done.52, ...), custom_call_target="tpu_custom_call" | custom-call | flops 51999997952 | bytes 20000000 | tf_op jit(solution)/shard_map/attention_backward/pallas_call | solution.py:741
  418.2 6.6 %weight_grads.12 = bf16[512,2560]{1,0:T(8,128)(2,1)} custom-call(bf16[1040,1024]{1,0:T(8,128)(2,1)} %get-tuple-element.324.refs_0_.refs_12_, bf16[1040,1024]{1,0:T(8,128)(2,1)} %get-tuple-element.323.x_ref.refs_1_.refs_0_, bf16[1040,256]{1,0:T(8,128)(2,1)S(1)} %copy-done.34, bf16[1040,256]{1,0:T(8,128)(2,1)S(1)} %copy-done.35, ...), custom_call_target="tpu_custom_call" | custom-call | flops 10905190400 | bytes 31948800 | tf_op jit(solution)/shard_map/weight_grads/pallas_call | solution.py:1010
  425.4 3.0 collective-permute-start.53
  428.4 12.7 %attention_backward.6 = (bf16[1040,256]{1,0:T(8,128)(2,1)S(1)}, bf16[1040,256]{1,0:T(8,128)(2,1)S(1)}, bf16[1040,256]{1,0:T(8,128)(2,1)S(1)}, f32[8,256]{1,0:T(8,128)S(1)}) custom-call(bf16[1040,256]{1,0:T(8,128)(2,1)S(1)} %copy-done.47, bf16[1040,256]{1,0:T(8,128)(2,1)S(1)} %copy-done.48, bf16[1040,256]{1,0:T(8,128)(2,1)S(1)} %copy-done.49, ...), custom_call_target="tpu_custom_call" | custom-call | flops 51999997952 | bytes 20000000 | tf_op jit(solution)/shard_map/attention_backward/pallas_call | solution.py:741
  443.6 7.6 %weight_grads.13 = bf16[512,2560]{1,0:T(8,128)(2,1)} custom-call(bf16[1040,1024]{1,0:T(8,128)(2,1)} %get-tuple-element.324.refs_0_.refs_12_, bf16[1040,1024]{1,0:T(8,128)(2,1)} %get-tuple-element.323.x_ref.refs_1_.refs_0_, bf16[1040,256]{1,0:T(8,128)(2,1)S(1)} %copy-done.34, bf16[1040,256]{1,0:T(8,128)(2,1)S(1)} %copy-done.35, ...), custom_call_target="tpu_custom_call" | custom-call | flops 10905190400 | bytes 31948800 | tf_op jit(solution)/shard_map/weight_grads/pallas_call | solution.py:1010
  451.2 2.2 fusion.62
  454.5 12.3 %attention_backward.7 = (bf16[1040,256]{1,0:T(8,128)(2,1)S(1)}, bf16[1040,256]{1,0:T(8,128)(2,1)S(1)}, bf16[1040,256]{1,0:T(8,128)(2,1)S(1)}, f32[8,256]{1,0:T(8,128)S(1)}) custom-call(bf16[1040,256]{1,0:T(8,128)(2,1)S(1)} %copy-done.44, bf16[1040,256]{1,0:T(8,128)(2,1)S(1)} %copy-done.45, bf16[1040,256]{1,0:T(8,128)(2,1)S(1)} %copy-done.46, ...), custom_call_target="tpu_custom_call" | custom-call | flops 51999997952 | bytes 20000000 | tf_op jit(solution)/shard_map/attention_backward/pallas_call | solution.py:741
  466.9 3.7 collective-permute-done.54
  471.7 3.7 weight_grads.14
  475.9 1.7 collective-permute-start.56
  477.6 11.4 %last.2 = (bf16[528,1024]{1,0:T(8,128)(2,1)}, f32[8,1024]{1,0:T(8,128)}) custom-call(bf16[1040,256]{1,0:T(8,128)(2,1)} %copy-done.38, bf16[1040,256]{1,0:T(8,128)(2,1)} %copy-done.39, bf16[1040,256]{1,0:T(8,128)(2,1)} %copy-done.40, bf16[1040,256]{1,0:T(8,128)(2,1)} %copy-done.41, bf16[1040,256]{1,0:T(8,128)(2,1)} %copy-done.42, ...), custom_call_target="tpu_custom_call" | custom-call | flops 17999998976 | bytes 90177536 | tf_op jit(solution)/shard_map/last/pallas_call | solution.py:779
  489.0 3.1 collective-permute-done.57
  494.6 4.3 weight_grads.15
  498.9 1.9 collective-permute-start.59
  503.1 11.2 %last.3 = (bf16[512,1024]{1,0:T(8,128)(2,1)}, f32[8,1024]{1,0:T(8,128)}) custom-call(bf16[1040,256]{1,0:T(8,128)(2,1)} %copy-done.38, bf16[1040,256]{1,0:T(8,128)(2,1)} %copy-done.39, bf16[1040,256]{1,0:T(8,128)(2,1)} %copy-done.40, bf16[1040,256]{1,0:T(8,128)(2,1)} %copy-done.41, bf16[1040,256]{1,0:T(8,128)(2,1)} %copy-done.42, ...), custom_call_target="tpu_custom_call" | custom-call | flops 17999998976 | bytes 90046464 | tf_op jit(solution)/shard_map/last/pallas_call | solution.py:779
  514.3 1.7 pad_maximum_fusion
  517.1 8.3 %collective-permute-done.58 = bf16[528,1024]{1,0:T(8,128)(2,1)S(1)} collective-permute-done((bf16[528,1024]{1,0:T(8,128)(2,1)}, bf16[528,1024]{1,0:T(8,128)(2,1)S(1)}, u32[]{:S(2)}, u32[]{:S(2)}) %collective-permute-start.58) | collective-permute-done | bytes 1081376 | tf_op jit(solution)/shard_map/ppermute | solution.py:437
  525.5 1.9 fusion.37
  531.1 2.0 reduce_sum.9
  536.4 2.4 collective-permute-done.67
  541.0 2.0 collective-permute-done.68
  543.0 2.5 collective-permute-start.69
  549.1 5.1 collective-permute-done.63
  554.3 2.7 collective-permute-start.64
  557.0 3.9 collective-permute-done.64
  (418 shorter events, 110.0 us)
Async XLA Ops:
  7.2 523.9 %all-gather.3.cloned.1.call-start = ((), (), s32[]{:S(2)}) async-start(), calls=%async_computation | async-start | bytes 2973696 | tf_op jit(solution)/shard_map/all_gather | solution.py:1178
  7.3 20.5 %collective-permute-start.16 = (s32[512,2]{0,1:T(2,128)}, s32[512,2]{0,1:T(2,128)}, u32[]{:S(2)}, u32[]{:S(2)}) collective-permute-start(s32[512,2]{0,1:T(2,128)} %param.20), channel_id=1, source_target_pairs={{0,1},{1,0},{2,3},{3,2},{4,5},{5,4},{6,7},{7,6},{8,9},{9,8},{10,11... | collective-permute-start | bytes 12296 | tf_op jit(solution)/shard_map/ppermute | solution.py:437
  12.6 10.0 %collective-permute-start.1 = (bf16[32,1664]{1,0:T(8,128)(2,1)S(1)}, bf16[32,1664]{1,0:T(8,128)(2,1)}, u32[]{:S(2)}, u32[]{:S(2)}) collective-permute-start(bf16[32,1664]{1,0:T(8,128)(2,1)S(1)} %fusion.36), channel_id=1, source_target_pairs={{0,16},{1,17},{2,18},{3,19},{4,20},{5,21},{6,22},{7,23},{8,24},{9,... | collective-permute-start | bytes 319496 | tf_op jit(solution)/shard_map/ppermute | solution.py:437
  17.0 33.5 %collective-permute-start = (bf16[512,1024]{1,0:T(8,128)(2,1)S(1)}, bf16[512,1024]{1,0:T(8,128)(2,1)S(1)}, u32[]{:S(2)}, u32[]{:S(2)}) collective-permute-start(bf16[512,1024]{1,0:T(8,128)(2,1)S(1)} %get-tuple-element.366), channel_id=1, source_target_pairs={{0,1},{1,0},{2,3},{3,2},{4,5},{5,4},{6,7},{7,6},{8,9},{9,8},{10,11... | collective-permute-start | bytes 3145736 | tf_op jit(solution)/shard_map/ppermute | solution.py:437
  23.5 6.2 %collective-permute-start.2 = (bf16[64,1664]{1,0:T(8,128)(2,1)S(1)}, bf16[64,1664]{1,0:T(8,128)(2,1)S(1)}, u32[]{:S(2)}, u32[]{:S(2)}) collective-permute-start(bf16[64,1664]{1,0:T(8,128)(2,1)S(1)} %pad_maximum_fusion.11), channel_id=1, source_target_pairs={{0,8},{1,9},{2,10},{3,11},{4,12},{5,13},{6,14},{7,15},{8,0},{9,1},... | collective-permute-start | bytes 638984 | tf_op jit(solution)/shard_map/ppermute | solution.py:437
  28.5 9.1 %collective-permute-start.7 = (bf16[32,2560]{1,0:T(8,128)(2,1)S(1)}, bf16[32,2560]{1,0:T(8,128)(2,1)S(1)}, u32[]{:S(2)}, u32[]{:S(2)}) collective-permute-start(bf16[32,2560]{1,0:T(8,128)(2,1)S(1)} %pad_maximum_fusion.12), channel_id=1, source_target_pairs={{0,16},{1,17},{2,18},{3,19},{4,20},{5,21},{6,22},{7,23},{8,24},{9,... | collective-permute-start | bytes 491528 | tf_op jit(solution)/shard_map/ppermute | solution.py:437
  29.8 10.1 %collective-permute-start.4 = (bf16[128,1664]{1,0:T(8,128)(2,1)S(1)}, bf16[128,1664]{1,0:T(8,128)(2,1)S(1)}, u32[]{:S(2)}, u32[]{:S(2)}) collective-permute-start(bf16[128,1664]{1,0:T(8,128)(2,1)S(1)} %pad_maximum_fusion.6.refs_0_), channel_id=1, source_target_pairs={{0,4},{1,5},{2,6},{3,7},{4,0},{5,1},{6,2},{7,3},{8,12},{9,13},{10,... | collective-permute-start | bytes 1277960 | tf_op jit(solution)/shard_map/ppermute | solution.py:437
  31.4 19.2 %collective-permute-start.3 = (bf16[128,1664]{1,0:T(8,128)(2,1)S(1)}, bf16[128,1664]{1,0:T(8,128)(2,1)S(1)}, u32[]{:S(2)}, u32[]{:S(2)}) collective-permute-start(bf16[128,1664]{1,0:T(8,128)(2,1)S(1)} %pad_maximum_fusion.6.refs_0_), channel_id=1, source_target_pairs={{0,1},{1,0},{2,3},{3,2},{4,5},{5,4},{6,7},{7,6},{8,9},{9,8},{10,11... | collective-permute-start | bytes 1277960 | tf_op jit(solution)/shard_map/ppermute | solution.py:437
  37.6 15.5 %collective-permute-start.8 = (bf16[64,2560]{1,0:T(8,128)(2,1)S(1)}, bf16[64,2560]{1,0:T(8,128)(2,1)S(1)}, u32[]{:S(2)}, u32[]{:S(2)}) collective-permute-start(bf16[64,2560]{1,0:T(8,128)(2,1)S(1)} %pad_maximum_fusion.10), channel_id=1, source_target_pairs={{0,8},{1,9},{2,10},{3,11},{4,12},{5,13},{6,14},{7,15},{8,0},{9,1},... | collective-permute-start | bytes 983048 | tf_op jit(solution)/shard_map/ppermute | solution.py:437
  37.7 15.4 %collective-permute-start.9 = (bf16[32,2816]{1,0:T(8,128)(2,1)S(1)}, bf16[32,2816]{1,0:T(8,128)(2,1)S(1)}, u32[]{:S(2)}, u32[]{:S(2)}) collective-permute-start(bf16[32,2816]{1,0:T(8,128)(2,1)S(1)} %pad.33), channel_id=1, source_target_pairs={{0,16},{1,17},{2,18},{3,19},{4,20},{5,21},{6,22},{7,23},{8,24},{9,... | collective-permute-start | bytes 540680 | tf_op jit(solution)/shard_map/ppermute | solution.py:437
  50.6 5.9 %collective-permute-start.6 = (bf16[64,1664]{1,0:T(8,128)(2,1)S(1)}, bf16[64,1664]{1,0:T(8,128)(2,1)S(1)}, u32[]{:S(2)}, u32[]{:S(2)}) collective-permute-start(bf16[64,1664]{1,0:T(8,128)(2,1)S(1)} %slice.388), channel_id=1, source_target_pairs={{0,4},{1,5},{2,6},{3,7},{4,0},{5,1},{6,2},{7,3},{8,12},{9,13},{10,... | collective-permute-start | bytes 638984 | tf_op jit(solution)/shard_map/ppermute | solution.py:437
  58.2 20.4 %collective-permute-start.10 = (bf16[512,1664]{1,0:T(8,128)(2,1)S(1)}, bf16[512,1664]{1,0:T(8,128)(2,1)S(1)}, u32[]{:S(2)}, u32[]{:S(2)}) collective-permute-start(bf16[512,1664]{1,0:T(8,128)(2,1)S(1)} %pack_rows.5.near_ref.qn_ref.kn_ref.vn_ref.refs_14_), channel_id=1, source_target_pairs={{0,2},{1,3},{2,0},{3,1},{4,6},{5,7},{6,4},{7,5},{8,10},{9,11},{10,... | collective-permute-start | bytes 5111816 | tf_op jit(solution)/shard_map/ppermute | solution.py:437
  61.2 17.2 %collective-permute-start.12 = (bf16[128,2560]{1,0:T(8,128)(2,1)S(1)}, bf16[128,2560]{1,0:T(8,128)(2,1)S(1)}, u32[]{:S(2)}, u32[]{:S(2)}) collective-permute-start(bf16[128,2560]{1,0:T(8,128)(2,1)S(1)} %constant_dynamic-update-slice_fusion.refs_0_), channel_id=1, source_target_pairs={{0,4},{1,5},{2,6},{3,7},{4,0},{5,1},{6,2},{7,3},{8,12},{9,13},{10,... | collective-permute-start | bytes 1966088 | tf_op jit(solution)/shard_map/ppermute | solution.py:437
  61.7 16.8 %collective-permute-start.11 = (bf16[128,2560]{1,0:T(8,128)(2,1)S(1)}, bf16[128,2560]{1,0:T(8,128)(2,1)S(1)}, u32[]{:S(2)}, u32[]{:S(2)}) collective-permute-start(bf16[128,2560]{1,0:T(8,128)(2,1)S(1)} %constant_dynamic-update-slice_fusion.refs_0_), channel_id=1, source_target_pairs={{0,1},{1,0},{2,3},{3,2},{4,5},{5,4},{6,7},{7,6},{8,9},{9,8},{10,11... | collective-permute-start | bytes 1966088 | tf_op jit(solution)/shard_map/ppermute | solution.py:437
  80.2 15.3 %collective-permute-start.15 = (bf16[64,2560]{1,0:T(8,128)(2,1)}, bf16[64,2560]{1,0:T(8,128)(2,1)S(1)}, u32[]{:S(2)}, u32[]{:S(2)}) collective-permute-start(bf16[64,2560]{1,0:T(8,128)(2,1)} %slice.393), channel_id=1, source_target_pairs={{0,4},{1,5},{2,6},{3,7},{4,0},{5,1},{6,2},{7,3},{8,12},{9,13},{10,... | collective-permute-start | bytes 983048 | tf_op jit(solution)/shard_map/ppermute | solution.py:437
  81.7 14.6 %collective-permute-start.14 = (bf16[64,2560]{1,0:T(8,128)(2,1)}, bf16[64,2560]{1,0:T(8,128)(2,1)S(1)}, u32[]{:S(2)}, u32[]{:S(2)}) collective-permute-start(bf16[64,2560]{1,0:T(8,128)(2,1)} %slice.392), channel_id=1, source_target_pairs={{0,1},{1,0},{2,3},{3,2},{4,5},{5,4},{6,7},{7,6},{8,9},{9,8},{10,11... | collective-permute-start | bytes 983048 | tf_op jit(solution)/shard_map/ppermute | solution.py:437
  82.2 12.2 %collective-permute-start.13 = (bf16[64,2816]{1,0:T(8,128)(2,1)S(1)}, bf16[64,2816]{1,0:T(8,128)(2,1)}, u32[]{:S(2)}, u32[]{:S(2)}) collective-permute-start(bf16[64,2816]{1,0:T(8,128)(2,1)S(1)} %pad_maximum_fusion.7), channel_id=1, source_target_pairs={{0,8},{1,9},{2,10},{3,11},{4,12},{5,13},{6,14},{7,15},{8,0},{9,1},... | collective-permute-start | bytes 1081352 | tf_op jit(solution)/shard_map/ppermute | solution.py:437
  97.0 19.1 %collective-permute-start.18 = (bf16[128,2816]{1,0:T(8,128)(2,1)S(1)}, bf16[128,2816]{1,0:T(8,128)(2,1)S(1)}, u32[]{:S(2)}, u32[]{:S(2)}) collective-permute-start(bf16[128,2816]{1,0:T(8,128)(2,1)S(1)} %constant_dynamic-update-slice_fusion.4.refs_0_), channel_id=1, source_target_pairs={{0,4},{1,5},{2,6},{3,7},{4,0},{5,1},{6,2},{7,3},{8,12},{9,13},{10,... | collective-permute-start | bytes 2162696 | tf_op jit(solution)/shard_map/ppermute | solution.py:437
  97.5 18.6 %collective-permute-start.17 = (bf16[128,2816]{1,0:T(8,128)(2,1)S(1)}, bf16[128,2816]{1,0:T(8,128)(2,1)S(1)}, u32[]{:S(2)}, u32[]{:S(2)}) collective-permute-start(bf16[128,2816]{1,0:T(8,128)(2,1)S(1)} %constant_dynamic-update-slice_fusion.4.refs_0_), channel_id=1, source_target_pairs={{0,1},{1,0},{2,3},{3,2},{4,5},{5,4},{6,7},{7,6},{8,9},{9,8},{10,11... | collective-permute-start | bytes 2162696 | tf_op jit(solution)/shard_map/ppermute | solution.py:437
  103.3 12.7 %collective-permute-start.19 = (bf16[32,2816]{1,0:T(8,128)(2,1)S(1)}, bf16[32,2816]{1,0:T(8,128)(2,1)S(1)}, u32[]{:S(2)}, u32[]{:S(2)}) collective-permute-start(bf16[32,2816]{1,0:T(8,128)(2,1)S(1)} %copy-done.70), channel_id=1, source_target_pairs={{0,16},{1,17},{2,18},{3,19},{4,20},{5,21},{6,22},{7,23},{8,24},{9,... | collective-permute-start | bytes 540680 | tf_op jit(solution)/shard_map/ppermute | solution.py:437
  103.7 29.2 %collective-permute-start.20 = (bf16[512,2560]{1,0:T(8,128)(2,1)S(1)}, bf16[512,2560]{1,0:T(8,128)(2,1)}, u32[]{:S(2)}, u32[]{:S(2)}) collective-permute-start(bf16[512,2560]{1,0:T(8,128)(2,1)S(1)} %pack_rows.6.qn_ref.kn_ref.vn_ref.na_ref.nb_ref.refs_16_), channel_id=1, source_target_pairs={{0,2},{1,3},{2,0},{3,1},{4,6},{5,7},{6,4},{7,5},{8,10},{9,11},{10,... | collective-permute-start | bytes 7864328 | tf_op jit(solution)/shard_map/ppermute | solution.py:437
  116.2 16.0 %collective-permute-start.22 = (bf16[64,2816]{1,0:T(8,128)(2,1)S(1)}, bf16[64,2816]{1,0:T(8,128)(2,1)S(1)}, u32[]{:S(2)}, u32[]{:S(2)}) collective-permute-start(bf16[64,2816]{1,0:T(8,128)(2,1)S(1)} %slice.397), channel_id=1, source_target_pairs={{0,4},{1,5},{2,6},{3,7},{4,0},{5,1},{6,2},{7,3},{8,12},{9,13},{10,... | collective-permute-start | bytes 1081352 | tf_op jit(solution)/shard_map/ppermute | solution.py:437
  117.7 14.5 %collective-permute-start.21 = (bf16[64,2816]{1,0:T(8,128)(2,1)S(1)}, bf16[64,2816]{1,0:T(8,128)(2,1)S(1)}, u32[]{:S(2)}, u32[]{:S(2)}) collective-permute-start(bf16[64,2816]{1,0:T(8,128)(2,1)S(1)} %slice.396), channel_id=1, source_target_pairs={{0,1},{1,0},{2,3},{3,2},{4,5},{5,4},{6,7},{7,6},{8,9},{9,8},{10,11... | collective-permute-start | bytes 1081352 | tf_op jit(solution)/shard_map/ppermute | solution.py:437
  118.3 13.2 %collective-permute-start.23 = (bf16[64,2816]{1,0:T(8,128)(2,1)S(1)}, bf16[64,2816]{1,0:T(8,128)(2,1)S(1)}, u32[]{:S(2)}, u32[]{:S(2)}) collective-permute-start(bf16[64,2816]{1,0:T(8,128)(2,1)S(1)} %pad_maximum_fusion.8), channel_id=1, source_target_pairs={{0,8},{1,9},{2,10},{3,11},{4,12},{5,13},{6,14},{7,15},{8,0},{9,1},... | collective-permute-start | bytes 1081352 | tf_op jit(solution)/shard_map/ppermute | solution.py:437
  132.9 17.7 %collective-permute-start.25 = (bf16[128,2816]{1,0:T(8,128)(2,1)}, bf16[128,2816]{1,0:T(8,128)(2,1)S(1)}, u32[]{:S(2)}, u32[]{:S(2)}) collective-permute-start(bf16[128,2816]{1,0:T(8,128)(2,1)} %constant_dynamic-update-slice_fusion.6.refs_0_), channel_id=1, source_target_pairs={{0,4},{1,5},{2,6},{3,7},{4,0},{5,1},{6,2},{7,3},{8,12},{9,13},{10,... | collective-permute-start | bytes 2162696 | tf_op jit(solution)/shard_map/ppermute | solution.py:437
  133.4 17.2 %collective-permute-start.24 = (bf16[128,2816]{1,0:T(8,128)(2,1)}, bf16[128,2816]{1,0:T(8,128)(2,1)S(1)}, u32[]{:S(2)}, u32[]{:S(2)}) collective-permute-start(bf16[128,2816]{1,0:T(8,128)(2,1)} %constant_dynamic-update-slice_fusion.6.refs_0_), channel_id=1, source_target_pairs={{0,1},{1,0},{2,3},{3,2},{4,5},{5,4},{6,7},{7,6},{8,9},{9,8},{10,11... | collective-permute-start | bytes 2162696 | tf_op jit(solution)/shard_map/ppermute | solution.py:437
  136.6 13.9 %collective-permute-start.27 = (bf16[32,2816]{1,0:T(8,128)(2,1)S(1)}, bf16[32,2816]{1,0:T(8,128)(2,1)S(1)}, u32[]{:S(2)}, u32[]{:S(2)}) collective-permute-start(bf16[32,2816]{1,0:T(8,128)(2,1)S(1)} %pad.36), channel_id=1, source_target_pairs={{0,16},{1,17},{2,18},{3,19},{4,20},{5,21},{6,22},{7,23},{8,24},{9,... | collective-permute-start | bytes 540680 | tf_op jit(solution)/shard_map/ppermute | solution.py:437
  138.8 11.8 %collective-permute-start.26 = (bf16[512,2816]{1,0:T(8,128)(2,1)S(1)}, bf16[512,2816]{1,0:T(8,128)(2,1)}, u32[]{:S(2)}, u32[]{:S(2)}) collective-permute-start(bf16[512,2816]{1,0:T(8,128)(2,1)S(1)} %pack_rows.7.gn_ref), channel_id=1, source_target_pairs={{0,2},{1,3},{2,0},{3,1},{4,6},{5,7},{6,4},{7,5},{8,10},{9,11},{10,... | collective-permute-start | bytes 8650760 | tf_op jit(solution)/shard_map/ppermute | solution.py:437
  150.7 16.8 %collective-permute-start.29 = (bf16[64,2816]{1,0:T(8,128)(2,1)S(1)}, bf16[64,2816]{1,0:T(8,128)(2,1)S(1)}, u32[]{:S(2)}, u32[]{:S(2)}) collective-permute-start(bf16[64,2816]{1,0:T(8,128)(2,1)S(1)} %slice.399), channel_id=1, source_target_pairs={{0,4},{1,5},{2,6},{3,7},{4,0},{5,1},{6,2},{7,3},{8,12},{9,13},{10,... | collective-permute-start | bytes 1081352 | tf_op jit(solution)/shard_map/ppermute | solution.py:437
  152.3 15.2 %collective-permute-start.28 = (bf16[64,2816]{1,0:T(8,128)(2,1)S(1)}, bf16[64,2816]{1,0:T(8,128)(2,1)S(1)}, u32[]{:S(2)}, u32[]{:S(2)}) collective-permute-start(bf16[64,2816]{1,0:T(8,128)(2,1)S(1)} %slice.398), channel_id=1, source_target_pairs={{0,1},{1,0},{2,3},{3,2},{4,5},{5,4},{6,7},{7,6},{8,9},{9,8},{10,11... | collective-permute-start | bytes 1081352 | tf_op jit(solution)/shard_map/ppermute | solution.py:437
  153.7 13.8 %collective-permute-start.30 = (bf16[64,2816]{1,0:T(8,128)(2,1)S(1)}, bf16[64,2816]{1,0:T(8,128)(2,1)S(1)}, u32[]{:S(2)}, u32[]{:S(2)}) collective-permute-start(bf16[64,2816]{1,0:T(8,128)(2,1)S(1)} %pad_maximum_fusion.9), channel_id=1, source_target_pairs={{0,8},{1,9},{2,10},{3,11},{4,12},{5,13},{6,14},{7,15},{8,0},{9,1},... | collective-permute-start | bytes 1081352 | tf_op jit(solution)/shard_map/ppermute | solution.py:437
  169.2 19.8 %collective-permute-start.31 = (bf16[512,2816]{1,0:T(8,128)(2,1)S(1)}, bf16[512,2816]{1,0:T(8,128)(2,1)}, u32[]{:S(2)}, u32[]{:S(2)}) collective-permute-start(bf16[512,2816]{1,0:T(8,128)(2,1)S(1)} %pack_rows.8.un_ref), channel_id=1, source_target_pairs={{0,2},{1,3},{2,0},{3,1},{4,6},{5,7},{6,4},{7,5},{8,10},{9,11},{10,... | collective-permute-start | bytes 8650760 | tf_op jit(solution)/shard_map/ppermute | solution.py:437
  170.6 18.2 %collective-permute-start.33 = (bf16[128,2816]{1,0:T(8,128)(2,1)S(1)}, bf16[128,2816]{1,0:T(8,128)(2,1)S(1)}, u32[]{:S(2)}, u32[]{:S(2)}) collective-permute-start(bf16[128,2816]{1,0:T(8,128)(2,1)S(1)} %constant_dynamic-update-slice_fusion.8.refs_0_), channel_id=1, source_target_pairs={{0,4},{1,5},{2,6},{3,7},{4,0},{5,1},{6,2},{7,3},{8,12},{9,13},{10,... | collective-permute-start | bytes 2162696 | tf_op jit(solution)/shard_map/ppermute | solution.py:437
  171.1 17.8 %collective-permute-start.32 = (bf16[128,2816]{1,0:T(8,128)(2,1)S(1)}, bf16[128,2816]{1,0:T(8,128)(2,1)S(1)}, u32[]{:S(2)}, u32[]{:S(2)}) collective-permute-start(bf16[128,2816]{1,0:T(8,128)(2,1)S(1)} %constant_dynamic-update-slice_fusion.8.refs_0_), channel_id=1, source_target_pairs={{0,1},{1,0},{2,3},{3,2},{4,5},{5,4},{6,7},{7,6},{8,9},{9,8},{10,11... | collective-permute-start | bytes 2162696 | tf_op jit(solution)/shard_map/ppermute | solution.py:437
  189.0 26.1 %collective-permute-start.35 = (bf16[64,2816]{1,0:T(8,128)(2,1)S(1)}, bf16[64,2816]{1,0:T(8,128)(2,1)S(1)}, u32[]{:S(2)}, u32[]{:S(2)}) collective-permute-start(bf16[64,2816]{1,0:T(8,128)(2,1)S(1)} %slice.401), channel_id=1, source_target_pairs={{0,4},{1,5},{2,6},{3,7},{4,0},{5,1},{6,2},{7,3},{8,12},{9,13},{10,... | collective-permute-start | bytes 1081352 | tf_op jit(solution)/shard_map/ppermute | solution.py:437
  190.6 24.5 %collective-permute-start.34 = (bf16[64,2816]{1,0:T(8,128)(2,1)S(1)}, bf16[64,2816]{1,0:T(8,128)(2,1)S(1)}, u32[]{:S(2)}, u32[]{:S(2)}) collective-permute-start(bf16[64,2816]{1,0:T(8,128)(2,1)S(1)} %slice.400), channel_id=1, source_target_pairs={{0,1},{1,0},{2,3},{3,2},{4,5},{5,4},{6,7},{7,6},{8,9},{9,8},{10,11... | collective-permute-start | bytes 1081352 | tf_op jit(solution)/shard_map/ppermute | solution.py:437
  191.2 30.8 %collective-permute-start.36 = (bf16[512,1024]{1,0:T(8,128)(2,1)S(1)}, bf16[512,1024]{1,0:T(8,128)(2,1)S(1)}, u32[]{:S(2)}, u32[]{:S(2)}) collective-permute-start(bf16[512,1024]{1,0:T(8,128)(2,1)S(1)} %get-tuple-element.241), channel_id=1, source_target_pairs={{0,1},{1,0},{2,3},{3,2},{4,5},{5,4},{6,7},{7,6},{8,9},{9,8},{10,11... | collective-permute-start | bytes 3145736 | tf_op jit(solution)/shard_map/ppermute | solution.py:437
  247.1 30.3 %collective-permute-start.38 = (bf16[528,1024]{1,0:T(8,128)(2,1)S(1)}, bf16[528,1024]{1,0:T(8,128)(2,1)S(1)}, u32[]{:S(2)}, u32[]{:S(2)}) collective-permute-start(bf16[528,1024]{1,0:T(8,128)(2,1)S(1)} %slice.402), channel_id=1, source_target_pairs={{0,1},{1,0},{2,3},{3,2},{4,5},{5,4},{6,7},{7,6},{8,9},{9,8},{10,11... | collective-permute-start | bytes 3244040 | tf_op jit(solution)/shard_map/ppermute | solution.py:437
  289.4 9.8 %collective-permute-start.39 = (bf16[512,5632]{1,0:T(8,128)(2,1)}, bf16[512,5632]{1,0:T(8,128)(2,1)}, u32[]{:S(2)}, u32[]{:S(2)}) collective-permute-start(bf16[512,5632]{1,0:T(8,128)(2,1)} %weight_grads.8), channel_id=1, source_target_pairs={{0,2},{1,3},{2,0},{3,1},{4,6},{5,7},{6,4},{7,5},{8,10},{9,11},{10,... | collective-permute-start | bytes 17301512 | tf_op jit(solution)/shard_map/ppermute | solution.py:437
  299.2 17.3 %collective-permute-start.40 = (bf16[512,2816]{1,0:T(8,128)(2,1)S(1)}, bf16[512,2816]{1,0:T(8,128)(2,1)S(1)}, u32[]{:S(2)}, u32[]{:S(2)}) collective-permute-start(bf16[512,2816]{1,0:T(8,128)(2,1)S(1)} %weight_grads.9), channel_id=1, source_target_pairs={{0,2},{1,3},{2,0},{3,1},{4,6},{5,7},{6,4},{7,5},{8,10},{9,11},{10,... | collective-permute-start | bytes 8650760 | tf_op jit(solution)/shard_map/ppermute | solution.py:437
  319.5 23.5 %collective-permute-start.42 = (bf16[64,5632]{1,0:T(8,128)(2,1)S(1)}, bf16[64,5632]{1,0:T(8,128)(2,1)S(1)}, u32[]{:S(2)}, u32[]{:S(2)}) collective-permute-start(bf16[64,5632]{1,0:T(8,128)(2,1)S(1)} %get-tuple-element.351), channel_id=1, source_target_pairs={{0,1},{1,0},{2,3},{3,2},{4,5},{5,4},{6,7},{7,6},{8,9},{9,8},{10,11... | collective-permute-start | bytes 2162696 | tf_op jit(solution)/shard_map/ppermute | solution.py:437
  321.0 23.2 %collective-permute-start.41 = (bf16[64,5632]{1,0:T(8,128)(2,1)S(1)}, bf16[64,5632]{1,0:T(8,128)(2,1)S(1)}, u32[]{:S(2)}, u32[]{:S(2)}) collective-permute-start(bf16[64,5632]{1,0:T(8,128)(2,1)S(1)} %get-tuple-element.353), channel_id=1, source_target_pairs={{0,4},{1,5},{2,6},{3,7},{4,0},{5,1},{6,2},{7,3},{8,12},{9,13},{10,... | collective-permute-start | bytes 2162696 | tf_op jit(solution)/shard_map/ppermute | solution.py:437
  346.3 32.5 %collective-permute-start.44 = (bf16[128,5632]{1,0:T(8,128)(2,1)S(1)}, bf16[128,5632]{1,0:T(8,128)(2,1)S(1)}, u32[]{:S(2)}, u32[]{:S(2)}) collective-permute-start(bf16[128,5632]{1,0:T(8,128)(2,1)S(1)} %pad_maximum_fusion.1), channel_id=1, source_target_pairs={{0,1},{1,0},{2,3},{3,2},{4,5},{5,4},{6,7},{7,6},{8,9},{9,8},{10,11... | collective-permute-start | bytes 4325384 | tf_op jit(solution)/shard_map/ppermute | solution.py:437
  346.9 32.6 %collective-permute-start.43 = (bf16[128,5632]{1,0:T(8,128)(2,1)S(1)}, bf16[128,5632]{1,0:T(8,128)(2,1)}, u32[]{:S(2)}, u32[]{:S(2)}) collective-permute-start(bf16[128,5632]{1,0:T(8,128)(2,1)S(1)} %pad_maximum_fusion.2), channel_id=1, source_target_pairs={{0,4},{1,5},{2,6},{3,7},{4,0},{5,1},{6,2},{7,3},{8,12},{9,13},{10,... | collective-permute-start | bytes 4325384 | tf_op jit(solution)/shard_map/ppermute | solution.py:437
  382.0 16.2 %collective-permute-start.45 = (bf16[64,5632]{1,0:T(8,128)(2,1)S(1)}, bf16[64,5632]{1,0:T(8,128)(2,1)S(1)}, u32[]{:S(2)}, u32[]{:S(2)}) collective-permute-start(bf16[64,5632]{1,0:T(8,128)(2,1)S(1)} %slice.415), channel_id=1, source_target_pairs={{0,8},{1,9},{2,10},{3,11},{4,12},{5,13},{6,14},{7,15},{8,0},{9,1},... | collective-permute-start | bytes 2162696 | tf_op jit(solution)/shard_map/ppermute | solution.py:437
  382.2 14.9 %collective-permute-start.47 = (bf16[64,2816]{1,0:T(8,128)(2,1)S(1)}, bf16[64,2816]{1,0:T(8,128)(2,1)S(1)}, u32[]{:S(2)}, u32[]{:S(2)}) collective-permute-start(bf16[64,2816]{1,0:T(8,128)(2,1)S(1)} %get-tuple-element.357), channel_id=1, source_target_pairs={{0,1},{1,0},{2,3},{3,2},{4,5},{5,4},{6,7},{7,6},{8,9},{9,8},{10,11... | collective-permute-start | bytes 1081352 | tf_op jit(solution)/shard_map/ppermute | solution.py:437
  383.3 13.8 %collective-permute-start.46 = (bf16[64,2816]{1,0:T(8,128)(2,1)S(1)}, bf16[64,2816]{1,0:T(8,128)(2,1)S(1)}, u32[]{:S(2)}, u32[]{:S(2)}) collective-permute-start(bf16[64,2816]{1,0:T(8,128)(2,1)S(1)} %get-tuple-element.359), channel_id=1, source_target_pairs={{0,4},{1,5},{2,6},{3,7},{4,0},{5,1},{6,2},{7,3},{8,12},{9,13},{10,... | collective-permute-start | bytes 1081352 | tf_op jit(solution)/shard_map/ppermute | solution.py:437
  398.4 17.0 %collective-permute-start.48 = (bf16[32,5632]{1,0:T(8,128)(2,1)S(1)}, bf16[32,5632]{1,0:T(8,128)(2,1)S(1)}, u32[]{:S(2)}, u32[]{:S(2)}) collective-permute-start(bf16[32,5632]{1,0:T(8,128)(2,1)S(1)} %slice.423), channel_id=1, source_target_pairs={{0,16},{1,17},{2,18},{3,19},{4,20},{5,21},{6,22},{7,23},{8,24},{9,... | collective-permute-start | bytes 1081352 | tf_op jit(solution)/shard_map/ppermute | solution.py:437
  400.9 15.5 %collective-permute-start.50 = (bf16[128,2816]{1,0:T(8,128)(2,1)S(1)}, bf16[128,2816]{1,0:T(8,128)(2,1)S(1)}, u32[]{:S(2)}, u32[]{:S(2)}) collective-permute-start(bf16[128,2816]{1,0:T(8,128)(2,1)S(1)} %pad_maximum_fusion.4), channel_id=1, source_target_pairs={{0,1},{1,0},{2,3},{3,2},{4,5},{5,4},{6,7},{7,6},{8,9},{9,8},{10,11... | collective-permute-start | bytes 2162696 | tf_op jit(solution)/shard_map/ppermute | solution.py:437
  402.8 13.7 %collective-permute-start.49 = (bf16[128,2816]{1,0:T(8,128)(2,1)S(1)}, bf16[128,2816]{1,0:T(8,128)(2,1)S(1)}, u32[]{:S(2)}, u32[]{:S(2)}) collective-permute-start(bf16[128,2816]{1,0:T(8,128)(2,1)S(1)} %pad_maximum_fusion.5), channel_id=1, source_target_pairs={{0,4},{1,5},{2,6},{3,7},{4,0},{5,1},{6,2},{7,3},{8,12},{9,13},{10,... | collective-permute-start | bytes 2162696 | tf_op jit(solution)/shard_map/ppermute | solution.py:437
  416.8 8.5 %collective-permute-start.51 = (bf16[64,2816]{1,0:T(8,128)(2,1)S(1)}, bf16[64,2816]{1,0:T(8,128)(2,1)S(1)}, u32[]{:S(2)}, u32[]{:S(2)}) collective-permute-start(bf16[64,2816]{1,0:T(8,128)(2,1)S(1)} %slice.426), channel_id=1, source_target_pairs={{0,8},{1,9},{2,10},{3,11},{4,12},{5,13},{6,14},{7,15},{8,0},{9,1},... | collective-permute-start | bytes 1081352 | tf_op jit(solution)/shard_map/ppermute | solution.py:437
  425.4 15.8 %collective-permute-start.53 = (bf16[32,2816]{1,0:T(8,128)(2,1)S(1)}, bf16[32,2816]{1,0:T(8,128)(2,1)S(1)}, u32[]{:S(2)}, u32[]{:S(2)}) collective-permute-start(bf16[32,2816]{1,0:T(8,128)(2,1)S(1)} %slice.428), channel_id=1, source_target_pairs={{0,16},{1,17},{2,18},{3,19},{4,20},{5,21},{6,22},{7,23},{8,24},{9,... | collective-permute-start | bytes 540680 | tf_op jit(solution)/shard_map/ppermute | solution.py:437
  428.4 13.7 %collective-permute-start.52 = (bf16[512,2560]{1,0:T(8,128)(2,1)}, bf16[512,2560]{1,0:T(8,128)(2,1)S(1)}, u32[]{:S(2)}, u32[]{:S(2)}) collective-permute-start(bf16[512,2560]{1,0:T(8,128)(2,1)} %weight_grads.12), channel_id=1, source_target_pairs={{0,2},{1,3},{2,0},{3,1},{4,6},{5,7},{6,4},{7,5},{8,10},{9,11},{10,... | collective-permute-start | bytes 7864328 | tf_op jit(solution)/shard_map/ppermute | solution.py:437
  453.5 17.1 %collective-permute-start.54 = (bf16[128,2560]{1,0:T(8,128)(2,1)S(1)}, bf16[128,2560]{1,0:T(8,128)(2,1)S(1)}, u32[]{:S(2)}, u32[]{:S(2)}) collective-permute-start(bf16[128,2560]{1,0:T(8,128)(2,1)S(1)} %get-tuple-element.362), channel_id=1, source_target_pairs={{0,4},{1,5},{2,6},{3,7},{4,0},{5,1},{6,2},{7,3},{8,12},{9,13},{10,... | collective-permute-start | bytes 1966088 | tf_op jit(solution)/shard_map/ppermute | solution.py:437
  475.5 16.6 %collective-permute-start.57 = (bf16[128,2560]{1,0:T(8,128)(2,1)}, bf16[128,2560]{1,0:T(8,128)(2,1)S(1)}, u32[]{:S(2)}, u32[]{:S(2)}) collective-permute-start(bf16[128,2560]{1,0:T(8,128)(2,1)} %add_convert_fusion.7), channel_id=1, source_target_pairs={{0,1},{1,0},{2,3},{3,2},{4,5},{5,4},{6,7},{7,6},{8,9},{9,8},{10,11... | collective-permute-start | bytes 1966088 | tf_op jit(solution)/shard_map/ppermute | solution.py:437
  475.9 17.1 %collective-permute-start.56 = (bf16[128,2560]{1,0:T(8,128)(2,1)}, bf16[128,2560]{1,0:T(8,128)(2,1)}, u32[]{:S(2)}, u32[]{:S(2)}) collective-permute-start(bf16[128,2560]{1,0:T(8,128)(2,1)} %get-tuple-element.321), channel_id=1, source_target_pairs={{0,4},{1,5},{2,6},{3,7},{4,0},{5,1},{6,2},{7,3},{8,12},{9,13},{10,... | collective-permute-start | bytes 1966088 | tf_op jit(solution)/shard_map/ppermute | solution.py:437
  477.6 16.9 %collective-permute-start.55 = (bf16[512,1536]{1,0:T(8,128)(2,1)S(1)}, bf16[512,1536]{1,0:T(8,128)(2,1)}, u32[]{:S(2)}, u32[]{:S(2)}) collective-permute-start(bf16[512,1536]{1,0:T(8,128)(2,1)S(1)} %weight_grads.14), channel_id=1, source_target_pairs={{0,2},{1,3},{2,0},{3,1},{4,6},{5,7},{6,4},{7,5},{8,10},{9,11},{10,... | collective-permute-start | bytes 4718600 | tf_op jit(solution)/shard_map/ppermute | solution.py:437
  498.9 17.1 %collective-permute-start.59 = (bf16[64,2560]{1,0:T(8,128)(2,1)S(1)}, bf16[64,2560]{1,0:T(8,128)(2,1)}, u32[]{:S(2)}, u32[]{:S(2)}) collective-permute-start(bf16[64,2560]{1,0:T(8,128)(2,1)S(1)} %slice.438), channel_id=1, source_target_pairs={{0,8},{1,9},{2,10},{3,11},{4,12},{5,13},{6,14},{7,15},{8,0},{9,1},... | collective-permute-start | bytes 983048 | tf_op jit(solution)/shard_map/ppermute | solution.py:437
  500.8 24.6 %collective-permute-start.58 = (bf16[528,1024]{1,0:T(8,128)(2,1)}, bf16[528,1024]{1,0:T(8,128)(2,1)S(1)}, u32[]{:S(2)}, u32[]{:S(2)}) collective-permute-start(bf16[528,1024]{1,0:T(8,128)(2,1)} %get-tuple-element.326), channel_id=1, source_target_pairs={{0,1},{1,0},{2,3},{3,2},{4,5},{5,4},{6,7},{7,6},{8,9},{9,8},{10,11... | collective-permute-start | bytes 3244040 | tf_op jit(solution)/shard_map/ppermute | solution.py:437
  502.0 27.1 %collective-permute-start.60 = (bf16[256,1536]{1,0:T(8,128)(2,1)S(1)}, bf16[256,1536]{1,0:T(8,128)(2,1)S(1)}, u32[]{:S(2)}, u32[]{:S(2)}) collective-permute-start(bf16[256,1536]{1,0:T(8,128)(2,1)S(1)} %pad_maximum_fusion.3), channel_id=1, source_target_pairs={{0,4},{1,5},{2,6},{3,7},{4,0},{5,1},{6,2},{7,3},{8,12},{9,13},{10,... | collective-permute-start | bytes 2359304 | tf_op jit(solution)/shard_map/ppermute | solution.py:437
  533.7 14.4 %collective-permute-start.61 = (bf16[32,2560]{1,0:T(8,128)(2,1)S(1)}, bf16[32,2560]{1,0:T(8,128)(2,1)S(1)}, u32[]{:S(2)}, u32[]{:S(2)}) collective-permute-start(bf16[32,2560]{1,0:T(8,128)(2,1)S(1)} %slice.444), channel_id=1, source_target_pairs={{0,16},{1,17},{2,18},{3,19},{4,20},{5,21},{6,22},{7,23},{8,24},{9,... | collective-permute-start | bytes 491528 | tf_op jit(solution)/shard_map/ppermute | solution.py:437
  533.8 14.4 %collective-permute-start.62 = (bf16[128,1536]{1,0:T(8,128)(2,1)S(1)}, bf16[128,1536]{1,0:T(8,128)(2,1)S(1)}, u32[]{:S(2)}, u32[]{:S(2)}) collective-permute-start(bf16[128,1536]{1,0:T(8,128)(2,1)S(1)} %slice.448), channel_id=1, source_target_pairs={{0,1},{1,0},{2,3},{3,2},{4,5},{5,4},{6,7},{7,6},{8,9},{9,8},{10,11... | collective-permute-start | bytes 1179656 | tf_op jit(solution)/shard_map/ppermute | solution.py:437
  548.3 5.9 %collective-permute-start.63 = (bf16[64,1536]{1,0:T(8,128)(2,1)S(1)}, bf16[64,1536]{1,0:T(8,128)(2,1)S(1)}, u32[]{:S(2)}, u32[]{:S(2)}) collective-permute-start(bf16[64,1536]{1,0:T(8,128)(2,1)S(1)} %slice.494), channel_id=1, source_target_pairs={{0,8},{1,9},{2,10},{3,11},{4,12},{5,13},{6,14},{7,15},{8,0},{9,1},... | collective-permute-start | bytes 589832 | tf_op jit(solution)/shard_map/ppermute | solution.py:437
  554.3 6.6 %collective-permute-start.64 = (bf16[32,1536]{1,0:T(8,128)(2,1)S(1)}, bf16[32,1536]{1,0:T(8,128)(2,1)S(1)}, u32[]{:S(2)}, u32[]{:S(2)}) collective-permute-start(bf16[32,1536]{1,0:T(8,128)(2,1)S(1)} %slice.496), channel_id=1, source_target_pairs={{0,16},{1,17},{2,18},{3,19},{4,20},{5,21},{6,22},{7,23},{8,24},{9,... | collective-permute-start | bytes 294920 | tf_op jit(solution)/shard_map/ppermute | solution.py:437
  (97 other events, 1175.2 us)
Sparse Core Ops, SparseCore 0:
  289.6 62.0 all-gather.2
